TPU v7x, 32 devices: a whole 2x2x4 slice. The times are simulated.
32 devices in a mesh: dp: 8 (over z, x), seq: 4 (over y, core).
Axes of the slice: x: 2, y: 2, z: 4, core: 2. Of those that a mesh axis runs over, the one named last changes fastest.
Arguments:
- tokens: bfloat16 [24, 280, 768], P('dp', 'seq'), may hold values from -6 to 6
- cotangent: bfloat16 [24, 280, 768], P('dp', 'seq'), may hold values from -6 to 6
- text_mask: int32 [24, 40], P('dp'), may hold values from 0 to 1, as said below
- patch_count: int32 [24], P('dp'), may hold values from 100 to 240, as said below
- w_query: bfloat16 [768, 768], P('dp', 'seq'), may hold values from -0.21875 to 0.21875
- w_key: bfloat16 [768, 768], P('dp', 'seq'), may hold values from -0.21875 to 0.21875
- w_value: bfloat16 [768, 768], P('dp', 'seq'), may hold values from -0.21875 to 0.21875
- w_out: bfloat16 [768, 768], P('dp', 'seq'), may hold values from -0.875 to 0.875
- w_up: bfloat16 [768, 3072], P('dp', 'seq'), may hold values from -0.21875 to 0.21875
- w_down: bfloat16 [3072, 768], P('dp', 'seq'), may hold values from -0.109375 to 0.109375
- norm1_gain: bfloat16 [768], P('dp'), may hold values from 0.25 to 1.75
- norm1_bias: bfloat16 [768], P('dp'), may hold values from -4 to 4
- query_bias: bfloat16 [768], P('dp'), may hold values from -4 to 4
- value_bias: bfloat16 [768], P('dp'), may hold values from -3 to 3
- out_bias: bfloat16 [768], P('dp'), may hold values from -4 to 4
- norm2_gain: bfloat16 [768], P('dp'), may hold values from 0.25 to 1.75
- norm2_bias: bfloat16 [768], P('dp'), may hold values from -4 to 4
- up_bias: bfloat16 [3072], P('dp'), may hold values from -6 to 6
- down_bias: bfloat16 [768], P('dp'), may hold values from -4 to 4
Outputs:
- result: bfloat16 [24, 280, 768], P('dp', 'seq')
- input_grad: bfloat16 [24, 280, 768], P('dp', 'seq')
- g_query: float32 [768, 768], P('dp', 'seq')
- g_key: float32 [768, 768], P('dp', 'seq')
- g_value: float32 [768, 768], P('dp', 'seq')
- g_out: float32 [768, 768], P('dp', 'seq')
- g_up: float32 [768, 3072], P('dp', 'seq')
- g_down: float32 [3072, 768], P('dp', 'seq')
- g_norm1_gain: float32 [768], P('dp')
- g_norm1_bias: float32 [768], P('dp')
- g_query_bias: float32 [768], P('dp')
- g_value_bias: float32 [768], P('dp')
- g_out_bias: float32 [768], P('dp')
- g_norm2_gain: float32 [768], P('dp')
- g_norm2_bias: float32 [768], P('dp')
- g_up_bias: float32 [3072], P('dp')
- g_down_bias: float32 [768], P('dp')
Inputs may be any that keep to these rules, and one draw needn't show every extreme that they name: `text_mask`: each item's word slots that hold words are a prefix of its 40 slots, and slot 0 always holds one. `patch_count`: in every aligned block of 3 items one item has all 240 patches.
All inputs are finite; a program needn't handle non-finite values.
Results may differ from a plain program's by a relative error of at most 0.015.
Values may be sent and summed in bfloat16 or wider, within the bound.
No kernel may reach another device: no remote copies, remote signals or barrier semaphores. Data moves between devices by JAX's collectives and lax.ppermute only.
A program may use at most 256 MiB of HBM per device.

v0:
```python
import jax
import jax.numpy as jnp
from jax import lax
from jax.sharding import PartitionSpec as P

HEADS = 12
MICRO = 3


EPS = 1e-05


def product(left, right):
    return jnp.dot(left, right, preferred_element_type=jnp.float32)


def product_back(left, right):
    return lax.dot_general(
        left, right, (((1,), (1,)), ((), ())), preferred_element_type=jnp.float32
    )


def inner_rows(left, right):
    return lax.dot_general(
        left, right, (((0,), (0,)), ((), ())), preferred_element_type=jnp.float32
    )


def column_sum(values):
    return jnp.sum(values.astype(jnp.float32), axis=0)


def layer_norm(values):
    center = values - jnp.mean(values, axis=-1, keepdims=True)
    return center * lax.rsqrt(jnp.mean(center * center, axis=-1, keepdims=True) + EPS)


def norm_affine(values, gain, shift):
    return layer_norm(values) * gain + shift


def gelu_exact(values):
    return jax.nn.gelu(values, approximate=False)


def key_valid(text_mask, patch_count, length):
    rows = lax.iota(jnp.int32, length)
    text_len = text_mask.shape[1]
    onehot = (rows[:, None] == lax.iota(jnp.int32, text_len)[None, :]).astype(jnp.int32)
    text_ok = jnp.sum(text_mask[:, None, :] * onehot[None, :, :], axis=-1) > 0
    patch_ok = rows[None, :] - text_len < patch_count[:, None]
    return jnp.where(rows[None, :] < text_len, text_ok, patch_ok)


def attention_scores(queries, all_keys, valid, heads):
    batch, length, width = all_keys.shape
    key_heads = all_keys.reshape(batch, length, heads, width // heads)
    scale = (width // heads) ** (-0.5)
    scores = (
        jnp.einsum("bqhd,bkhd->bhqk", queries, key_heads, preferred_element_type=jnp.float32)
        * scale
    )
    return jnp.where(valid[:, None, None, :], scores, -1e30)


def fetch_weights(matrices, vectors):
    columns = (
        lax.all_gather(matrices[0], "seq", axis=1, tiled=True),
        lax.all_gather(matrices[1], "seq", axis=1, tiled=True),
        lax.all_gather(matrices[2], "seq", axis=1, tiled=True),
        lax.all_gather(matrices[3], "seq", axis=1, tiled=True),
        lax.all_gather(matrices[4], "seq", axis=1, tiled=True),
        lax.all_gather(matrices[5], "seq", axis=1, tiled=True),
    )
    gathered = (
        lax.all_gather(columns[0], "dp", axis=0, tiled=True),
        lax.all_gather(columns[1], "dp", axis=0, tiled=True),
        lax.all_gather(columns[2], "dp", axis=0, tiled=True),
        lax.all_gather(columns[3], "dp", axis=0, tiled=True),
        lax.all_gather(columns[4], "dp", axis=0, tiled=True),
        lax.all_gather(columns[5], "dp", axis=0, tiled=True),
        lax.all_gather(vectors[0], "dp", axis=0, tiled=True),
        lax.all_gather(vectors[1], "dp", axis=0, tiled=True),
        lax.all_gather(vectors[2], "dp", axis=0, tiled=True),
        lax.all_gather(vectors[3], "dp", axis=0, tiled=True),
        lax.all_gather(vectors[4], "dp", axis=0, tiled=True),
        lax.all_gather(vectors[5], "dp", axis=0, tiled=True),
        lax.all_gather(vectors[6], "dp", axis=0, tiled=True),
        lax.all_gather(vectors[7], "dp", axis=0, tiled=True),
        lax.all_gather(vectors[8], "dp", axis=0, tiled=True),
    )
    return tuple(gathered[:6]) + tuple((piece.astype(jnp.float32) for piece in gathered[6:]))


def reduce_grads(grads):
    row_done = (
        lax.psum_scatter(grads[0], "dp", scatter_dimension=0, tiled=True),
        lax.psum_scatter(grads[1], "dp", scatter_dimension=0, tiled=True),
        lax.psum_scatter(grads[2], "dp", scatter_dimension=0, tiled=True),
        lax.psum_scatter(grads[3], "dp", scatter_dimension=0, tiled=True),
        lax.psum_scatter(grads[4], "dp", scatter_dimension=0, tiled=True),
        lax.psum_scatter(grads[5], "dp", scatter_dimension=0, tiled=True),
        lax.psum_scatter(grads[6], "dp", scatter_dimension=0, tiled=True),
        lax.psum_scatter(grads[7], "dp", scatter_dimension=0, tiled=True),
        lax.psum_scatter(grads[8], "dp", scatter_dimension=0, tiled=True),
        lax.psum_scatter(grads[9], "dp", scatter_dimension=0, tiled=True),
        lax.psum_scatter(grads[10], "dp", scatter_dimension=0, tiled=True),
        lax.psum_scatter(grads[11], "dp", scatter_dimension=0, tiled=True),
        lax.psum_scatter(grads[12], "dp", scatter_dimension=0, tiled=True),
        lax.psum_scatter(grads[13], "dp", scatter_dimension=0, tiled=True),
        lax.psum_scatter(grads[14], "dp", scatter_dimension=0, tiled=True),
    )
    matrix_done = (
        lax.psum_scatter(
            row_done[0].astype(jnp.bfloat16), "seq", scatter_dimension=1, tiled=True
        ).astype(jnp.float32),
        lax.psum_scatter(
            row_done[1].astype(jnp.bfloat16), "seq", scatter_dimension=1, tiled=True
        ).astype(jnp.float32),
        lax.psum_scatter(
            row_done[2].astype(jnp.bfloat16), "seq", scatter_dimension=1, tiled=True
        ).astype(jnp.float32),
        lax.psum_scatter(
            row_done[3].astype(jnp.bfloat16), "seq", scatter_dimension=1, tiled=True
        ).astype(jnp.float32),
        lax.psum_scatter(
            row_done[4].astype(jnp.bfloat16), "seq", scatter_dimension=1, tiled=True
        ).astype(jnp.float32),
        lax.psum_scatter(
            row_done[5].astype(jnp.bfloat16), "seq", scatter_dimension=1, tiled=True
        ).astype(jnp.float32),
    )
    vector_done = lax.psum(
        (
            row_done[6],
            row_done[7],
            row_done[8],
            row_done[9],
            row_done[10],
            row_done[11],
            row_done[12],
            row_done[13],
            row_done[14],
        ),
        "seq",
    )
    return tuple(matrix_done) + tuple(vector_done)


def micro_step(weights, batch_parts):
    (
        w_query,
        w_key,
        w_value,
        w_out,
        w_up,
        w_down,
        norm1_gain,
        norm1_bias,
        query_bias,
        value_bias,
        out_bias,
        norm2_gain,
        norm2_bias,
        up_bias,
        down_bias,
    ) = weights
    tokens, cotangent, text_mask, patch_count = batch_parts
    batch, rows, width = tokens.shape
    heads = HEADS
    head = width // heads
    scale = head ** (-0.5)
    flat = batch * rows
    length = rows * lax.axis_size("seq")
    valid = key_valid(text_mask, patch_count, length)
    inputs = tokens.astype(jnp.float32)
    normed1_full, norm1_back = jax.vjp(norm_affine, inputs, norm1_gain, norm1_bias)
    normed1 = normed1_full.astype(jnp.bfloat16).reshape(flat, width)
    queries = (
        (product(normed1, w_query) + query_bias)
        .astype(jnp.bfloat16)
        .reshape(batch, rows, heads, head)
    )
    keys = product(normed1, w_key).astype(jnp.bfloat16).reshape(batch, rows, width)
    values = (
        (product(normed1, w_value) + value_bias).astype(jnp.bfloat16).reshape(batch, rows, width)
    )
    all_keys, all_values = (
        lax.all_gather(keys, "seq", axis=1, tiled=True),
        lax.all_gather(values, "seq", axis=1, tiled=True),
    )
    scores = attention_scores(queries, all_keys, valid, heads)
    top = jnp.max(scores, axis=-1, keepdims=True)
    expo = jnp.exp(scores - top)
    total = jnp.sum(expo, axis=-1, keepdims=True)
    log_total = top + jnp.log(total)
    probs = (expo / total).astype(jnp.bfloat16)
    value_heads = all_values.reshape(batch, length, heads, head)
    mixed = jnp.einsum("bhqk,bkhd->bqhd", probs, value_heads, preferred_element_type=jnp.float32)
    mixed = mixed.astype(jnp.bfloat16).reshape(flat, width)
    attended = (product(mixed, w_out) + out_bias).reshape(batch, rows, width)
    resid = inputs + attended
    normed2_full, norm2_back = jax.vjp(norm_affine, resid, norm2_gain, norm2_bias)
    normed2 = normed2_full.astype(jnp.bfloat16).reshape(flat, width)
    hidden = product(normed2, w_up) + up_bias
    gelu_vals, gelu_back = jax.vjp(gelu_exact, hidden)
    active = gelu_vals.astype(jnp.bfloat16)
    branch = product(active, w_down) + down_bias
    result = (resid + branch.reshape(batch, rows, width)).astype(jnp.bfloat16)
    grad_output = cotangent.astype(jnp.float32).reshape(flat, width)
    grad_branch = grad_output.astype(jnp.bfloat16)
    g_down = inner_rows(active, grad_branch)
    g_down_bias = column_sum(grad_branch)
    grad_active = product_back(grad_branch, w_down)
    grad_hidden = gelu_back(grad_active)[0].astype(jnp.bfloat16)
    g_up = inner_rows(normed2, grad_hidden)
    g_up_bias = column_sum(grad_hidden)
    grad_normed2 = product_back(grad_hidden, w_up).reshape(batch, rows, width)
    grad_resid, g_norm2_gain, g_norm2_bias = norm2_back(grad_normed2)
    grad_resid = grad_resid + grad_output.reshape(batch, rows, width)
    grad_attended = grad_resid.astype(jnp.bfloat16).reshape(flat, width)
    g_out = inner_rows(mixed, grad_attended)
    g_out_bias = column_sum(grad_attended)
    grad_mixed = (
        product_back(grad_attended, w_out).astype(jnp.bfloat16).reshape(batch, rows, heads, head)
    )
    back_keys, back_values = (
        lax.all_gather(keys, "seq", axis=1, tiled=True),
        lax.all_gather(values, "seq", axis=1, tiled=True),
    )
    scores = attention_scores(queries, back_keys, valid, heads)
    probs_full = jnp.exp(scores - log_total)
    probs_low = probs_full.astype(jnp.bfloat16)
    value_heads = back_values.reshape(batch, length, heads, head)
    key_heads = back_keys.reshape(batch, length, heads, head)
    grad_probs = jnp.einsum(
        "bqhd,bkhd->bhqk", grad_mixed, value_heads, preferred_element_type=jnp.float32
    )
    grad_values_all = jnp.einsum(
        "bhqk,bqhd->bkhd", probs_low, grad_mixed, preferred_element_type=jnp.float32
    ).reshape(batch, length, width)
    grad_scores = probs_full * (
        grad_probs - jnp.sum(probs_full * grad_probs, axis=-1, keepdims=True)
    )
    grad_scores = grad_scores.astype(jnp.bfloat16)
    grad_queries = jnp.einsum(
        "bhqk,bkhd->bqhd", grad_scores, key_heads, preferred_element_type=jnp.float32
    )
    grad_queries = (grad_queries * scale).astype(jnp.bfloat16).reshape(flat, width)
    grad_keys_all = jnp.einsum(
        "bhqk,bqhd->bkhd", grad_scores, queries, preferred_element_type=jnp.float32
    )
    grad_keys_all = (grad_keys_all * scale).reshape(batch, length, width)
    grad_keys, grad_values = (
        lax.psum_scatter(grad_keys_all, "seq", scatter_dimension=1, tiled=True),
        lax.psum_scatter(grad_values_all, "seq", scatter_dimension=1, tiled=True),
    )
    grad_keys = grad_keys.astype(jnp.bfloat16).reshape(flat, width)
    grad_values = grad_values.astype(jnp.bfloat16).reshape(flat, width)
    g_query = inner_rows(normed1, grad_queries)
    g_query_bias = column_sum(grad_queries)
    g_key = inner_rows(normed1, grad_keys)
    g_value = inner_rows(normed1, grad_values)
    g_value_bias = column_sum(grad_values)
    grad_normed1 = (
        product_back(grad_queries, w_query)
        + product_back(grad_keys, w_key)
        + product_back(grad_values, w_value)
    ).reshape(batch, rows, width)
    grad_inputs, g_norm1_gain, g_norm1_bias = norm1_back(grad_normed1)
    input_grad = (grad_resid + grad_inputs).astype(jnp.bfloat16)
    grads = (
        g_query,
        g_key,
        g_value,
        g_out,
        g_up,
        g_down,
        g_norm1_gain,
        g_norm1_bias,
        g_query_bias,
        g_value_bias,
        g_out_bias,
        g_norm2_gain,
        g_norm2_bias,
        g_up_bias,
        g_down_bias,
    )
    return (result, input_grad, grads)


def add_tuples(first, second):
    return tuple((left + right for left, right in zip(first, second)))


def local(
    tokens,
    cotangent,
    text_mask,
    patch_count,
    w_query,
    w_key,
    w_value,
    w_out,
    w_up,
    w_down,
    norm1_gain,
    norm1_bias,
    query_bias,
    value_bias,
    out_bias,
    norm2_gain,
    norm2_bias,
    up_bias,
    down_bias,
):
    matrices = (w_query, w_key, w_value, w_out, w_up, w_down)
    vectors = (
        norm1_gain,
        norm1_bias,
        query_bias,
        value_bias,
        out_bias,
        norm2_gain,
        norm2_bias,
        up_bias,
        down_bias,
    )
    per_batch = tokens.shape[0] // MICRO
    results = []
    input_grads = []
    shards = None
    for index in range(MICRO):
        weights = fetch_weights(matrices, vectors)
        begin = index * per_batch
        finish = begin + per_batch
        result, input_grad, grads = micro_step(
            weights,
            (
                tokens[begin:finish],
                cotangent[begin:finish],
                text_mask[begin:finish],
                patch_count[begin:finish],
            ),
        )
        results.append(result)
        input_grads.append(input_grad)
        reduced = reduce_grads(grads)
        shards = reduced if shards is None else add_tuples(shards, reduced)
    result = jnp.concatenate(results, axis=0)
    input_grad = jnp.concatenate(input_grads, axis=0)
    return (
        result,
        input_grad,
        shards[0],
        shards[1],
        shards[2],
        shards[3],
        shards[4],
        shards[5],
        shards[6],
        shards[7],
        shards[8],
        shards[9],
        shards[10],
        shards[11],
        shards[12],
        shards[13],
        shards[14],
    )


def solution(mesh):
    return jax.shard_map(
        local,
        mesh=mesh,
        in_specs=(
            P("dp", "seq", None),
            P("dp", "seq", None),
            P("dp", None),
            P("dp"),
            P("dp", "seq"),
            P("dp", "seq"),
            P("dp", "seq"),
            P("dp", "seq"),
            P("dp", "seq"),
            P("dp", "seq"),
            P("dp"),
            P("dp"),
            P("dp"),
            P("dp"),
            P("dp"),
            P("dp"),
            P("dp"),
            P("dp"),
            P("dp"),
        ),
        out_specs=(
            P("dp", "seq", None),
            P("dp", "seq", None),
            P("dp", "seq"),
            P("dp", "seq"),
            P("dp", "seq"),
            P("dp", "seq"),
            P("dp", "seq"),
            P("dp", "seq"),
            P("dp"),
            P("dp"),
            P("dp"),
            P("dp"),
            P("dp"),
            P("dp"),
            P("dp"),
            P("dp"),
            P("dp"),
        ),
        check_vma=False,
    )
```

profile of v0, /device:TPU:5, one launch (start us, length us, event | category | flops | bytes accessed | tf_op | source)
XLA Modules:
  0.0 3318.2 jit_solution(1509533341621631868)
XLA Ops:
  8.2 6.1 all_gather.60
  16.1 5.6 all_gather.56
  22.7 5.6 all_gather.63
  29.3 5.6 all_gather.66
  35.9 8.2 all_gather.71
  44.3 8.1 all_gather.74
  56.8 30.6 all-reduce.27
  87.5 21.3 all-gather.8
  118.8 17.7 all-gather.11
  138.9 6.8 all-gather.9
  149.4 6.8 all-gather.12
  159.8 7.3 all-gather.10
  176.0 7.2 all-gather.26.cloned.1.call-done
  192.6 71.4 %all-gather.28.cloned.1.call-done = bf16[768,3072]{1,0:T(8,128)(2,1)} async-done(((bf16[96,3072]{1,0:T(8,128)(2,1)}), bf16[768,3072]{1,0:T(8,128)(2,1)}) %all-gather.28.cloned.1.call-update) | async-done | bytes 4718608 | tf_op jit(solution)/shard_map/all_gather | solution.py:80
  264.1 4.3 convolution_add_fusion.1
  268.4 77.4 %all-gather.30.cloned.1.call-done = bf16[3072,768]{0,1:T(8,128)(2,1)} async-done(((bf16[384,768]{0,1:T(8,128)(2,1)}), bf16[3072,768]{0,1:T(8,128)(2,1)}) %all-gather.30.cloned.1.call-update) | async-done | bytes 4718608 | tf_op jit(solution)/shard_map/all_gather | solution.py:81
  345.8 6.1 convert_reduce_fusion.1
  402.2 466.0 %all-reduce.30 = (bf16[1,280,768]{2,0,1:T(2,128)(2,1)}, bf16[1,280,768]{2,0,1:T(2,128)(2,1)}, bf16[1,280,768]{2,0,1:T(2,128)(2,1)}, bf16[1,280,768]{2,0,1:T(2,128)(2,1)}) all-reduce(f32[1,280,768]{2,0,1:T(1,128)} %copy.184, f32[1,280,768]{2,0,1:T(1,128)} %copy.182, ...), channel_id=29, replica_groups=mesh['dp'=8,'seq'=4] {'seq'}, use_global_device_ids=true, to_apply=%region_32.33.clone | all-reduce | flops 860160 | bytes 5160960
  886.9 7.3 all-gather.6
  900.1 7.3 all-gather.7
  924.3 6.2 convert_reduce_fusion.2
  949.5 236.2 %all-reduce.31 = (bf16[1,280,768]{2,0,1:T(2,128)(2,1)}, bf16[1,280,768]{2,0,1:T(2,128)(2,1)}) all-reduce(f32[1,280,768]{2,0,1:T(1,128)} %copy.179, f32[1,280,768]{2,0,1:T(1,128)} %copy.177), channel_id=27, replica_groups=mesh['dp'=8,'seq'=4] {'seq'}, use_global_device_ids=true, to_apply=%region_25.26.clone | all-reduce | flops 430080 | bytes 2580480
  1221.7 7.9 fusion.138
  1229.8 8.0 fusion.126
  1237.9 8.0 fusion.132
  1247.0 5.1 fusion.195
  1253.1 6.2 fusion.192
  1260.2 6.2 fusion.189
  1272.2 55.3 %reduce-scatter.73.cloned.1.call-done = f32[96,768]{1,0:T(8,128)} async-done(((f32[768,768]{1,0:T(8,128)}), f32[96,768]{1,0:T(8,128)}) %reduce-scatter.73.cloned.1.call-update) | async-done | bytes 294928 | tf_op jit(solution)/shard_map/reduce_scatter | solution.py:98
  1329.4 69.7 %reduce-scatter.81.cloned.1.call-done = f32[96,768]{1,0:T(8,128)} async-done(((f32[768,768]{1,0:T(8,128)}), f32[96,768]{1,0:T(8,128)}) %reduce-scatter.81.cloned.1.call-update) | async-done | bytes 294928 | tf_op jit(solution)/shard_map/reduce_scatter | solution.py:99
  1400.9 69.6 %reduce-scatter.83.cloned.1.call-done = f32[96,768]{1,0:T(8,128)} async-done(((f32[768,768]{1,0:T(8,128)}), f32[96,768]{1,0:T(8,128)}) %reduce-scatter.83.cloned.1.call-update) | async-done | bytes 294928 | tf_op jit(solution)/shard_map/reduce_scatter | solution.py:99
  1472.3 69.7 %reduce-scatter.75.cloned.1.call-done = f32[96,768]{1,0:T(8,128)} async-done(((f32[768,768]{1,0:T(8,128)}), f32[96,768]{1,0:T(8,128)}) %reduce-scatter.75.cloned.1.call-update) | async-done | bytes 294928 | tf_op jit(solution)/shard_map/reduce_scatter | solution.py:98
  1543.9 69.6 %reduce-scatter.77.cloned.1.call-done = f32[96,768]{1,0:T(8,128)} async-done(((f32[768,768]{1,0:T(8,128)}), f32[96,768]{1,0:T(8,128)}) %reduce-scatter.77.cloned.1.call-update) | async-done | bytes 294928 | tf_op jit(solution)/shard_map/reduce_scatter | solution.py:98
  1615.4 69.6 %reduce-scatter.71.cloned.1.call-done = f32[96,768]{1,0:T(8,128)} async-done(((f32[768,768]{1,0:T(8,128)}), f32[96,768]{1,0:T(8,128)}) %reduce-scatter.71.cloned.1.call-update) | async-done | bytes 294928 | tf_op jit(solution)/shard_map/reduce_scatter | solution.py:97
  1686.9 69.5 %reduce-scatter.69.cloned.1.call-done = f32[96,768]{1,0:T(8,128)} async-done(((f32[768,768]{1,0:T(8,128)}), f32[96,768]{1,0:T(8,128)}) %reduce-scatter.69.cloned.1.call-update) | async-done | bytes 294928 | tf_op jit(solution)/shard_map/reduce_scatter | solution.py:97
  1758.5 69.3 %reduce-scatter.67.cloned.1.call-done = f32[96,768]{1,0:T(8,128)} async-done(((f32[768,768]{1,0:T(8,128)}), f32[96,768]{1,0:T(8,128)}) %reduce-scatter.67.cloned.1.call-update) | async-done | bytes 294928 | tf_op jit(solution)/shard_map/reduce_scatter | solution.py:97
  1831.0 68.2 %reduce-scatter.85.cloned.1.call-done = f32[96,768]{1,0:T(8,128)} async-done(((f32[768,768]{1,0:T(8,128)}), f32[96,768]{1,0:T(8,128)}) %reduce-scatter.85.cloned.1.call-update) | async-done | bytes 294928 | tf_op jit(solution)/shard_map/reduce_scatter | solution.py:100
  1901.1 6.4 fusion.25
  1907.5 159.0 %reduce-scatter.103.cloned.1.call-done = f32[384,768]{1,0:T(8,128)} async-done(((f32[3072,768]{1,0:T(8,128)}), f32[384,768]{1,0:T(8,128)}) %reduce-scatter.103.cloned.1.call-update) | async-done | bytes 1179664 | tf_op jit(solution)/shard_map/reduce_scatter | solution.py:102
  2070.8 6.4 fusion.24
  2077.2 6.1 fusion.26
  2083.4 149.0 %reduce-scatter.107.cloned.1.call-done = f32[384,768]{1,0:T(8,128)} async-done(((f32[3072,768]{1,0:T(8,128)}), f32[384,768]{1,0:T(8,128)}) %reduce-scatter.107.cloned.1.call-update) | async-done | bytes 1179664 | tf_op jit(solution)/shard_map/reduce_scatter | solution.py:102
  2239.5 159.0 %reduce-scatter.105.cloned.1.call-done = f32[384,768]{1,0:T(8,128)} async-done(((f32[3072,768]{1,0:T(8,128)}), f32[384,768]{1,0:T(8,128)}) %reduce-scatter.105.cloned.1.call-update) | async-done | bytes 1179664 | tf_op jit(solution)/shard_map/reduce_scatter | solution.py:102
  2401.6 163.1 %reduce-scatter.91.cloned.1.call-done = f32[96,3072]{1,0:T(8,128)} async-done(((f32[768,3072]{1,0:T(8,128)}), f32[96,3072]{1,0:T(8,128)}) %reduce-scatter.91.cloned.1.call-update) | async-done | bytes 1179664 | tf_op jit(solution)/shard_map/reduce_scatter | solution.py:101
  2567.4 163.5 %reduce-scatter.95.cloned.1.call-done = f32[96,3072]{1,0:T(8,128)} async-done(((f32[768,3072]{1,0:T(8,128)}), f32[96,3072]{1,0:T(8,128)}) %reduce-scatter.95.cloned.1.call-update) | async-done | bytes 1179664 | tf_op jit(solution)/shard_map/reduce_scatter | solution.py:101
  2733.9 163.0 %reduce-scatter.99.cloned.1.call-done = f32[96,3072]{1,0:T(8,128)} async-done(((f32[768,3072]{1,0:T(8,128)}), f32[96,3072]{1,0:T(8,128)}) %reduce-scatter.99.cloned.1.call-update) | async-done | bytes 1179664 | tf_op jit(solution)/shard_map/reduce_scatter | solution.py:101
  2899.9 28.6 all-reduce.23
  2929.2 13.3 all-reduce.24
  2944.3 16.9 reduce-scatter.121.cloned.1.call-done
  2962.1 21.3 reduce-scatter.115.cloned.1.call-done
  2984.3 21.3 reduce-scatter.123.cloned.1.call-done
  3006.6 21.2 reduce-scatter.125.cloned.1.call-done
  3028.6 21.3 reduce-scatter.117.cloned.1.call-done
  3050.9 21.3 reduce-scatter.119.cloned.1.call-done
  3073.1 21.7 reduce-scatter.113.cloned.1.call-done
  3095.7 21.9 reduce-scatter.111.cloned.1.call-done
  3118.5 21.3 reduce-scatter.109.cloned.1.call-done
  3140.8 21.2 reduce-scatter.127.cloned.1.call-done
  3165.5 21.1 reduce-scatter.133.cloned.1.call-done
  3187.6 23.6 reduce-scatter.137.cloned.1.call-done
  3212.2 23.4 reduce-scatter.135.cloned.1.call-done
  3237.6 22.6 reduce-scatter.93.cloned.1.call-done
  3260.2 24.6 reduce-scatter.97.cloned.1.call-done
  3284.8 24.6 reduce-scatter.101.cloned.1.call-done
  (735 shorter events, 260.1 us)
Async XLA Ops:
  7.2 106.7 %all-gather.22.cloned.1.call-start = ((), (), s32[]{:S(2)}) async-start(), calls=%async_computation.37 | async-start | bytes 1327104 | tf_op jit(solution)/shard_map/all_gather | solution.py:76
  15.1 102.0 %all-gather.20.cloned.1.call-start = ((), (), s32[]{:S(2)}) async-start(), calls=%async_computation.36 | async-start | bytes 1327104 | tf_op jit(solution)/shard_map/all_gather | solution.py:78
  22.5 125.3 %all-gather.24.cloned.1.call-start = ((), (), s32[]{:S(2)}) async-start(), calls=%async_computation.38 | async-start | bytes 1327104 | tf_op jit(solution)/shard_map/all_gather | solution.py:77
  29.1 154.0 %all-gather.26.cloned.1.call-start = ((), (), s32[]{:S(2)}) async-start(), calls=%async_computation.39 | async-start | bytes 1327104 | tf_op jit(solution)/shard_map/all_gather | solution.py:79
  35.9 228.2 %all-gather.28.cloned.1.call-start = ((), (), s32[]{:S(2)}) async-start(), calls=%async_computation.40 | async-start | bytes 5308416 | tf_op jit(solution)/shard_map/all_gather | solution.py:80
  44.2 301.6 %all-gather.30.cloned.1.call-start = ((), (), s32[]{:S(2)}) async-start(), calls=%async_computation.41 | async-start | bytes 5308416 | tf_op jit(solution)/shard_map/all_gather | solution.py:81
  52.4 1214.1 %reduce-scatter.87.cloned.1.call-start = ((), (), s32[]{:S(2)}) async-start(), calls=%async_computation.52 | async-start | bytes 2654208 | tf_op jit(solution)/shard_map/reduce_scatter | solution.py:100
  873.7 394.7 %reduce-scatter.89.cloned.1.call-start = ((), (), s32[]{:S(2)}) async-start(), calls=%async_computation.53 | async-start | bytes 2654208 | tf_op jit(solution)/shard_map/reduce_scatter | solution.py:100
  920.6 349.7 %reduce-scatter.79.cloned.1.call-start = ((), (), s32[]{:S(2)}) async-start(), calls=%async_computation.48 | async-start | bytes 2654208 | tf_op jit(solution)/shard_map/reduce_scatter | solution.py:99
  949.5 238.0 %copy-start.6 = (bf16[3,70,768]{2,1,0:T(8,128)(2,1)S(1)}, bf16[3,70,768]{2,1,0:T(8,128)(2,1)}, u32[]{:S(2)}) copy-start(bf16[3,70,768]{2,1,0:T(8,128)(2,1)} %param.19) | copy-start | bytes 967684
  949.5 238.0 %copy-start.111 = (f32[70]{0:T(128)S(1)}, f32[70]{0:T(128)}, u32[]{:S(2)}) copy-start(f32[70]{0:T(128)} %broadcast_multiply_fusion.5) | copy-start | bytes 844
  949.5 238.0 %copy-start.113 = (f32[70]{0:T(128)S(1)}, f32[70]{0:T(128)}, u32[]{:S(2)}) copy-start(f32[70]{0:T(128)} %copy-done.112) | copy-start | bytes 844
  1189.5 138.0 %reduce-scatter.73.cloned.1.call-start = ((), (), s32[]{:S(2)}) async-start(), calls=%async_computation.45 | async-start | bytes 2654208 | tf_op jit(solution)/shard_map/reduce_scatter | solution.py:98
  1193.5 205.6 %reduce-scatter.81.cloned.1.call-start = ((), (), s32[]{:S(2)}) async-start(), calls=%async_computation.49 | async-start | bytes 2654208 | tf_op jit(solution)/shard_map/reduce_scatter | solution.py:99
  1197.1 273.3 %reduce-scatter.83.cloned.1.call-start = ((), (), s32[]{:S(2)}) async-start(), calls=%async_computation.50 | async-start | bytes 2654208 | tf_op jit(solution)/shard_map/reduce_scatter | solution.py:99
  1200.7 341.4 %reduce-scatter.75.cloned.1.call-start = ((), (), s32[]{:S(2)}) async-start(), calls=%async_computation.46 | async-start | bytes 2654208 | tf_op jit(solution)/shard_map/reduce_scatter | solution.py:98
  1203.7 409.8 %reduce-scatter.77.cloned.1.call-start = ((), (), s32[]{:S(2)}) async-start(), calls=%async_computation.47 | async-start | bytes 2654208 | tf_op jit(solution)/shard_map/reduce_scatter | solution.py:98
  1206.7 478.3 %reduce-scatter.71.cloned.1.call-start = ((), (), s32[]{:S(2)}) async-start(), calls=%async_computation.44 | async-start | bytes 2654208 | tf_op jit(solution)/shard_map/reduce_scatter | solution.py:97
  1209.8 546.6 %reduce-scatter.69.cloned.1.call-start = ((), (), s32[]{:S(2)}) async-start(), calls=%async_computation.43 | async-start | bytes 2654208 | tf_op jit(solution)/shard_map/reduce_scatter | solution.py:97
  1212.8 615.0 %reduce-scatter.67.cloned.1.call-start = ((), (), s32[]{:S(2)}) async-start(), calls=%async_computation.42 | async-start | bytes 2654208 | tf_op jit(solution)/shard_map/reduce_scatter | solution.py:97
  1217.7 681.5 %reduce-scatter.85.cloned.1.call-start = ((), (), s32[]{:S(2)}) async-start(), calls=%async_computation.51 | async-start | bytes 2654208 | tf_op jit(solution)/shard_map/reduce_scatter | solution.py:100
  1220.7 845.7 %reduce-scatter.103.cloned.1.call-start = ((), (), s32[]{:S(2)}) async-start(), calls=%async_computation.60 | async-start | bytes 10616832 | tf_op jit(solution)/shard_map/reduce_scatter | solution.py:102
  1229.6 1002.8 %reduce-scatter.107.cloned.1.call-start = ((), (), s32[]{:S(2)}) async-start(), calls=%async_computation.62 | async-start | bytes 10616832 | tf_op jit(solution)/shard_map/reduce_scatter | solution.py:102
  1237.8 1160.7 %reduce-scatter.105.cloned.1.call-start = ((), (), s32[]{:S(2)}) async-start(), calls=%async_computation.61 | async-start | bytes 10616832 | tf_op jit(solution)/shard_map/reduce_scatter | solution.py:102
  1245.9 1318.8 %reduce-scatter.91.cloned.1.call-start = ((), (), s32[]{:S(2)}) async-start(), calls=%async_computation.54 | async-start | bytes 10616832 | tf_op jit(solution)/shard_map/reduce_scatter | solution.py:101
  1252.2 1478.7 %reduce-scatter.95.cloned.1.call-start = ((), (), s32[]{:S(2)}) async-start(), calls=%async_computation.56 | async-start | bytes 10616832 | tf_op jit(solution)/shard_map/reduce_scatter | solution.py:101
  1259.3 1637.6 %reduce-scatter.99.cloned.1.call-start = ((), (), s32[]{:S(2)}) async-start(), calls=%async_computation.58 | async-start | bytes 10616832 | tf_op jit(solution)/shard_map/reduce_scatter | solution.py:101
  1266.4 1676.1 %reduce-scatter.129.cloned.1.call-start = ((), (), s32[]{:S(2)}) async-start(), calls=%async_computation.73 | async-start | bytes 245760
  1268.3 1675.1 %reduce-scatter.131.cloned.1.call-start = ((), (), s32[]{:S(2)}) async-start(), calls=%async_computation.74 | async-start | bytes 245760
  1270.2 1691.0 %reduce-scatter.121.cloned.1.call-start = ((), (), s32[]{:S(2)}) async-start(), calls=%async_computation.69 | async-start | bytes 245760
  1272.1 1711.3 %reduce-scatter.115.cloned.1.call-start = ((), (), s32[]{:S(2)}) async-start(), calls=%async_computation.66 | async-start | bytes 245760
  1329.3 1676.4 %reduce-scatter.123.cloned.1.call-start = ((), (), s32[]{:S(2)}) async-start(), calls=%async_computation.70 | async-start | bytes 245760
  1400.9 1626.9 %reduce-scatter.125.cloned.1.call-start = ((), (), s32[]{:S(2)}) async-start(), calls=%async_computation.71 | async-start | bytes 245760
  1472.3 1577.7 %reduce-scatter.117.cloned.1.call-start = ((), (), s32[]{:S(2)}) async-start(), calls=%async_computation.67 | async-start | bytes 245760
  1543.8 1528.4 %reduce-scatter.119.cloned.1.call-start = ((), (), s32[]{:S(2)}) async-start(), calls=%async_computation.68 | async-start | bytes 245760
  1615.3 1479.5 %reduce-scatter.113.cloned.1.call-start = ((), (), s32[]{:S(2)}) async-start(), calls=%async_computation.65 | async-start | bytes 245760
  1686.8 1430.8 %reduce-scatter.111.cloned.1.call-start = ((), (), s32[]{:S(2)}) async-start(), calls=%async_computation.64 | async-start | bytes 245760
  1758.2 1381.6 %reduce-scatter.109.cloned.1.call-start = ((), (), s32[]{:S(2)}) async-start(), calls=%async_computation.63 | async-start | bytes 245760
  1829.7 1332.3 %reduce-scatter.127.cloned.1.call-start = ((), (), s32[]{:S(2)}) async-start(), calls=%async_computation.72 | async-start | bytes 245760
  1901.1 1285.5 %reduce-scatter.133.cloned.1.call-start = ((), (), s32[]{:S(2)}) async-start(), calls=%async_computation.75 | async-start | bytes 737280
  2070.7 1140.4 %reduce-scatter.137.cloned.1.call-start = ((), (), s32[]{:S(2)}) async-start(), calls=%async_computation.77 | async-start | bytes 737280
  2234.9 1000.7 %reduce-scatter.135.cloned.1.call-start = ((), (), s32[]{:S(2)}) async-start(), calls=%async_computation.76 | async-start | bytes 737280
  2401.1 859.2 %reduce-scatter.93.cloned.1.call-start = ((), (), s32[]{:S(2)}) async-start(), calls=%async_computation.55 | async-start | bytes 737280 | tf_op jit(solution)/shard_map/reduce_scatter | solution.py:126
  2401.6 165.6 %copy-start.135 = (f32[768]{0:T(1024)S(1)}, f32[768]{0:T(1024)}, u32[]{:S(2)}) copy-start(f32[768]{0:T(1024)} %get-tuple-element.181) | copy-start | bytes 9220
  2401.6 165.6 %copy-start.136 = (f32[768]{0:T(1024)S(1)}, f32[768]{0:T(1024)}, u32[]{:S(2)}) copy-start(f32[768]{0:T(1024)} %get-tuple-element.194) | copy-start | bytes 9220
  2401.6 165.6 %copy-start.142 = (f32[768]{0:T(1024)S(1)}, f32[768]{0:T(1024)}, u32[]{:S(2)}) copy-start(f32[768]{0:T(1024)} %get-tuple-element.192) | copy-start | bytes 9220
  2401.6 165.6 %copy-start.139 = (f32[768]{0:T(1024)S(1)}, f32[768]{0:T(1024)}, u32[]{:S(2)}) copy-start(f32[768]{0:T(1024)} %get-tuple-element.136) | copy-start | bytes 9220
  2401.6 165.6 %copy-start.140 = (f32[768]{0:T(1024)S(1)}, f32[768]{0:T(1024)}, u32[]{:S(2)}) copy-start(f32[768]{0:T(1024)} %get-tuple-element.137) | copy-start | bytes 9220
  2401.6 165.6 %copy-start.141 = (f32[768]{0:T(1024)S(1)}, f32[768]{0:T(1024)}, u32[]{:S(2)}) copy-start(f32[768]{0:T(1024)} %get-tuple-element.138) | copy-start | bytes 9220
  2566.9 717.9 %reduce-scatter.97.cloned.1.call-start = ((), (), s32[]{:S(2)}) async-start(), calls=%async_computation.57 | async-start | bytes 737280 | tf_op jit(solution)/shard_map/reduce_scatter | solution.py:126
  2567.1 166.3 %copy-start.54 = (bf16[1,70,768]{2,0,1:T(2,128)(2,1)S(1)}, bf16[1,70,768]{2,0,1:T(2,128)(2,1)}, u32[]{:S(2)}) copy-start(bf16[1,70,768]{2,0,1:T(2,128)(2,1)} %copy-done.52) | copy-start | bytes 322564
  2567.3 166.2 %copy-start.137 = (f32[768]{0:T(1024)S(1)}, f32[768]{0:T(1024)}, u32[]{:S(2)}) copy-start(f32[768]{0:T(1024)} %get-tuple-element.230) | copy-start | bytes 9220
  2567.3 166.2 %copy-start.117 = (f32[12,64]{1,0:T(8,128)S(1)}, f32[12,64]{1,0:T(8,128)}, u32[]{:S(2)}) copy-start(f32[12,64]{1,0:T(8,128)} %get-tuple-element.236) | copy-start | bytes 9220
  2567.3 166.2 %copy-start.118 = (f32[12,64]{1,0:T(8,128)S(1)}, f32[12,64]{1,0:T(8,128)}, u32[]{:S(2)}) copy-start(f32[12,64]{1,0:T(8,128)} %get-tuple-element.232) | copy-start | bytes 9220
  2567.3 166.2 %copy-start.119 = (f32[12,64]{1,0:T(8,128)S(1)}, f32[12,64]{1,0:T(8,128)}, u32[]{:S(2)}) copy-start(f32[12,64]{1,0:T(8,128)} %get-tuple-element.234) | copy-start | bytes 9220
  2567.3 166.2 %copy-start.151 = (f32[3072]{0:T(1024)S(1)}, f32[3072]{0:T(1024)}, u32[]{:S(2)}) copy-start(f32[3072]{0:T(1024)} %get-tuple-element.244) | copy-start | bytes 36868
  2567.3 166.2 %copy-start.152 = (f32[3072]{0:T(1024)S(1)}, f32[3072]{0:T(1024)}, u32[]{:S(2)}) copy-start(f32[3072]{0:T(1024)} %get-tuple-element.240) | copy-start | bytes 36868
  2567.3 166.2 %copy-start.153 = (f32[3072]{0:T(1024)S(1)}, f32[3072]{0:T(1024)}, u32[]{:S(2)}) copy-start(f32[3072]{0:T(1024)} %get-tuple-element.242) | copy-start | bytes 36868
  2567.4 166.2 %copy-start.41 = (f32[1,70,768]{2,1,0:T(8,128)S(1)}, f32[1,70,768]{2,1,0:T(8,128)}, u32[]{:S(2)}) copy-start(f32[1,70,768]{2,1,0:T(8,128)} %copy-done.40) | copy-start | bytes 645124
  2567.4 166.2 %copy-start.45 = (f32[1,70,768]{2,1,0:T(8,128)S(1)}, f32[1,70,768]{2,1,0:T(8,128)}, u32[]{:S(2)}) copy-start(f32[1,70,768]{2,1,0:T(8,128)} %copy-done.44) | copy-start | bytes 645124
  2567.4 166.2 %copy-start.124 = (f32[70]{0:T(128)S(1)}, f32[70]{0:T(128)}, u32[]{:S(2)}) copy-start(f32[70]{0:T(128)} %copy-done.122) | copy-start | bytes 844
  2567.4 166.2 %copy-start.158 = (f32[70]{0:T(128)S(1)}, f32[70]{0:T(128)}, u32[]{:S(2)}) copy-start(f32[70]{0:T(128)} %copy-done.157) | copy-start | bytes 844
  2567.4 166.2 %copy-start.160 = (f32[70]{0:T(128)S(1)}, f32[70]{0:T(128)}, u32[]{:S(2)}) copy-start(f32[70]{0:T(128)} %copy-done.159) | copy-start | bytes 844
  2733.0 576.4 %reduce-scatter.101.cloned.1.call-start = ((), (), s32[]{:S(2)}) async-start(), calls=%async_computation.59 | async-start | bytes 737280 | tf_op jit(solution)/shard_map/reduce_scatter | solution.py:126
  (169 other events, 2473.8 us)
Sparse Core Ops, SparseCore 0:
  15.2 40.5 all-gather.21
  58.5 39.9 all-gather.19
  101.3 39.8 all-gather.23
  143.3 39.8 all-gather.25
  185.1 78.8 all-gather.27
  266.0 79.7 all-gather.29
  873.8 65.7 reduce-scatter.86
  943.1 68.0 reduce-scatter.88
  1189.6 66.3 reduce-scatter.78
  1259.4 68.0 reduce-scatter.72
  1331.0 68.0 reduce-scatter.80
  1402.4 68.0 reduce-scatter.82
  1474.0 68.0 reduce-scatter.74
  1545.4 68.0 reduce-scatter.76
  1616.8 68.1 reduce-scatter.70
  1688.4 68.0 reduce-scatter.68
  1759.8 68.0 reduce-scatter.66
  1831.2 68.0 reduce-scatter.84
  1902.8 163.6 reduce-scatter.102
  2069.9 162.4 reduce-scatter.106
  2236.0 162.5 reduce-scatter.104
  2402.1 162.5 reduce-scatter.90
  2568.3 162.5 reduce-scatter.94
  2734.3 162.5 reduce-scatter.98
  2899.4 17.6 reduce-scatter.128
  2919.3 19.7 reduce-scatter.130
  2941.4 19.7 reduce-scatter.120
  2963.7 19.7 reduce-scatter.114
  2985.9 19.7 reduce-scatter.122
  3008.0 19.7 reduce-scatter.124
  3030.2 19.7 reduce-scatter.116
  3052.4 19.7 reduce-scatter.118
  3075.1 19.7 reduce-scatter.112
  3097.9 19.7 reduce-scatter.110
  3120.1 19.7 reduce-scatter.108
  3142.2 19.7 reduce-scatter.126
  3164.3 22.2 reduce-scatter.132
  3189.0 22.0 reduce-scatter.136
  3213.5 22.0 reduce-scatter.134
  3238.1 22.0 reduce-scatter.92
  3262.7 22.0 reduce-scatter.96
  3287.3 22.0 reduce-scatter.100
where the time goes:
time: 3330 us; the launch traced here: 3320 us
  waiting for transfers between devices  2070 us (62%)
  blocking collectives  889 us (27%)
  matrix products  174 us (5%)
  local copies, waits for them, and re-layouts  115 us (3%)
  other arithmetic  44.6 us (1%)
    unnamed x4, blocking collectives  761 us
    reduce_scatter x3, waiting for transfers between devices, reduce_grads(): lax.psum_scatter(grads[4], 'dp', scatter_dimension=0, tiled=True)  490 us
    reduce_scatter x3, waiting for transfers between devices, reduce_grads(): lax.psum_scatter(grads[5], 'dp', scatter_dimension=0, tiled=True)  467 us
    unnamed x57, waiting for transfers between devices  278 us
    reduce_scatter x3, waiting for transfers between devices, reduce_grads(): lax.psum_scatter(grads[0], 'dp', scatter_dimension=0, tiled=True)  208 us
    reduce_scatter x3, waiting for transfers between devices, reduce_grads(): lax.psum_scatter(grads[1], 'dp', scatter_dimension=0, tiled=True)  195 us
    reduce_scatter x3, waiting for transfers between devices, reduce_grads(): lax.psum_scatter(grads[2], 'dp', scatter_dimension=0, tiled=True)  139 us
    all_gather x1, waiting for transfers between devices, fetch_weights(): lax.all_gather(columns[5], 'dp', axis=0, tiled=True)  77.4 us
  transfers between devices with their start and end apart: 42, of which 34 were waited for; matrix products, arithmetic and copies ran while one was open for 8% of the time, Pallas kernels for 0%

commit v1 on v0

v1 whole, which is shorter than its diff:
```python
import functools
from types import SimpleNamespace

import jax
import jax.numpy as jnp
from jax import lax
from jax.experimental import pallas as pl
from jax.experimental.pallas import tpu as pltpu
from jax.sharding import PartitionSpec as P

HEADS = 12
EPS = 1e-05
LOW = jnp.bfloat16
F32 = jnp.float32
VECS = 16
SQRT_HALF = 0.7071067811865476
PDF_SCALE = 0.3989422804014327


def dot(left, right):
    return jnp.dot(left, right, preferred_element_type=F32)


def dot_t(left, right):
    return lax.dot_general(left, right, (((1,), (1,)), ((), ())), preferred_element_type=F32)


def t_dot(left, right):
    return lax.dot_general(left, right, (((0,), (0,)), ((), ())), preferred_element_type=F32)


def col_sum(values):
    return jnp.sum(values, axis=0, keepdims=True)


def ds(start, size, align=16):
    if not isinstance(start, int):
        start = pl.multiple_of(start, align)
    return pl.ds(start, size)


def pallas(body, outs, ins, scratch=(), flops=0, smem=1, name=None):
    nbytes = sum(a.size * a.dtype.itemsize for a in ins)
    nbytes += sum(s.size * jnp.dtype(s.dtype).itemsize for s in outs)
    return pl.pallas_call(
        body,
        out_shape=outs,
        in_specs=[pl.BlockSpec(memory_space=pltpu.SMEM)] * smem
        + [pl.BlockSpec(memory_space=pltpu.VMEM)] * (len(ins) - smem),
        out_specs=[pl.BlockSpec(memory_space=pltpu.VMEM)] * len(outs),
        scratch_shapes=list(scratch),
        compiler_params=pltpu.CompilerParams(vmem_limit_bytes=56 * 2**20),
        cost_estimate=pl.CostEstimate(flops=flops, bytes_accessed=nbytes, transcendentals=0),
        name=name,
    )(*ins)


def shape(*dims, dtype=LOW):
    return jax.ShapeDtypeStruct(dims, dtype)


def part_index(m, sc, part):
    z, x = sc[1], sc[2]
    k = part % m.nz
    side = x if part < m.nz else 1 - x
    return lax.rem(z - k + m.nz, m.nz) * 2 + side


def layer_norm(x):
    center = x - jnp.mean(x, axis=-1, keepdims=True)
    rstd = lax.rsqrt(jnp.mean(center * center, axis=-1, keepdims=True) + EPS)
    return center * rstd, rstd


def norm_back(grad, gain, xhat, rstd):
    scaled = grad * gain
    first = jnp.mean(scaled, axis=-1, keepdims=True)
    second = jnp.mean(scaled * xhat, axis=-1, keepdims=True)
    return rstd * (scaled - first - xhat * second)


def attend_kernel(m, nparts, *refs):
    sc, counts = refs[:2]
    tokens = refs[2 : 2 + m.S]
    parts = refs[2 + m.S : 2 + m.S + nparts]
    qkv, xhat_ref, normed, probs, packed, vecs, w_ref, x_scr = refs[2 + m.S + nparts :]
    me = sc[0]
    if nparts == 1:
        w_ref[...] = parts[0][...]
    else:
        for p, part in enumerate(parts):
            w_ref[ds(part_index(m, sc, p) * m.rows, m.rows), :] = part[...]
    base = (3 * m.WH) // 128 * 128
    turned = w_ref[:, base : base + 128].astype(F32).T
    vecs[...] = turned[3 * m.WH - base : 3 * m.WH - base + VECS]
    gain, shift = vecs[0:1, :], vecs[1:2, :]
    q_bias = jnp.zeros((1, m.WH), F32)
    v_bias = jnp.zeros((1, m.WH), F32)
    for c in range(m.S):
        here = me == c
        q_bias = jnp.where(here, vecs[2:3, c * m.WH : (c + 1) * m.WH], q_bias)
        v_bias = jnp.where(here, vecs[3:4, c * m.WH : (c + 1) * m.WH], v_bias)
    bias = jnp.concatenate([q_bias, jnp.zeros((1, m.WH), F32), v_bias], axis=1)

    lane = lax.broadcasted_iota(jnp.int32, (1, m.IT), 1)
    place = jnp.full((1, m.IT), 1 << 20, jnp.int32)
    for d in range(m.S):
        row = lane - d * m.RP
        here = jnp.where(row < m.R, (me ^ d) * m.R + row, 1 << 20)
        place = jnp.where(row < 0, place, here)
    x_scr[...] = jnp.zeros_like(x_scr)

    def item(b, carry):
        at = ds(b * m.IT, m.IT)
        for d in range(m.S):
            x_scr[d * m.RP : d * m.RP + m.R, :] = tokens[d][b].astype(F32)
        xhat, _ = layer_norm(x_scr[...])
        low = (xhat * gain + shift).astype(LOW)
        xhat_ref[at, :] = xhat.astype(LOW)
        normed[at, :] = low
        qkv[at, :] = (dot(low, w_ref[:, : 3 * m.WH]) + bias).astype(LOW)
        masked = jnp.where(
            place < m.TXT,
            jnp.where(place < counts[b], 0.0, -1e30),
            jnp.where(place - m.TXT < counts[m.B + b], 0.0, -1e30),
        )
        half = m.IT // 2
        for h in range(m.H):
            q = qkv[at, h * m.hd : (h + 1) * m.hd] * LOW(m.hd**-0.5)
            k = qkv[at, m.WH + h * m.hd : m.WH + (h + 1) * m.hd]
            v = qkv[at, 2 * m.WH + h * m.hd : 2 * m.WH + (h + 1) * m.hd]
            s = dot_t(q, k) + masked
            e = jnp.exp(s - jnp.max(s, axis=-1, keepdims=True))
            p = (e * (1.0 / jnp.sum(e, axis=-1, keepdims=True))).astype(LOW)
            probs[b * m.H + h] = p
            o = dot(p, v).astype(LOW)
            packed[ds(b * half, half), h * m.hd : (h + 1) * m.hd] = o[:half]
            packed[ds(b * half, half), m.WH + h * m.hd : m.WH + (h + 1) * m.hd] = o[half:]
        return carry

    lax.fori_loop(0, m.B, item, 0)


def early_kernel(m, nparts, *refs):
    sc = refs[0]
    cots = refs[1 : 1 + m.S]
    parts = refs[1 + m.S : 1 + m.S + nparts]
    w_up, w_down, w_out, cot, g_act = refs[1 + m.S + nparts :]
    me = sc[0]
    if nparts == 1:
        whole = parts[0]
        w_up[...] = whole[0]
        w_down[...] = whole[1]
        for e in range(m.S):
            w_out[e * m.WH : (e + 1) * m.WH, :] = whole[2, ds((me ^ e) * m.WH, m.WH), :]
    else:
        per = m.N // m.S
        for p, part in enumerate(parts):
            i = part_index(m, sc, p)
            w_up[ds(i * m.rows, m.rows), :] = part[0]
            w_down[ds(i * m.hrows, m.hrows), :] = part[1]
            block = me ^ lax.div(i, per)
            w_out[ds(block * m.WH + lax.rem(i, per) * m.rows, m.rows), :] = part[2]
    cot[...] = jnp.zeros_like(cot)
    for b in range(m.B):
        for d in range(m.S):
            start = (b * m.S + d) * m.RP
            cot[start : start + m.R, :] = cots[d][b]

    def item(b, carry):
        at = ds(b * m.IT, m.IT)
        g_act[at, :] = dot_t(cot[at, :], w_down[...])
        return carry

    lax.fori_loop(0, m.B, item, 0)


def forward_kernel(m, *refs):
    sc = refs[0]
    tokens = refs[1 : 1 + m.S]
    packed = refs[1 + m.S : 1 + 2 * m.S]
    w_out, w_up, g_act, vecs = refs[1 + 2 * m.S : 5 + 2 * m.S]
    (normed, active, g_hidden, mixed, keep0, keep1, send, resid_own, xhat_own, rstd_own, x_scr) = refs[
        5 + 2 * m.S :
    ]
    me = sc[0]
    out_bias, gain, shift = vecs[4:5, :], vecs[5:6, :], vecs[6:7, :]
    up_bias = vecs[pl.ds(8 + me, 1), :]
    x_scr[...] = jnp.zeros_like(x_scr)

    def item(b, carry):
        at = ds(b * m.IT, m.IT)
        half = m.IT // 2
        for d in range(m.S):
            x_scr[d * m.RP : d * m.RP + m.R, :] = tokens[d][b].astype(F32)
        for e in range(m.S):
            for side in range(2):
                piece = packed[e][ds(b * half, half), side * m.WH : (side + 1) * m.WH]
                for t in range(2):
                    d = (2 * side + t) ^ e
                    mixed[ds(b * m.IT + d * m.RP, m.RP), e * m.WH : (e + 1) * m.WH] = piece[
                        t * m.RP : (t + 1) * m.RP
                    ]
        resid = x_scr[...] + (dot(mixed[at, :], w_out[...]) + out_bias)
        xhat, rstd = layer_norm(resid)
        own = ds(b * m.RP, m.RP)
        resid_own[own, :] = resid[: m.RP]
        xhat_own[own, :] = xhat[: m.RP]
        rstd_own[own, :] = jnp.broadcast_to(rstd[: m.RP], (m.RP, 128))
        low = (xhat * gain + shift).astype(LOW)
        normed[at, :] = low
        hidden = dot(low, w_up[...]) + up_bias
        cdf = 0.5 + 0.5 * lax.erf(hidden * SQRT_HALF)
        active[at, :] = (hidden * cdf).astype(LOW)
        slope = cdf + hidden * (PDF_SCALE * jnp.exp(-0.5 * hidden * hidden))
        back = (g_act[at, :] * slope).astype(LOW)
        g_hidden[at, :] = back
        grad = dot_t(back, w_up[...]).astype(LOW)
        keep0[own, :] = grad[: m.RP]
        send[0, own, :] = grad[m.RP : 2 * m.RP]
        keep1[own, :] = grad[2 * m.RP : 3 * m.RP]
        send[1, own, :] = grad[3 * m.RP : 4 * m.RP]
        return carry

    lax.fori_loop(0, m.B, item, 0)


def give_shards(m, sc, total, keep, send, first, rows):
    for k in range(m.nz):
        z = lax.rem(sc[1] + k, m.nz)
        here = (2 * z + sc[2]) * rows
        there = (2 * z + 1 - sc[2]) * rows
        keep[k, first : first + rows, :] = total[ds(here, rows), :].astype(LOW)
        send[k, first : first + rows, :] = total[ds(there, rows), :].astype(LOW)


def ff_grads_kernel(m, *refs):
    sc, active, g_hidden, normed, cot, w_down = refs[:6]
    keep0, keep1, send, vec, g_first, g_second, total = refs[6:]
    vec[...] = jnp.zeros_like(vec)

    def item(b, carry):
        at = ds(b * m.IT, m.IT)
        own = ds(b * m.RP, m.RP)
        part = dot(active[at, :], w_down[...]).astype(LOW)
        keep0[own, :] = part[: m.RP]
        send[0, own, :] = part[m.RP : 2 * m.RP]
        keep1[own, :] = part[2 * m.RP : 3 * m.RP]
        send[1, own, :] = part[3 * m.RP : 4 * m.RP]
        vec[0:1, :] += col_sum(cot[ds(b * m.IT, m.RP), :].astype(F32))
        vec[1:2, :] += col_sum(g_hidden[at, :].astype(F32))
        return carry

    lax.fori_loop(0, m.B, item, 0)
    step = 256
    for pair in ((normed, g_hidden), (active, cot)):
        first = pair[0] is active
        for begin in range(0, m.D, step):
            total[begin : begin + step, :] = t_dot(pair[0][:, begin : begin + step], pair[1][...])
        if m.fast:
            give_shards(m, sc, total, g_first, g_second, m.rows if first else 0, m.rows)
        elif first:
            g_second[...] = total[...].astype(LOW)
        else:
            g_first[...] = total[...].astype(LOW)


def middle_kernel(m, *refs):
    sc, keep0, core, far, xhat_own, rstd_own, cot, w_out, vecs = refs[:9]
    g_resid = refs[9]
    blocks = refs[10 : 10 + m.S]
    vec, low_scr = refs[10 + m.S :]
    me = sc[0]
    gain = vecs[5:6, :]
    grad = keep0[...].astype(F32) + core[0].astype(F32) + far[...].astype(F32)
    xhat = xhat_own[...]
    back = norm_back(grad, gain, xhat, rstd_own[:, 0:1])
    vec[...] = jnp.zeros_like(vec)
    vec[0:1, :] = col_sum(grad * xhat)
    vec[1:2, :] = col_sum(grad)
    for b in range(m.B):
        own = slice(b * m.RP, (b + 1) * m.RP)
        full = back[own] + cot[b * m.IT : b * m.IT + m.RP, :].astype(F32)
        g_resid[own, :] = full
        low_scr[own, :] = full.astype(LOW)
    low = low_scr[...]
    vec[2:3, :] = col_sum(low.astype(F32))
    g_mixed = dot_t(low, w_out[...]).astype(LOW)
    for e in range(m.S):
        blocks[e][:, : m.WH] = g_mixed[:, e * m.WH : (e + 1) * m.WH]
        picked = low[:, : m.WH]
        for c in range(1, m.S):
            picked = jnp.where((me ^ e) == c, low[:, c * m.WH : (c + 1) * m.WH], picked)
        blocks[e][:, m.WH :] = picked


def attend_back_kernel(m, *refs):
    sc, qkv, probs = refs[:3]
    blocks = refs[3 : 3 + m.S]
    normed, xhat, mixed, w, vec_mid, vec_ff = refs[3 + m.S : 9 + m.S]
    keep0, keep1, send, g_first, g_second, g_scr, ga_scr, v_scr, total = refs[9 + m.S :]
    me = sc[0]
    own_rows = m.B * m.RP
    v_scr[...] = jnp.zeros_like(v_scr)
    scale = m.hd**-0.5

    def item(b, carry):
        at = ds(b * m.IT, m.IT)
        own = ds(b * m.RP, m.RP)
        for d in range(m.S):
            ga_scr[ds(b * m.IT + d * m.RP, m.RP), :] = blocks[d][own, m.WH :]
        gm_all = jnp.concatenate([blocks[d][own, : m.WH] for d in range(m.S)], axis=0)
        for h in range(m.H):
            lanes = slice(h * m.hd, (h + 1) * m.hd)
            q = qkv[at, h * m.hd : (h + 1) * m.hd]
            k = qkv[at, m.WH + h * m.hd : m.WH + (h + 1) * m.hd]
            v = qkv[at, 2 * m.WH + h * m.hd : 2 * m.WH + (h + 1) * m.hd]
            gm = gm_all[:, lanes]
            low = probs[b * m.H + h]
            p = low.astype(F32)
            gp = dot_t(gm, v)
            gs = (p * (gp - jnp.sum(p * gp, axis=-1, keepdims=True))).astype(LOW)
            gq = (dot(gs, k) * scale).astype(LOW)
            gk = (t_dot(gs, q) * scale).astype(LOW)
            gv = t_dot(low, gm).astype(LOW)
            g_scr[at, h * m.hd : (h + 1) * m.hd] = gq
            g_scr[at, m.WH + h * m.hd : m.WH + (h + 1) * m.hd] = gk
            g_scr[at, 2 * m.WH + h * m.hd : 2 * m.WH + (h + 1) * m.hd] = gv
        grad = dot_t(g_scr[at, :], w[:, : 3 * m.WH])
        v_scr[0:1, :] += col_sum(grad * xhat[at, :].astype(F32))
        v_scr[1:2, :] += col_sum(grad)
        grad = grad.astype(LOW)
        keep0[own, :] = grad[: m.RP]
        send[0, own, :] = grad[m.RP : 2 * m.RP]
        keep1[own, :] = grad[2 * m.RP : 3 * m.RP]
        send[1, own, :] = grad[3 * m.RP : 4 * m.RP]
        return carry

    lax.fori_loop(0, m.B, item, 0)
    sums = col_sum(g_scr[...].astype(F32))
    for c in range(m.S):
        here = me == c
        lanes = slice(c * m.WH, (c + 1) * m.WH)
        v_scr[2:3, lanes] = jnp.where(here, sums[:, : m.WH], 0.0)
        v_scr[3:4, lanes] = jnp.where(here, sums[:, 2 * m.WH :], 0.0)
        v_scr[8 + c : 9 + c, :] = jnp.where(here, vec_ff[1:2, :], 0.0)
    v_scr[4:5, :] = vec_mid[2:3, :]
    v_scr[5:6, :] = vec_mid[0:1, :]
    v_scr[6:7, :] = vec_mid[1:2, :]
    v_scr[7:8, :] = vec_ff[0:1, :]
    values = v_scr[...].astype(LOW)
    tail = slice(own_rows, own_rows + VECS)
    keep0[tail, :] = values
    keep1[tail, :] = values
    send[0, tail, :] = values
    send[1, tail, :] = values
    total[:, : 3 * m.WH] = t_dot(normed[...], g_scr[...])
    g_out = t_dot(mixed[...], ga_scr[...])
    for e in range(m.S):
        total[ds((me ^ e) * m.WH, m.WH), 3 * m.WH :] = g_out[e * m.WH : (e + 1) * m.WH]
    if m.fast:
        give_shards(m, sc, total, g_first, g_second, 0, m.rows)
    else:
        g_first[...] = total[...].astype(LOW)
        g_second[...] = jnp.zeros_like(g_second)


def finish_kernel(m, *refs):
    keep0, core, far, tokens, g_resid, vecs, b_keep, b_core, b_far, resid = refs[1:11]
    result, input_grad = refs[11:]
    gain, down_bias = vecs[0:1, :], vecs[7:8, :]
    for b in range(m.B):
        own = slice(b * m.RP, b * m.RP + m.R)
        grad = keep0[own, :].astype(F32) + core[0, own, :].astype(F32) + far[own, :].astype(F32)
        xhat, rstd = layer_norm(tokens[b].astype(F32))
        back = norm_back(grad, gain, xhat, rstd)
        input_grad[b] = (g_resid[own, :] + back).astype(LOW)
        branch = b_keep[own, :].astype(F32) + b_core[0, own, :].astype(F32) + b_far[own, :].astype(F32)
        result[b] = (resid[own, :] + (branch + down_bias)).astype(LOW)


def plan(mesh, tokens, text_mask, w_query, w_up):
    m = SimpleNamespace()
    m.N, m.S = mesh.shape["dp"], mesh.shape["seq"]
    m.B, m.R, m.D = tokens.shape
    m.RP = -(-m.R // 16) * 16
    m.IT = m.S * m.RP
    m.RA = m.B * m.IT
    m.OWN = m.B * m.RP
    m.TXT = text_mask.shape[1]
    m.rows, m.WH = w_query.shape
    m.hd = m.D // HEADS
    m.H = HEADS // m.S
    m.FD = w_up.shape[1]
    m.hrows = m.FD // m.N
    m.fast = m.N == 8
    m.nz = m.N // 2
    m.vcols = 8 + m.S
    return m


def local(
    mesh,
    tokens,
    cotangent,
    text_mask,
    patch_count,
    w_query,
    w_key,
    w_value,
    w_out,
    w_up,
    w_down,
    norm1_gain,
    norm1_bias,
    query_bias,
    value_bias,
    out_bias,
    norm2_gain,
    norm2_bias,
    up_bias,
    down_bias,
):
    m = plan(mesh, tokens, text_mask, w_query, w_up)
    N, S, rows, WH, D = m.N, m.S, m.rows, m.WH, m.D
    dp = lax.axis_index("dp").astype(jnp.int32)
    me = lax.axis_index("seq").astype(jnp.int32)
    sc = jnp.stack([me, dp // 2, dp % 2])
    counts = jnp.concatenate([jnp.sum(text_mask, axis=1), patch_count])

    def seq_to(x, e):
        return lax.ppermute(x, "seq", [(i, i ^ e) for i in range(S)])

    def x_swap(x):
        return lax.ppermute(x, "dp", [(i, i ^ 1) for i in range(N)])

    def z_shift(x, k):
        return lax.ppermute(x, "dp", [(i, (i + 2 * k) % N) for i in range(N)])

    def gather_dp(x, axis):
        if not m.fast:
            return [lax.all_gather(x, "dp", axis=axis, tiled=True)]
        same = [x] + [z_shift(x, k) for k in range(1, m.nz)]
        return same + [x_swap(v) for v in same]

    def gather_seq(x):
        far = seq_to(x, 2)
        return [x, seq_to(x, 1), far, seq_to(far, 1)]

    vec_cols = jnp.stack(
        [norm1_gain, norm1_bias, query_bias, value_bias, out_bias, norm2_gain, norm2_bias, down_bias], axis=1
    )
    vec_cols = jnp.concatenate([vec_cols, up_bias.reshape(S, m.hrows).T], axis=1)
    wide = -(-(3 * WH + VECS) // 128) * 128
    first = jnp.concatenate(
        [w_query, w_key, w_value, vec_cols, jnp.zeros((rows, wide - 3 * WH - m.vcols), LOW)], axis=1
    )
    first_parts = gather_dp(first, 0)
    token_blocks = gather_seq(tokens)
    cot_blocks = gather_seq(cotangent)

    per = N // S
    up_parts = w_up.reshape(rows, per, S, m.hrows).transpose(2, 0, 1, 3).reshape(S, rows, WH)
    down_parts = w_down.reshape(S, m.hrows, WH)
    out_parts = jnp.broadcast_to(w_out, (S, rows, WH))
    mixed_parts = jnp.stack([up_parts, down_parts, out_parts], axis=1)
    swapped = lax.all_to_all(mixed_parts, "seq", 0, 0, tiled=True)
    second = swapped.transpose(1, 2, 0, 3).reshape(3, rows, D)
    second_parts = gather_dp(second, 1)

    qkv, xhat, normed, probs, packed, vecs, w_first = pallas(
        functools.partial(attend_kernel, m, len(first_parts)),
        [
            shape(m.RA, 3 * WH),
            shape(m.RA, D),
            shape(m.RA, D),
            shape(m.B * m.H, m.IT, m.IT),
            shape(m.B * m.IT // 2, 2 * WH),
            shape(VECS, D, dtype=F32),
            shape(D, wide),
        ],
        [sc, counts, *token_blocks, *first_parts],
        [pltpu.VMEM((m.IT, D), F32)],
        flops=2 * m.RA * D * 3 * WH + 4 * m.B * m.H * m.IT * m.IT * m.hd,
        smem=2,
        name="attend",
    )
    packed_blocks = gather_seq(packed)

    w_up_all, w_down_all, w_out_all, cot, g_act = pallas(
        functools.partial(early_kernel, m, len(second_parts)),
        [shape(D, m.FD), shape(m.FD, D), shape(D, D), shape(m.RA, D), shape(m.RA, m.FD, dtype=F32)],
        [sc, *cot_blocks, *second_parts],
        flops=2 * m.RA * D * m.FD,
        name="early",
    )

    normed2, active, g_hidden, mixed, keep0, keep1, send, resid, xhat2, rstd2 = pallas(
        functools.partial(forward_kernel, m),
        [
            shape(m.RA, D),
            shape(m.RA, m.FD),
            shape(m.RA, m.FD),
            shape(m.RA, D),
            shape(m.OWN, D),
            shape(m.OWN, D),
            shape(2, m.OWN, D),
            shape(m.OWN, D, dtype=F32),
            shape(m.OWN, D, dtype=F32),
            shape(m.OWN, 128, dtype=F32),
        ],
        [sc, *token_blocks, *packed_blocks, w_out_all, w_up_all, g_act, vecs],
        [pltpu.VMEM((m.IT, D), F32)],
        flops=2 * m.RA * D * (D + 2 * m.FD),
        name="forward",
    )

    def add_pair(left, right):
        return (left.astype(F32) + right.astype(F32)).astype(LOW)

    def reduce_seq(keep1, send):
        core = seq_to(send, 1)
        return core, seq_to(add_pair(keep1, core[1]), 2)

    core2, far2 = reduce_seq(keep1, send)

    if m.fast:
        ff_shapes = [shape(m.nz, 2 * rows, D), shape(m.nz, 2 * rows, D)]
        a_shapes = [shape(m.nz, rows, D), shape(m.nz, rows, D)]
    else:
        ff_shapes = [shape(D, m.FD), shape(m.FD, D)]
        a_shapes = [shape(D, D), shape(8, 128)]

    b_keep0, b_keep1, b_send, vec_ff, ff_keep, ff_send = pallas(
        functools.partial(ff_grads_kernel, m),
        [
            shape(m.OWN, D),
            shape(m.OWN, D),
            shape(2, m.OWN, D),
            shape(8, D, dtype=F32),
            *ff_shapes,
        ],
        [sc, active, g_hidden, normed2, cot, w_down_all],
        [pltpu.VMEM((D, D), F32)],
        flops=2 * m.RA * D * 3 * m.FD,
        name="ff_grads",
    )

    g_resid, *blocks, vec_mid = pallas(
        functools.partial(middle_kernel, m),
        [
            shape(m.OWN, D, dtype=F32),
            *[shape(m.OWN, 2 * WH)] * S,
            shape(8, D, dtype=F32),
        ],
        [sc, keep0, core2, far2, xhat2, rstd2, cot, w_out_all, vecs],
        [pltpu.VMEM((m.OWN, D), LOW)],
        flops=2 * m.OWN * D * D,
        name="middle",
    )
    blocks = [blocks[0]] + [seq_to(blocks[e], e) for e in range(1, S)]

    def scatter_dp(keep, send):
        got = x_swap(send)
        total = keep.astype(F32) + got.astype(F32)
        low = total.astype(LOW)
        out = total[0]
        for k in range(1, m.nz):
            out = out + z_shift(low[k], k).astype(F32)
        return out

    if m.fast:
        g_ff = scatter_dp(ff_keep, ff_send)
    else:
        g_ff = jnp.concatenate(
            [lax.psum_scatter(g, "dp", scatter_dimension=0, tiled=True) for g in (ff_keep, ff_send)], axis=0
        ).astype(F32)
    g_ff = lax.all_to_all(g_ff.astype(LOW).reshape(2 * rows, S, WH).transpose(1, 0, 2), "seq", 0, 0, tiled=True)
    g_ff = g_ff.astype(F32)
    g_up = g_ff[:, :rows].reshape(S, rows, per, m.hrows).transpose(1, 2, 0, 3).reshape(rows, m.FD)
    g_down = g_ff[:, rows:].reshape(S * m.hrows, WH)

    keep0, keep1, send, a_keep, a_send = pallas(
        functools.partial(attend_back_kernel, m),
        [
            shape(m.OWN + VECS, D),
            shape(m.OWN + VECS, D),
            shape(2, m.OWN + VECS, D),
            *a_shapes,
        ],
        [sc, qkv, probs, *blocks, normed, xhat, mixed, w_first, vec_mid, vec_ff],
        [
            pltpu.VMEM((m.RA, 3 * WH), LOW),
            pltpu.VMEM((m.RA, WH), LOW),
            pltpu.VMEM((VECS, D), F32),
            pltpu.VMEM((D, D), F32),
        ],
        flops=2 * m.RA * D * 7 * WH + 8 * m.B * m.H * m.IT * m.IT * m.hd,
        name="attend_back",
    )
    if m.fast:
        g_a = scatter_dp(a_keep, a_send)
    else:
        g_a = lax.psum_scatter(a_keep, "dp", scatter_dimension=0, tiled=True).astype(F32)
    core1, far1 = reduce_seq(keep1, send)
    b_core, b_far = reduce_seq(b_keep1, b_send)

    vec = keep0[m.OWN :].astype(F32) + core1[0, m.OWN :].astype(F32) + far1[m.OWN :].astype(F32)
    if m.fast:
        vec = vec + x_swap(vec)
        vec = vec + sum(z_shift(vec, k) for k in range(1, m.nz))
    else:
        vec = lax.psum(vec, "dp")
    vec = lax.dynamic_slice(vec, (0, dp * rows), (VECS, rows))

    result, input_grad = pallas(
        functools.partial(finish_kernel, m),
        [shape(m.B, m.R, D), shape(m.B, m.R, D)],
        [sc, keep0, core1, far1, tokens, g_resid, vecs, b_keep0, b_core, b_far, resid],
        name="finish",
    )
    return (
        result,
        input_grad,
        g_a[:, :WH],
        g_a[:, WH : 2 * WH],
        g_a[:, 2 * WH : 3 * WH],
        g_a[:, 3 * WH :],
        g_up,
        g_down,
        vec[0],
        vec[1],
        vec[2],
        vec[3],
        vec[4],
        vec[5],
        vec[6],
        vec[8 : 8 + S].reshape(-1),
        vec[7],
    )


def solution(mesh):
    rows3, mat, vec = P("dp", "seq", None), P("dp", "seq"), P("dp")
    return jax.shard_map(
        functools.partial(local, mesh),
        mesh=mesh,
        in_specs=(rows3, rows3, P("dp", None), vec) + (mat,) * 6 + (vec,) * 9,
        out_specs=(rows3, rows3) + (mat,) * 6 + (vec,) * 9,
        check_vma=False,
    )
```

time: 3330 us -> 237 us (0.07)
  waiting for transfers between devices: 2070 us -> 84.4 us
  blocking collectives: 889 us -> 0 us
  matrix products: 174 us -> 0 us
  local copies, waits for them, and re-layouts: 115 us -> 21.1 us
  Pallas kernels: 0 us -> 61.6 us
  starting transfers between devices: 2.39 us -> 55.4 us
  other arithmetic: 44.6 us -> 8.54 us
    reduce_scatter x21 -> x0, waiting for transfers between devices: 1640 us -> none  [the longest x3 490 us: reduce_grads(): lax.psum_scatter(grads[4], 'dp', scatter_dimension=0, tiled=True)]
    unnamed x4 -> x0, blocking collectives: 761 us -> none
    unnamed x57 -> x0, waiting for transfers between devices: 278 us -> none
    dot_general x72 -> x0, matrix products: 174 us -> none  [the longest x18 70.9 us: inner_rows(): lax.dot_general(left, right, (((0,), (0,)), ((), ())), preferred_element_...]
    all_gather x6 -> x0, waiting for transfers between devices: 156 us -> none  [the longest x1 77.4 us: fetch_weights(): lax.all_gather(columns[5], 'dp', axis=0, tiled=True)]
    all_gather x13 -> x0, blocking collectives: 114 us -> none  [the longest x3 31.9 us: micro_step(): lax.all_gather(values, 'seq', axis=1, tiled=True)]
    ppermute x0 -> x44, waiting for transfers between devices: none -> 80.8 us  [the longest x11 29.8 us: x_swap(): return lax.ppermute(x, 'dp', [(i, i ^ 1) for i in range(N)])]
    pallas_call x0 -> x7, Pallas kernels: none -> 61.6 us  [pallas(): pl.pallas_call(body, out_shape=outs, in_specs=[pl.BlockSpec(memory_space=...]
  transfers between devices with their start and end apart: 42 -> 46, of which waited for: 34 -> 12; matrix products, arithmetic and copies ran while one was open for 8% -> 7% of each run, Pallas kernels for 0% -> 21%
where the time goes in v1:
time: 237 us; the launch traced here: 232 us
  waiting for transfers between devices  84.4 us (36%)
  Pallas kernels  61.6 us (26%)
  starting transfers between devices  55.4 us (23%)
  local copies, waits for them, and re-layouts  21.1 us (9%)
  other arithmetic  8.54 us (4%)
    pallas_call x7, Pallas kernels, pallas(): pl.pallas_call(body, out_shape=outs, in_specs=[pl.BlockSpec(memory_space=...  61.6 us
    ppermute x11, waiting for transfers between devices, x_swap(): return lax.ppermute(x, 'dp', [(i, i ^ 1) for i in range(N)])  29.8 us
    ppermute x15, waiting for transfers between devices, z_shift(): return lax.ppermute(x, 'dp', [(i, (i + 2 * k) % N) for i in range(N)])  29.4 us
    ppermute x18, waiting for transfers between devices, seq_to(): return lax.ppermute(x, 'seq', [(i, i ^ e) for i in range(S)])  21.5 us
    ppermute x15, starting transfers between devices, z_shift(): return lax.ppermute(x, 'dp', [(i, (i + 2 * k) % N) for i in range(N)])  15.8 us
    ppermute x18, starting transfers between devices, seq_to(): return lax.ppermute(x, 'seq', [(i, i ^ e) for i in range(S)])  15.3 us
    ppermute x11, starting transfers between devices, x_swap(): return lax.ppermute(x, 'dp', [(i, i ^ 1) for i in range(N)])  10.8 us
    all_to_all x1, starting transfers between devices, local(): swapped = lax.all_to_all(mixed_parts, 'seq', 0, 0, tiled=True)  6.96 us
  transfers between devices with their start and end apart: 46, of which 12 were waited for; matrix products, arithmetic and copies ran while one was open for 7% of the time, Pallas kernels for 21%

profile of v1, /device:TPU:5, one launch (start us, length us, event | category | flops | bytes accessed | tf_op | source)
XLA Modules:
  0.0 232.2 jit_solution(5143499893573187329)
XLA Ops:
  0.7 0.8 reshape.66
  1.6 0.8 copy.62
  2.4 0.8 copy.63
  3.2 0.8 copy.64
  3.9 0.8 copy.65
  4.7 0.8 copy.66
  5.5 0.8 copy.67
  6.3 0.8 copy.68
  7.0 0.8 copy.69
  7.8 1.0 concatenate.7.refs_6_
  8.8 3.4 %collective-permute-start.5 = (bf16[96,640]{1,0:T(8,128)(2,1)S(1)}, bf16[96,640]{1,0:T(8,128)(2,1)S(1)}, u32[]{:S(2)}, u32[]{:S(2)}) collective-permute-start(bf16[96,640]{1,0:T(8,128)(2,1)S(1)} %concatenate.7.refs_6_), channel_id=1, source_target_pairs={{0,24},{4,28},{8,0},{12,4},{16,8},{20,12},{24,16},{28,20},{1,25},{... | collective-permute-start | bytes 368648 | tf_op jit(solution)/shard_map/ppermute | solution.py:438
  12.2 1.2 collective-permute-start.6
  14.1 1.1 reshape.67
  16.1 0.9 pad_maximum_fusion
  17.1 7.0 %all-to-all-start = ((bf16[4,3,96,192]{3,2,1,0:T(8,128)(2,1)}), bf16[4,3,96,192]{3,2,1,0:T(8,128)(2,1)S(1)}, u32[]{:S(2)}, u32[]{:S(2)}) async-start(bf16[4,3,96,192]{3,2,1,0:T(8,128)(2,1)} %pad_maximum_fusion), calls=%async_computation | async-start | bytes 1179648 | tf_op jit(solution)/shard_map/all_to_all | solution.py:467
  24.8 1.2 collective-permute-start.8
  26.0 3.3 %collective-permute-done.8.refs_12_ = bf16[96,640]{1,0:T(8,128)(2,1)S(1)} collective-permute-done((bf16[96,640]{1,0:T(8,128)(2,1)S(1)}, bf16[96,640]{1,0:T(8,128)(2,1)S(1)}, u32[]{:S(2)}, u32[]{:S(2)}) %collective-permute-start.8) | collective-permute-done | bytes 122912 | tf_op jit(solution)/shard_map/ppermute | solution.py:435
  29.3 1.2 collective-permute-start.7
  30.5 1.5 collective-permute-start.2
  33.2 5.6 %collective-permute-done.14.refs_3_ = bf16[3,70,768]{2,1,0:T(8,128)(2,1)S(1)} collective-permute-done((bf16[3,70,768]{2,1,0:T(8,128)(2,1)S(1)}, bf16[3,70,768]{2,1,0:T(8,128)(2,1)S(1)}, u32[]{:S(2)}, u32[]{:S(2)}) %collective-permute-start.14) | collective-permute-done | bytes 322592 | tf_op jit(solution)/shard_map/ppermute | solution.py:432
  39.4 3.0 %collective-permute-start.18 = (bf16[3,96,768]{2,1,0:T(8,128)(2,1)S(1)}, bf16[3,96,768]{2,1,0:T(8,128)(2,1)S(1)}, u32[]{:S(2)}, u32[]{:S(2)}) collective-permute-start(bf16[3,96,768]{2,1,0:T(8,128)(2,1)S(1)} %reshape.68.refs_5_), channel_id=1, source_target_pairs={{0,24},{4,28},{8,0},{12,4},{16,8},{20,12},{24,16},{28,20},{1,25},{... | collective-permute-start | bytes 1327112 | tf_op jit(solution)/shard_map/ppermute | solution.py:438
  43.3 1.2 pad_add_fusion.1.refs_1_
  45.9 11.3 %attend.1 = (bf16[960,576]{1,0:T(8,128)(2,1)}, bf16[960,768]{1,0:T(8,128)(2,1)}, bf16[960,768]{1,0:T(8,128)(2,1)}, bf16[9,320,320]{2,1,0:T(8,128)(2,1)}, bf16[48...) custom-call(s32[3]{0:T(128)} %pad_add_fusion.refs_0_, s32[6]{0:T(128)} %pad_add_fusion.1.refs_1_, ...), custom_call_target="tpu_custom_call" | custom-call | flops 1085276160 | bytes 9572388 | tf_op jit(solution)/shard_map/attend/pallas_call | solution.py:45
  57.3 1.4 collective-permute-start.11
  59.5 22.0 %collective-permute-done.17.refs_7_ = bf16[3,96,768]{2,1,0:T(8,128)(2,1)S(1)} collective-permute-done((bf16[3,96,768]{2,1,0:T(8,128)(2,1)S(1)}, bf16[3,96,768]{2,1,0:T(8,128)(2,1)S(1)}, u32[]{:S(2)}, u32[]{:S(2)}) %collective-permute-start.17) | collective-permute-done | bytes 442400 | tf_op jit(solution)/shard_map/ppermute | solution.py:438
  81.5 1.2 collective-permute-start.21
  82.9 1.4 collective-permute-start.10
  84.5 7.9 %collective-permute-done.21.refs_11_ = bf16[3,96,768]{2,1,0:T(8,128)(2,1)S(1)} collective-permute-done((bf16[3,96,768]{2,1,0:T(8,128)(2,1)S(1)}, bf16[3,96,768]{2,1,0:T(8,128)(2,1)S(1)}, u32[]{:S(2)}, u32[]{:S(2)}) %collective-permute-start.21) | collective-permute-done | bytes 442400 | tf_op jit(solution)/shard_map/ppermute | solution.py:435
  92.3 9.5 %collective-permute-done.20.refs_10_ = bf16[3,96,768]{2,1,0:T(8,128)(2,1)S(1)} collective-permute-done((bf16[3,96,768]{2,1,0:T(8,128)(2,1)S(1)}, bf16[3,96,768]{2,1,0:T(8,128)(2,1)S(1)}, u32[]{:S(2)}, u32[]{:S(2)}) %collective-permute-start.20) | collective-permute-done | bytes 442400 | tf_op jit(solution)/shard_map/ppermute | solution.py:435
  101.8 0.8 copy-done.12
  102.6 7.1 %early.1 = (bf16[768,768]{1,0:T(8,128)(2,1)}, bf16[768,768]{1,0:T(8,128)(2,1)}, bf16[768,768]{1,0:T(8,128)(2,1)}, bf16[960,768]{1,0:T(8,128)(2,1)}, f32[960,768]{1,0:T(8,128)}) custom-call(s32[3]{0:T(128)} %pad_add_fusion.refs_0_, bf16[3,70,768]{2,1,0:T(8,128)(2,1)} %refs_1_.2, bf16[3,70,768]{2,1,0:T(8,128)(2,1)} %copy-done.20, ...), custom_call_target="tpu_custom_call" | custom-call | flops 1132462080 | bytes 12791820 | tf_op jit(solution)/shard_map/early/pallas_call | solution.py:45
  110.6 11.8 %forward.1 = (bf16[960,768]{1,0:T(8,128)(2,1)}, bf16[960,768]{1,0:T(8,128)(2,1)}, bf16[960,768]{1,0:T(8,128)(2,1)}, bf16[960,768]{1,0:T(8,128)(2,1)}, bf16[240,7...) custom-call(s32[3]{0:T(128)} %pad_add_fusion.refs_0_, ...), custom_call_target="tpu_custom_call" | custom-call | flops 3397386240 | bytes 17092620 | tf_op jit(solution)/shard_map/forward/pallas_call | solution.py:45
  122.4 1.8 collective-permute-start.23
  124.2 9.0 %ff_grads.1 = (bf16[240,768]{1,0:T(8,128)(2,1)}, bf16[240,768]{1,0:T(8,128)(2,1)}, bf16[2,240,768]{2,1,0:T(8,128)(2,1)}, f32[8,768]{1,0:T(8,128)}, bf16[4,192,76...) custom-call(s32[3]{0:T(128)} %pad_add_fusion.refs_0_, bf16[960,768]{1,0:T(8,128)(2,1)} %get-tuple-element.80.refs_1_, ...), custom_call_target="tpu_custom_call" | custom-call | flops 3397386240 | bytes 10936332 | tf_op jit(solution)/shard_map/ff_grads/pallas_call | solution.py:45
  133.2 1.2 collective-permute-start.36
  134.5 1.5 collective-permute-start.24
  136.5 7.9 %collective-permute-done.24.refs_3_ = bf16[240,768]{1,0:T(8,128)(2,1)S(1)} collective-permute-done((bf16[240,768]{1,0:T(8,128)(2,1)S(1)}, bf16[240,768]{1,0:T(8,128)(2,1)S(1)}, u32[]{:S(2)}, u32[]{:S(2)}) %collective-permute-start.24) | collective-permute-done | bytes 368672 | tf_op jit(solution)/shard_map/ppermute | solution.py:432
  145.2 4.3 %middle.1 = (f32[240,768]{1,0:T(8,128)}, bf16[240,384]{1,0:T(8,128)(2,1)}, bf16[240,384]{1,0:T(8,128)(2,1)}, bf16[240,384]{1,0:T(8,128)(2,1)}, bf16[240,384]{1,0:T(8,128)(2,1)}, /*index=5*/f32[8,768]{1,0:T(8,128)}) custom-call(s32[3]{0:T(128)} %pad_add_fusion.refs_0_, bf16[240,768]{1,0:T(8,128)(2,1)} %get-tuple-element.65.refs_1_, ...), custom_call_target="tpu_custom_call" | custom-call | flops 283115520 | bytes 6537228 | tf_op jit(solution)/shard_map/middle/pallas_call | solution.py:45
  149.5 1.1 collective-permute-start.25
  150.6 1.4 collective-permute-start.26
  152.3 8.7 %collective-permute-done.36 = bf16[4,192,768]{2,1,0:T(8,128)(2,1)S(1)} collective-permute-done((bf16[4,192,768]{2,1,0:T(8,128)(2,1)}, bf16[4,192,768]{2,1,0:T(8,128)(2,1)S(1)}, u32[]{:S(2)}, u32[]{:S(2)}) %collective-permute-start.36) | collective-permute-done | bytes 1179680 | tf_op jit(solution)/shard_map/ppermute | solution.py:435
  161.3 0.9 slice_bitcast_fusion.6
  162.2 3.2 %collective-permute-start.39 = (bf16[192,768]{1,0:T(8,128)(2,1)}, bf16[192,768]{1,0:T(8,128)(2,1)}, u32[]{:S(2)}, u32[]{:S(2)}) collective-permute-start(bf16[192,768]{1,0:T(8,128)(2,1)} %get-tuple-element.119), channel_id=1, source_target_pairs={{0,24},{4,28},{8,0},{12,4},{16,8},{20,12},{24,16},{28,20},{1,25},{... | collective-permute-start | bytes 884744 | tf_op jit(solution)/shard_map/ppermute | solution.py:438
  166.2 14.2 %attend_back.1 = (bf16[256,768]{1,0:T(8,128)(2,1)}, bf16[256,768]{1,0:T(8,128)(2,1)}, bf16[2,256,768]{2,1,0:T(8,128)(2,1)}, bf16[4,96,768]{2,1,0:T(8,128)(2,1)}, bf16[4,96,768]{2,1,0:T(8,128)(2,1)}) custom-call(s32[3]{0:T(128)} %pad_add_fusion.refs_0_, bf16[960,576]{1,0:T(8,128)(2,1)} %get-tuple-element.58.refs_1_, ...), custom_call_target="tpu_custom_call" | custom-call | flops 2453667840 | bytes 11894796 | tf_op jit(solution)/shard_map/attend_back/pallas_call | solution.py:45
  180.4 1.4 collective-permute-start.28
  181.7 1.2 collective-permute-start.32
  183.0 6.2 %collective-permute-done.38 = bf16[192,768]{1,0:T(8,128)(2,1)} collective-permute-done((bf16[192,768]{1,0:T(8,128)(2,1)S(1)}, bf16[192,768]{1,0:T(8,128)(2,1)}, u32[]{:S(2)}, u32[]{:S(2)}) %collective-permute-start.38) | collective-permute-done | bytes 294944 | tf_op jit(solution)/shard_map/ppermute | solution.py:438
  189.2 1.3 fusion.6
  190.8 0.8 copy.78
  191.7 6.4 %all-to-all-start.1 = ((bf16[4,192,192]{2,1,0:T(8,128)(2,1)}), bf16[4,192,192]{2,1,0:T(8,128)(2,1)S(1)}, u32[]{:S(2)}, u32[]{:S(2)}) async-start(bf16[4,192,192]{2,1,0:T(8,128)(2,1)} %bitcast.86), calls=%async_computation.1 | async-start | bytes 786432 | tf_op jit(solution)/shard_map/all_to_all | solution.py:578
  198.1 1.8 fusion.1
  200.0 3.6 %all-to-all-done.1 = bf16[4,192,192]{2,1,0:T(8,128)(2,1)S(1)} async-done(((bf16[4,192,192]{2,1,0:T(8,128)(2,1)}), bf16[4,192,192]{2,1,0:T(8,128)(2,1)S(1)}, u32[]{:S(2)}, u32[]{:S(2)}) %all-to-all-start.1) | async-done | bytes 294944 | tf_op jit(solution)/shard_map/all_to_all | solution.py:578
  203.7 0.9 copy.75
  205.1 1.0 reshape.71
  206.2 1.2 collective-permute-start.29
  207.4 1.2 fusion.11
  208.7 3.3 %collective-permute-start.35 = (bf16[96,768]{1,0:T(8,128)(2,1)S(1)}, bf16[96,768]{1,0:T(8,128)(2,1)S(1)}, u32[]{:S(2)}, u32[]{:S(2)}) collective-permute-start(bf16[96,768]{1,0:T(8,128)(2,1)S(1)} %get-tuple-element.124), channel_id=1, source_target_pairs={{0,24},{4,28},{8,0},{12,4},{16,8},{20,12},{24,16},{28,20},{1,25},{... | collective-permute-start | bytes 442376 | tf_op jit(solution)/shard_map/ppermute | solution.py:438
  211.9 8.0 %collective-permute-done.29.refs_3_ = bf16[256,768]{1,0:T(8,128)(2,1)S(1)} collective-permute-done((bf16[256,768]{1,0:T(8,128)(2,1)S(1)}, bf16[256,768]{1,0:T(8,128)(2,1)S(1)}, u32[]{:S(2)}, u32[]{:S(2)}) %collective-permute-start.29) | collective-permute-done | bytes 393248 | tf_op jit(solution)/shard_map/ppermute | solution.py:432
  219.9 0.7 fusion.10
  220.7 1.5 collective-permute-start.40
  222.2 1.2 collective-permute-done.34
  224.7 0.8 collective-permute-start.41
  225.5 0.8 fusion.14
  227.0 3.9 %finish.1 = (bf16[3,70,768]{2,1,0:T(8,128)(2,1)}, bf16[3,70,768]{2,1,0:T(8,128)(2,1)}) custom-call(s32[3]{0:T(128)} %pad_add_fusion.refs_0_, bf16[256,768]{1,0:T(8,128)(2,1)} %get-tuple-element.85.refs_1_, bf16[2,256,768]{2,1,0:T(8,128)(2,1)} %copy-done, bf16[256,768]{1,0:T(8,128)(2,1)} %copy-done.5, bf16[3,70,768]{2,1,0:T(8,128)(2,1)} %refs_4_.1, ...), custom_call_target="tpu_custom_call" | custom-call | bytes 5538828 | tf_op jit(solution)/shard_map/finish/pallas_call | solution.py:45
  (161 shorter events, 15.6 us)
Async XLA Ops:
  0.7 14.9 %copy-start.26 = (bf16[384,192]{0,1:T(8,128)(2,1)S(1)}, bf16[384,192]{0,1:T(8,128)(2,1)}, u32[]{:S(2)}) copy-start(bf16[384,192]{0,1:T(8,128)(2,1)} %param.28) | copy-start | bytes 442372
  0.7 15.4 %copy-start.28 = (bf16[96,192]{1,0:T(8,128)(2,1)S(1)}, bf16[96,192]{1,0:T(8,128)(2,1)}, u32[]{:S(2)}) copy-start(bf16[96,192]{1,0:T(8,128)(2,1)} %param.26) | copy-start | bytes 110596
  8.8 6.9 %collective-permute-start.5 = (bf16[96,640]{1,0:T(8,128)(2,1)S(1)}, bf16[96,640]{1,0:T(8,128)(2,1)S(1)}, u32[]{:S(2)}, u32[]{:S(2)}) collective-permute-start(bf16[96,640]{1,0:T(8,128)(2,1)S(1)} %concatenate.7.refs_6_), channel_id=1, source_target_pairs={{0,24},{4,28},{8,0},{12,4},{16,8},{20,12},{24,16},{28,20},{1,25},{... | collective-permute-start | bytes 368648 | tf_op jit(solution)/shard_map/ppermute | solution.py:438
  12.2 11.8 %collective-permute-start.6 = (bf16[96,640]{1,0:T(8,128)(2,1)S(1)}, bf16[96,640]{1,0:T(8,128)(2,1)S(1)}, u32[]{:S(2)}, u32[]{:S(2)}) collective-permute-start(bf16[96,640]{1,0:T(8,128)(2,1)S(1)} %concatenate.7.refs_6_), channel_id=1, source_target_pairs={{0,4},{4,0},{8,12},{12,8},{16,20},{20,16},{24,28},{28,24},{1,5},{5... | collective-permute-start | bytes 368648 | tf_op jit(solution)/shard_map/ppermute | solution.py:435
  13.4 10.7 %collective-permute-start.4 = (bf16[96,640]{1,0:T(8,128)(2,1)S(1)}, bf16[96,640]{1,0:T(8,128)(2,1)S(1)}, u32[]{:S(2)}, u32[]{:S(2)}) collective-permute-start(bf16[96,640]{1,0:T(8,128)(2,1)S(1)} %concatenate.7.refs_6_), channel_id=1, source_target_pairs={{0,16},{4,20},{8,24},{12,28},{16,0},{20,4},{24,8},{28,12},{1,17},{... | collective-permute-start | bytes 368648 | tf_op jit(solution)/shard_map/ppermute | solution.py:438
  13.4 11.1 %collective-permute-start.3 = (bf16[96,640]{1,0:T(8,128)(2,1)S(1)}, bf16[96,640]{1,0:T(8,128)(2,1)S(1)}, u32[]{:S(2)}, u32[]{:S(2)}) collective-permute-start(bf16[96,640]{1,0:T(8,128)(2,1)S(1)} %concatenate.7.refs_6_), channel_id=1, source_target_pairs={{0,8},{4,12},{8,16},{12,20},{16,24},{20,28},{24,0},{28,4},{1,9},{5... | collective-permute-start | bytes 368648 | tf_op jit(solution)/shard_map/ppermute | solution.py:438
  13.9 16.7 %collective-permute-start.1 = (bf16[3,70,768]{2,1,0:T(8,128)(2,1)}, bf16[3,70,768]{2,1,0:T(8,128)(2,1)}, u32[]{:S(2)}, u32[]{:S(2)}) collective-permute-start(bf16[3,70,768]{2,1,0:T(8,128)(2,1)} %refs_4_.1), channel_id=1, source_target_pairs={{0,2},{1,3},{2,0},{3,1},{4,6},{5,7},{6,4},{7,5},{8,10},{9,11},{10,... | collective-permute-start | bytes 967688 | tf_op jit(solution)/shard_map/ppermute | solution.py:432
  15.7 9.0 %collective-permute-start.9 = (bf16[96,640]{1,0:T(8,128)(2,1)S(1)}, bf16[96,640]{1,0:T(8,128)(2,1)S(1)}, u32[]{:S(2)}, u32[]{:S(2)}) collective-permute-start(bf16[96,640]{1,0:T(8,128)(2,1)S(1)} %collective-permute-done.5.refs_9_), channel_id=1, source_target_pairs={{0,4},{4,0},{8,12},{12,8},{16,20},{20,16},{24,28},{28,24},{1,5},{5... | collective-permute-start | bytes 368648 | tf_op jit(solution)/shard_map/ppermute | solution.py:435
  16.1 15.9 %copy-start.29 = (s32[3,40]{1,0:T(4,128)S(1)}, s32[3,40]{1,0:T(4,128)}, u32[]{:S(2)}) copy-start(s32[3,40]{1,0:T(4,128)} %param.21) | copy-start | bytes 1444
  17.1 15.1 %all-to-all-start = ((bf16[4,3,96,192]{3,2,1,0:T(8,128)(2,1)}), bf16[4,3,96,192]{3,2,1,0:T(8,128)(2,1)S(1)}, u32[]{:S(2)}, u32[]{:S(2)}) async-start(bf16[4,3,96,192]{3,2,1,0:T(8,128)(2,1)} %pad_maximum_fusion), calls=%async_computation | async-start | bytes 1179648 | tf_op jit(solution)/shard_map/all_to_all | solution.py:467
  24.0 14.7 %collective-permute-start.14 = (bf16[3,70,768]{2,1,0:T(8,128)(2,1)S(1)}, bf16[3,70,768]{2,1,0:T(8,128)(2,1)S(1)}, u32[]{:S(2)}, u32[]{:S(2)}) collective-permute-start(bf16[3,70,768]{2,1,0:T(8,128)(2,1)S(1)} %copy-done.18), channel_id=1, source_target_pairs={{0,2},{1,3},{2,0},{3,1},{4,6},{5,7},{6,4},{7,5},{8,10},{9,11},{10,... | collective-permute-start | bytes 967688 | tf_op jit(solution)/shard_map/ppermute | solution.py:432
  24.2 18.2 %collective-permute-start.13 = (bf16[3,70,768]{2,1,0:T(8,128)(2,1)S(1)}, bf16[3,70,768]{2,1,0:T(8,128)(2,1)S(1)}, u32[]{:S(2)}, u32[]{:S(2)}) collective-permute-start(bf16[3,70,768]{2,1,0:T(8,128)(2,1)S(1)} %copy-done.18), channel_id=1, source_target_pairs={{0,1},{1,0},{2,3},{3,2},{4,5},{5,4},{6,7},{7,6},{8,9},{9,8},{10,11... | collective-permute-start | bytes 967688 | tf_op jit(solution)/shard_map/ppermute | solution.py:432
  24.6 17.8 %copy-start.36 = (bf16[96,640]{1,0:T(8,128)(2,1)}, bf16[96,640]{1,0:T(8,128)(2,1)S(1)}, u32[]{:S(2)}) copy-start(bf16[96,640]{1,0:T(8,128)(2,1)S(1)} %collective-permute-done.3.refs_7_) | copy-start | bytes 368644
  24.6 18.3 %collective-permute-start = (bf16[3,70,768]{2,1,0:T(8,128)(2,1)S(1)}, bf16[3,70,768]{2,1,0:T(8,128)(2,1)}, u32[]{:S(2)}, u32[]{:S(2)}) collective-permute-start(bf16[3,70,768]{2,1,0:T(8,128)(2,1)S(1)} %copy-done.22), channel_id=1, source_target_pairs={{0,1},{1,0},{2,3},{3,2},{4,5},{5,4},{6,7},{7,6},{8,9},{9,8},{10,11... | collective-permute-start | bytes 967688 | tf_op jit(solution)/shard_map/ppermute | solution.py:432
  24.8 4.5 %collective-permute-start.8 = (bf16[96,640]{1,0:T(8,128)(2,1)S(1)}, bf16[96,640]{1,0:T(8,128)(2,1)S(1)}, u32[]{:S(2)}, u32[]{:S(2)}) collective-permute-start(bf16[96,640]{1,0:T(8,128)(2,1)S(1)} %collective-permute-done.4.refs_8_), channel_id=1, source_target_pairs={{0,4},{4,0},{8,12},{12,8},{16,20},{20,16},{24,28},{28,24},{1,5},{5... | collective-permute-start | bytes 368648 | tf_op jit(solution)/shard_map/ppermute | solution.py:435
  29.3 16.6 %copy-start.38 = (bf16[96,640]{1,0:T(8,128)(2,1)}, bf16[96,640]{1,0:T(8,128)(2,1)S(1)}, u32[]{:S(2)}) copy-start(bf16[96,640]{1,0:T(8,128)(2,1)S(1)} %collective-permute-done.8.refs_12_) | copy-start | bytes 368644
  29.3 10.1 %collective-permute-start.7 = (bf16[96,640]{1,0:T(8,128)(2,1)S(1)}, bf16[96,640]{1,0:T(8,128)(2,1)S(1)}, u32[]{:S(2)}, u32[]{:S(2)}) collective-permute-start(bf16[96,640]{1,0:T(8,128)(2,1)S(1)} %collective-permute-done.3.refs_7_), channel_id=1, source_target_pairs={{0,4},{4,0},{8,12},{12,8},{16,20},{20,16},{24,28},{28,24},{1,5},{5... | collective-permute-start | bytes 368648 | tf_op jit(solution)/shard_map/ppermute | solution.py:435
  30.5 14.6 %collective-permute-start.2 = (bf16[3,70,768]{2,1,0:T(8,128)(2,1)}, bf16[3,70,768]{2,1,0:T(8,128)(2,1)}, u32[]{:S(2)}, u32[]{:S(2)}) collective-permute-start(bf16[3,70,768]{2,1,0:T(8,128)(2,1)} %collective-permute-done.1.refs_4_.refs_3_), channel_id=1, source_target_pairs={{0,1},{1,0},{2,3},{3,2},{4,5},{5,4},{6,7},{7,6},{8,9},{9,8},{10,11... | collective-permute-start | bytes 967688 | tf_op jit(solution)/shard_map/ppermute | solution.py:432
  33.2 24.1 %copy-start.1 = (bf16[3,96,768]{2,1,0:T(8,128)(2,1)}, bf16[3,96,768]{2,1,0:T(8,128)(2,1)S(1)}, u32[]{:S(2)}) copy-start(bf16[3,96,768]{2,1,0:T(8,128)(2,1)S(1)} %reshape.68.refs_5_) | copy-start | bytes 1327108
  38.8 18.5 %copy-start.19 = (bf16[3,70,768]{2,1,0:T(8,128)(2,1)}, bf16[3,70,768]{2,1,0:T(8,128)(2,1)S(1)}, u32[]{:S(2)}) copy-start(bf16[3,70,768]{2,1,0:T(8,128)(2,1)S(1)} %collective-permute-done.14.refs_3_) | copy-start | bytes 967684
  38.8 18.5 %collective-permute-start.15 = (bf16[3,70,768]{2,1,0:T(8,128)(2,1)S(1)}, bf16[3,70,768]{2,1,0:T(8,128)(2,1)S(1)}, u32[]{:S(2)}, u32[]{:S(2)}) collective-permute-start(bf16[3,70,768]{2,1,0:T(8,128)(2,1)S(1)} %collective-permute-done.14.refs_3_), channel_id=1, source_target_pairs={{0,1},{1,0},{2,3},{3,2},{4,5},{5,4},{6,7},{7,6},{8,9},{9,8},{10,11... | collective-permute-start | bytes 967688 | tf_op jit(solution)/shard_map/ppermute | solution.py:432
  39.4 19.3 %collective-permute-start.18 = (bf16[3,96,768]{2,1,0:T(8,128)(2,1)S(1)}, bf16[3,96,768]{2,1,0:T(8,128)(2,1)S(1)}, u32[]{:S(2)}, u32[]{:S(2)}) collective-permute-start(bf16[3,96,768]{2,1,0:T(8,128)(2,1)S(1)} %reshape.68.refs_5_), channel_id=1, source_target_pairs={{0,24},{4,28},{8,0},{12,4},{16,8},{20,12},{24,16},{28,20},{1,25},{... | collective-permute-start | bytes 1327112 | tf_op jit(solution)/shard_map/ppermute | solution.py:438
  42.4 14.8 %copy-start.20 = (bf16[3,70,768]{2,1,0:T(8,128)(2,1)}, bf16[3,70,768]{2,1,0:T(8,128)(2,1)S(1)}, u32[]{:S(2)}) copy-start(bf16[3,70,768]{2,1,0:T(8,128)(2,1)S(1)} %collective-permute-done.13.refs_2_) | copy-start | bytes 967684
  42.4 39.0 %collective-permute-start.17 = (bf16[3,96,768]{2,1,0:T(8,128)(2,1)S(1)}, bf16[3,96,768]{2,1,0:T(8,128)(2,1)S(1)}, u32[]{:S(2)}, u32[]{:S(2)}) collective-permute-start(bf16[3,96,768]{2,1,0:T(8,128)(2,1)S(1)} %reshape.68.refs_5_), channel_id=1, source_target_pairs={{0,16},{4,20},{8,24},{12,28},{16,0},{20,4},{24,8},{28,12},{1,17},{... | collective-permute-start | bytes 1327112 | tf_op jit(solution)/shard_map/ppermute | solution.py:438
  42.9 39.8 %collective-permute-start.16 = (bf16[3,96,768]{2,1,0:T(8,128)(2,1)S(1)}, bf16[3,96,768]{2,1,0:T(8,128)(2,1)S(1)}, u32[]{:S(2)}, u32[]{:S(2)}) collective-permute-start(bf16[3,96,768]{2,1,0:T(8,128)(2,1)S(1)} %reshape.68.refs_5_), channel_id=1, source_target_pairs={{0,8},{4,12},{8,16},{12,20},{16,24},{20,28},{24,0},{28,4},{1,9},{5... | collective-permute-start | bytes 1327112 | tf_op jit(solution)/shard_map/ppermute | solution.py:438
  45.2 37.8 %collective-permute-start.19 = (bf16[3,96,768]{2,1,0:T(8,128)(2,1)S(1)}, bf16[3,96,768]{2,1,0:T(8,128)(2,1)S(1)}, u32[]{:S(2)}, u32[]{:S(2)}) collective-permute-start(bf16[3,96,768]{2,1,0:T(8,128)(2,1)S(1)} %reshape.68.refs_5_), channel_id=1, source_target_pairs={{0,4},{4,0},{8,12},{12,8},{16,20},{20,16},{24,28},{28,24},{1,5},{5... | collective-permute-start | bytes 1327112 | tf_op jit(solution)/shard_map/ppermute | solution.py:435
  57.3 44.5 %copy-start.21 = (bf16[3,70,768]{2,1,0:T(8,128)(2,1)}, bf16[3,70,768]{2,1,0:T(8,128)(2,1)S(1)}, u32[]{:S(2)}) copy-start(bf16[3,70,768]{2,1,0:T(8,128)(2,1)S(1)} %collective-permute-done.15.refs_4_) | copy-start | bytes 967684
  57.3 27.1 %collective-permute-start.11 = (bf16[480,384]{1,0:T(8,128)(2,1)}, bf16[480,384]{1,0:T(8,128)(2,1)S(1)}, u32[]{:S(2)}, u32[]{:S(2)}) collective-permute-start(bf16[480,384]{1,0:T(8,128)(2,1)} %get-tuple-element.60.refs_5_), channel_id=1, source_target_pairs={{0,2},{1,3},{2,0},{3,1},{4,6},{5,7},{6,4},{7,5},{8,10},{9,11},{10,... | collective-permute-start | bytes 1105928 | tf_op jit(solution)/shard_map/ppermute | solution.py:432
  58.7 43.1 %copy-start.6 = (bf16[3,96,768]{2,1,0:T(8,128)(2,1)}, bf16[3,96,768]{2,1,0:T(8,128)(2,1)S(1)}, u32[]{:S(2)}) copy-start(bf16[3,96,768]{2,1,0:T(8,128)(2,1)S(1)} %collective-permute-done.18.refs_8_) | copy-start | bytes 1327108
  58.7 25.7 %collective-permute-start.22 = (bf16[3,96,768]{2,1,0:T(8,128)(2,1)S(1)}, bf16[3,96,768]{2,1,0:T(8,128)(2,1)S(1)}, u32[]{:S(2)}, u32[]{:S(2)}) collective-permute-start(bf16[3,96,768]{2,1,0:T(8,128)(2,1)S(1)} %collective-permute-done.18.refs_8_), channel_id=1, source_target_pairs={{0,4},{4,0},{8,12},{12,8},{16,20},{20,16},{24,28},{28,24},{1,5},{5... | collective-permute-start | bytes 1327112 | tf_op jit(solution)/shard_map/ppermute | solution.py:435
  81.5 20.3 %copy-start.7 = (bf16[3,96,768]{2,1,0:T(8,128)(2,1)}, bf16[3,96,768]{2,1,0:T(8,128)(2,1)S(1)}, u32[]{:S(2)}) copy-start(bf16[3,96,768]{2,1,0:T(8,128)(2,1)S(1)} %collective-permute-done.17.refs_7_) | copy-start | bytes 1327108
  81.5 10.8 %collective-permute-start.21 = (bf16[3,96,768]{2,1,0:T(8,128)(2,1)S(1)}, bf16[3,96,768]{2,1,0:T(8,128)(2,1)S(1)}, u32[]{:S(2)}, u32[]{:S(2)}) collective-permute-start(bf16[3,96,768]{2,1,0:T(8,128)(2,1)S(1)} %collective-permute-done.17.refs_7_), channel_id=1, source_target_pairs={{0,4},{4,0},{8,12},{12,8},{16,20},{20,16},{24,28},{28,24},{1,5},{5... | collective-permute-start | bytes 1327112 | tf_op jit(solution)/shard_map/ppermute | solution.py:435
  82.7 19.1 %copy-start.8 = (bf16[3,96,768]{2,1,0:T(8,128)(2,1)}, bf16[3,96,768]{2,1,0:T(8,128)(2,1)S(1)}, u32[]{:S(2)}) copy-start(bf16[3,96,768]{2,1,0:T(8,128)(2,1)S(1)} %collective-permute-done.16.refs_6_) | copy-start | bytes 1327108
  82.7 19.1 %collective-permute-start.20 = (bf16[3,96,768]{2,1,0:T(8,128)(2,1)S(1)}, bf16[3,96,768]{2,1,0:T(8,128)(2,1)S(1)}, u32[]{:S(2)}, u32[]{:S(2)}) collective-permute-start(bf16[3,96,768]{2,1,0:T(8,128)(2,1)S(1)} %collective-permute-done.16.refs_6_), channel_id=1, source_target_pairs={{0,4},{4,0},{8,12},{12,8},{16,20},{20,16},{24,28},{28,24},{1,5},{5... | collective-permute-start | bytes 1327112 | tf_op jit(solution)/shard_map/ppermute | solution.py:435
  82.9 18.9 %copy-start.9 = (bf16[3,96,768]{2,1,0:T(8,128)(2,1)}, bf16[3,96,768]{2,1,0:T(8,128)(2,1)S(1)}, u32[]{:S(2)}) copy-start(bf16[3,96,768]{2,1,0:T(8,128)(2,1)S(1)} %collective-permute-done.19.refs_9_) | copy-start | bytes 1327108
  82.9 26.8 %collective-permute-start.10 = (bf16[480,384]{1,0:T(8,128)(2,1)}, bf16[480,384]{1,0:T(8,128)(2,1)S(1)}, u32[]{:S(2)}, u32[]{:S(2)}) collective-permute-start(bf16[480,384]{1,0:T(8,128)(2,1)} %get-tuple-element.60.refs_5_), channel_id=1, source_target_pairs={{0,1},{1,0},{2,3},{3,2},{4,5},{5,4},{6,7},{7,6},{8,9},{9,8},{10,11... | collective-permute-start | bytes 1105928 | tf_op jit(solution)/shard_map/ppermute | solution.py:432
  84.4 25.4 %copy-start.30 = (bf16[480,384]{1,0:T(8,128)(2,1)}, bf16[480,384]{1,0:T(8,128)(2,1)S(1)}, u32[]{:S(2)}) copy-start(bf16[480,384]{1,0:T(8,128)(2,1)S(1)} %collective-permute-done.11.refs_7_) | copy-start | bytes 1105924
  84.4 25.4 %collective-permute-start.12 = (bf16[480,384]{1,0:T(8,128)(2,1)S(1)}, bf16[480,384]{1,0:T(8,128)(2,1)S(1)}, u32[]{:S(2)}, u32[]{:S(2)}) collective-permute-start(bf16[480,384]{1,0:T(8,128)(2,1)S(1)} %collective-permute-done.11.refs_7_), channel_id=1, source_target_pairs={{0,1},{1,0},{2,3},{3,2},{4,5},{5,4},{6,7},{7,6},{8,9},{9,8},{10,11... | collective-permute-start | bytes 1105928 | tf_op jit(solution)/shard_map/ppermute | solution.py:432
  84.5 17.4 %copy-start.10 = (bf16[3,96,768]{2,1,0:T(8,128)(2,1)}, bf16[3,96,768]{2,1,0:T(8,128)(2,1)S(1)}, u32[]{:S(2)}) copy-start(bf16[3,96,768]{2,1,0:T(8,128)(2,1)S(1)} %collective-permute-done.22.refs_12_) | copy-start | bytes 1327108
  122.4 12.0 %collective-permute-start.23 = (bf16[2,240,768]{2,1,0:T(8,128)(2,1)}, bf16[2,240,768]{2,1,0:T(8,128)(2,1)S(1)}, u32[]{:S(2)}, u32[]{:S(2)}) collective-permute-start(bf16[2,240,768]{2,1,0:T(8,128)(2,1)} %get-tuple-element.66), channel_id=1, source_target_pairs={{0,1},{1,0},{2,3},{3,2},{4,5},{5,4},{6,7},{7,6},{8,9},{9,8},{10,11... | collective-permute-start | bytes 2211848 | tf_op jit(solution)/shard_map/ppermute | solution.py:432
  124.2 10.2 %copy-start.16 = (bf16[240,768]{1,0:T(8,128)(2,1)S(1)}, bf16[240,768]{1,0:T(8,128)(2,1)}, u32[]{:S(2)}) copy-start(bf16[240,768]{1,0:T(8,128)(2,1)} %get-tuple-element.67) | copy-start | bytes 1105924
  133.2 27.8 %collective-permute-start.36 = (bf16[4,192,768]{2,1,0:T(8,128)(2,1)}, bf16[4,192,768]{2,1,0:T(8,128)(2,1)S(1)}, u32[]{:S(2)}, u32[]{:S(2)}) collective-permute-start(bf16[4,192,768]{2,1,0:T(8,128)(2,1)} %get-tuple-element.98), channel_id=1, source_target_pairs={{0,4},{4,0},{8,12},{12,8},{16,20},{20,16},{24,28},{28,24},{1,5},{5... | collective-permute-start | bytes 3538952 | tf_op jit(solution)/shard_map/ppermute | solution.py:435
  134.5 9.9 %collective-permute-start.24 = (bf16[240,768]{1,0:T(8,128)(2,1)S(1)}, bf16[240,768]{1,0:T(8,128)(2,1)S(1)}, u32[]{:S(2)}, u32[]{:S(2)}) collective-permute-start(bf16[240,768]{1,0:T(8,128)(2,1)S(1)} %fusion.2), channel_id=1, source_target_pairs={{0,2},{1,3},{2,0},{3,1},{4,6},{5,7},{6,4},{7,5},{8,10},{9,11},{10,... | collective-permute-start | bytes 1105928 | tf_op jit(solution)/shard_map/ppermute | solution.py:432
  135.9 62.1 %collective-permute-start.30 = (bf16[2,240,768]{2,1,0:T(8,128)(2,1)}, bf16[2,240,768]{2,1,0:T(8,128)(2,1)}, u32[]{:S(2)}, u32[]{:S(2)}) collective-permute-start(bf16[2,240,768]{2,1,0:T(8,128)(2,1)} %get-tuple-element.90), channel_id=1, source_target_pairs={{0,1},{1,0},{2,3},{3,2},{4,5},{5,4},{6,7},{7,6},{8,9},{9,8},{10,11... | collective-permute-start | bytes 2211848 | tf_op jit(solution)/shard_map/ppermute | solution.py:432
  145.2 15.8 %copy-start.3 = (bf16[4,192,768]{2,1,0:T(8,128)(2,1)S(1)}, bf16[4,192,768]{2,1,0:T(8,128)(2,1)}, u32[]{:S(2)}) copy-start(bf16[4,192,768]{2,1,0:T(8,128)(2,1)} %get-tuple-element.97) | copy-start | bytes 3538948
  149.5 12.7 %collective-permute-start.25 = (bf16[240,384]{1,0:T(8,128)(2,1)}, bf16[240,384]{1,0:T(8,128)(2,1)S(1)}, u32[]{:S(2)}, u32[]{:S(2)}) collective-permute-start(bf16[240,384]{1,0:T(8,128)(2,1)} %get-tuple-element.72), channel_id=1, source_target_pairs={{0,1},{1,0},{2,3},{3,2},{4,5},{5,4},{6,7},{7,6},{8,9},{9,8},{10,11... | collective-permute-start | bytes 552968 | tf_op jit(solution)/shard_map/ppermute | solution.py:432
  150.6 14.8 %collective-permute-start.26 = (bf16[240,384]{1,0:T(8,128)(2,1)}, bf16[240,384]{1,0:T(8,128)(2,1)S(1)}, u32[]{:S(2)}, u32[]{:S(2)}) collective-permute-start(bf16[240,384]{1,0:T(8,128)(2,1)} %get-tuple-element.73), channel_id=1, source_target_pairs={{0,2},{1,3},{2,0},{3,1},{4,6},{5,7},{6,4},{7,5},{8,10},{9,11},{10,... | collective-permute-start | bytes 552968 | tf_op jit(solution)/shard_map/ppermute | solution.py:432
  152.0 13.4 %collective-permute-start.27 = (bf16[240,384]{1,0:T(8,128)(2,1)}, bf16[240,384]{1,0:T(8,128)(2,1)S(1)}, u32[]{:S(2)}, u32[]{:S(2)}) collective-permute-start(bf16[240,384]{1,0:T(8,128)(2,1)} %get-tuple-element.74), channel_id=1, source_target_pairs={{0,3},{1,2},{2,1},{3,0},{4,7},{5,6},{6,5},{7,4},{8,11},{9,10},{10,... | collective-permute-start | bytes 552968 | tf_op jit(solution)/shard_map/ppermute | solution.py:432
  162.1 19.6 %collective-permute-start.37 = (bf16[192,768]{1,0:T(8,128)(2,1)}, bf16[192,768]{1,0:T(8,128)(2,1)}, u32[]{:S(2)}, u32[]{:S(2)}) collective-permute-start(bf16[192,768]{1,0:T(8,128)(2,1)} %get-tuple-element.118), channel_id=1, source_target_pairs={{0,8},{4,12},{8,16},{12,20},{16,24},{20,28},{24,0},{28,4},{1,9},{5... | collective-permute-start | bytes 884744 | tf_op jit(solution)/shard_map/ppermute | solution.py:438
  162.2 20.8 %collective-permute-start.39 = (bf16[192,768]{1,0:T(8,128)(2,1)}, bf16[192,768]{1,0:T(8,128)(2,1)}, u32[]{:S(2)}, u32[]{:S(2)}) collective-permute-start(bf16[192,768]{1,0:T(8,128)(2,1)} %get-tuple-element.119), channel_id=1, source_target_pairs={{0,24},{4,28},{8,0},{12,4},{16,8},{20,12},{24,16},{28,20},{1,25},{... | collective-permute-start | bytes 884744 | tf_op jit(solution)/shard_map/ppermute | solution.py:438
  165.4 23.8 %collective-permute-start.38 = (bf16[192,768]{1,0:T(8,128)(2,1)S(1)}, bf16[192,768]{1,0:T(8,128)(2,1)}, u32[]{:S(2)}, u32[]{:S(2)}) collective-permute-start(bf16[192,768]{1,0:T(8,128)(2,1)S(1)} %get-tuple-element.120), channel_id=1, source_target_pairs={{0,16},{4,20},{8,24},{12,28},{16,0},{20,4},{24,8},{28,12},{1,17},{... | collective-permute-start | bytes 884744 | tf_op jit(solution)/shard_map/ppermute | solution.py:438
  180.4 25.7 %collective-permute-start.28 = (bf16[2,256,768]{2,1,0:T(8,128)(2,1)}, bf16[2,256,768]{2,1,0:T(8,128)(2,1)S(1)}, u32[]{:S(2)}, u32[]{:S(2)}) collective-permute-start(bf16[2,256,768]{2,1,0:T(8,128)(2,1)} %get-tuple-element.86), channel_id=1, source_target_pairs={{0,1},{1,0},{2,3},{3,2},{4,5},{5,4},{6,7},{7,6},{8,9},{9,8},{10,11... | collective-permute-start | bytes 2359304 | tf_op jit(solution)/shard_map/ppermute | solution.py:432
  181.7 25.6 %collective-permute-start.32 = (bf16[4,96,768]{2,1,0:T(8,128)(2,1)}, bf16[4,96,768]{2,1,0:T(8,128)(2,1)}, u32[]{:S(2)}, u32[]{:S(2)}) collective-permute-start(bf16[4,96,768]{2,1,0:T(8,128)(2,1)} %get-tuple-element.96), channel_id=1, source_target_pairs={{0,4},{4,0},{8,12},{12,8},{16,20},{20,16},{24,28},{28,24},{1,5},{5... | collective-permute-start | bytes 1769480 | tf_op jit(solution)/shard_map/ppermute | solution.py:435
  191.7 12.0 %all-to-all-start.1 = ((bf16[4,192,192]{2,1,0:T(8,128)(2,1)}), bf16[4,192,192]{2,1,0:T(8,128)(2,1)S(1)}, u32[]{:S(2)}, u32[]{:S(2)}) async-start(bf16[4,192,192]{2,1,0:T(8,128)(2,1)} %bitcast.86), calls=%async_computation.1 | async-start | bytes 786432 | tf_op jit(solution)/shard_map/all_to_all | solution.py:578
  199.9 26.4 %collective-permute-start.31 = (bf16[240,768]{1,0:T(8,128)(2,1)}, bf16[240,768]{1,0:T(8,128)(2,1)S(1)}, u32[]{:S(2)}, u32[]{:S(2)}) collective-permute-start(bf16[240,768]{1,0:T(8,128)(2,1)} %fusion.1), channel_id=1, source_target_pairs={{0,2},{1,3},{2,0},{3,1},{4,6},{5,7},{6,4},{7,5},{8,10},{9,11},{10,... | collective-permute-start | bytes 1105928 | tf_op jit(solution)/shard_map/ppermute | solution.py:432
  206.1 13.9 %copy-start = (bf16[2,256,768]{2,1,0:T(8,128)(2,1)}, bf16[2,256,768]{2,1,0:T(8,128)(2,1)S(1)}, u32[]{:S(2)}) copy-start(bf16[2,256,768]{2,1,0:T(8,128)(2,1)S(1)} %collective-permute-done.28.refs_2_) | copy-start | bytes 2359300
  206.2 13.8 %collective-permute-start.29 = (bf16[256,768]{1,0:T(8,128)(2,1)S(1)}, bf16[256,768]{1,0:T(8,128)(2,1)S(1)}, u32[]{:S(2)}, u32[]{:S(2)}) collective-permute-start(bf16[256,768]{1,0:T(8,128)(2,1)S(1)} %fusion), channel_id=1, source_target_pairs={{0,2},{1,3},{2,0},{3,1},{4,6},{5,7},{6,4},{7,5},{8,10},{9,11},{10,... | collective-permute-start | bytes 1179656 | tf_op jit(solution)/shard_map/ppermute | solution.py:432
  208.6 13.6 %collective-permute-start.33 = (bf16[96,768]{1,0:T(8,128)(2,1)S(1)}, bf16[96,768]{1,0:T(8,128)(2,1)S(1)}, u32[]{:S(2)}, u32[]{:S(2)}) collective-permute-start(bf16[96,768]{1,0:T(8,128)(2,1)S(1)} %get-tuple-element.123), channel_id=1, source_target_pairs={{0,8},{4,12},{8,16},{12,20},{16,24},{20,28},{24,0},{28,4},{1,9},{5... | collective-permute-start | bytes 442376 | tf_op jit(solution)/shard_map/ppermute | solution.py:438
  208.7 13.5 %collective-permute-start.35 = (bf16[96,768]{1,0:T(8,128)(2,1)S(1)}, bf16[96,768]{1,0:T(8,128)(2,1)S(1)}, u32[]{:S(2)}, u32[]{:S(2)}) collective-permute-start(bf16[96,768]{1,0:T(8,128)(2,1)S(1)} %get-tuple-element.124), channel_id=1, source_target_pairs={{0,24},{4,28},{8,0},{12,4},{16,8},{20,12},{24,16},{28,20},{1,25},{... | collective-permute-start | bytes 442376 | tf_op jit(solution)/shard_map/ppermute | solution.py:438
  211.9 11.5 %collective-permute-start.34 = (bf16[96,768]{1,0:T(8,128)(2,1)S(1)}, bf16[96,768]{1,0:T(8,128)(2,1)S(1)}, u32[]{:S(2)}, u32[]{:S(2)}) collective-permute-start(bf16[96,768]{1,0:T(8,128)(2,1)S(1)} %get-tuple-element.125), channel_id=1, source_target_pairs={{0,16},{4,20},{8,24},{12,28},{16,0},{20,4},{24,8},{28,12},{1,17},{... | collective-permute-start | bytes 442376 | tf_op jit(solution)/shard_map/ppermute | solution.py:438
  220.7 3.3 %collective-permute-start.40 = (f32[16,768]{1,0:T(8,128)S(1)}, f32[16,768]{1,0:T(8,128)S(1)}, u32[]{:S(2)}, u32[]{:S(2)}) collective-permute-start(f32[16,768]{1,0:T(8,128)S(1)} %fusion.10), channel_id=1, source_target_pairs={{0,4},{4,0},{8,12},{12,8},{16,20},{20,16},{24,28},{28,24},{1,5},{5... | collective-permute-start | bytes 147464 | tf_op jit(solution)/shard_map/ppermute | solution.py:435
  224.0 6.9 %collective-permute-start.43 = (f32[16,768]{1,0:T(8,128)S(1)}, f32[16,768]{1,0:T(8,128)S(1)}, u32[]{:S(2)}, u32[]{:S(2)}) collective-permute-start(f32[16,768]{1,0:T(8,128)S(1)} %add.73), channel_id=1, source_target_pairs={{0,24},{4,28},{8,0},{12,4},{16,8},{20,12},{24,16},{28,20},{1,25},{... | collective-permute-start | bytes 147464 | tf_op jit(solution)/shard_map/ppermute | solution.py:438
  224.7 6.2 %collective-permute-start.42 = (f32[16,768]{1,0:T(8,128)S(1)}, f32[16,768]{1,0:T(8,128)S(1)}, u32[]{:S(2)}, u32[]{:S(2)}) collective-permute-start(f32[16,768]{1,0:T(8,128)S(1)} %add.73), channel_id=1, source_target_pairs={{0,16},{4,20},{8,24},{12,28},{16,0},{20,4},{24,8},{28,12},{1,17},{... | collective-permute-start | bytes 147464 | tf_op jit(solution)/shard_map/ppermute | solution.py:438
  224.7 6.2 %collective-permute-start.41 = (f32[16,768]{1,0:T(8,128)S(1)}, f32[16,768]{1,0:T(8,128)S(1)}, u32[]{:S(2)}, u32[]{:S(2)}) collective-permute-start(f32[16,768]{1,0:T(8,128)S(1)} %add.73), channel_id=1, source_target_pairs={{0,8},{4,12},{8,16},{12,20},{16,24},{20,28},{24,0},{28,4},{1,9},{5... | collective-permute-start | bytes 147464 | tf_op jit(solution)/shard_map/ppermute | solution.py:438
  (22 other events, 99.6 us)

commit v2 on v1

v2 whole, which is shorter than its diff:
```python
import functools
from types import SimpleNamespace

import jax
import jax.numpy as jnp
from jax import lax
from jax.experimental import pallas as pl
from jax.experimental.pallas import tpu as pltpu
from jax.sharding import PartitionSpec as P

HEADS = 12
EPS = 1e-05
LOW = jnp.bfloat16
F32 = jnp.float32
VECS = 16
UP_BIAS = 12
SQRT_HALF = 0.7071067811865476
PDF_SCALE = 0.3989422804014327


def dot(left, right):
    return jnp.dot(left, right, preferred_element_type=F32)


def dot_t(left, right):
    return lax.dot_general(left, right, (((1,), (1,)), ((), ())), preferred_element_type=F32)


def t_dot(left, right):
    return lax.dot_general(left, right, (((0,), (0,)), ((), ())), preferred_element_type=F32)


def col_sum(values):
    return jnp.sum(values, axis=0, keepdims=True)


def ds(start, size, align=16):
    if not isinstance(start, int):
        start = pl.multiple_of(start, align)
    return pl.ds(start, size)


def pallas(body, outs, ins, scratch=(), smem=0, here=False, name=None, mib=8, long=False):
    flops = 10**10 if long else 1000
    nbytes = sum(a.size * a.dtype.itemsize for a in ins)
    nbytes += sum(s.size * jnp.dtype(s.dtype).itemsize for s in outs)
    near = pl.BlockSpec(memory_space=pltpu.VMEM)

    def run(*refs):
        if here:
            dp = lax.axis_index("dp")
            body((lax.axis_index("seq"), lax.div(dp, 2), lax.rem(dp, 2)), *refs)
        else:
            body(*refs)

    return pl.pallas_call(
        run,
        out_shape=outs,
        in_specs=[pl.BlockSpec(memory_space=pltpu.SMEM)] * smem + [near] * (len(ins) - smem),
        out_specs=[near] * len(outs),
        scratch_shapes=list(scratch),
        compiler_params=pltpu.CompilerParams(vmem_limit_bytes=mib * 2**20),
        cost_estimate=pl.CostEstimate(flops=flops, bytes_accessed=nbytes, transcendentals=0),
        name=name,
    )(*ins)


def shape(*dims, dtype=LOW):
    return jax.ShapeDtypeStruct(dims, dtype)


def part_index(m, sc, part):
    z, x = sc[1], sc[2]
    k = part % m.nz
    side = x if part < m.nz else 1 - x
    return lax.rem(z - k + m.nz, m.nz) * 2 + side


def layer_norm(x):
    center = x - jnp.mean(x, axis=-1, keepdims=True)
    rstd = lax.rsqrt(jnp.mean(center * center, axis=-1, keepdims=True) + EPS)
    return center * rstd, rstd


def norm_back(grad, gain, xhat, rstd):
    scaled = grad * gain
    first = jnp.mean(scaled, axis=-1, keepdims=True)
    second = jnp.mean(scaled * xhat, axis=-1, keepdims=True)
    return rstd * (scaled - first - xhat * second)


def pack_kernel(m, query, key, value, *refs):
    vecs, first, rows = refs[:9], refs[9], refs[10]
    first[:, : m.WH] = query[...]
    first[:, m.WH : 2 * m.WH] = key[...]
    first[:, 2 * m.WH : 3 * m.WH] = value[...]
    first[:, 3 * m.WH :] = jnp.zeros((m.rows, m.wide - 3 * m.WH), LOW)
    rows[...] = jnp.zeros_like(rows)
    for k in range(8):
        rows[k : k + 1, :] = vecs[k][...].astype(F32).reshape(1, m.rows)
    up_bias = vecs[8][...].astype(F32).reshape(1, m.S * m.hrows)
    for c in range(m.S):
        rows[8 + c : 9 + c, :] = up_bias[:, c * m.hrows : (c + 1) * m.hrows]
    first[:, 3 * m.WH : 3 * m.WH + VECS] = rows[...].T.astype(LOW)


def pack_up_kernel(m, up, out, far, packed):
    half = m.rows // 2
    packed[: m.rows, :] = up[...]
    for side in range(2):
        at = slice(side * half, (side + 1) * half)
        packed[m.rows :, 2 * side * m.WH : (2 * side + 1) * m.WH] = out[at, :]
        packed[m.rows :, (2 * side + 1) * m.WH : (2 * side + 2) * m.WH] = far[at, :]


def split_down_kernel(m, sc, down_t, first, second):
    half = m.WH // 2
    for x in range(2):

        @pl.when(sc[2] == x)
        def _(x=x):
            first[...] = down_t[x * half : (x + 1) * half, :]
            second[...] = down_t[(1 - x) * half : (2 - x) * half, :]


def join_down_kernel(m, sc, first, second, down):
    width = m.FD // 2
    for x in range(2):

        @pl.when(sc[2] == x)
        def _(x=x):
            down[:, x * width : (x + 1) * width] = first[...]
            down[:, (1 - x) * width : (2 - x) * width] = second[...]


def norm_kernel(m, *refs):
    tokens, (xhat, x_scr) = refs[: m.S], refs[m.S :]
    x_scr[...] = jnp.zeros_like(x_scr)

    def item(b, carry):
        for d in range(m.S):
            x_scr[d * m.RP : d * m.RP + m.R, :] = tokens[d][b].astype(F32)
        xhat[ds(b * m.IT, m.IT), :], _ = layer_norm(x_scr[...])
        return carry

    lax.fori_loop(0, m.B, item, 0)


def attend_kernel(m, nparts, *refs):
    sc, text_mask, patch_count, xhat_ref = refs[:4]
    parts = refs[4 : 4 + nparts]
    qkv, normed, probs, packed, vecs, w_ref = refs[4 + nparts :]
    me = sc[0]
    if nparts == 1:
        w_ref[...] = parts[0][...]
    else:
        for p, part in enumerate(parts):
            w_ref[ds(part_index(m, sc, p) * m.rows, m.rows), :] = part[...]
    base = (3 * m.WH) // 128 * 128
    turned = w_ref[:, base : base + 128].astype(F32).T
    vecs[...] = turned[3 * m.WH - base : 3 * m.WH - base + VECS]
    for c in range(m.S):

        @pl.when(me == c)
        def _(c=c):
            for t in range(m.N // m.S):
                for k in range(m.S):
                    lanes = slice((t * m.S + k) * m.hrows, (t * m.S + k + 1) * m.hrows)
                    begin = c * m.WH + t * m.rows
                    vecs[UP_BIAS : UP_BIAS + 1, lanes] = vecs[8 + k : 9 + k, begin : begin + m.rows]

    gain, shift = vecs[0:1, :], vecs[1:2, :]
    q_bias = jnp.zeros((1, m.WH), F32)
    v_bias = jnp.zeros((1, m.WH), F32)
    for c in range(m.S):
        here = me == c
        q_bias = jnp.where(here, vecs[2:3, c * m.WH : (c + 1) * m.WH], q_bias)
        v_bias = jnp.where(here, vecs[3:4, c * m.WH : (c + 1) * m.WH], v_bias)
    bias = jnp.concatenate([q_bias, jnp.zeros((1, m.WH), F32), v_bias], axis=1)

    lane = lax.broadcasted_iota(jnp.int32, (1, m.IT), 1)
    place = jnp.full((1, m.IT), 1 << 20, jnp.int32)
    for d in range(m.S):
        row = lane - d * m.RP
        here = jnp.where(row < m.R, (me ^ d) * m.R + row, 1 << 20)
        place = jnp.where(row < 0, place, here)

    def item(b, carry):
        at = ds(b * m.IT, m.IT)
        low = (xhat_ref[at, :] * gain + shift).astype(LOW)
        normed[at, :] = low
        qkv[at, :] = (dot(low, w_ref[:, : 3 * m.WH]) + bias).astype(LOW)
        words = text_mask[b, 0]
        for k in range(1, m.TXT):
            words = words + text_mask[b, k]
        masked = jnp.where(
            place < m.TXT,
            jnp.where(place < words, 0.0, -1e30),
            jnp.where(place - m.TXT < patch_count[b], 0.0, -1e30),
        )
        half = m.IT // 2
        for h in range(m.H):
            q = qkv[at, h * m.hd : (h + 1) * m.hd] * LOW(m.hd**-0.5)
            k = qkv[at, m.WH + h * m.hd : m.WH + (h + 1) * m.hd]
            v = qkv[at, 2 * m.WH + h * m.hd : 2 * m.WH + (h + 1) * m.hd]
            s = dot_t(q, k) + masked
            e = jnp.exp(s - jnp.max(s, axis=-1, keepdims=True))
            p = (e * (1.0 / jnp.sum(e, axis=-1, keepdims=True))).astype(LOW)
            probs[b * m.H + h] = p
            o = dot(p, v).astype(LOW)
            packed[ds(b * half, half), h * m.hd : (h + 1) * m.hd] = o[:half]
            packed[ds(b * half, half), m.WH + h * m.hd : m.WH + (h + 1) * m.hd] = o[half:]
        return carry

    lax.fori_loop(0, m.B, item, 0)


def assemble_kernel(m, nparts, *refs):
    sc = refs[0]
    parts = refs[1 : 1 + nparts]
    w_up, w_out = refs[1 + nparts :]
    half = m.rows // 2
    per = m.N // m.S
    for p, part in enumerate(parts):
        i = part_index(m, sc, p)
        w_up[ds(i * m.rows, m.rows), :] = part[: m.rows]
        start = (sc[0] ^ lax.div(i, per)) * m.WH + lax.rem(i, per) * m.rows
        w_out[ds(start, half), :] = part[m.rows :, : 2 * m.WH]
        w_out[ds(start + half, half), :] = part[m.rows :, 2 * m.WH :]


def join_kernel(m, sc, own, other, *refs):
    cots = refs[: m.S]
    w_out, cot = refs[m.S :]
    for c in range(m.S):

        @pl.when(sc[0] == c)
        def _(c=c):
            for d in range(m.S):
                half = (own, other)[d % 2]
                lanes = slice((c ^ d) * m.WH, ((c ^ d) + 1) * m.WH)
                for e in range(m.S):
                    rows = slice((e ^ (d % 2)) * m.WH, ((e ^ (d % 2)) + 1) * m.WH)
                    w_out[e * m.WH : (e + 1) * m.WH, lanes] = half[rows, d // 2 * m.WH : (d // 2 + 1) * m.WH]

    pad_cot(m, cots, cot)


def pad_cot(m, cots, cot):
    cot[...] = jnp.zeros_like(cot)
    for b in range(m.B):
        for d in range(m.S):
            start = (b * m.S + d) * m.RP
            cot[start : start + m.R, :] = cots[d][b]


def forward_kernel(m, *refs):
    sc = refs[0]
    tokens = refs[1 : 1 + m.S]
    packed = refs[1 + m.S : 1 + 2 * m.S]
    w_out, w_up, vecs = refs[1 + 2 * m.S : 4 + 2 * m.S]
    normed, active, slope, mixed, resid_own, xhat_own, rstd_own, x_scr = refs[4 + 2 * m.S :]
    me = sc[0]
    out_bias, gain, shift = vecs[4:5, :], vecs[5:6, :], vecs[6:7, :]
    up_bias = vecs[UP_BIAS : UP_BIAS + 1, :]
    x_scr[...] = jnp.zeros_like(x_scr)

    def item(b, carry):
        at = ds(b * m.IT, m.IT)
        half = m.IT // 2
        for d in range(m.S):
            x_scr[d * m.RP : d * m.RP + m.R, :] = tokens[d][b].astype(F32)
        for e in range(m.S):
            for side in range(2):
                piece = packed[e][ds(b * half, half), side * m.WH : (side + 1) * m.WH]
                for t in range(2):
                    d = (2 * side + t) ^ e
                    mixed[ds(b * m.IT + d * m.RP, m.RP), e * m.WH : (e + 1) * m.WH] = piece[
                        t * m.RP : (t + 1) * m.RP
                    ]
        resid = x_scr[...] + (dot(mixed[at, :], w_out[...]) + out_bias)
        xhat, rstd = layer_norm(resid)
        own = ds(b * m.RP, m.RP)
        resid_own[own, :] = resid[: m.RP]
        xhat_own[own, :] = xhat[: m.RP]
        rstd_own[own, :] = jnp.broadcast_to(rstd[: m.RP], (m.RP, 128))
        low = (xhat * gain + shift).astype(LOW)
        normed[at, :] = low
        hidden = dot(low, w_up[...]) + up_bias
        cdf = 0.5 + 0.5 * lax.erf(hidden * SQRT_HALF)
        active[at, :] = (hidden * cdf).astype(LOW)
        slope[at, :] = cdf + hidden * (PDF_SCALE * jnp.exp(-0.5 * hidden * hidden))
        return carry

    lax.fori_loop(0, m.B, item, 0)


def hidden_back_kernel(m, nparts, *refs):
    sc, cot, slope, w_up = refs[:4]
    parts = refs[4 : 4 + nparts]
    g_hidden, w_down, keep0, keep1, send = refs[4 + nparts :]
    if nparts == 1:
        w_down[...] = parts[0][...]
    else:
        for p, part in enumerate(parts):
            w_down[ds(part_index(m, sc, p) * m.rows, m.rows), :] = part[...]

    def item(b, carry):
        at = ds(b * m.IT, m.IT)
        back = (dot(cot[at, :], w_down[...]) * slope[at, :]).astype(LOW)
        g_hidden[at, :] = back
        give_rows(m, b, dot_t(back, w_up[...]).astype(LOW), keep0, keep1, send)
        return carry

    lax.fori_loop(0, m.B, item, 0)


def give_shards(m, sc, total, keep, send):
    for k in range(m.nz):
        z = lax.rem(sc[1] + k, m.nz)
        keep[k] = total[ds((2 * z + sc[2]) * m.rows, m.rows), :].astype(LOW)
        send[k] = total[ds((2 * z + 1 - sc[2]) * m.rows, m.rows), :].astype(LOW)


def give(m, sc, total, keep, send):
    if m.fast:
        give_shards(m, sc, total, keep, send)
    else:
        keep[...] = total[...].astype(LOW)
        send[...] = jnp.zeros_like(send)


def give_rows(m, b, values, keep0, keep1, send):
    own = ds(b * m.RP, m.RP)
    keep0[own, :] = values[: m.RP]
    send[0, own, :] = values[m.RP : 2 * m.RP]
    keep1[own, :] = values[2 * m.RP : 3 * m.RP]
    send[1, own, :] = values[3 * m.RP : 4 * m.RP]


def weight_grad_kernel(m, sc, left, right, keep, send, total):
    step = 256
    for begin in range(0, m.D, step):
        total[begin : begin + step, :] = t_dot(left[:, begin : begin + step], right[...])
    give(m, sc, total, keep, send)


def branch_kernel(m, active, w_down, g_hidden, cot, keep0, keep1, send, vec):
    vec[...] = jnp.zeros_like(vec)

    def item(b, carry):
        at = ds(b * m.IT, m.IT)
        give_rows(m, b, dot_t(active[at, :], w_down[...]).astype(LOW), keep0, keep1, send)
        vec[0:1, :] += col_sum(cot[ds(b * m.IT, m.RP), :].astype(F32))
        vec[1:2, :] += col_sum(g_hidden[at, :].astype(F32))
        return carry

    lax.fori_loop(0, m.B, item, 0)


def pair_kernel(m, keep, core, out):
    out[...] = (keep[...].astype(F32) + core[1].astype(F32)).astype(LOW)


def add_kernel(m, left, right, out):
    out[...] = left[...] + right[...]


def middle_kernel(m, *refs):
    sc, keep0, core, far, xhat_own, rstd_own, cot, w_out, vecs = refs[:9]
    g_resid = refs[9]
    blocks = refs[10 : 10 + m.S]
    vec, low_scr = refs[10 + m.S :]
    me = sc[0]
    gain = vecs[5:6, :]
    grad = keep0[...].astype(F32) + core[0].astype(F32) + far[...].astype(F32)
    xhat = xhat_own[...]
    back = norm_back(grad, gain, xhat, rstd_own[:, 0:1])
    vec[...] = jnp.zeros_like(vec)
    vec[0:1, :] = col_sum(grad * xhat)
    vec[1:2, :] = col_sum(grad)
    for b in range(m.B):
        own = slice(b * m.RP, (b + 1) * m.RP)
        full = back[own] + cot[b * m.IT : b * m.IT + m.RP, :].astype(F32)
        g_resid[own, :] = full
        low_scr[own, :] = full.astype(LOW)
    low = low_scr[...]
    vec[2:3, :] = col_sum(low.astype(F32))
    g_mixed = dot_t(low, w_out[...]).astype(LOW)
    for e in range(m.S):
        blocks[e][:, : m.WH] = g_mixed[:, e * m.WH : (e + 1) * m.WH]
        picked = low[:, : m.WH]
        for c in range(1, m.S):
            picked = jnp.where((me ^ e) == c, low[:, c * m.WH : (c + 1) * m.WH], picked)
        blocks[e][:, m.WH :] = picked


def value_back_kernel(m, *refs):
    sc, probs = refs[:2]
    blocks = refs[2 : 2 + m.S]
    normed, mixed = refs[2 + m.S : 4 + m.S]
    g_value, g_mixed, keep, send, ga_scr, total = refs[4 + m.S :]

    def item(b, carry):
        at = ds(b * m.IT, m.IT)
        own = ds(b * m.RP, m.RP)
        for d in range(m.S):
            ga_scr[ds(b * m.IT + d * m.RP, m.RP), :] = blocks[d][own, m.WH :]
            g_mixed[ds(b * m.IT + d * m.RP, m.RP), :] = blocks[d][own, : m.WH]
        for h in range(m.H):
            lanes = slice(h * m.hd, (h + 1) * m.hd)
            g_value[at, lanes] = t_dot(probs[b * m.H + h], g_mixed[at, lanes]).astype(LOW)
        return carry

    lax.fori_loop(0, m.B, item, 0)
    total[:, : m.WH] = t_dot(normed[...], g_value[...])
    g_out = t_dot(mixed[...], ga_scr[...])
    for e in range(m.S):
        total[ds((sc[0] ^ e) * m.WH, m.WH), m.WH :] = g_out[e * m.WH : (e + 1) * m.WH]
    give(m, sc, total, keep, send)


def attend_back_kernel(m, qkv, probs, g_mixed, g_qk):
    scale = m.hd**-0.5

    def item(b, carry):
        at = ds(b * m.IT, m.IT)
        for h in range(m.H):
            lanes = slice(h * m.hd, (h + 1) * m.hd)
            q = qkv[at, h * m.hd : (h + 1) * m.hd]
            k = qkv[at, m.WH + h * m.hd : m.WH + (h + 1) * m.hd]
            v = qkv[at, 2 * m.WH + h * m.hd : 2 * m.WH + (h + 1) * m.hd]
            p = probs[b * m.H + h].astype(F32)
            gp = dot_t(g_mixed[at, lanes], v)
            gs = (p * (gp - jnp.sum(p * gp, axis=-1, keepdims=True))).astype(LOW)
            g_qk[at, h * m.hd : (h + 1) * m.hd] = (dot(gs, k) * scale).astype(LOW)
            g_qk[at, m.WH + h * m.hd : m.WH + (h + 1) * m.hd] = (t_dot(gs, q) * scale).astype(LOW)
        return carry

    lax.fori_loop(0, m.B, item, 0)


def input_back_kernel(m, sc, g_qk, g_value, xhat, w, vec_mid, vec_ff, b_keep1, b_send, keep0, keep1, send, v_scr):
    me = sc[0]
    v_scr[...] = jnp.zeros_like(v_scr)

    def item(b, carry):
        at = ds(b * m.IT, m.IT)
        grad = dot_t(g_qk[at, :], w[:, : 2 * m.WH]) + dot_t(g_value[at, :], w[:, 2 * m.WH : 3 * m.WH])
        v_scr[0:1, :] += col_sum(grad * xhat[at, :])
        v_scr[1:2, :] += col_sum(grad)
        give_rows(m, b, grad.astype(LOW), keep0, keep1, send)
        return carry

    lax.fori_loop(0, m.B, item, 0)
    q_sum = col_sum(g_qk[:, : m.WH].astype(F32))
    v_sum = col_sum(g_value[...].astype(F32))
    for c in range(m.S):
        here = me == c
        lanes = slice(c * m.WH, (c + 1) * m.WH)
        v_scr[2:3, lanes] = jnp.where(here, q_sum, 0.0)
        v_scr[3:4, lanes] = jnp.where(here, v_sum, 0.0)
        for t in range(m.N // m.S):
            for k in range(m.S):
                begin = c * m.WH + t * m.rows
                part = vec_ff[1:2, (t * m.S + k) * m.hrows : (t * m.S + k + 1) * m.hrows]
                v_scr[8 + k : 9 + k, begin : begin + m.rows] = jnp.where(here, part, 0.0)
    v_scr[4:5, :] = vec_mid[2:3, :]
    v_scr[5:6, :] = vec_mid[0:1, :]
    v_scr[6:7, :] = vec_mid[1:2, :]
    v_scr[7:8, :] = vec_ff[0:1, :]
    keep1[m.OWN :, :] = b_keep1[...]
    send[0, m.OWN :, :] = b_send[0]
    send[1, m.OWN :, :] = b_send[1]


def sum_x_kernel(m, keep, got, own, *outs):
    own[...] = keep[0].astype(F32) + got[0].astype(F32)
    for k, out in enumerate(outs):
        out[...] = (keep[k + 1].astype(F32) + got[k + 1].astype(F32)).astype(LOW)


def last_x_kernel(m, keep, got, vec, vec_got, own, vec_own, *outs):
    own[...] = keep[0].astype(F32) + got[0].astype(F32)
    values = vec[...] + vec_got[...]
    half = m.D // 2
    vec_own[:VECS, :] = values[:, :half]
    vec_own[VECS:, :] = values[:, half:]
    for k, out in enumerate(outs):
        out[: m.rows, :] = (keep[k + 1].astype(F32) + got[k + 1].astype(F32)).astype(LOW)
        out[m.rows :, :] = vec_own[...].astype(LOW)


def sum_z_kernel(m, *refs):
    own, rest, outs = refs[0], refs[1 : m.nz], refs[m.nz :]
    total = own[...]
    for r in rest:
        total = total + r[...].astype(F32)
    outs[0][...] = total[:, : m.WH]
    outs[1][...] = total[:, m.WH :]


def last_z_kernel(m, sc, own, vec_own, *refs):
    rest, (first, second), vecs, picked = refs[: m.nz - 1], refs[m.nz - 1 : m.nz + 1], refs[m.nz + 1 : -1], refs[-1]
    total, values = own[...], vec_own[...]
    for r in rest:
        total = total + r[: m.rows, :].astype(F32)
        values = values + r[m.rows :, :].astype(F32)
    first[...] = total[:, : m.WH]
    second[...] = total[:, m.WH :]
    for i in range(m.N):

        @pl.when(2 * sc[1] + sc[2] == i)
        def _(i=i):
            side, lane = divmod(i * m.rows, m.D // 2)
            picked[...] = values[side * VECS : (side + 1) * VECS, lane : lane + m.rows]

    for k in range(8):
        vecs[k][...] = picked[k : k + 1, :].reshape(m.rows)
    vecs[8][...] = jnp.concatenate([picked[8 + c : 9 + c, :] for c in range(m.S)], axis=1).reshape(m.S * m.rows)


def sum_down_kernel(m, sc, own, *refs):
    rest, (first, second) = refs[:-2], refs[-2:]
    total = own[...]
    for r in rest:
        total = total + r[...].astype(F32)
    width = m.FD // 2
    for x in range(2):

        @pl.when(sc[2] == x)
        def _(x=x):
            first[...] = total[:, x * width : (x + 1) * width].astype(LOW)
            second[...] = total[:, (1 - x) * width : (2 - x) * width].astype(LOW)


def sum_up_kernel(m, own, *refs):
    rest, out = refs[:-1], refs[-1]
    total = own[...]
    for r in rest:
        total = total + r[...].astype(F32)
    out[...] = total


def give_down_kernel(m, sc, first, second, g_down):
    for x in range(2):

        @pl.when(sc[2] == x)
        def _(x=x):
            g_down[x * m.rows : (x + 1) * m.rows, :] = first[...].astype(F32)
            g_down[(1 - x) * m.rows : (2 - x) * m.rows, :] = second[...].astype(F32)


def finish_kernel(m, *refs):
    keep0, core, far, tokens, g_resid, vecs, b_keep, resid = refs[:8]
    result, input_grad = refs[8:]
    gain, down_bias = vecs[0:1, :], vecs[7:8, :]
    for b in range(m.B):
        own = slice(b * m.RP, b * m.RP + m.R)
        also = slice(m.OWN + b * m.RP, m.OWN + b * m.RP + m.R)
        grad = keep0[own, :].astype(F32) + core[0, own, :].astype(F32) + far[own, :].astype(F32)
        xhat, rstd = layer_norm(tokens[b].astype(F32))
        back = norm_back(grad, gain, xhat, rstd)
        input_grad[b] = (g_resid[own, :] + back).astype(LOW)
        branch = b_keep[own, :].astype(F32) + core[0, also, :].astype(F32) + far[also, :].astype(F32)
        result[b] = (resid[own, :] + (branch + down_bias)).astype(LOW)


def plan(mesh, tokens, text_mask, w_query, w_up):
    m = SimpleNamespace()
    m.N, m.S = mesh.shape["dp"], mesh.shape["seq"]
    m.B, m.R, m.D = tokens.shape
    m.RP = -(-m.R // 16) * 16
    m.IT = m.S * m.RP
    m.RA = m.B * m.IT
    m.OWN = m.B * m.RP
    m.TXT = text_mask.shape[1]
    m.rows, m.WH = w_query.shape
    m.hd = m.D // HEADS
    m.H = HEADS // m.S
    m.FD = w_up.shape[1]
    m.hrows = m.FD // m.N
    m.fast = m.N == 2 * m.S
    m.nz = m.N // 2
    m.wide = -(-(3 * m.WH + VECS) // 128) * 128
    m.up_rows = m.rows + m.rows // 2
    return m


def local(
    mesh,
    tokens,
    cotangent,
    text_mask,
    patch_count,
    w_query,
    w_key,
    w_value,
    w_out,
    w_up,
    w_down,
    norm1_gain,
    norm1_bias,
    query_bias,
    value_bias,
    out_bias,
    norm2_gain,
    norm2_bias,
    up_bias,
    down_bias,
):
    m = plan(mesh, tokens, text_mask, w_query, w_up)
    N, S, rows, WH, D, nz = m.N, m.S, m.rows, m.WH, m.D, m.nz
    dp = lax.axis_index("dp").astype(jnp.int32)
    me = lax.axis_index("seq").astype(jnp.int32)
    fn = functools.partial

    def seq_to(x, e):
        return lax.ppermute(x, "seq", [(i, i ^ e) for i in range(S)])

    def x_swap(x):
        return lax.ppermute(x, "dp", [(i, i ^ 1) for i in range(N)])

    def z_shift(x, k):
        return lax.ppermute(x, "dp", [(i, (i + 2 * k) % N) for i in range(N)])

    def gate(x, *others):
        return lax.optimization_barrier((x, *others))[0]

    def direct(x):
        same = [x] + [z_shift(x, k) for k in range(1, nz)]
        return same + [x_swap(v) for v in same]

    def around(x):
        a, b = z_shift(x, 1), z_shift(x, nz - 1)
        return [x, a, z_shift(a, 1), b]

    def exchange(x, k):
        pairs = []
        for i in range(N):
            for j in range(S):
                to = 2 * j + (i + k) % 2
                pairs.append((i * S + j, to * S + i // 2))
        return lax.ppermute(x, ("dp", "seq"), pairs)

    def gather_seq(x):
        far = seq_to(x, 2)
        return [x, seq_to(x, 1), far, seq_to(far, 1)]

    vectors = [norm1_gain, norm1_bias, query_bias, value_bias, out_bias, norm2_gain, norm2_bias, down_bias, up_bias]
    if m.fast:
        out_far = seq_to(w_out, 2)
        (first,) = pallas(
            fn(pack_kernel, m),
            [shape(rows, m.wide)],
            [w_query, w_key, w_value, *vectors],
            [pltpu.VMEM((VECS, rows), F32)],
            name="pack",
            mib=60,
        )
        first_parts = direct(first)
        (up_out,) = pallas(
            fn(pack_up_kernel, m), [shape(m.up_rows, D)], [gate(w_up, first), w_out, out_far], name="pack_up"
        )
        halves = pallas(
            fn(split_down_kernel, m),
            [shape(WH // 2, S * m.hrows)] * 2,
            [gate(w_down.T, first)],
            here=True,
            name="split_down",
        )
        (down,) = pallas(
            fn(join_down_kernel, m),
            [shape(rows, m.FD)],
            [exchange(halves[k], k) for k in range(2)],
            here=True,
            name="join_down",
        )
        token_blocks = gather_seq(gate(tokens, first))
        cot_blocks = gather_seq(gate(cotangent, token_blocks[2]))
        up_same = around(up_out)
        up_side = x_swap(up_out)
        down_same = around(down)
        down_side = x_swap(down)
        norm_after = [up_out]
        held = []
    else:
        token_blocks = gather_seq(tokens)
        cot_blocks = gather_seq(cotangent)
        held = norm_after = []
        pad = jnp.zeros((rows, m.wide - 3 * WH - VECS), LOW)
        vec_rows = jnp.concatenate(vectors + [jnp.zeros(((VECS - 8 - S) * rows,), LOW)]).reshape(VECS, rows)
        first = jnp.concatenate([w_query, w_key, w_value, vec_rows.T, pad], axis=1)
        first_parts = [lax.all_gather(first, "dp", axis=0, tiled=True)]
        up_all = lax.all_gather(w_up, "dp", axis=0, tiled=True)
        down_all = lax.all_gather(w_down, "dp", axis=0, tiled=True)
        down_parts = [lax.all_to_all(down_all, "seq", 0, 1, tiled=True).T]
        heads = lax.all_gather(lax.all_gather(w_out, "seq", axis=1, tiled=True), "dp", axis=0, tiled=True)
        heads = heads.reshape(S, WH, D)
        out_all = jnp.concatenate([lax.dynamic_index_in_dim(heads, me ^ e, keepdims=False) for e in range(S)])

    (xhat,) = pallas(
        fn(norm_kernel, m),
        [shape(m.RA, D, dtype=F32)],
        [gate(token_blocks[0], *norm_after), *token_blocks[1:]],
        [pltpu.VMEM((m.IT, D), F32)],
        name="norm",
        long=False,
    )
    qkv, normed, probs, packed, vecs, w_first = pallas(
        fn(attend_kernel, m, len(first_parts)),
        [
            shape(m.RA, 3 * WH),
            shape(m.RA, D),
            shape(m.B * m.H, m.IT, m.IT),
            shape(m.B * m.IT // 2, 2 * WH),
            shape(VECS, D, dtype=F32),
            shape(D, m.wide),
        ],
        [text_mask, patch_count, gate(xhat, *held), *first_parts],
        long=False,
        smem=2,
        here=True,
        name="attend",
    )
    packed_blocks = gather_seq(packed)
    if m.fast:
        up_parts = up_same + [up_side] + [x_swap(v) for v in up_same[1:]]
        down_parts = down_same + [down_side] + [x_swap(v) for v in down_same[1:]]

    if m.fast:
        up_all, half = pallas(
            fn(assemble_kernel, m, len(up_parts)),
            [shape(D, m.FD), shape(D, 2 * WH)],
            [*up_parts],
            here=True,
            name="assemble",
        )
        out_all, cot = pallas(
            fn(join_kernel, m),
            [shape(D, D), shape(m.RA, D)],
            [half, seq_to(half, 1), *cot_blocks],
            here=True,
            name="join",
        )
    else:

        def only_pad(*refs):
            pad_cot(m, refs[:S], refs[S])

        (cot,) = pallas(only_pad, [shape(m.RA, D)], cot_blocks, name="pad_cot")

    normed2, active, slope, mixed, resid, xhat2, rstd2 = pallas(
        fn(forward_kernel, m),
        [
            shape(m.RA, D),
            shape(m.RA, m.FD),
            shape(m.RA, m.FD, dtype=F32),
            shape(m.RA, D),
            shape(m.OWN, D, dtype=F32),
            shape(m.OWN, D, dtype=F32),
            shape(m.OWN, 128, dtype=F32),
        ],
        [*token_blocks, *packed_blocks, out_all, up_all, vecs],
        [pltpu.VMEM((m.IT, D), F32)],
        here=True,
        name="forward",
    )
    def shards(width, height=D):
        if m.fast:
            return [shape(nz, rows, width)] * 2
        return [shape(height, width), shape(8, 128)]

    def weight_grad(left, right, name):
        return pallas(
            fn(weight_grad_kernel, m),
            shards(D),
            [left, right],
            [pltpu.VMEM((D, D), F32)],
            here=True,
            name=name,
            long=name == "up_grad",
        )

    down_keep, down_send = weight_grad(cot, active, "down_grad")
    g_hidden, down_all, keep0, keep1, send = pallas(
        fn(hidden_back_kernel, m, len(down_parts)),
        [shape(m.RA, m.FD), shape(D, m.FD), shape(m.OWN, D), shape(m.OWN, D), shape(2, m.OWN, D)],
        [cot, gate(slope, down_keep), up_all, *down_parts],
        here=True,
        name="hidden_back",
    )

    def add_pair(keep, core):
        (out,) = pallas(fn(pair_kernel, m), [shape(*keep.shape)], [keep, core], name="pair")
        return out

    def add(left, right):
        (out,) = pallas(fn(add_kernel, m), [shape(*left.shape, dtype=F32)], [left, right], name="add")
        return out

    core2 = seq_to(send, 1)
    pair2 = add_pair(keep1, core2)
    far2 = seq_to(pair2, 2)

    up_keep, up_send = weight_grad(normed2, gate(g_hidden, pair2), "up_grad")
    b_keep0, b_keep1, b_send, vec_ff = pallas(
        fn(branch_kernel, m),
        [shape(m.OWN, D), shape(m.OWN, D), shape(2, m.OWN, D), shape(8, D, dtype=F32)],
        [gate(active, up_keep), down_all, g_hidden, cot],
        name="branch",
        long=True,
    )

    g_resid, *blocks, vec_mid = pallas(
        fn(middle_kernel, m),
        [shape(m.OWN, D, dtype=F32), *[shape(m.OWN, 2 * WH)] * S, shape(8, D, dtype=F32)],
        [gate(keep0, b_keep0), core2, far2, xhat2, rstd2, cot, out_all, vecs],
        [pltpu.VMEM((m.OWN, D), LOW)],
        here=True,
        name="middle",
    )
    blocks = [blocks[0]] + [seq_to(blocks[e], e) for e in range(1, S)]

    def sum_x(keep, got, width):
        return pallas(
            fn(sum_x_kernel, m),
            [shape(rows, width, dtype=F32)] + [shape(rows, width)] * (nz - 1),
            [keep, got],
            name="sum_x",
        )

    def to_z(parts):
        return [z_shift(part, k + 1) for k, part in enumerate(parts)]

    def scatter(full):
        return lax.psum_scatter(full, "dp", scatter_dimension=0, tiled=True).astype(F32)

    if m.fast:
        down_got, up_got = x_swap(down_send), x_swap(up_send)
        down_own, *down_sums = sum_x(gate(down_keep, blocks[0]), down_got, D)
        down_z = to_z(down_sums)
        blocks[0] = gate(blocks[0], down_own)
    g_value, g_mixed, vo_keep, vo_send = pallas(
        fn(value_back_kernel, m),
        [shape(m.RA, WH), shape(m.RA, WH), *shards(2 * WH)],
        [probs, *blocks, normed, mixed],
        [pltpu.VMEM((m.RA, WH), LOW), pltpu.VMEM((D, 2 * WH), F32)],
        here=True,
        name="value_back",
        long=True,
    )
    if m.fast:
        vo_got = x_swap(vo_send)
        up_own, *up_sums = sum_x(gate(up_keep, g_value), up_got, D)
        up_z = to_z(up_sums)
        g_mixed = gate(g_mixed, up_own)

        def sum_down(after):
            return pallas(
                fn(sum_down_kernel, m),
                [shape(rows, m.FD // 2)] * 2,
                [gate(down_own, after), *down_z],
                here=True,
                name="sum_down",
            )

    (g_qk,) = pallas(
        fn(attend_back_kernel, m),
        [shape(m.RA, 2 * WH)],
        [qkv, probs, g_mixed],
        name="attend_back",
        long=True,
    )
    g_last = g_qk
    if m.fast:
        halves = sum_down(g_qk)
        down_halves = [exchange(halves[k], k) for k in range(2)]
        g_last = gate(g_qk, halves[0])
    qk_keep, qk_send = pallas(
        fn(weight_grad_kernel, m),
        shards(2 * WH),
        [normed, g_last],
        [pltpu.VMEM((D, 2 * WH), F32)],
        here=True,
        name="qk_grad",
    )
    keep0, keep1, send, vec = pallas(
        fn(input_back_kernel, m),
        [shape(m.OWN, D), shape(2 * m.OWN, D), shape(2, 2 * m.OWN, D), shape(VECS, D, dtype=F32)],
        [gate(g_qk, qk_keep), g_value, xhat, w_first, vec_mid, vec_ff, b_keep1, b_send],
        here=True,
        name="input_back",
    )
    vec_core, core1 = seq_to(vec, 1), seq_to(send, 1)
    vec = add(vec, vec_core)
    vec_far = seq_to(vec, 2)
    if m.fast:
        vo_own, *vo_sums = sum_x(gate(vo_keep, vec), vo_got, 2 * WH)
        vo_z = to_z(vo_sums)
        keep1 = gate(keep1, vo_own)
    pair1 = add_pair(gate(keep1, vec), core1)
    far1 = seq_to(pair1, 2)
    if m.fast:
        qk_got = x_swap(qk_send)
        (g_up,) = pallas(
            fn(sum_up_kernel, m), [shape(rows, m.FD, dtype=F32)], [gate(up_own, pair1), *up_z], name="sum_up"
        )
        vec = add(gate(vec, g_up), vec_far)
        vec_got = x_swap(vec)
        qk_own, vec_own, *qk_sums = pallas(
            fn(last_x_kernel, m),
            [shape(rows, 2 * WH, dtype=F32), shape(2 * VECS, D // 2, dtype=F32)]
            + [shape(rows + 2 * VECS, 2 * WH)] * (nz - 1),
            [qk_keep, qk_got, vec, vec_got],
            name="last_x",
        )
        qk_z = to_z(qk_sums)
        keep0 = gate(keep0, qk_own)
    else:
        vec = lax.psum(vec + vec_far, "dp")
        vec = lax.dynamic_slice(vec, (0, dp * rows), (VECS, rows))
        g_vo, g_qk = scatter(vo_keep), scatter(qk_keep)
        g_value, g_out, g_query, g_key = g_vo[:, :WH], g_vo[:, WH:], g_qk[:, :WH], g_qk[:, WH:]
        g_up = scatter(up_keep)
        g_down = scatter(lax.all_to_all(down_keep.T, "seq", 1, 0, tiled=True))
        vec_outs = [vec[k] for k in range(8)] + [vec[8 : 8 + S].reshape(-1)]

    result, input_grad = pallas(
        fn(finish_kernel, m),
        [shape(m.B, m.R, D), shape(m.B, m.R, D)],
        [keep0, core1, far1, tokens, g_resid, vecs, b_keep0, resid],
        name="finish",
    )
    if m.fast:
        g_value, g_out = pallas(
            fn(sum_z_kernel, m),
            [shape(rows, WH, dtype=F32)] * 2,
            [gate(vo_own, result), *vo_z],
            name="value_out",
        )
        (g_down,) = pallas(
            fn(give_down_kernel, m),
            [shape(WH, S * m.hrows, dtype=F32)],
            [gate(down_halves[0], g_value), down_halves[1]],
            here=True,
            name="give_down",
        )
        g_down = g_down.T
        g_query, g_key, *vec_outs = pallas(
            fn(last_z_kernel, m),
            [shape(rows, WH, dtype=F32)] * 2 + [shape(rows, dtype=F32)] * 8 + [shape(S * m.hrows, dtype=F32)],
            [gate(qk_own, g_down), vec_own, *qk_z],
            [pltpu.VMEM((VECS, rows), F32)],
            here=True,
            name="query_key",
        )
    return (
        result,
        input_grad,
        g_query,
        g_key,
        g_value,
        g_out,
        g_up,
        g_down,
        *vec_outs[:7],
        vec_outs[8],
        vec_outs[7],
    )


def solution(mesh):
    rows3, mat, vec = P("dp", "seq", None), P("dp", "seq"), P("dp")
    return jax.shard_map(
        functools.partial(local, mesh),
        mesh=mesh,
        in_specs=(rows3, rows3, P("dp", None), vec) + (mat,) * 6 + (vec,) * 9,
        out_specs=(rows3, rows3) + (mat,) * 6 + (vec,) * 9,
        check_vma=False,
    )
```

time: 237 us -> 186 us (0.78)
  Pallas kernels: 61.6 us -> 42.2 us
  local copies, waits for them, and re-layouts: 21.1 us -> 3.61 us
  waiting for transfers between devices: 84.4 us -> 71.2 us
  starting transfers between devices: 55.4 us -> 65.5 us
  other arithmetic: 8.54 us -> 0 us
    pallas_call x7 -> x32, Pallas kernels: 61.6 us -> 42.2 us  [pallas(): pl.pallas_call(run, out_shape=outs, in_specs=[pl.BlockSpec(memory_space=p...]
    all_to_all x2 -> x0, starting transfers between devices: 13.4 us -> none  [the longest x1 6.96 us: local(): swapped = lax.all_to_all(mixed_parts, 'seq', 0, 0, tiled=True)]
    ppermute x0 -> x4, starting transfers between devices: none -> 13 us  [exchange(): return lax.ppermute(x, ('dp', 'seq'), pairs)]
    ppermute x15 -> x21, starting transfers between devices: 15.8 us -> 23.6 us  [z_shift(): return lax.ppermute(x, 'dp', [(i, (i + 2 * k) % N) for i in range(N)])]
    another operation x10 -> x0, local copies, waits for them, and re-layouts: 6.34 us -> none  [the longest x8 6.2 us: local(): jnp.stack([norm1_gain, norm1_bias, query_bias, value_bias, out_bias, norm...]
    ppermute x11 -> x17, waiting for transfers between devices: 29.8 us -> 23.6 us  [x_swap(): return lax.ppermute(x, 'dp', [(i, i ^ 1) for i in range(N)])]
    ppermute x18 -> x20, waiting for transfers between devices: 21.5 us -> 15.7 us  [seq_to(): return lax.ppermute(x, 'seq', [(i, i ^ e) for i in range(S)])]
    reshape x10 -> x0, local copies, waits for them, and re-layouts: 5.84 us -> none  [the longest x2 1.3 us: local(): w_up.reshape(rows, per, S, m.hrows).transpose(2, 0, 1, 3)]
  transfers between devices with their start and end apart: 46 -> 62, of which waited for: 12 -> 25; matrix products, arithmetic and copies ran while one was open for 7% -> 0% of each run, Pallas kernels for 21% -> 18%
where the time goes in v2:
time: 186 us; the launch traced here: 184 us
  waiting for transfers between devices  71.2 us (38%)
  starting transfers between devices  65.5 us (35%)
  Pallas kernels  42.2 us (23%)
  local copies, waits for them, and re-layouts  3.61 us (2%)
    pallas_call x32, Pallas kernels, pallas(): pl.pallas_call(run, out_shape=outs, in_specs=[pl.BlockSpec(memory_space=p...  42.2 us
    ppermute x21, waiting for transfers between devices, z_shift(): return lax.ppermute(x, 'dp', [(i, (i + 2 * k) % N) for i in range(N)])  27.1 us
    ppermute x17, waiting for transfers between devices, x_swap(): return lax.ppermute(x, 'dp', [(i, i ^ 1) for i in range(N)])  23.6 us
    ppermute x21, starting transfers between devices, z_shift(): return lax.ppermute(x, 'dp', [(i, (i + 2 * k) % N) for i in range(N)])  23.6 us
    ppermute x20, starting transfers between devices, seq_to(): return lax.ppermute(x, 'seq', [(i, i ^ e) for i in range(S)])  17.1 us
    ppermute x20, waiting for transfers between devices, seq_to(): return lax.ppermute(x, 'seq', [(i, i ^ e) for i in range(S)])  15.7 us
    ppermute x4, starting transfers between devices, exchange(): return lax.ppermute(x, ('dp', 'seq'), pairs)  13 us
    ppermute x17, starting transfers between devices, x_swap(): return lax.ppermute(x, 'dp', [(i, i ^ 1) for i in range(N)])  11.8 us
  transfers between devices with their start and end apart: 62, of which 25 were waited for; matrix products, arithmetic and copies ran while one was open for 0% of the time, Pallas kernels for 18%

profile of v2, /device:TPU:5, one launch (start us, length us, event | category | flops | bytes accessed | tf_op | source)
XLA Modules:
  0.0 183.5 jit_solution(574774183227203904)
XLA Ops:
  0.7 1.8 pack.1.refs_3_
  3.4 5.7 %collective-permute-start.25 = (bf16[96,384]{1,0:T(8,128)(2,1)S(1)}, bf16[96,384]{1,0:T(8,128)(2,1)S(1)}, u32[]{:S(2)}, u32[]{:S(2)}) collective-permute-start(bf16[96,384]{1,0:T(8,128)(2,1)S(1)} %get-tuple-element.141), channel_id=1, source_target_pairs={{0,0},{1,8},{2,16},{3,24},{4,4},{5,12},{6,20},{7,28},{8,1},{9,9},{... | collective-permute-start | bytes 221192 | tf_op jit(solution)/shard_map/ppermute | solution.py:644
  9.1 1.3 collective-permute-start.7
  11.3 2.1 %collective-permute-start.6 = (bf16[96,640]{1,0:T(8,128)(2,1)}, bf16[96,640]{1,0:T(8,128)(2,1)S(1)}, u32[]{:S(2)}, u32[]{:S(2)}) collective-permute-start(bf16[96,640]{1,0:T(8,128)(2,1)} %pack.1.refs_3_), channel_id=1, source_target_pairs={{0,24},{4,28},{8,0},{12,4},{16,8},{20,12},{24,16},{28,20},{1,25},{... | collective-permute-start | bytes 368648 | tf_op jit(solution)/shard_map/ppermute | solution.py:625
  13.4 1.4 collective-permute-done.refs_2_
  17.0 1.1 collective-permute-done.26.refs_1_
  19.5 1.5 collective-permute-start.10
  21.0 9.9 %collective-permute-done.5.refs_5_ = bf16[96,640]{1,0:T(8,128)(2,1)S(1)} collective-permute-done((bf16[96,640]{1,0:T(8,128)(2,1)}, bf16[96,640]{1,0:T(8,128)(2,1)S(1)}, u32[]{:S(2)}, u32[]{:S(2)}) %collective-permute-start.5) | collective-permute-done | bytes 122912 | tf_op jit(solution)/shard_map/ppermute | solution.py:625
  31.2 1.2 collective-permute-start.8
  33.1 2.1 %collective-permute-done.9.refs_9_ = bf16[96,640]{1,0:T(8,128)(2,1)S(1)} collective-permute-done((bf16[96,640]{1,0:T(8,128)(2,1)S(1)}, bf16[96,640]{1,0:T(8,128)(2,1)S(1)}, u32[]{:S(2)}, u32[]{:S(2)}) %collective-permute-start.9) | collective-permute-done | bytes 122912 | tf_op jit(solution)/shard_map/ppermute | solution.py:622
  35.2 2.6 %collective-permute-done.8.refs_8_ = bf16[96,640]{1,0:T(8,128)(2,1)S(1)} collective-permute-done((bf16[96,640]{1,0:T(8,128)(2,1)S(1)}, bf16[96,640]{1,0:T(8,128)(2,1)S(1)}, u32[]{:S(2)}, u32[]{:S(2)}) %collective-permute-start.8) | collective-permute-done | bytes 122912 | tf_op jit(solution)/shard_map/ppermute | solution.py:622
  37.8 2.4 %collective-permute-start.1 = (bf16[3,70,768]{2,1,0:T(8,128)(2,1)}, bf16[3,70,768]{2,1,0:T(8,128)(2,1)S(1)}, u32[]{:S(2)}, u32[]{:S(2)}) collective-permute-start(bf16[3,70,768]{2,1,0:T(8,128)(2,1)} %refs_3_.3), channel_id=1, source_target_pairs={{0,1},{1,0},{2,3},{3,2},{4,5},{5,4},{6,7},{7,6},{8,9},{9,8},{10,11... | collective-permute-start | bytes 967688 | tf_op jit(solution)/shard_map/ppermute | solution.py:619
  41.8 1.2 collective-permute-done.12.refs_2_
  44.6 1.0 copy-done
  45.6 0.9 norm.1.refs_2_
  46.6 7.5 %attend.1 = (bf16[960,576]{1,0:T(8,128)(2,1)S(1)}, bf16[960,768]{1,0:T(8,128)(2,1)S(1)}, bf16[9,320,320]{2,1,0:T(8,128)(2,1)S(1)}, bf16[480,384]{1,0:T(8,128)(2,...) custom-call(s32[3,40]{1,0:T(4,128)S(1)} %copy-done.7, s32[3]{0:T(128)S(1)} %copy-done.8, ...), custom_call_target="tpu_custom_call" | custom-call | flops 1000 | bytes 9757164 | tf_op jit(solution)/shard_map/attend/pallas_call | solution.py:56
  54.8 2.6 %collective-permute-done.16.refs_6_ = bf16[144,768]{1,0:T(8,128)(2,1)S(1)} collective-permute-done((bf16[144,768]{1,0:T(8,128)(2,1)S(1)}, bf16[144,768]{1,0:T(8,128)(2,1)S(1)}, u32[]{:S(2)}, u32[]{:S(2)}) %collective-permute-start.16) | collective-permute-done | bytes 221216 | tf_op jit(solution)/shard_map/ppermute | solution.py:622
  57.5 2.0 %collective-permute-start.18 = (bf16[768,384]{1,0:T(8,128)(2,1)S(1)}, bf16[768,384]{1,0:T(8,128)(2,1)S(1)}, u32[]{:S(2)}, u32[]{:S(2)}) collective-permute-start(bf16[768,384]{1,0:T(8,128)(2,1)S(1)} %get-tuple-element.129.refs_0_), channel_id=1, source_target_pairs={{0,1},{1,0},{2,3},{3,2},{4,5},{5,4},{6,7},{7,6},{8,9},{9,8},{10,11... | collective-permute-start | bytes 1769480 | tf_op jit(solution)/shard_map/ppermute | solution.py:619
  59.5 3.5 %collective-permute-start.29 = (bf16[96,768]{1,0:T(8,128)(2,1)S(1)}, bf16[96,768]{1,0:T(8,128)(2,1)S(1)}, u32[]{:S(2)}, u32[]{:S(2)}) collective-permute-start(bf16[96,768]{1,0:T(8,128)(2,1)S(1)} %join_down.1.refs_3_), channel_id=1, source_target_pairs={{0,24},{4,28},{8,0},{12,4},{16,8},{20,12},{24,16},{28,20},{1,25},{... | collective-permute-start | bytes 442376 | tf_op jit(solution)/shard_map/ppermute | solution.py:625
  63.0 3.2 %collective-permute-done.29.refs_6_ = bf16[96,768]{1,0:T(8,128)(2,1)S(1)} collective-permute-done((bf16[96,768]{1,0:T(8,128)(2,1)S(1)}, bf16[96,768]{1,0:T(8,128)(2,1)S(1)}, u32[]{:S(2)}, u32[]{:S(2)}) %collective-permute-start.29) | collective-permute-done | bytes 147488 | tf_op jit(solution)/shard_map/ppermute | solution.py:625
  66.2 1.3 collective-permute-start.22
  67.5 2.4 %collective-permute-done.28.refs_5_ = bf16[96,768]{1,0:T(8,128)(2,1)S(1)} collective-permute-done((bf16[96,768]{1,0:T(8,128)(2,1)S(1)}, bf16[96,768]{1,0:T(8,128)(2,1)S(1)}, u32[]{:S(2)}, u32[]{:S(2)}) %collective-permute-start.28) | collective-permute-done | bytes 147488 | tf_op jit(solution)/shard_map/ppermute | solution.py:625
  69.9 1.2 collective-permute-start.19
  72.8 1.0 collective-permute-start.31
  74.3 1.0 collective-permute-start.32
  75.9 5.6 %forward.1 = (bf16[960,768]{1,0:T(8,128)(2,1)S(1)}, bf16[960,768]{1,0:T(8,128)(2,1)S(1)}, f32[960,768]{1,0:T(8,128)S(1)}, bf16[960,768]{1,0:T(8,128)(2,1)S(1)}, ...) custom-call(bf16[3,70,768]{2,1,0:T(8,128)(2,1)S(1)} %copy-done.1, ...), custom_call_target="tpu_custom_call" | custom-call | flops 1000 | bytes 14143488 | tf_op jit(solution)/shard_map/forward/pallas_call | solution.py:56
  81.5 1.6 down_grad.1
  83.7 3.2 %collective-permute-done.32.refs_9_ = bf16[96,768]{1,0:T(8,128)(2,1)S(1)} collective-permute-done((bf16[96,768]{1,0:T(8,128)(2,1)S(1)}, bf16[96,768]{1,0:T(8,128)(2,1)S(1)}, u32[]{:S(2)}, u32[]{:S(2)}) %collective-permute-start.32) | collective-permute-done | bytes 147488 | tf_op jit(solution)/shard_map/ppermute | solution.py:622
  86.9 3.3 %hidden_back.1 = (bf16[960,768]{1,0:T(8,128)(2,1)S(1)}, bf16[768,768]{1,0:T(8,128)(2,1)S(1)}, bf16[240,768]{1,0:T(8,128)(2,1)S(1)}, bf16[240,768]{1,0:T(8,128)(2,1)S(1)}, bf16[2,240,768]{2,1,0:T(8,128)(2,1)S(1)}) custom-call(bf16[960,768]{1,0:T(8,128)(2,1)S(1)} %get-tuple-element.131.refs_0_.refs_3_.refs_5_, f32[960,768]{1,0:T(8,128)S(1)} %get-tuple-element.139.refs_1_, ...), custom_call_target="tpu_custom_call" | custom-call | flops 1000 | bytes 10911744 | tf_op jit(solution)/shard_map/hidden_back/pallas_call | solution.py:56
  90.2 1.3 collective-permute-start.34
  92.0 1.3 collective-permute-done.34.refs_1_
  93.4 1.1 collective-permute-start.35
  94.5 1.6 up_grad.1
  96.0 1.8 %branch.1 = (bf16[240,768]{1,0:T(8,128)(2,1)S(1)}, bf16[240,768]{1,0:T(8,128)(2,1)S(1)}, bf16[2,240,768]{2,1,0:T(8,128)(2,1)S(1)}, f32[8,768]{1,0:T(8,128)S(1)}) custom-call(bf16[960,768]{1,0:T(8,128)(2,1)S(1)} %get-tuple-element.150.refs_1_.refs_0_, bf16[768,768]{1,0:T(8,128)(2,1)S(1)} %get-tuple-element.151.refs_1_, ...), custom_call_target="tpu_custom_call" | custom-call | flops 10000000000 | bytes 7102464 | tf_op jit(solution)/shard_map/branch/pallas_call | solution.py:56
  97.9 5.4 %collective-permute-done.35.refs_2_ = bf16[240,768]{1,0:T(8,128)(2,1)S(1)} collective-permute-done((bf16[240,768]{1,0:T(8,128)(2,1)S(1)}, bf16[240,768]{1,0:T(8,128)(2,1)S(1)}, u32[]{:S(2)}, u32[]{:S(2)}) %collective-permute-start.35) | collective-permute-done | bytes 368672 | tf_op jit(solution)/shard_map/ppermute | solution.py:619
  103.3 1.1 middle.1
  104.4 1.3 collective-permute-start.37
  105.7 1.0 collective-permute-start.38
  108.3 1.4 collective-permute-start.41
  110.0 1.9 %collective-permute-done.38.refs_3_ = bf16[240,384]{1,0:T(8,128)(2,1)S(1)} collective-permute-done((bf16[240,384]{1,0:T(8,128)(2,1)S(1)}, bf16[240,384]{1,0:T(8,128)(2,1)S(1)}, u32[]{:S(2)}, u32[]{:S(2)}) %collective-permute-start.38) | collective-permute-done | bytes 184352 | tf_op jit(solution)/shard_map/ppermute | solution.py:619
  111.9 1.4 collective-permute-start.43
  113.2 3.0 %collective-permute-done.39.refs_4_ = bf16[240,384]{1,0:T(8,128)(2,1)S(1)} collective-permute-done((bf16[240,384]{1,0:T(8,128)(2,1)S(1)}, bf16[240,384]{1,0:T(8,128)(2,1)S(1)}, u32[]{:S(2)}, u32[]{:S(2)}) %collective-permute-start.39) | collective-permute-done | bytes 184352 | tf_op jit(solution)/shard_map/ppermute | solution.py:619
  116.3 2.7 %value_back.1 = (bf16[960,192]{1,0:T(8,128)(2,1)S(1)}, bf16[960,192]{1,0:T(8,128)(2,1)S(1)}, bf16[4,96,384]{2,1,0:T(8,128)(2,1)S(1)}, bf16[4,96,384]{2,1,0:T(8,128)(2,1)S(1)}) custom-call(bf16[9,320,320]{2,1,0:T(8,128)(2,1)S(1)} %get-tuple-element.128.refs_0_.refs_1_, bf16[240,384]{1,0:T(8,128)(2,1)S(1)} %get-tuple-element.160.refs_1_, ...), custom_call_target="tpu_custom_call" | custom-call | flops 10000000000 | bytes 6856704 | tf_op jit(solution)/shard_map/value_back/pallas_call | solution.py:56
  119.0 3.2 %collective-permute-done.40.refs_1_ = bf16[4,96,768]{2,1,0:T(8,128)(2,1)S(1)} collective-permute-done((bf16[4,96,768]{2,1,0:T(8,128)(2,1)S(1)}, bf16[4,96,768]{2,1,0:T(8,128)(2,1)S(1)}, u32[]{:S(2)}, u32[]{:S(2)}) %collective-permute-start.40) | collective-permute-done | bytes 589856 | tf_op jit(solution)/shard_map/ppermute | solution.py:622
  122.3 4.5 %attend_back.1.refs_1_.refs_0_ = bf16[960,384]{1,0:T(8,128)(2,1)S(1)} custom-call(bf16[960,576]{1,0:T(8,128)(2,1)S(1)} %get-tuple-element.127.refs_0_, bf16[9,320,320]{2,1,0:T(8,128)(2,1)S(1)} %get-tuple-element.128.refs_0_.refs_1_, bf16[960,192]{1,0:T(8,128)(2,1)S(1)} %get-tuple-element.171.refs_2_), custom_call_target="tpu_custom_call" | custom-call | flops 10000000000 | bytes 4055040 | tf_op jit(solution)/shard_map/attend_back/pallas_call | solution.py:56
  127.1 1.1 qk_grad.1
  128.2 2.1 %input_back.1 = (bf16[240,768]{1,0:T(8,128)(2,1)S(1)}, bf16[480,768]{1,0:T(8,128)(2,1)S(1)}, bf16[2,480,768]{2,1,0:T(8,128)(2,1)S(1)}, f32[16,768]{1,0:T(8,128)S(1)}) custom-call(bf16[960,384]{1,0:T(8,128)(2,1)S(1)} %attend_back.1.refs_1_.refs_0_, bf16[960,192]{1,0:T(8,128)(2,1)S(1)} %get-tuple-element.167.refs_1_, f32[960,768]{1,0:T(8,128)S(1)} %norm.1.refs_2_, ...), custom_call_target="tpu_custom_call" | custom-call | flops 1000 | bytes 8822784 | tf_op jit(solution)/shard_map/input_back/pallas_call | solution.py:56
  130.4 1.0 collective-permute-start.47
  132.5 1.9 %collective-permute-done.45.refs_1_ = f32[16,768]{1,0:T(8,128)S(1)} collective-permute-done((f32[16,768]{1,0:T(8,128)S(1)}, f32[16,768]{1,0:T(8,128)S(1)}, u32[]{:S(2)}, u32[]{:S(2)}) %collective-permute-start.45) | collective-permute-done | bytes 49184 | tf_op jit(solution)/shard_map/ppermute | solution.py:619
  134.4 5.6 %collective-permute-done.46.refs_1_ = bf16[4,96,384]{2,1,0:T(8,128)(2,1)S(1)} collective-permute-done((bf16[4,96,384]{2,1,0:T(8,128)(2,1)S(1)}, bf16[4,96,384]{2,1,0:T(8,128)(2,1)S(1)}, u32[]{:S(2)}, u32[]{:S(2)}) %collective-permute-start.46) | collective-permute-done | bytes 294944 | tf_op jit(solution)/shard_map/ppermute | solution.py:622
  140.3 1.1 collective-permute-start.53
  141.4 1.2 collective-permute-start.44
  142.5 1.4 collective-permute-start.48
  144.2 1.8 collective-permute-start.50
  146.0 2.5 %collective-permute-done.48.refs_1_ = bf16[96,768]{1,0:T(8,128)(2,1)S(1)} collective-permute-done((bf16[96,768]{1,0:T(8,128)(2,1)S(1)}, bf16[96,768]{1,0:T(8,128)(2,1)S(1)}, u32[]{:S(2)}, u32[]{:S(2)}) %collective-permute-start.48) | collective-permute-done | bytes 147488 | tf_op jit(solution)/shard_map/ppermute | solution.py:625
  148.6 7.8 %collective-permute-done.49.refs_2_ = bf16[96,768]{1,0:T(8,128)(2,1)S(1)} collective-permute-done((bf16[96,768]{1,0:T(8,128)(2,1)S(1)}, bf16[96,768]{1,0:T(8,128)(2,1)S(1)}, u32[]{:S(2)}, u32[]{:S(2)}) %collective-permute-start.49) | collective-permute-done | bytes 147488 | tf_op jit(solution)/shard_map/ppermute | solution.py:625
  156.4 2.7 %collective-permute-start.56 = (bf16[96,384]{1,0:T(8,128)(2,1)S(1)}, bf16[96,384]{1,0:T(8,128)(2,1)S(1)}, u32[]{:S(2)}, u32[]{:S(2)}) collective-permute-start(bf16[96,384]{1,0:T(8,128)(2,1)S(1)} %get-tuple-element.209), channel_id=1, source_target_pairs={{0,16},{4,20},{8,24},{12,28},{16,0},{20,4},{24,8},{28,12},{1,17},{... | collective-permute-start | bytes 221192 | tf_op jit(solution)/shard_map/ppermute | solution.py:625
  159.9 2.8 %collective-permute-start.57 = (bf16[96,384]{1,0:T(8,128)(2,1)S(1)}, bf16[96,384]{1,0:T(8,128)(2,1)S(1)}, u32[]{:S(2)}, u32[]{:S(2)}) collective-permute-start(bf16[96,384]{1,0:T(8,128)(2,1)S(1)} %get-tuple-element.210), channel_id=1, source_target_pairs={{0,24},{4,28},{8,0},{12,4},{16,8},{20,12},{24,16},{28,20},{1,25},{... | collective-permute-start | bytes 221192 | tf_op jit(solution)/shard_map/ppermute | solution.py:625
  163.1 3.0 %collective-permute-done.52.refs_3_ = f32[16,768]{1,0:T(8,128)S(1)} collective-permute-done((f32[16,768]{1,0:T(8,128)S(1)}, f32[16,768]{1,0:T(8,128)S(1)}, u32[]{:S(2)}, u32[]{:S(2)}) %collective-permute-start.52) | collective-permute-done | bytes 49184 | tf_op jit(solution)/shard_map/ppermute | solution.py:622
  166.3 3.2 %collective-permute-start.61 = (bf16[128,384]{1,0:T(8,128)(2,1)S(1)}, bf16[128,384]{1,0:T(8,128)(2,1)S(1)}, u32[]{:S(2)}, u32[]{:S(2)}) collective-permute-start(bf16[128,384]{1,0:T(8,128)(2,1)S(1)} %get-tuple-element.218), channel_id=1, source_target_pairs={{0,24},{4,28},{8,0},{12,4},{16,8},{20,12},{24,16},{28,20},{1,25},{... | collective-permute-start | bytes 294920 | tf_op jit(solution)/shard_map/ppermute | solution.py:625
  169.5 4.9 %collective-permute-start.54 = (bf16[96,384]{1,0:T(8,128)(2,1)S(1)}, bf16[96,384]{1,0:T(8,128)(2,1)S(1)}, u32[]{:S(2)}, u32[]{:S(2)}) collective-permute-start(bf16[96,384]{1,0:T(8,128)(2,1)S(1)} %get-tuple-element.176), channel_id=1, source_target_pairs={{0,0},{1,8},{2,16},{3,24},{4,4},{5,12},{6,20},{7,28},{8,1},{9,9},{... | collective-permute-start | bytes 221192 | tf_op jit(solution)/shard_map/ppermute | solution.py:644
  174.4 1.5 collective-permute-start.58
  176.0 1.5 finish.1
  178.9 3.0 %collective-permute-done.58.refs_1_ = bf16[96,384]{1,0:T(8,128)(2,1)S(1)} collective-permute-done((bf16[96,384]{1,0:T(8,128)(2,1)S(1)}, bf16[96,384]{1,0:T(8,128)(2,1)S(1)}, u32[]{:S(2)}, u32[]{:S(2)}) %collective-permute-start.58) | collective-permute-done | bytes 73760 | tf_op jit(solution)/shard_map/ppermute | solution.py:644
  (110 shorter events, 23.0 us)
Async XLA Ops:
  3.4 11.4 %collective-permute-start.25 = (bf16[96,384]{1,0:T(8,128)(2,1)S(1)}, bf16[96,384]{1,0:T(8,128)(2,1)S(1)}, u32[]{:S(2)}, u32[]{:S(2)}) collective-permute-start(bf16[96,384]{1,0:T(8,128)(2,1)S(1)} %get-tuple-element.141), channel_id=1, source_target_pairs={{0,0},{1,8},{2,16},{3,24},{4,4},{5,12},{6,20},{7,28},{8,1},{9,9},{... | collective-permute-start | bytes 221192 | tf_op jit(solution)/shard_map/ppermute | solution.py:644
  9.1 9.5 %collective-permute-start.7 = (bf16[96,640]{1,0:T(8,128)(2,1)}, bf16[96,640]{1,0:T(8,128)(2,1)S(1)}, u32[]{:S(2)}, u32[]{:S(2)}) collective-permute-start(bf16[96,640]{1,0:T(8,128)(2,1)} %pack.1.refs_3_), channel_id=1, source_target_pairs={{0,4},{4,0},{8,12},{12,8},{16,20},{20,16},{24,28},{28,24},{1,5},{5... | collective-permute-start | bytes 368648 | tf_op jit(solution)/shard_map/ppermute | solution.py:622
  10.4 7.7 %collective-permute-start.26 = (bf16[96,384]{1,0:T(8,128)(2,1)S(1)}, bf16[96,384]{1,0:T(8,128)(2,1)S(1)}, u32[]{:S(2)}, u32[]{:S(2)}) collective-permute-start(bf16[96,384]{1,0:T(8,128)(2,1)S(1)} %get-tuple-element.142), channel_id=1, source_target_pairs={{0,4},{1,12},{2,20},{3,28},{4,0},{5,8},{6,16},{7,24},{8,5},{9,13},... | collective-permute-start | bytes 221192 | tf_op jit(solution)/shard_map/ppermute | solution.py:644
  11.3 3.5 %collective-permute-start = (bf16[96,192]{1,0:T(8,128)(2,1)}, bf16[96,192]{1,0:T(8,128)(2,1)S(1)}, u32[]{:S(2)}, u32[]{:S(2)}) collective-permute-start(bf16[96,192]{1,0:T(8,128)(2,1)} %refs_1_.4), channel_id=1, source_target_pairs={{0,2},{1,3},{2,0},{3,1},{4,6},{5,7},{6,4},{7,5},{8,10},{9,11},{10,... | collective-permute-start | bytes 110600 | tf_op jit(solution)/shard_map/ppermute | solution.py:619
  11.3 8.2 %collective-permute-start.6 = (bf16[96,640]{1,0:T(8,128)(2,1)}, bf16[96,640]{1,0:T(8,128)(2,1)S(1)}, u32[]{:S(2)}, u32[]{:S(2)}) collective-permute-start(bf16[96,640]{1,0:T(8,128)(2,1)} %pack.1.refs_3_), channel_id=1, source_target_pairs={{0,24},{4,28},{8,0},{12,4},{16,8},{20,12},{24,16},{28,20},{1,25},{... | collective-permute-start | bytes 368648 | tf_op jit(solution)/shard_map/ppermute | solution.py:625
  14.8 16.1 %collective-permute-start.5 = (bf16[96,640]{1,0:T(8,128)(2,1)}, bf16[96,640]{1,0:T(8,128)(2,1)S(1)}, u32[]{:S(2)}, u32[]{:S(2)}) collective-permute-start(bf16[96,640]{1,0:T(8,128)(2,1)} %pack.1.refs_3_), channel_id=1, source_target_pairs={{0,16},{4,20},{8,24},{12,28},{16,0},{20,4},{24,8},{28,12},{1,17},{... | collective-permute-start | bytes 368648 | tf_op jit(solution)/shard_map/ppermute | solution.py:625
  14.8 25.5 %collective-permute-start.2 = (bf16[3,70,768]{2,1,0:T(8,128)(2,1)}, bf16[3,70,768]{2,1,0:T(8,128)(2,1)S(1)}, u32[]{:S(2)}, u32[]{:S(2)}) collective-permute-start(bf16[3,70,768]{2,1,0:T(8,128)(2,1)} %refs_3_.3), channel_id=1, source_target_pairs={{0,2},{1,3},{2,0},{3,1},{4,6},{5,7},{6,4},{7,5},{8,10},{9,11},{10,... | collective-permute-start | bytes 967688 | tf_op jit(solution)/shard_map/ppermute | solution.py:619
  18.1 17.1 %collective-permute-start.11 = (bf16[144,768]{1,0:T(8,128)(2,1)S(1)}, bf16[144,768]{1,0:T(8,128)(2,1)S(1)}, u32[]{:S(2)}, u32[]{:S(2)}) collective-permute-start(bf16[144,768]{1,0:T(8,128)(2,1)S(1)} %pack_up.1.refs_0_), channel_id=1, source_target_pairs={{0,8},{4,12},{8,16},{12,20},{16,24},{20,28},{24,0},{28,4},{1,9},{5... | collective-permute-start | bytes 663560 | tf_op jit(solution)/shard_map/ppermute | solution.py:625
  18.7 12.5 %collective-permute-start.4 = (bf16[96,640]{1,0:T(8,128)(2,1)}, bf16[96,640]{1,0:T(8,128)(2,1)S(1)}, u32[]{:S(2)}, u32[]{:S(2)}) collective-permute-start(bf16[96,640]{1,0:T(8,128)(2,1)} %pack.1.refs_3_), channel_id=1, source_target_pairs={{0,8},{4,12},{8,16},{12,20},{16,24},{20,28},{24,0},{28,4},{1,9},{5... | collective-permute-start | bytes 368648 | tf_op jit(solution)/shard_map/ppermute | solution.py:625
  19.5 12.9 %collective-permute-start.10 = (bf16[96,640]{1,0:T(8,128)(2,1)S(1)}, bf16[96,640]{1,0:T(8,128)(2,1)S(1)}, u32[]{:S(2)}, u32[]{:S(2)}) collective-permute-start(bf16[96,640]{1,0:T(8,128)(2,1)S(1)} %collective-permute-done.6.refs_6_), channel_id=1, source_target_pairs={{0,4},{4,0},{8,12},{12,8},{16,20},{20,16},{24,28},{28,24},{1,5},{5... | collective-permute-start | bytes 368648 | tf_op jit(solution)/shard_map/ppermute | solution.py:622
  31.0 4.2 %collective-permute-start.9 = (bf16[96,640]{1,0:T(8,128)(2,1)S(1)}, bf16[96,640]{1,0:T(8,128)(2,1)S(1)}, u32[]{:S(2)}, u32[]{:S(2)}) collective-permute-start(bf16[96,640]{1,0:T(8,128)(2,1)S(1)} %collective-permute-done.5.refs_5_), channel_id=1, source_target_pairs={{0,4},{4,0},{8,12},{12,8},{16,20},{20,16},{24,28},{28,24},{1,5},{5... | collective-permute-start | bytes 368648 | tf_op jit(solution)/shard_map/ppermute | solution.py:622
  31.2 6.6 %collective-permute-start.8 = (bf16[96,640]{1,0:T(8,128)(2,1)S(1)}, bf16[96,640]{1,0:T(8,128)(2,1)S(1)}, u32[]{:S(2)}, u32[]{:S(2)}) collective-permute-start(bf16[96,640]{1,0:T(8,128)(2,1)S(1)} %collective-permute-done.4.refs_4_), channel_id=1, source_target_pairs={{0,4},{4,0},{8,12},{12,8},{16,20},{20,16},{24,28},{28,24},{1,5},{5... | collective-permute-start | bytes 368648 | tf_op jit(solution)/shard_map/ppermute | solution.py:622
  32.4 7.9 %collective-permute-start.13 = (bf16[144,768]{1,0:T(8,128)(2,1)S(1)}, bf16[144,768]{1,0:T(8,128)(2,1)S(1)}, u32[]{:S(2)}, u32[]{:S(2)}) collective-permute-start(bf16[144,768]{1,0:T(8,128)(2,1)S(1)} %pack_up.1.refs_0_), channel_id=1, source_target_pairs={{0,24},{4,28},{8,0},{12,4},{16,8},{20,12},{24,16},{28,20},{1,25},{... | collective-permute-start | bytes 663560 | tf_op jit(solution)/shard_map/ppermute | solution.py:625
  35.2 6.4 %collective-permute-start.14 = (bf16[144,768]{1,0:T(8,128)(2,1)S(1)}, bf16[144,768]{1,0:T(8,128)(2,1)S(1)}, u32[]{:S(2)}, u32[]{:S(2)}) collective-permute-start(bf16[144,768]{1,0:T(8,128)(2,1)S(1)} %pack_up.1.refs_0_), channel_id=1, source_target_pairs={{0,4},{4,0},{8,12},{12,8},{16,20},{20,16},{24,28},{28,24},{1,5},{5... | collective-permute-start | bytes 663560 | tf_op jit(solution)/shard_map/ppermute | solution.py:622
  35.2 7.8 %collective-permute-start.12 = (bf16[144,768]{1,0:T(8,128)(2,1)S(1)}, bf16[144,768]{1,0:T(8,128)(2,1)S(1)}, u32[]{:S(2)}, u32[]{:S(2)}) collective-permute-start(bf16[144,768]{1,0:T(8,128)(2,1)S(1)} %collective-permute-done.11.refs_1_), channel_id=1, source_target_pairs={{0,8},{4,12},{8,16},{12,20},{16,24},{20,28},{24,0},{28,4},{1,9},{5... | collective-permute-start | bytes 663560 | tf_op jit(solution)/shard_map/ppermute | solution.py:625
  37.8 5.4 %collective-permute-start.1 = (bf16[3,70,768]{2,1,0:T(8,128)(2,1)}, bf16[3,70,768]{2,1,0:T(8,128)(2,1)S(1)}, u32[]{:S(2)}, u32[]{:S(2)}) collective-permute-start(bf16[3,70,768]{2,1,0:T(8,128)(2,1)} %refs_3_.3), channel_id=1, source_target_pairs={{0,1},{1,0},{2,3},{3,2},{4,5},{5,4},{6,7},{7,6},{8,9},{9,8},{10,11... | collective-permute-start | bytes 967688 | tf_op jit(solution)/shard_map/ppermute | solution.py:619
  40.3 3.9 %collective-permute-start.3 = (bf16[3,70,768]{2,1,0:T(8,128)(2,1)S(1)}, bf16[3,70,768]{2,1,0:T(8,128)(2,1)S(1)}, u32[]{:S(2)}, u32[]{:S(2)}) collective-permute-start(bf16[3,70,768]{2,1,0:T(8,128)(2,1)S(1)} %collective-permute-done.2.refs_2_), channel_id=1, source_target_pairs={{0,1},{1,0},{2,3},{3,2},{4,5},{5,4},{6,7},{7,6},{8,9},{9,8},{10,11... | collective-permute-start | bytes 967688 | tf_op jit(solution)/shard_map/ppermute | solution.py:619
  40.3 13.8 %collective-permute-start.17 = (bf16[144,768]{1,0:T(8,128)(2,1)S(1)}, bf16[144,768]{1,0:T(8,128)(2,1)S(1)}, u32[]{:S(2)}, u32[]{:S(2)}) collective-permute-start(bf16[144,768]{1,0:T(8,128)(2,1)S(1)} %collective-permute-done.13.refs_3_), channel_id=1, source_target_pairs={{0,4},{4,0},{8,12},{12,8},{16,20},{20,16},{24,28},{28,24},{1,5},{5... | collective-permute-start | bytes 663560 | tf_op jit(solution)/shard_map/ppermute | solution.py:622
  41.6 13.2 %collective-permute-start.15 = (bf16[144,768]{1,0:T(8,128)(2,1)S(1)}, bf16[144,768]{1,0:T(8,128)(2,1)S(1)}, u32[]{:S(2)}, u32[]{:S(2)}) collective-permute-start(bf16[144,768]{1,0:T(8,128)(2,1)S(1)} %collective-permute-done.11.refs_1_), channel_id=1, source_target_pairs={{0,4},{4,0},{8,12},{12,8},{16,20},{20,16},{24,28},{28,24},{1,5},{5... | collective-permute-start | bytes 663560 | tf_op jit(solution)/shard_map/ppermute | solution.py:622
  43.0 14.3 %collective-permute-start.16 = (bf16[144,768]{1,0:T(8,128)(2,1)S(1)}, bf16[144,768]{1,0:T(8,128)(2,1)S(1)}, u32[]{:S(2)}, u32[]{:S(2)}) collective-permute-start(bf16[144,768]{1,0:T(8,128)(2,1)S(1)} %collective-permute-done.12.refs_2_), channel_id=1, source_target_pairs={{0,4},{4,0},{8,12},{12,8},{16,20},{20,16},{24,28},{28,24},{1,5},{5... | collective-permute-start | bytes 663560 | tf_op jit(solution)/shard_map/ppermute | solution.py:622
  43.3 27.8 %collective-permute-start.20 = (bf16[3,70,768]{2,1,0:T(8,128)(2,1)}, bf16[3,70,768]{2,1,0:T(8,128)(2,1)S(1)}, u32[]{:S(2)}, u32[]{:S(2)}) collective-permute-start(bf16[3,70,768]{2,1,0:T(8,128)(2,1)} %refs_2_.2), channel_id=1, source_target_pairs={{0,2},{1,3},{2,0},{3,1},{4,6},{5,7},{6,4},{7,5},{8,10},{9,11},{10,... | collective-permute-start | bytes 967688 | tf_op jit(solution)/shard_map/ppermute | solution.py:619
  44.2 18.8 %collective-permute-start.27 = (bf16[96,768]{1,0:T(8,128)(2,1)S(1)}, bf16[96,768]{1,0:T(8,128)(2,1)S(1)}, u32[]{:S(2)}, u32[]{:S(2)}) collective-permute-start(bf16[96,768]{1,0:T(8,128)(2,1)S(1)} %join_down.1.refs_3_), channel_id=1, source_target_pairs={{0,8},{4,12},{8,16},{12,20},{16,24},{20,28},{24,0},{28,4},{1,9},{5... | collective-permute-start | bytes 442376 | tf_op jit(solution)/shard_map/ppermute | solution.py:625
  54.1 15.8 %copy-start.3 = (bf16[3,70,768]{2,1,0:T(8,128)(2,1)S(1)}, bf16[3,70,768]{2,1,0:T(8,128)(2,1)}, u32[]{:S(2)}) copy-start(bf16[3,70,768]{2,1,0:T(8,128)(2,1)} %refs_2_.2) | copy-start | bytes 967684
  54.1 17.0 %collective-permute-start.23 = (bf16[480,384]{1,0:T(8,128)(2,1)S(1)}, bf16[480,384]{1,0:T(8,128)(2,1)S(1)}, u32[]{:S(2)}, u32[]{:S(2)}) collective-permute-start(bf16[480,384]{1,0:T(8,128)(2,1)S(1)} %get-tuple-element.132.refs_4_), channel_id=1, source_target_pairs={{0,2},{1,3},{2,0},{3,1},{4,6},{5,7},{6,4},{7,5},{8,10},{9,11},{10,... | collective-permute-start | bytes 1105928 | tf_op jit(solution)/shard_map/ppermute | solution.py:619
  57.5 18.4 %copy-start.1 = (bf16[3,70,768]{2,1,0:T(8,128)(2,1)S(1)}, bf16[3,70,768]{2,1,0:T(8,128)(2,1)}, u32[]{:S(2)}) copy-start(bf16[3,70,768]{2,1,0:T(8,128)(2,1)} %refs_3_.3) | copy-start | bytes 967684
  57.5 16.8 %collective-permute-start.18 = (bf16[768,384]{1,0:T(8,128)(2,1)S(1)}, bf16[768,384]{1,0:T(8,128)(2,1)S(1)}, u32[]{:S(2)}, u32[]{:S(2)}) collective-permute-start(bf16[768,384]{1,0:T(8,128)(2,1)S(1)} %get-tuple-element.129.refs_0_), channel_id=1, source_target_pairs={{0,1},{1,0},{2,3},{3,2},{4,5},{5,4},{6,7},{7,6},{8,9},{9,8},{10,11... | collective-permute-start | bytes 1769480 | tf_op jit(solution)/shard_map/ppermute | solution.py:619
  59.5 6.7 %collective-permute-start.29 = (bf16[96,768]{1,0:T(8,128)(2,1)S(1)}, bf16[96,768]{1,0:T(8,128)(2,1)S(1)}, u32[]{:S(2)}, u32[]{:S(2)}) collective-permute-start(bf16[96,768]{1,0:T(8,128)(2,1)S(1)} %join_down.1.refs_3_), channel_id=1, source_target_pairs={{0,24},{4,28},{8,0},{12,4},{16,8},{20,12},{24,16},{28,20},{1,25},{... | collective-permute-start | bytes 442376 | tf_op jit(solution)/shard_map/ppermute | solution.py:625
  63.0 6.9 %collective-permute-start.28 = (bf16[96,768]{1,0:T(8,128)(2,1)S(1)}, bf16[96,768]{1,0:T(8,128)(2,1)S(1)}, u32[]{:S(2)}, u32[]{:S(2)}) collective-permute-start(bf16[96,768]{1,0:T(8,128)(2,1)S(1)} %collective-permute-done.27.refs_4_), channel_id=1, source_target_pairs={{0,8},{4,12},{8,16},{12,20},{16,24},{20,28},{24,0},{28,4},{1,9},{5... | collective-permute-start | bytes 442376 | tf_op jit(solution)/shard_map/ppermute | solution.py:625
  66.2 7.6 %collective-permute-start.22 = (bf16[480,384]{1,0:T(8,128)(2,1)S(1)}, bf16[480,384]{1,0:T(8,128)(2,1)S(1)}, u32[]{:S(2)}, u32[]{:S(2)}) collective-permute-start(bf16[480,384]{1,0:T(8,128)(2,1)S(1)} %get-tuple-element.132.refs_4_), channel_id=1, source_target_pairs={{0,1},{1,0},{2,3},{3,2},{4,5},{5,4},{6,7},{7,6},{8,9},{9,8},{10,11... | collective-permute-start | bytes 1105928 | tf_op jit(solution)/shard_map/ppermute | solution.py:619
  69.9 2.4 %collective-permute-start.19 = (bf16[3,70,768]{2,1,0:T(8,128)(2,1)S(1)}, bf16[3,70,768]{2,1,0:T(8,128)(2,1)S(1)}, u32[]{:S(2)}, u32[]{:S(2)}) collective-permute-start(bf16[3,70,768]{2,1,0:T(8,128)(2,1)S(1)} %copy-done.3), channel_id=1, source_target_pairs={{0,1},{1,0},{2,3},{3,2},{4,5},{5,4},{6,7},{7,6},{8,9},{9,8},{10,11... | collective-permute-start | bytes 967688 | tf_op jit(solution)/shard_map/ppermute | solution.py:619
  71.1 1.8 collective-permute-start.21
  71.1 4.7 %collective-permute-start.24 = (bf16[480,384]{1,0:T(8,128)(2,1)S(1)}, bf16[480,384]{1,0:T(8,128)(2,1)S(1)}, u32[]{:S(2)}, u32[]{:S(2)}) collective-permute-start(bf16[480,384]{1,0:T(8,128)(2,1)S(1)} %collective-permute-done.23.refs_6_), channel_id=1, source_target_pairs={{0,1},{1,0},{2,3},{3,2},{4,5},{5,4},{6,7},{7,6},{8,9},{9,8},{10,11... | collective-permute-start | bytes 1105928 | tf_op jit(solution)/shard_map/ppermute | solution.py:619
  72.3 10.7 %collective-permute-start.30 = (bf16[96,768]{1,0:T(8,128)(2,1)S(1)}, bf16[96,768]{1,0:T(8,128)(2,1)S(1)}, u32[]{:S(2)}, u32[]{:S(2)}) collective-permute-start(bf16[96,768]{1,0:T(8,128)(2,1)S(1)} %join_down.1.refs_3_), channel_id=1, source_target_pairs={{0,4},{4,0},{8,12},{12,8},{16,20},{20,16},{24,28},{28,24},{1,5},{5... | collective-permute-start | bytes 442376 | tf_op jit(solution)/shard_map/ppermute | solution.py:622
  72.8 10.9 %collective-permute-start.31 = (bf16[96,768]{1,0:T(8,128)(2,1)S(1)}, bf16[96,768]{1,0:T(8,128)(2,1)S(1)}, u32[]{:S(2)}, u32[]{:S(2)}) collective-permute-start(bf16[96,768]{1,0:T(8,128)(2,1)S(1)} %collective-permute-done.27.refs_4_), channel_id=1, source_target_pairs={{0,4},{4,0},{8,12},{12,8},{16,20},{20,16},{24,28},{28,24},{1,5},{5... | collective-permute-start | bytes 442376 | tf_op jit(solution)/shard_map/ppermute | solution.py:622
  73.8 9.9 %collective-permute-start.33 = (bf16[96,768]{1,0:T(8,128)(2,1)S(1)}, bf16[96,768]{1,0:T(8,128)(2,1)S(1)}, u32[]{:S(2)}, u32[]{:S(2)}) collective-permute-start(bf16[96,768]{1,0:T(8,128)(2,1)S(1)} %collective-permute-done.29.refs_6_), channel_id=1, source_target_pairs={{0,4},{4,0},{8,12},{12,8},{16,20},{20,16},{24,28},{28,24},{1,5},{5... | collective-permute-start | bytes 442376 | tf_op jit(solution)/shard_map/ppermute | solution.py:622
  74.3 12.6 %collective-permute-start.32 = (bf16[96,768]{1,0:T(8,128)(2,1)S(1)}, bf16[96,768]{1,0:T(8,128)(2,1)S(1)}, u32[]{:S(2)}, u32[]{:S(2)}) collective-permute-start(bf16[96,768]{1,0:T(8,128)(2,1)S(1)} %collective-permute-done.28.refs_5_), channel_id=1, source_target_pairs={{0,4},{4,0},{8,12},{12,8},{16,20},{20,16},{24,28},{28,24},{1,5},{5... | collective-permute-start | bytes 442376 | tf_op jit(solution)/shard_map/ppermute | solution.py:622
  90.2 3.1 %collective-permute-start.34 = (bf16[2,240,768]{2,1,0:T(8,128)(2,1)S(1)}, bf16[2,240,768]{2,1,0:T(8,128)(2,1)S(1)}, u32[]{:S(2)}, u32[]{:S(2)}) collective-permute-start(bf16[2,240,768]{2,1,0:T(8,128)(2,1)S(1)} %get-tuple-element.147), channel_id=1, source_target_pairs={{0,1},{1,0},{2,3},{3,2},{4,5},{5,4},{6,7},{7,6},{8,9},{9,8},{10,11... | collective-permute-start | bytes 2211848 | tf_op jit(solution)/shard_map/ppermute | solution.py:619
  91.5 16.7 %collective-permute-start.36 = (bf16[4,96,768]{2,1,0:T(8,128)(2,1)S(1)}, bf16[4,96,768]{2,1,0:T(8,128)(2,1)S(1)}, u32[]{:S(2)}, u32[]{:S(2)}) collective-permute-start(bf16[4,96,768]{2,1,0:T(8,128)(2,1)S(1)} %get-tuple-element.158), channel_id=1, source_target_pairs={{0,4},{4,0},{8,12},{12,8},{16,20},{20,16},{24,28},{28,24},{1,5},{5... | collective-permute-start | bytes 1769480 | tf_op jit(solution)/shard_map/ppermute | solution.py:622
  93.4 9.9 %collective-permute-start.35 = (bf16[240,768]{1,0:T(8,128)(2,1)S(1)}, bf16[240,768]{1,0:T(8,128)(2,1)S(1)}, u32[]{:S(2)}, u32[]{:S(2)}) collective-permute-start(bf16[240,768]{1,0:T(8,128)(2,1)S(1)} %pair.2), channel_id=1, source_target_pairs={{0,2},{1,3},{2,0},{3,1},{4,6},{5,7},{6,4},{7,5},{8,10},{9,11},{10,... | collective-permute-start | bytes 1105928 | tf_op jit(solution)/shard_map/ppermute | solution.py:619
  104.4 5.3 %collective-permute-start.37 = (bf16[240,384]{1,0:T(8,128)(2,1)S(1)}, bf16[240,384]{1,0:T(8,128)(2,1)S(1)}, u32[]{:S(2)}, u32[]{:S(2)}) collective-permute-start(bf16[240,384]{1,0:T(8,128)(2,1)S(1)} %get-tuple-element.161), channel_id=1, source_target_pairs={{0,1},{1,0},{2,3},{3,2},{4,5},{5,4},{6,7},{7,6},{8,9},{9,8},{10,11... | collective-permute-start | bytes 552968 | tf_op jit(solution)/shard_map/ppermute | solution.py:619
  105.7 6.2 %collective-permute-start.38 = (bf16[240,384]{1,0:T(8,128)(2,1)S(1)}, bf16[240,384]{1,0:T(8,128)(2,1)S(1)}, u32[]{:S(2)}, u32[]{:S(2)}) collective-permute-start(bf16[240,384]{1,0:T(8,128)(2,1)S(1)} %get-tuple-element.162), channel_id=1, source_target_pairs={{0,2},{1,3},{2,0},{3,1},{4,6},{5,7},{6,4},{7,5},{8,10},{9,11},{10,... | collective-permute-start | bytes 552968 | tf_op jit(solution)/shard_map/ppermute | solution.py:619
  106.7 9.6 %collective-permute-start.39 = (bf16[240,384]{1,0:T(8,128)(2,1)S(1)}, bf16[240,384]{1,0:T(8,128)(2,1)S(1)}, u32[]{:S(2)}, u32[]{:S(2)}) collective-permute-start(bf16[240,384]{1,0:T(8,128)(2,1)S(1)} %get-tuple-element.163), channel_id=1, source_target_pairs={{0,3},{1,2},{2,1},{3,0},{4,7},{5,6},{6,5},{7,4},{8,11},{9,10},{10,... | collective-permute-start | bytes 552968 | tf_op jit(solution)/shard_map/ppermute | solution.py:619
  107.4 14.8 %collective-permute-start.40 = (bf16[4,96,768]{2,1,0:T(8,128)(2,1)S(1)}, bf16[4,96,768]{2,1,0:T(8,128)(2,1)S(1)}, u32[]{:S(2)}, u32[]{:S(2)}) collective-permute-start(bf16[4,96,768]{2,1,0:T(8,128)(2,1)S(1)} %get-tuple-element.169), channel_id=1, source_target_pairs={{0,4},{4,0},{8,12},{12,8},{16,20},{20,16},{24,28},{28,24},{1,5},{5... | collective-permute-start | bytes 1769480 | tf_op jit(solution)/shard_map/ppermute | solution.py:622
  108.3 18.5 %collective-permute-start.41 = (bf16[96,768]{1,0:T(8,128)(2,1)S(1)}, bf16[96,768]{1,0:T(8,128)(2,1)S(1)}, u32[]{:S(2)}, u32[]{:S(2)}) collective-permute-start(bf16[96,768]{1,0:T(8,128)(2,1)S(1)} %get-tuple-element.173), channel_id=1, source_target_pairs={{0,8},{4,12},{8,16},{12,20},{16,24},{20,28},{24,0},{28,4},{1,9},{5... | collective-permute-start | bytes 442376 | tf_op jit(solution)/shard_map/ppermute | solution.py:625
  109.7 17.1 %collective-permute-start.42 = (bf16[96,768]{1,0:T(8,128)(2,1)S(1)}, bf16[96,768]{1,0:T(8,128)(2,1)S(1)}, u32[]{:S(2)}, u32[]{:S(2)}) collective-permute-start(bf16[96,768]{1,0:T(8,128)(2,1)S(1)} %get-tuple-element.174), channel_id=1, source_target_pairs={{0,16},{4,20},{8,24},{12,28},{16,0},{20,4},{24,8},{28,12},{1,17},{... | collective-permute-start | bytes 442376 | tf_op jit(solution)/shard_map/ppermute | solution.py:625
  111.9 14.9 %collective-permute-start.43 = (bf16[96,768]{1,0:T(8,128)(2,1)S(1)}, bf16[96,768]{1,0:T(8,128)(2,1)S(1)}, u32[]{:S(2)}, u32[]{:S(2)}) collective-permute-start(bf16[96,768]{1,0:T(8,128)(2,1)S(1)} %get-tuple-element.175), channel_id=1, source_target_pairs={{0,24},{4,28},{8,0},{12,4},{16,8},{20,12},{24,16},{28,20},{1,25},{... | collective-permute-start | bytes 442376 | tf_op jit(solution)/shard_map/ppermute | solution.py:625
  130.4 9.7 %collective-permute-start.47 = (bf16[2,480,768]{2,1,0:T(8,128)(2,1)S(1)}, bf16[2,480,768]{2,1,0:T(8,128)(2,1)S(1)}, u32[]{:S(2)}, u32[]{:S(2)}) collective-permute-start(bf16[2,480,768]{2,1,0:T(8,128)(2,1)S(1)} %get-tuple-element.195), channel_id=1, source_target_pairs={{0,1},{1,0},{2,3},{3,2},{4,5},{5,4},{6,7},{7,6},{8,9},{9,8},{10,11... | collective-permute-start | bytes 4423688 | tf_op jit(solution)/shard_map/ppermute | solution.py:619
  131.4 8.6 %collective-permute-start.46 = (bf16[4,96,384]{2,1,0:T(8,128)(2,1)S(1)}, bf16[4,96,384]{2,1,0:T(8,128)(2,1)S(1)}, u32[]{:S(2)}, u32[]{:S(2)}) collective-permute-start(bf16[4,96,384]{2,1,0:T(8,128)(2,1)S(1)} %get-tuple-element.191), channel_id=1, source_target_pairs={{0,4},{4,0},{8,12},{12,8},{16,20},{20,16},{24,28},{28,24},{1,5},{5... | collective-permute-start | bytes 884744 | tf_op jit(solution)/shard_map/ppermute | solution.py:622
  132.2 2.2 %collective-permute-start.45 = (f32[16,768]{1,0:T(8,128)S(1)}, f32[16,768]{1,0:T(8,128)S(1)}, u32[]{:S(2)}, u32[]{:S(2)}) collective-permute-start(f32[16,768]{1,0:T(8,128)S(1)} %get-tuple-element.187.refs_0_), channel_id=1, source_target_pairs={{0,1},{1,0},{2,3},{3,2},{4,5},{5,4},{6,7},{7,6},{8,9},{9,8},{10,11... | collective-permute-start | bytes 147464 | tf_op jit(solution)/shard_map/ppermute | solution.py:619
  140.3 34.1 %collective-permute-start.53 = (bf16[480,768]{1,0:T(8,128)(2,1)S(1)}, bf16[480,768]{1,0:T(8,128)(2,1)S(1)}, u32[]{:S(2)}, u32[]{:S(2)}) collective-permute-start(bf16[480,768]{1,0:T(8,128)(2,1)S(1)} %pair.3), channel_id=1, source_target_pairs={{0,2},{1,3},{2,0},{3,1},{4,6},{5,7},{6,4},{7,5},{8,10},{9,11},{10,... | collective-permute-start | bytes 2211848 | tf_op jit(solution)/shard_map/ppermute | solution.py:619
  141.4 21.4 %collective-permute-start.44 = (bf16[4,96,384]{2,1,0:T(8,128)(2,1)S(1)}, bf16[4,96,384]{2,1,0:T(8,128)(2,1)S(1)}, u32[]{:S(2)}, u32[]{:S(2)}) collective-permute-start(bf16[4,96,384]{2,1,0:T(8,128)(2,1)S(1)} %get-tuple-element.186), channel_id=1, source_target_pairs={{0,4},{4,0},{8,12},{12,8},{16,20},{20,16},{24,28},{28,24},{1,5},{5... | collective-permute-start | bytes 884744 | tf_op jit(solution)/shard_map/ppermute | solution.py:622
  142.5 6.0 %collective-permute-start.48 = (bf16[96,768]{1,0:T(8,128)(2,1)S(1)}, bf16[96,768]{1,0:T(8,128)(2,1)S(1)}, u32[]{:S(2)}, u32[]{:S(2)}) collective-permute-start(bf16[96,768]{1,0:T(8,128)(2,1)S(1)} %get-tuple-element.197), channel_id=1, source_target_pairs={{0,8},{4,12},{8,16},{12,20},{16,24},{20,28},{24,0},{28,4},{1,9},{5... | collective-permute-start | bytes 442376 | tf_op jit(solution)/shard_map/ppermute | solution.py:625
  143.9 12.5 %collective-permute-start.49 = (bf16[96,768]{1,0:T(8,128)(2,1)S(1)}, bf16[96,768]{1,0:T(8,128)(2,1)S(1)}, u32[]{:S(2)}, u32[]{:S(2)}) collective-permute-start(bf16[96,768]{1,0:T(8,128)(2,1)S(1)} %get-tuple-element.198), channel_id=1, source_target_pairs={{0,16},{4,20},{8,24},{12,28},{16,0},{20,4},{24,8},{28,12},{1,17},{... | collective-permute-start | bytes 442376 | tf_op jit(solution)/shard_map/ppermute | solution.py:625
  144.2 12.2 %collective-permute-start.50 = (bf16[96,768]{1,0:T(8,128)(2,1)S(1)}, bf16[96,768]{1,0:T(8,128)(2,1)S(1)}, u32[]{:S(2)}, u32[]{:S(2)}) collective-permute-start(bf16[96,768]{1,0:T(8,128)(2,1)S(1)} %get-tuple-element.199), channel_id=1, source_target_pairs={{0,24},{4,28},{8,0},{12,4},{16,8},{20,12},{24,16},{28,20},{1,25},{... | collective-permute-start | bytes 442376 | tf_op jit(solution)/shard_map/ppermute | solution.py:625
  148.5 11.4 %collective-permute-start.51 = (f32[16,768]{1,0:T(8,128)S(1)}, f32[16,768]{1,0:T(8,128)S(1)}, u32[]{:S(2)}, u32[]{:S(2)}) collective-permute-start(f32[16,768]{1,0:T(8,128)S(1)} %add.2.refs_0_), channel_id=1, source_target_pairs={{0,2},{1,3},{2,0},{3,1},{4,6},{5,7},{6,4},{7,5},{8,10},{9,11},{10,... | collective-permute-start | bytes 147464 | tf_op jit(solution)/shard_map/ppermute | solution.py:619
  156.4 9.8 %collective-permute-start.55 = (bf16[96,384]{1,0:T(8,128)(2,1)S(1)}, bf16[96,384]{1,0:T(8,128)(2,1)S(1)}, u32[]{:S(2)}, u32[]{:S(2)}) collective-permute-start(bf16[96,384]{1,0:T(8,128)(2,1)S(1)} %get-tuple-element.208), channel_id=1, source_target_pairs={{0,8},{4,12},{8,16},{12,20},{16,24},{20,28},{24,0},{28,4},{1,9},{5... | collective-permute-start | bytes 221192 | tf_op jit(solution)/shard_map/ppermute | solution.py:625
  156.4 9.9 %collective-permute-start.56 = (bf16[96,384]{1,0:T(8,128)(2,1)S(1)}, bf16[96,384]{1,0:T(8,128)(2,1)S(1)}, u32[]{:S(2)}, u32[]{:S(2)}) collective-permute-start(bf16[96,384]{1,0:T(8,128)(2,1)S(1)} %get-tuple-element.209), channel_id=1, source_target_pairs={{0,16},{4,20},{8,24},{12,28},{16,0},{20,4},{24,8},{28,12},{1,17},{... | collective-permute-start | bytes 221192 | tf_op jit(solution)/shard_map/ppermute | solution.py:625
  159.9 9.6 %collective-permute-start.57 = (bf16[96,384]{1,0:T(8,128)(2,1)S(1)}, bf16[96,384]{1,0:T(8,128)(2,1)S(1)}, u32[]{:S(2)}, u32[]{:S(2)}) collective-permute-start(bf16[96,384]{1,0:T(8,128)(2,1)S(1)} %get-tuple-element.210), channel_id=1, source_target_pairs={{0,24},{4,28},{8,0},{12,4},{16,8},{20,12},{24,16},{28,20},{1,25},{... | collective-permute-start | bytes 221192 | tf_op jit(solution)/shard_map/ppermute | solution.py:625
  162.8 3.3 %collective-permute-start.52 = (f32[16,768]{1,0:T(8,128)S(1)}, f32[16,768]{1,0:T(8,128)S(1)}, u32[]{:S(2)}, u32[]{:S(2)}) collective-permute-start(f32[16,768]{1,0:T(8,128)S(1)} %add.3.refs_2_), channel_id=1, source_target_pairs={{0,4},{4,0},{8,12},{12,8},{16,20},{20,16},{24,28},{28,24},{1,5},{5... | collective-permute-start | bytes 147464 | tf_op jit(solution)/shard_map/ppermute | solution.py:622
  166.1 16.5 %collective-permute-start.59 = (bf16[128,384]{1,0:T(8,128)(2,1)S(1)}, bf16[128,384]{1,0:T(8,128)(2,1)S(1)}, u32[]{:S(2)}, u32[]{:S(2)}) collective-permute-start(bf16[128,384]{1,0:T(8,128)(2,1)S(1)} %get-tuple-element.216), channel_id=1, source_target_pairs={{0,8},{4,12},{8,16},{12,20},{16,24},{20,28},{24,0},{28,4},{1,9},{5... | collective-permute-start | bytes 294920 | tf_op jit(solution)/shard_map/ppermute | solution.py:625
  166.2 16.5 %collective-permute-start.60 = (bf16[128,384]{1,0:T(8,128)(2,1)S(1)}, bf16[128,384]{1,0:T(8,128)(2,1)S(1)}, u32[]{:S(2)}, u32[]{:S(2)}) collective-permute-start(bf16[128,384]{1,0:T(8,128)(2,1)S(1)} %get-tuple-element.217), channel_id=1, source_target_pairs={{0,16},{4,20},{8,24},{12,28},{16,0},{20,4},{24,8},{28,12},{1,17},{... | collective-permute-start | bytes 294920 | tf_op jit(solution)/shard_map/ppermute | solution.py:625
  166.3 16.4 %collective-permute-start.61 = (bf16[128,384]{1,0:T(8,128)(2,1)S(1)}, bf16[128,384]{1,0:T(8,128)(2,1)S(1)}, u32[]{:S(2)}, u32[]{:S(2)}) collective-permute-start(bf16[128,384]{1,0:T(8,128)(2,1)S(1)} %get-tuple-element.218), channel_id=1, source_target_pairs={{0,24},{4,28},{8,0},{12,4},{16,8},{20,12},{24,16},{28,20},{1,25},{... | collective-permute-start | bytes 294920 | tf_op jit(solution)/shard_map/ppermute | solution.py:625
  169.5 9.4 %collective-permute-start.54 = (bf16[96,384]{1,0:T(8,128)(2,1)S(1)}, bf16[96,384]{1,0:T(8,128)(2,1)S(1)}, u32[]{:S(2)}, u32[]{:S(2)}) collective-permute-start(bf16[96,384]{1,0:T(8,128)(2,1)S(1)} %get-tuple-element.176), channel_id=1, source_target_pairs={{0,0},{1,8},{2,16},{3,24},{4,4},{5,12},{6,20},{7,28},{8,1},{9,9},{... | collective-permute-start | bytes 221192 | tf_op jit(solution)/shard_map/ppermute | solution.py:644
  174.4 7.5 %collective-permute-start.58 = (bf16[96,384]{1,0:T(8,128)(2,1)S(1)}, bf16[96,384]{1,0:T(8,128)(2,1)S(1)}, u32[]{:S(2)}, u32[]{:S(2)}) collective-permute-start(bf16[96,384]{1,0:T(8,128)(2,1)S(1)} %get-tuple-element.213), channel_id=1, source_target_pairs={{0,4},{1,12},{2,20},{3,28},{4,0},{5,8},{6,16},{7,24},{8,5},{9,13},... | collective-permute-start | bytes 221192 | tf_op jit(solution)/shard_map/ppermute | solution.py:644
  (7 other events, 10.8 us)

commit v3 on v2

--- a/solution.py
+++ b/solution.py
@@ -9,6 +9,8 @@
 from jax.sharding import PartitionSpec as P
 
 HEADS = 12
+COST = {'up_grad': 10000000000, 'branch': 10000000000, 'value_back': 10000000000, 'attend_back': 10000000000, 'finish': 10000000000, 'pack': 3000000000, 'sum_down': 1000, 'sum_up': 1000, 'last_x': 30000000000, 'hidden_back': 3000000000, 'qk_grad': 1000000000}
+CFG = {'pair': 1, 'add': 1, 'za': 'direct', 'zu': 'bidir', 'zd': 'bidir', 'xu': 0, 'xd': 0, 'norm': 3, 'held': 0, 'split': 3, 'cot': 1, 'tok': 1, 'ord': 1, 'up': 0, 'vo': 0, 'br': 1, 'both': 0, 'og': 3, 'sa': 'each', 'su': 'each', 'sd': 'rest', 'gd': 2}
 EPS = 1e-05
 LOW = jnp.bfloat16
 F32 = jnp.float32
@@ -40,8 +42,8 @@
     return pl.ds(start, size)
 
 
-def pallas(body, outs, ins, scratch=(), smem=0, here=False, name=None, mib=8, long=False):
-    flops = 10**10 if long else 1000
+def pallas(body, outs, ins, scratch=(), smem=0, here=False, name=None, mib=8):
+    flops = COST.get(name, 1000)
     nbytes = sum(a.size * a.dtype.itemsize for a in ins)
     nbytes += sum(s.size * jnp.dtype(s.dtype).itemsize for s in outs)
     near = pl.BlockSpec(memory_space=pltpu.VMEM)
@@ -74,6 +76,13 @@
     k = part % m.nz
     side = x if part < m.nz else 1 - x
     return lax.rem(z - k + m.nz, m.nz) * 2 + side
+
+
+def spread(parts):
+    out = []
+    for part in parts:
+        out += [part.at[k] for k in range(part.shape[0])] if len(part.shape) == 3 else [part]
+    return out
 
 
 def layer_norm(x):
@@ -133,6 +142,11 @@
             down[:, (1 - x) * width : (2 - x) * width] = second[...]
 
 
+def stack_kernel(m, *refs):
+    for k, ref in enumerate(refs[:-1]):
+        refs[-1][k] = ref[...]
+
+
 def norm_kernel(m, *refs):
     tokens, (xhat, x_scr) = refs[: m.S], refs[m.S :]
     x_scr[...] = jnp.zeros_like(x_scr)
@@ -154,7 +168,7 @@
     if nparts == 1:
         w_ref[...] = parts[0][...]
     else:
-        for p, part in enumerate(parts):
+        for p, part in enumerate(spread(parts)):
             w_ref[ds(part_index(m, sc, p) * m.rows, m.rows), :] = part[...]
     base = (3 * m.WH) // 128 * 128
     turned = w_ref[:, base : base + 128].astype(F32).T
@@ -221,7 +235,7 @@
     w_up, w_out = refs[1 + nparts :]
     half = m.rows // 2
     per = m.N // m.S
-    for p, part in enumerate(parts):
+    for p, part in enumerate(spread(parts)):
         i = part_index(m, sc, p)
         w_up[ds(i * m.rows, m.rows), :] = part[: m.rows]
         start = (sc[0] ^ lax.div(i, per)) * m.WH + lax.rem(i, per) * m.rows
@@ -302,7 +316,7 @@
     if nparts == 1:
         w_down[...] = parts[0][...]
     else:
-        for p, part in enumerate(parts):
+        for p, part in enumerate(spread(parts)):
             w_down[ds(part_index(m, sc, p) * m.rows, m.rows), :] = part[...]
 
     def item(b, carry):
@@ -480,6 +494,33 @@
         out[...] = (keep[k + 1].astype(F32) + got[k + 1].astype(F32)).astype(LOW)
 
 
+def both_x_kernel(m, up_keep, up_got, vo_keep, vo_got, up_own, vo_own, *outs):
+    half = m.rows // 2
+    up_own[...] = up_keep[0].astype(F32) + up_got[0].astype(F32)
+    vo_own[...] = vo_keep[0].astype(F32) + vo_got[0].astype(F32)
+    for k, out in enumerate(outs):
+        out[: m.rows, :] = (up_keep[k + 1].astype(F32) + up_got[k + 1].astype(F32)).astype(LOW)
+        total = (vo_keep[k + 1].astype(F32) + vo_got[k + 1].astype(F32)).astype(LOW)
+        out[m.rows :, : 2 * m.WH] = total[:half]
+        out[m.rows :, 2 * m.WH :] = total[half:]
+
+
+def both_z_kernel(m, up_own, vo_own, *refs):
+    rest, (g_up, first, second) = refs[: m.nz - 1], refs[m.nz - 1 :]
+    half = m.rows // 2
+    total = up_own[...]
+    for r in rest:
+        total = total + r[: m.rows, :].astype(F32)
+    g_up[...] = total
+    for side in range(2):
+        at = slice(side * half, (side + 1) * half)
+        total = vo_own[at, :]
+        for r in rest:
+            total = total + r[m.rows :, 2 * m.WH * side : 2 * m.WH * (side + 1)].astype(F32)
+        first[at, :] = total[:, : m.WH]
+        second[at, :] = total[:, m.WH :]
+
+
 def last_x_kernel(m, keep, got, vec, vec_got, own, vec_own, *outs):
     own[...] = keep[0].astype(F32) + got[0].astype(F32)
     values = vec[...] + vec_got[...]
@@ -631,9 +672,24 @@
         same = [x] + [z_shift(x, k) for k in range(1, nz)]
         return same + [x_swap(v) for v in same]
 
-    def around(x):
+    def around(x, kind):
+        if kind == "direct":
+            return [x] + [z_shift(x, k) for k in range(1, nz)]
+        if kind == "ring":
+            out = [x]
+            for _ in range(1, nz):
+                out.append(z_shift(out[-1], 1))
+            return out
         a, b = z_shift(x, 1), z_shift(x, nz - 1)
         return [x, a, z_shift(a, 1), b]
+
+    def swapped(same, kind, name, after=()):
+        if kind == "each":
+            return [x_swap(same[0])] + [x_swap(gate(v, *after)) for v in same[1:]]
+        begin = 1 if kind == "rest" else 0
+        rest = [gate(same[begin], *after), *same[begin + 1 :]]
+        (stacked,) = pallas(fn(stack_kernel, m), [shape(len(rest), *same[0].shape)], rest, name=name)
+        return [x_swap(same[0])] * begin + [x_swap(stacked)]
 
     def exchange(x, k):
         pairs = []
@@ -649,7 +705,6 @@
 
     vectors = [norm1_gain, norm1_bias, query_bias, value_bias, out_bias, norm2_gain, norm2_bias, down_bias, up_bias]
     if m.fast:
-        out_far = seq_to(w_out, 2)
         (first,) = pallas(
             fn(pack_kernel, m),
             [shape(rows, m.wide)],
@@ -658,14 +713,16 @@
             name="pack",
             mib=60,
         )
-        first_parts = direct(first)
+        first_same = around(first, CFG["za"])
+        first_parts = first_same + swapped(first_same, CFG["sa"], "stack_first")
+        out_far = seq_to(gate(w_out, *{0: [], 1: [first_parts[nz]], 2: [first_same[1]], 3: [first]}[CFG["og"]]), 2)
         (up_out,) = pallas(
             fn(pack_up_kernel, m), [shape(m.up_rows, D)], [gate(w_up, first), w_out, out_far], name="pack_up"
         )
         halves = pallas(
             fn(split_down_kernel, m),
             [shape(WH // 2, S * m.hrows)] * 2,
-            [gate(w_down.T, first)],
+            [gate(w_down.T, *{0: [], 1: [first], 2: [up_out], 3: [first_same[1]], 4: first_same[1:]}[CFG["split"]])],
             here=True,
             name="split_down",
         )
@@ -676,14 +733,12 @@
             here=True,
             name="join_down",
         )
-        token_blocks = gather_seq(gate(tokens, first))
-        cot_blocks = gather_seq(gate(cotangent, token_blocks[2]))
-        up_same = around(up_out)
-        up_side = x_swap(up_out)
-        down_same = around(down)
-        down_side = x_swap(down)
-        norm_after = [up_out]
-        held = []
+        token_blocks = gather_seq(gate(tokens, *{0: [], 1: [first]}[CFG["tok"]]))
+        cot_blocks = gather_seq(gate(cotangent, *{0: [first], 1: [token_blocks[2]], 2: [up_out]}[CFG["cot"]]))
+        up_same = around(up_out, CFG["zu"])
+        down_same = around(down, CFG["zd"])
+        norm_after = {0: [], 1: [up_out], 2: [up_out, down], 3: [up_out, *first_same[1:]], 4: [up_out, down, *first_same[1:]]}[CFG["norm"]]
+        held = {0: [], 1: [cot_blocks[2]], 2: [up_same[1]], 3: [up_same[1], up_same[-1]], 4: [down]}[CFG["held"]]
     else:
         token_blocks = gather_seq(tokens)
         cot_blocks = gather_seq(cotangent)
@@ -705,7 +760,6 @@
         [gate(token_blocks[0], *norm_after), *token_blocks[1:]],
         [pltpu.VMEM((m.IT, D), F32)],
         name="norm",
-        long=False,
     )
     qkv, normed, probs, packed, vecs, w_first = pallas(
         fn(attend_kernel, m, len(first_parts)),
@@ -718,15 +772,16 @@
             shape(D, m.wide),
         ],
         [text_mask, patch_count, gate(xhat, *held), *first_parts],
-        long=False,
         smem=2,
         here=True,
         name="attend",
     )
     packed_blocks = gather_seq(packed)
     if m.fast:
-        up_parts = up_same + [up_side] + [x_swap(v) for v in up_same[1:]]
-        down_parts = down_same + [down_side] + [x_swap(v) for v in down_same[1:]]
+        after = [packed] if CFG["xu"] else []
+        up_parts = up_same + swapped(up_same, CFG["su"], "stack_up", after)
+        after = [packed] if CFG["xd"] else []
+        down_parts = down_same + swapped(down_same, CFG["sd"], "stack_down", after)
 
     if m.fast:
         up_all, half = pallas(
@@ -779,7 +834,6 @@
             [pltpu.VMEM((D, D), F32)],
             here=True,
             name=name,
-            long=name == "up_grad",
         )
 
     down_keep, down_send = weight_grad(cot, active, "down_grad")
@@ -791,43 +845,49 @@
         name="hidden_back",
     )
 
-    def add_pair(keep, core):
-        (out,) = pallas(fn(pair_kernel, m), [shape(*keep.shape)], [keep, core], name="pair")
+    def add_pair(keep, core, name):
+        (out,) = pallas(fn(pair_kernel, m), [shape(*keep.shape)], [keep, core], name=name)
         return out
 
-    def add(left, right):
-        (out,) = pallas(fn(add_kernel, m), [shape(*left.shape, dtype=F32)], [left, right], name="add")
+    def add(left, right, name):
+        (out,) = pallas(fn(add_kernel, m), [shape(*left.shape, dtype=F32)], [left, right], name=name)
         return out
 
     core2 = seq_to(send, 1)
-    pair2 = add_pair(keep1, core2)
+    pair2 = add_pair(keep1, core2, "pair2")
     far2 = seq_to(pair2, 2)
 
     up_keep, up_send = weight_grad(normed2, gate(g_hidden, pair2), "up_grad")
-    b_keep0, b_keep1, b_send, vec_ff = pallas(
-        fn(branch_kernel, m),
-        [shape(m.OWN, D), shape(m.OWN, D), shape(2, m.OWN, D), shape(8, D, dtype=F32)],
-        [gate(active, up_keep), down_all, g_hidden, cot],
-        name="branch",
-        long=True,
-    )
-
+    def branch(after):
+        return pallas(
+            fn(branch_kernel, m),
+            [shape(m.OWN, D), shape(m.OWN, D), shape(2, m.OWN, D), shape(8, D, dtype=F32)],
+            [gate(active, after), down_all, g_hidden, cot],
+            name="branch",
+        )
+
+    if not CFG["br"]:
+        b_keep0, b_keep1, b_send, vec_ff = branch(up_keep)
     g_resid, *blocks, vec_mid = pallas(
         fn(middle_kernel, m),
         [shape(m.OWN, D, dtype=F32), *[shape(m.OWN, 2 * WH)] * S, shape(8, D, dtype=F32)],
-        [gate(keep0, b_keep0), core2, far2, xhat2, rstd2, cot, out_all, vecs],
+        [gate(keep0, up_keep if CFG["br"] else b_keep0), core2, far2, xhat2, rstd2, cot, out_all, vecs],
         [pltpu.VMEM((m.OWN, D), LOW)],
         here=True,
         name="middle",
     )
+    if CFG["br"]:
+        b_keep0, b_keep1, b_send, vec_ff = branch(g_resid)
     blocks = [blocks[0]] + [seq_to(blocks[e], e) for e in range(1, S)]
-
-    def sum_x(keep, got, width):
+    if CFG["br"] == 1:
+        blocks[0] = gate(blocks[0], b_keep0)
+
+    def sum_x(keep, got, width, name):
         return pallas(
             fn(sum_x_kernel, m),
             [shape(rows, width, dtype=F32)] + [shape(rows, width)] * (nz - 1),
             [keep, got],
-            name="sum_x",
+            name=name,
         )
 
     def to_z(parts):
@@ -838,7 +898,7 @@
 
     if m.fast:
         down_got, up_got = x_swap(down_send), x_swap(up_send)
-        down_own, *down_sums = sum_x(gate(down_keep, blocks[0]), down_got, D)
+        down_own, *down_sums = sum_x(gate(down_keep, blocks[0]), down_got, D, "down_x")
         down_z = to_z(down_sums)
         blocks[0] = gate(blocks[0], down_own)
     g_value, g_mixed, vo_keep, vo_send = pallas(
@@ -848,13 +908,9 @@
         [pltpu.VMEM((m.RA, WH), LOW), pltpu.VMEM((D, 2 * WH), F32)],
         here=True,
         name="value_back",
-        long=True,
     )
     if m.fast:
         vo_got = x_swap(vo_send)
-        up_own, *up_sums = sum_x(gate(up_keep, g_value), up_got, D)
-        up_z = to_z(up_sums)
-        g_mixed = gate(g_mixed, up_own)
 
         def sum_down(after):
             return pallas(
@@ -870,43 +926,71 @@
         [shape(m.RA, 2 * WH)],
         [qkv, probs, g_mixed],
         name="attend_back",
-        long=True,
     )
     g_last = g_qk
     if m.fast:
-        halves = sum_down(g_qk)
+        up_own, vo_own, *both = pallas(
+            fn(both_x_kernel, m),
+            [shape(rows, m.FD, dtype=F32), shape(rows, 2 * WH, dtype=F32)]
+            + [shape(m.up_rows, m.FD)] * (nz - 1),
+            [gate(up_keep, g_qk), up_got, vo_keep, vo_got],
+            name="both_x",
+        )
+        both_z = to_z(both)
+        halves = sum_down(up_own)
         down_halves = [exchange(halves[k], k) for k in range(2)]
         g_last = gate(g_qk, halves[0])
-    qk_keep, qk_send = pallas(
-        fn(weight_grad_kernel, m),
-        shards(2 * WH),
-        [normed, g_last],
-        [pltpu.VMEM((D, 2 * WH), F32)],
-        here=True,
-        name="qk_grad",
-    )
+
+        def give_down(*after):
+            (out,) = pallas(
+                fn(give_down_kernel, m),
+                [shape(WH, S * m.hrows, dtype=F32)],
+                [gate(down_halves[0], *after), down_halves[1]],
+                here=True,
+                name="give_down",
+            )
+            return out
+
+    def qk_grad(after):
+        return pallas(
+            fn(weight_grad_kernel, m),
+            shards(2 * WH),
+            [normed, gate(g_last, after)],
+            [pltpu.VMEM((D, 2 * WH), F32)],
+            here=True,
+            name="qk_grad",
+        )
+
+    if not CFG["ord"]:
+        qk_keep, qk_send = qk_grad(g_qk)
     keep0, keep1, send, vec = pallas(
         fn(input_back_kernel, m),
         [shape(m.OWN, D), shape(2 * m.OWN, D), shape(2, 2 * m.OWN, D), shape(VECS, D, dtype=F32)],
-        [gate(g_qk, qk_keep), g_value, xhat, w_first, vec_mid, vec_ff, b_keep1, b_send],
+        [gate(g_last, *([] if CFG["ord"] else [qk_keep])), g_value, xhat, w_first, vec_mid, vec_ff, b_keep1, b_send],
         here=True,
         name="input_back",
     )
+    if CFG["ord"]:
+        qk_keep, qk_send = qk_grad(vec)
     vec_core, core1 = seq_to(vec, 1), seq_to(send, 1)
-    vec = add(vec, vec_core)
+    vec = add(vec, vec_core, "add_core")
     vec_far = seq_to(vec, 2)
-    if m.fast:
-        vo_own, *vo_sums = sum_x(gate(vo_keep, vec), vo_got, 2 * WH)
-        vo_z = to_z(vo_sums)
-        keep1 = gate(keep1, vo_own)
-    pair1 = add_pair(gate(keep1, vec), core1)
+    pair1 = add_pair(gate(keep1, *([vec_far] if CFG["pair"] else [vec])), core1, "pair1")
     far1 = seq_to(pair1, 2)
     if m.fast:
         qk_got = x_swap(qk_send)
-        (g_up,) = pallas(
-            fn(sum_up_kernel, m), [shape(rows, m.FD, dtype=F32)], [gate(up_own, pair1), *up_z], name="sum_up"
-        )
-        vec = add(gate(vec, g_up), vec_far)
+
+        def both_out(after):
+            return pallas(
+                fn(both_z_kernel, m),
+                [shape(rows, m.FD, dtype=F32)] + [shape(rows, WH, dtype=F32)] * 2,
+                [gate(up_own, after), vo_own, *both_z],
+                name="both_out",
+            )
+
+        if CFG["gd"]:
+            g_down = give_down(pair1)
+        vec = add(gate(vec, *([pair1] if CFG["add"] else []), *([g_down] if CFG["gd"] == 1 else [])), vec_far, "add_far")
         vec_got = x_swap(vec)
         qk_own, vec_own, *qk_sums = pallas(
             fn(last_x_kernel, m),
@@ -915,7 +999,17 @@
             [qk_keep, qk_got, vec, vec_got],
             name="last_x",
         )
+        if CFG["both"] == 2:
+            g_up, g_value, g_out = both_out(qk_own)
+            qk_sums[0] = gate(qk_sums[0], g_up)
+            qk_sums[1] = gate(qk_sums[1], g_up)
+            qk_sums[2] = gate(qk_sums[2], g_up)
+        if CFG["gd"] == 2:
+            qk_sums[0] = gate(qk_sums[0], g_down)
         qk_z = to_z(qk_sums)
+        if CFG["both"] == 0:
+            g_up, g_value, g_out = both_out(qk_own)
+            keep0 = gate(keep0, g_up)
         keep0 = gate(keep0, qk_own)
     else:
         vec = lax.psum(vec + vec_far, "dp")
@@ -933,19 +1027,10 @@
         name="finish",
     )
     if m.fast:
-        g_value, g_out = pallas(
-            fn(sum_z_kernel, m),
-            [shape(rows, WH, dtype=F32)] * 2,
-            [gate(vo_own, result), *vo_z],
-            name="value_out",
-        )
-        (g_down,) = pallas(
-            fn(give_down_kernel, m),
-            [shape(WH, S * m.hrows, dtype=F32)],
-            [gate(down_halves[0], g_value), down_halves[1]],
-            here=True,
-            name="give_down",
-        )
+        if CFG["both"] == 1:
+            g_up, g_value, g_out = both_out(result)
+        if not CFG["gd"]:
+            g_down = give_down(g_value, result)
         g_down = g_down.T
         g_query, g_key, *vec_outs = pallas(
             fn(last_z_kernel, m),

time: 186 us -> 174 us (0.935); the launches traced: 184 us -> 174 us
  waiting for transfers between devices: 71.2 us -> 49.5 us
  starting transfers between devices: 65.5 us -> 81.8 us
  local copies, waits for them, and re-layouts: 3.61 us -> 0.04 us
    ppermute x20, starting transfers between devices: 17.1 us -> 36.6 us  [seq_to(): return lax.ppermute(x, 'seq', [(i, i ^ e) for i in range(S)])]
    ppermute x17 -> x15, waiting for transfers between devices: 23.6 us -> 6.42 us  [x_swap(): return lax.ppermute(x, 'dp', [(i, i ^ 1) for i in range(N)])]
    ppermute x21 -> x18, waiting for transfers between devices: 27.1 us -> 19.6 us  [z_shift(): return lax.ppermute(x, 'dp', [(i, (i + 2 * k) % N) for i in range(N)])]
    ppermute x21 -> x18, starting transfers between devices: 23.6 us -> 19.5 us  [z_shift(): return lax.ppermute(x, 'dp', [(i, (i + 2 * k) % N) for i in range(N)])]
    unnamed x18 -> x16, local copies, waits for them, and re-layouts: 3.61 us -> 0.04 us
    ppermute x4, waiting for transfers between devices: 4.83 us -> 8.02 us  [exchange(): return lax.ppermute(x, ('dp', 'seq'), pairs)]
    ppermute x17 -> x15, starting transfers between devices: 11.8 us -> 12.7 us  [x_swap(): return lax.ppermute(x, 'dp', [(i, i ^ 1) for i in range(N)])]
    pallas_call x32 -> x31, Pallas kernels: 42.2 us -> 41.3 us  [pallas(): pl.pallas_call(run, out_shape=outs, in_specs=[pl.BlockSpec(memory_space=p...]
  transfers between devices with their start and end apart: 62 -> 57, of which waited for: 25 -> 21; matrix products, arithmetic and copies ran while one was open for 0% -> 0% of each run, Pallas kernels for 18% -> 19%
where the time goes in v3:
time: 174 us
  starting transfers between devices  81.8 us (47%)
  waiting for transfers between devices  49.5 us (28%)
  Pallas kernels  41.3 us (24%)
    pallas_call x31, Pallas kernels, pallas(): pl.pallas_call(run, out_shape=outs, in_specs=[pl.BlockSpec(memory_space=p...  41.3 us
    ppermute x20, starting transfers between devices, seq_to(): return lax.ppermute(x, 'seq', [(i, i ^ e) for i in range(S)])  36.6 us
    ppermute x18, waiting for transfers between devices, z_shift(): return lax.ppermute(x, 'dp', [(i, (i + 2 * k) % N) for i in range(N)])  19.6 us
    ppermute x18, starting transfers between devices, z_shift(): return lax.ppermute(x, 'dp', [(i, (i + 2 * k) % N) for i in range(N)])  19.5 us
    ppermute x20, waiting for transfers between devices, seq_to(): return lax.ppermute(x, 'seq', [(i, i ^ e) for i in range(S)])  15.5 us
    ppermute x4, starting transfers between devices, exchange(): return lax.ppermute(x, ('dp', 'seq'), pairs)  13 us
    ppermute x15, starting transfers between devices, x_swap(): return lax.ppermute(x, 'dp', [(i, i ^ 1) for i in range(N)])  12.7 us
    ppermute x4, waiting for transfers between devices, exchange(): return lax.ppermute(x, ('dp', 'seq'), pairs)  8.02 us
  transfers between devices with their start and end apart: 57, of which 21 were waited for; matrix products, arithmetic and copies ran while one was open for 0% of the time, Pallas kernels for 19%

profile of v3, /device:TPU:5, one launch (start us, length us, event | category | flops | bytes accessed | tf_op | source)
XLA Modules:
  0.0 173.8 jit_solution(811350701564280576)
XLA Ops:
  0.7 1.9 %pack.1.refs_3_ = bf16[96,640]{1,0:T(8,128)(2,1)} custom-call(bf16[96,192]{1,0:T(8,128)(2,1)} %refs_0_.2, bf16[96,192]{1,0:T(8,128)(2,1)} %refs_1_.3, bf16[96,192]{1,0:T(8,128)(2,1)} %refs_2_.1, bf16[96]{0:T(256)(128)(2,1)} %refs_3_.2, bf16[96]{0:T(256)(128)(2,1)} %refs_4_.1, bf16[96]{0:T(256)(128)(2,1)} %refs_5_.1, bf16[96]{0:T(256)(128)(2,1)} %refs_6_.1, ...), custom_call_target="tpu_custom_call" | custom-call | flops 3000000000 | bytes 235776 | tf_op jit(solution)/shard_map/pack/pallas_call | solution.py:58
  2.6 1.3 collective-permute-start.1
  4.1 1.2 collective-permute-start.5
  5.4 2.1 %collective-permute-start.3 = (bf16[96,640]{1,0:T(8,128)(2,1)}, bf16[96,640]{1,0:T(8,128)(2,1)S(1)}, u32[]{:S(2)}, u32[]{:S(2)}) collective-permute-start(bf16[96,640]{1,0:T(8,128)(2,1)} %pack.1.refs_3_), channel_id=1, source_target_pairs={{0,24},{4,28},{8,0},{12,4},{16,8},{20,12},{24,16},{28,20},{1,25},{... | collective-permute-start | bytes 368648 | tf_op jit(solution)/shard_map/ppermute | solution.py:666
  7.5 1.2 collective-permute-start.7
  8.7 0.8 collective-permute-start.2
  9.5 1.0 collective-permute-start.11
  10.5 1.8 %collective-permute-done.3.refs_6_ = bf16[96,640]{1,0:T(8,128)(2,1)S(1)} collective-permute-done((bf16[96,640]{1,0:T(8,128)(2,1)}, bf16[96,640]{1,0:T(8,128)(2,1)S(1)}, u32[]{:S(2)}, u32[]{:S(2)}) %collective-permute-start.3) | collective-permute-done | bytes 122912 | tf_op jit(solution)/shard_map/ppermute | solution.py:666
  12.4 6.1 %collective-permute-start.25 = (bf16[96,384]{1,0:T(8,128)(2,1)S(1)}, bf16[96,384]{1,0:T(8,128)(2,1)S(1)}, u32[]{:S(2)}, u32[]{:S(2)}) collective-permute-start(bf16[96,384]{1,0:T(8,128)(2,1)S(1)} %get-tuple-element.140), channel_id=1, source_target_pairs={{0,0},{1,8},{2,16},{3,24},{4,4},{5,12},{6,20},{7,28},{8,1},{9,9},{... | collective-permute-start | bytes 221192 | tf_op jit(solution)/shard_map/ppermute | solution.py:700
  18.5 1.6 collective-permute-start.10
  20.0 1.9 %collective-permute-done.2.refs_5_ = bf16[96,640]{1,0:T(8,128)(2,1)S(1)} collective-permute-done((bf16[96,640]{1,0:T(8,128)(2,1)}, bf16[96,640]{1,0:T(8,128)(2,1)S(1)}, u32[]{:S(2)}, u32[]{:S(2)}) %collective-permute-start.2) | collective-permute-done | bytes 122912 | tf_op jit(solution)/shard_map/ppermute | solution.py:666
  22.4 4.5 %collective-permute-start.4 = (bf16[3,70,768]{2,1,0:T(8,128)(2,1)S(1)}, bf16[3,70,768]{2,1,0:T(8,128)(2,1)S(1)}, u32[]{:S(2)}, u32[]{:S(2)}) collective-permute-start(bf16[3,70,768]{2,1,0:T(8,128)(2,1)S(1)} %copy-done), channel_id=1, source_target_pairs={{0,1},{1,0},{2,3},{3,2},{4,5},{5,4},{6,7},{7,6},{8,9},{9,8},{10,11... | collective-permute-start | bytes 967688 | tf_op jit(solution)/shard_map/ppermute | solution.py:660
  26.9 2.6 %collective-permute-done.26.refs_1_ = bf16[96,384]{1,0:T(8,128)(2,1)S(1)} collective-permute-done((bf16[96,384]{1,0:T(8,128)(2,1)S(1)}, bf16[96,384]{1,0:T(8,128)(2,1)S(1)}, u32[]{:S(2)}, u32[]{:S(2)}) %collective-permute-start.26) | collective-permute-done | bytes 73760 | tf_op jit(solution)/shard_map/ppermute | solution.py:700
  29.5 0.8 collective-permute-start.9
  30.3 1.5 collective-permute-start.12
  31.8 4.2 %collective-permute-start.6 = (bf16[3,70,768]{2,1,0:T(8,128)(2,1)S(1)}, bf16[3,70,768]{2,1,0:T(8,128)(2,1)S(1)}, u32[]{:S(2)}, u32[]{:S(2)}) collective-permute-start(bf16[3,70,768]{2,1,0:T(8,128)(2,1)S(1)} %collective-permute-done.5.refs_2_), channel_id=1, source_target_pairs={{0,1},{1,0},{2,3},{3,2},{4,5},{5,4},{6,7},{7,6},{8,9},{9,8},{10,11... | collective-permute-start | bytes 967688 | tf_op jit(solution)/shard_map/ppermute | solution.py:660
  36.0 1.6 collective-permute-start.8
  38.2 2.0 %collective-permute-done.8.refs_8_ = bf16[96,640]{1,0:T(8,128)(2,1)S(1)} collective-permute-done((bf16[96,640]{1,0:T(8,128)(2,1)S(1)}, bf16[96,640]{1,0:T(8,128)(2,1)S(1)}, u32[]{:S(2)}, u32[]{:S(2)}) %collective-permute-start.8) | collective-permute-done | bytes 122912 | tf_op jit(solution)/shard_map/ppermute | solution.py:663
  40.2 1.5 collective-permute-start.17
  41.7 1.4 collective-permute-start.16
  43.1 2.9 %collective-permute-start.20 = (bf16[3,70,768]{2,1,0:T(8,128)(2,1)S(1)}, bf16[3,70,768]{2,1,0:T(8,128)(2,1)S(1)}, u32[]{:S(2)}, u32[]{:S(2)}) collective-permute-start(bf16[3,70,768]{2,1,0:T(8,128)(2,1)S(1)} %copy-done.1), channel_id=1, source_target_pairs={{0,2},{1,3},{2,0},{3,1},{4,6},{5,7},{6,4},{7,5},{8,10},{9,11},{10,... | collective-permute-start | bytes 967688 | tf_op jit(solution)/shard_map/ppermute | solution.py:660
  46.1 0.9 norm.1.refs_2_
  47.1 2.1 %collective-permute-start.29 = (bf16[96,768]{1,0:T(8,128)(2,1)S(1)}, bf16[96,768]{1,0:T(8,128)(2,1)S(1)}, u32[]{:S(2)}, u32[]{:S(2)}) collective-permute-start(bf16[96,768]{1,0:T(8,128)(2,1)S(1)} %join_down.1.refs_3_), channel_id=1, source_target_pairs={{0,24},{4,28},{8,0},{12,4},{16,8},{20,12},{24,16},{28,20},{1,25},{... | collective-permute-start | bytes 442376 | tf_op jit(solution)/shard_map/ppermute | solution.py:666
  49.2 7.5 %attend.1 = (bf16[960,576]{1,0:T(8,128)(2,1)S(1)}, bf16[960,768]{1,0:T(8,128)(2,1)S(1)}, bf16[9,320,320]{2,1,0:T(8,128)(2,1)S(1)}, bf16[480,384]{1,0:T(8,128)(2,...) custom-call(s32[3,40]{1,0:T(4,128)S(1)} %copy-done.6, s32[3]{0:T(128)S(1)} %copy-done.7, ...), custom_call_target="tpu_custom_call" | custom-call | flops 1000 | bytes 9757164 | tf_op jit(solution)/shard_map/attend/pallas_call | solution.py:58
  57.0 4.4 %collective-permute-start.19 = (bf16[3,70,768]{2,1,0:T(8,128)(2,1)S(1)}, bf16[3,70,768]{2,1,0:T(8,128)(2,1)S(1)}, u32[]{:S(2)}, u32[]{:S(2)}) collective-permute-start(bf16[3,70,768]{2,1,0:T(8,128)(2,1)S(1)} %copy-done.1), channel_id=1, source_target_pairs={{0,1},{1,0},{2,3},{3,2},{4,5},{5,4},{6,7},{7,6},{8,9},{9,8},{10,11... | collective-permute-start | bytes 967688 | tf_op jit(solution)/shard_map/ppermute | solution.py:660
  61.7 0.9 collective-permute-done.27.refs_0_.refs_4_
  62.6 5.3 %collective-permute-start.21 = (bf16[3,70,768]{2,1,0:T(8,128)(2,1)S(1)}, bf16[3,70,768]{2,1,0:T(8,128)(2,1)S(1)}, u32[]{:S(2)}, u32[]{:S(2)}) collective-permute-start(bf16[3,70,768]{2,1,0:T(8,128)(2,1)S(1)} %collective-permute-done.20.refs_4_), channel_id=1, source_target_pairs={{0,1},{1,0},{2,3},{3,2},{4,5},{5,4},{6,7},{7,6},{8,9},{9,8},{10,11... | collective-permute-start | bytes 967688 | tf_op jit(solution)/shard_map/ppermute | solution.py:660
  68.7 1.2 collective-permute-start.31
  69.9 5.2 %collective-permute-start.22 = (bf16[480,384]{1,0:T(8,128)(2,1)S(1)}, bf16[480,384]{1,0:T(8,128)(2,1)S(1)}, u32[]{:S(2)}, u32[]{:S(2)}) collective-permute-start(bf16[480,384]{1,0:T(8,128)(2,1)S(1)} %get-tuple-element.131.refs_4_), channel_id=1, source_target_pairs={{0,1},{1,0},{2,3},{3,2},{4,5},{5,4},{6,7},{7,6},{8,9},{9,8},{10,11... | collective-permute-start | bytes 1105928 | tf_op jit(solution)/shard_map/ppermute | solution.py:660
  75.2 1.6 collective-permute-start.30
  77.4 5.5 %forward.1 = (bf16[960,768]{1,0:T(8,128)(2,1)S(1)}, bf16[960,768]{1,0:T(8,128)(2,1)S(1)}, f32[960,768]{1,0:T(8,128)S(1)}, bf16[960,768]{1,0:T(8,128)(2,1)S(1)}, ...) custom-call(bf16[3,70,768]{2,1,0:T(8,128)(2,1)S(1)} %copy-done, ...), custom_call_target="tpu_custom_call" | custom-call | flops 1000 | bytes 14143488 | tf_op jit(solution)/shard_map/forward/pallas_call | solution.py:58
  82.9 1.5 down_grad.1
  84.5 3.3 %hidden_back.1 = (bf16[960,768]{1,0:T(8,128)(2,1)S(1)}, bf16[768,768]{1,0:T(8,128)(2,1)S(1)}, bf16[240,768]{1,0:T(8,128)(2,1)S(1)}, bf16[240,768]{1,0:T(8,128)(2,1)S(1)}, bf16[2,240,768]{2,1,0:T(8,128)(2,1)S(1)}) custom-call(bf16[960,768]{1,0:T(8,128)(2,1)S(1)} %get-tuple-element.130.refs_0_.refs_5_.refs_3_, f32[960,768]{1,0:T(8,128)S(1)} %get-tuple-element.138.refs_1_, ...), custom_call_target="tpu_custom_call" | custom-call | flops 3000000000 | bytes 10911744 | tf_op jit(solution)/shard_map/hidden_back/pallas_call | solution.py:58
  87.8 1.9 %collective-permute-start.32 = (bf16[2,240,768]{2,1,0:T(8,128)(2,1)S(1)}, bf16[2,240,768]{2,1,0:T(8,128)(2,1)S(1)}, u32[]{:S(2)}, u32[]{:S(2)}) collective-permute-start(bf16[2,240,768]{2,1,0:T(8,128)(2,1)S(1)} %get-tuple-element.146), channel_id=1, source_target_pairs={{0,1},{1,0},{2,3},{3,2},{4,5},{5,4},{6,7},{7,6},{8,9},{9,8},{10,11... | collective-permute-start | bytes 2211848 | tf_op jit(solution)/shard_map/ppermute | solution.py:660
  89.8 1.8 %collective-permute-done.32.refs_1_ = bf16[2,240,768]{2,1,0:T(8,128)(2,1)S(1)} collective-permute-done((bf16[2,240,768]{2,1,0:T(8,128)(2,1)S(1)}, bf16[2,240,768]{2,1,0:T(8,128)(2,1)S(1)}, u32[]{:S(2)}, u32[]{:S(2)}) %collective-permute-start.32) | collective-permute-done | bytes 737312 | tf_op jit(solution)/shard_map/ppermute | solution.py:660
  91.8 1.5 up_grad.1
  94.0 7.5 %collective-permute-done.33.refs_2_ = bf16[240,768]{1,0:T(8,128)(2,1)S(1)} collective-permute-done((bf16[240,768]{1,0:T(8,128)(2,1)S(1)}, bf16[240,768]{1,0:T(8,128)(2,1)S(1)}, u32[]{:S(2)}, u32[]{:S(2)}) %collective-permute-start.33) | collective-permute-done | bytes 368672 | tf_op jit(solution)/shard_map/ppermute | solution.py:660
  101.6 1.1 middle.1
  102.6 1.3 collective-permute-start.35
  103.9 1.7 collective-permute-start.37
  105.6 1.9 %branch.1 = (bf16[240,768]{1,0:T(8,128)(2,1)S(1)}, bf16[240,768]{1,0:T(8,128)(2,1)S(1)}, bf16[2,240,768]{2,1,0:T(8,128)(2,1)S(1)}, f32[8,768]{1,0:T(8,128)S(1)}) custom-call(bf16[960,768]{1,0:T(8,128)(2,1)S(1)} %get-tuple-element.154.refs_1_.refs_0_, bf16[768,768]{1,0:T(8,128)(2,1)S(1)} %get-tuple-element.155.refs_1_, ...), custom_call_target="tpu_custom_call" | custom-call | flops 10000000000 | bytes 7102464 | tf_op jit(solution)/shard_map/branch/pallas_call | solution.py:58
  107.7 1.2 collective-permute-start.41
  108.9 1.2 collective-permute-done.36.refs_3_
  110.1 1.0 collective-permute-start.42
  111.1 3.4 %collective-permute-done.37.refs_4_ = bf16[240,384]{1,0:T(8,128)(2,1)S(1)} collective-permute-done((bf16[240,384]{1,0:T(8,128)(2,1)S(1)}, bf16[240,384]{1,0:T(8,128)(2,1)S(1)}, u32[]{:S(2)}, u32[]{:S(2)}) %collective-permute-start.37) | collective-permute-done | bytes 184352 | tf_op jit(solution)/shard_map/ppermute | solution.py:660
  114.5 2.7 %value_back.1 = (bf16[960,192]{1,0:T(8,128)(2,1)S(1)}, bf16[960,192]{1,0:T(8,128)(2,1)S(1)}, bf16[4,96,384]{2,1,0:T(8,128)(2,1)S(1)}, bf16[4,96,384]{2,1,0:T(8,128)(2,1)S(1)}) custom-call(bf16[9,320,320]{2,1,0:T(8,128)(2,1)S(1)} %get-tuple-element.127.refs_0_.refs_1_, bf16[240,384]{1,0:T(8,128)(2,1)S(1)} %get-tuple-element.161.refs_1_, ...), custom_call_target="tpu_custom_call" | custom-call | flops 10000000000 | bytes 6856704 | tf_op jit(solution)/shard_map/value_back/pallas_call | solution.py:58
  117.3 4.5 %attend_back.1.refs_0_.refs_1_ = bf16[960,384]{1,0:T(8,128)(2,1)S(1)} custom-call(bf16[960,576]{1,0:T(8,128)(2,1)S(1)} %get-tuple-element.126.refs_0_, bf16[9,320,320]{2,1,0:T(8,128)(2,1)S(1)} %get-tuple-element.127.refs_0_.refs_1_, bf16[960,192]{1,0:T(8,128)(2,1)S(1)} %get-tuple-element.167.refs_2_), custom_call_target="tpu_custom_call" | custom-call | flops 10000000000 | bytes 4055040 | tf_op jit(solution)/shard_map/attend_back/pallas_call | solution.py:58
  121.8 4.2 %collective-permute-done.39.refs_3_ = bf16[4,96,384]{2,1,0:T(8,128)(2,1)S(1)} collective-permute-done((bf16[4,96,384]{2,1,0:T(8,128)(2,1)S(1)}, bf16[4,96,384]{2,1,0:T(8,128)(2,1)S(1)}, u32[]{:S(2)}, u32[]{:S(2)}) %collective-permute-start.39) | collective-permute-done | bytes 294944 | tf_op jit(solution)/shard_map/ppermute | solution.py:663
  126.6 2.1 %input_back.1 = (bf16[240,768]{1,0:T(8,128)(2,1)S(1)}, bf16[480,768]{1,0:T(8,128)(2,1)S(1)}, bf16[2,480,768]{2,1,0:T(8,128)(2,1)S(1)}, f32[16,768]{1,0:T(8,128)S(1)}) custom-call(bf16[960,384]{1,0:T(8,128)(2,1)S(1)} %attend_back.1.refs_0_.refs_1_, bf16[960,192]{1,0:T(8,128)(2,1)S(1)} %get-tuple-element.179.refs_1_, f32[960,768]{1,0:T(8,128)S(1)} %norm.1.refs_2_, ...), custom_call_target="tpu_custom_call" | custom-call | flops 1000 | bytes 8822784 | tf_op jit(solution)/shard_map/input_back/pallas_call | solution.py:58
  128.7 0.8 collective-permute-start.46
  129.5 1.1 qk_grad.1
  131.0 1.5 collective-permute-done.44.refs_1_
  132.6 4.5 %collective-permute-start.52 = (bf16[96,384]{1,0:T(8,128)(2,1)S(1)}, bf16[96,384]{1,0:T(8,128)(2,1)S(1)}, u32[]{:S(2)}, u32[]{:S(2)}) collective-permute-start(bf16[96,384]{1,0:T(8,128)(2,1)S(1)} %get-tuple-element.177), channel_id=1, source_target_pairs={{0,0},{1,8},{2,16},{3,24},{4,4},{5,12},{6,20},{7,28},{8,1},{9,9},{... | collective-permute-start | bytes 221192 | tf_op jit(solution)/shard_map/ppermute | solution.py:700
  137.1 2.4 %collective-permute-start.53 = (bf16[96,384]{1,0:T(8,128)(2,1)S(1)}, bf16[96,384]{1,0:T(8,128)(2,1)S(1)}, u32[]{:S(2)}, u32[]{:S(2)}) collective-permute-start(bf16[96,384]{1,0:T(8,128)(2,1)S(1)} %get-tuple-element.207), channel_id=1, source_target_pairs={{0,4},{1,12},{2,20},{3,28},{4,0},{5,8},{6,16},{7,24},{8,5},{9,13},... | collective-permute-start | bytes 221192 | tf_op jit(solution)/shard_map/ppermute | solution.py:700
  141.2 4.3 %collective-permute-done.53.refs_1_ = bf16[96,384]{1,0:T(8,128)(2,1)S(1)} collective-permute-done((bf16[96,384]{1,0:T(8,128)(2,1)S(1)}, bf16[96,384]{1,0:T(8,128)(2,1)S(1)}, u32[]{:S(2)}, u32[]{:S(2)}) %collective-permute-start.53) | collective-permute-done | bytes 73760 | tf_op jit(solution)/shard_map/ppermute | solution.py:700
  145.5 0.7 give_down.1
  146.2 2.1 %collective-permute-start.51 = (bf16[480,768]{1,0:T(8,128)(2,1)S(1)}, bf16[480,768]{1,0:T(8,128)(2,1)S(1)}, u32[]{:S(2)}, u32[]{:S(2)}) collective-permute-start(bf16[480,768]{1,0:T(8,128)(2,1)S(1)} %pair1.1), channel_id=1, source_target_pairs={{0,2},{1,3},{2,0},{3,1},{4,6},{5,7},{6,4},{7,5},{8,10},{9,11},{10,... | collective-permute-start | bytes 2211848 | tf_op jit(solution)/shard_map/ppermute | solution.py:660
  149.1 0.8 collective-permute-start.56
  149.9 9.0 %collective-permute-done.49.refs_3_ = bf16[144,768]{1,0:T(8,128)(2,1)S(1)} collective-permute-done((bf16[144,768]{1,0:T(8,128)(2,1)S(1)}, bf16[144,768]{1,0:T(8,128)(2,1)S(1)}, u32[]{:S(2)}, u32[]{:S(2)}) %collective-permute-start.49) | collective-permute-done | bytes 221216 | tf_op jit(solution)/shard_map/ppermute | solution.py:666
  158.9 7.6 %collective-permute-start.54 = (bf16[128,384]{1,0:T(8,128)(2,1)S(1)}, bf16[128,384]{1,0:T(8,128)(2,1)S(1)}, u32[]{:S(2)}, u32[]{:S(2)}) collective-permute-start(bf16[128,384]{1,0:T(8,128)(2,1)S(1)} %get-tuple-element.211), channel_id=1, source_target_pairs={{0,8},{4,12},{8,16},{12,20},{16,24},{20,28},{24,0},{28,4},{1,9},{5... | collective-permute-start | bytes 294920 | tf_op jit(solution)/shard_map/ppermute | solution.py:666
  166.5 0.9 both_out.1
  167.7 3.7 %collective-permute-done.54.refs_2_ = bf16[128,384]{1,0:T(8,128)(2,1)S(1)} collective-permute-done((bf16[128,384]{1,0:T(8,128)(2,1)S(1)}, bf16[128,384]{1,0:T(8,128)(2,1)S(1)}, u32[]{:S(2)}, u32[]{:S(2)}) %collective-permute-start.54) | collective-permute-done | bytes 98336 | tf_op jit(solution)/shard_map/ppermute | solution.py:666
  171.4 0.8 query_key.1
  172.3 1.5 finish.1
  (97 shorter events, 8.5 us)
Async XLA Ops:
  0.7 3.2 %copy-start.5 = (bf16[96,192]{1,0:T(8,128)(2,1)S(1)}, bf16[96,192]{1,0:T(8,128)(2,1)}, u32[]{:S(2)}) copy-start(bf16[96,192]{1,0:T(8,128)(2,1)} %refs_1_.4) | copy-start | bytes 110596
  0.7 3.4 %copy-start = (bf16[3,70,768]{2,1,0:T(8,128)(2,1)S(1)}, bf16[3,70,768]{2,1,0:T(8,128)(2,1)}, u32[]{:S(2)}) copy-start(bf16[3,70,768]{2,1,0:T(8,128)(2,1)} %refs_3_.3) | copy-start | bytes 967684
  0.7 8.8 %copy-start.2 = (bf16[96,768]{1,0:T(8,128)(2,1)S(1)}, bf16[96,768]{1,0:T(8,128)(2,1)}, u32[]{:S(2)}) copy-start(bf16[96,768]{1,0:T(8,128)(2,1)} %refs_0_.3) | copy-start | bytes 442372
  0.7 9.8 %copy-start.3 = (bf16[384,192]{0,1:T(8,128)(2,1)S(1)}, bf16[384,192]{0,1:T(8,128)(2,1)}, u32[]{:S(2)}) copy-start(bf16[384,192]{0,1:T(8,128)(2,1)} %param.28) | copy-start | bytes 442372
  0.7 42.4 %copy-start.1 = (bf16[3,70,768]{2,1,0:T(8,128)(2,1)S(1)}, bf16[3,70,768]{2,1,0:T(8,128)(2,1)}, u32[]{:S(2)}) copy-start(bf16[3,70,768]{2,1,0:T(8,128)(2,1)} %refs_2_.2) | copy-start | bytes 967684
  2.6 6.9 %collective-permute-start.1 = (bf16[96,640]{1,0:T(8,128)(2,1)}, bf16[96,640]{1,0:T(8,128)(2,1)S(1)}, u32[]{:S(2)}, u32[]{:S(2)}) collective-permute-start(bf16[96,640]{1,0:T(8,128)(2,1)} %pack.1.refs_3_), channel_id=1, source_target_pairs={{0,8},{4,12},{8,16},{12,20},{16,24},{20,28},{24,0},{28,4},{1,9},{5... | collective-permute-start | bytes 368648 | tf_op jit(solution)/shard_map/ppermute | solution.py:666
  3.9 4.8 %collective-permute-start = (bf16[96,192]{1,0:T(8,128)(2,1)S(1)}, bf16[96,192]{1,0:T(8,128)(2,1)S(1)}, u32[]{:S(2)}, u32[]{:S(2)}) collective-permute-start(bf16[96,192]{1,0:T(8,128)(2,1)S(1)} %copy-done.5), channel_id=1, source_target_pairs={{0,2},{1,3},{2,0},{3,1},{4,6},{5,7},{6,4},{7,5},{8,10},{9,11},{10,... | collective-permute-start | bytes 110600 | tf_op jit(solution)/shard_map/ppermute | solution.py:660
  4.1 27.7 %collective-permute-start.5 = (bf16[3,70,768]{2,1,0:T(8,128)(2,1)S(1)}, bf16[3,70,768]{2,1,0:T(8,128)(2,1)S(1)}, u32[]{:S(2)}, u32[]{:S(2)}) collective-permute-start(bf16[3,70,768]{2,1,0:T(8,128)(2,1)S(1)} %copy-done), channel_id=1, source_target_pairs={{0,2},{1,3},{2,0},{3,1},{4,6},{5,7},{6,4},{7,5},{8,10},{9,11},{10,... | collective-permute-start | bytes 967688 | tf_op jit(solution)/shard_map/ppermute | solution.py:660
  5.4 7.0 %collective-permute-start.3 = (bf16[96,640]{1,0:T(8,128)(2,1)}, bf16[96,640]{1,0:T(8,128)(2,1)S(1)}, u32[]{:S(2)}, u32[]{:S(2)}) collective-permute-start(bf16[96,640]{1,0:T(8,128)(2,1)} %pack.1.refs_3_), channel_id=1, source_target_pairs={{0,24},{4,28},{8,0},{12,4},{16,8},{20,12},{24,16},{28,20},{1,25},{... | collective-permute-start | bytes 368648 | tf_op jit(solution)/shard_map/ppermute | solution.py:666
  7.5 11.0 %collective-permute-start.7 = (bf16[96,640]{1,0:T(8,128)(2,1)}, bf16[96,640]{1,0:T(8,128)(2,1)S(1)}, u32[]{:S(2)}, u32[]{:S(2)}) collective-permute-start(bf16[96,640]{1,0:T(8,128)(2,1)} %pack.1.refs_3_), channel_id=1, source_target_pairs={{0,4},{4,0},{8,12},{12,8},{16,20},{20,16},{24,28},{28,24},{1,5},{5... | collective-permute-start | bytes 368648 | tf_op jit(solution)/shard_map/ppermute | solution.py:663
  8.7 13.3 %collective-permute-start.2 = (bf16[96,640]{1,0:T(8,128)(2,1)}, bf16[96,640]{1,0:T(8,128)(2,1)S(1)}, u32[]{:S(2)}, u32[]{:S(2)}) collective-permute-start(bf16[96,640]{1,0:T(8,128)(2,1)} %pack.1.refs_3_), channel_id=1, source_target_pairs={{0,16},{4,20},{8,24},{12,28},{16,0},{20,4},{24,8},{28,12},{1,17},{... | collective-permute-start | bytes 368648 | tf_op jit(solution)/shard_map/ppermute | solution.py:666
  9.5 20.8 %collective-permute-start.11 = (bf16[144,768]{1,0:T(8,128)(2,1)S(1)}, bf16[144,768]{1,0:T(8,128)(2,1)S(1)}, u32[]{:S(2)}, u32[]{:S(2)}) collective-permute-start(bf16[144,768]{1,0:T(8,128)(2,1)S(1)} %pack_up.1.refs_0_), channel_id=1, source_target_pairs={{0,8},{4,12},{8,16},{12,20},{16,24},{20,28},{24,0},{28,4},{1,9},{5... | collective-permute-start | bytes 663560 | tf_op jit(solution)/shard_map/ppermute | solution.py:666
  12.4 10.1 %collective-permute-start.25 = (bf16[96,384]{1,0:T(8,128)(2,1)S(1)}, bf16[96,384]{1,0:T(8,128)(2,1)S(1)}, u32[]{:S(2)}, u32[]{:S(2)}) collective-permute-start(bf16[96,384]{1,0:T(8,128)(2,1)S(1)} %get-tuple-element.140), channel_id=1, source_target_pairs={{0,0},{1,8},{2,16},{3,24},{4,4},{5,12},{6,20},{7,28},{8,1},{9,9},{... | collective-permute-start | bytes 221192 | tf_op jit(solution)/shard_map/ppermute | solution.py:700
  18.5 11.9 %collective-permute-start.10 = (bf16[96,640]{1,0:T(8,128)(2,1)S(1)}, bf16[96,640]{1,0:T(8,128)(2,1)S(1)}, u32[]{:S(2)}, u32[]{:S(2)}) collective-permute-start(bf16[96,640]{1,0:T(8,128)(2,1)S(1)} %collective-permute-done.3.refs_6_), channel_id=1, source_target_pairs={{0,4},{4,0},{8,12},{12,8},{16,20},{20,16},{24,28},{28,24},{1,5},{5... | collective-permute-start | bytes 368648 | tf_op jit(solution)/shard_map/ppermute | solution.py:663
  21.9 7.6 %collective-permute-start.26 = (bf16[96,384]{1,0:T(8,128)(2,1)S(1)}, bf16[96,384]{1,0:T(8,128)(2,1)S(1)}, u32[]{:S(2)}, u32[]{:S(2)}) collective-permute-start(bf16[96,384]{1,0:T(8,128)(2,1)S(1)} %get-tuple-element.141), channel_id=1, source_target_pairs={{0,4},{1,12},{2,20},{3,28},{4,0},{5,8},{6,16},{7,24},{8,5},{9,13},... | collective-permute-start | bytes 221192 | tf_op jit(solution)/shard_map/ppermute | solution.py:700
  22.4 19.3 %collective-permute-start.4 = (bf16[3,70,768]{2,1,0:T(8,128)(2,1)S(1)}, bf16[3,70,768]{2,1,0:T(8,128)(2,1)S(1)}, u32[]{:S(2)}, u32[]{:S(2)}) collective-permute-start(bf16[3,70,768]{2,1,0:T(8,128)(2,1)S(1)} %copy-done), channel_id=1, source_target_pairs={{0,1},{1,0},{2,3},{3,2},{4,5},{5,4},{6,7},{7,6},{8,9},{9,8},{10,11... | collective-permute-start | bytes 967688 | tf_op jit(solution)/shard_map/ppermute | solution.py:660
  29.5 6.5 %collective-permute-start.9 = (bf16[96,640]{1,0:T(8,128)(2,1)S(1)}, bf16[96,640]{1,0:T(8,128)(2,1)S(1)}, u32[]{:S(2)}, u32[]{:S(2)}) collective-permute-start(bf16[96,640]{1,0:T(8,128)(2,1)S(1)} %collective-permute-done.2.refs_5_), channel_id=1, source_target_pairs={{0,4},{4,0},{8,12},{12,8},{16,20},{20,16},{24,28},{28,24},{1,5},{5... | collective-permute-start | bytes 368648 | tf_op jit(solution)/shard_map/ppermute | solution.py:663
  30.3 7.7 %collective-permute-start.13 = (bf16[144,768]{1,0:T(8,128)(2,1)S(1)}, bf16[144,768]{1,0:T(8,128)(2,1)S(1)}, u32[]{:S(2)}, u32[]{:S(2)}) collective-permute-start(bf16[144,768]{1,0:T(8,128)(2,1)S(1)} %pack_up.1.refs_0_), channel_id=1, source_target_pairs={{0,24},{4,28},{8,0},{12,4},{16,8},{20,12},{24,16},{28,20},{1,25},{... | collective-permute-start | bytes 663560 | tf_op jit(solution)/shard_map/ppermute | solution.py:666
  30.3 11.3 %collective-permute-start.12 = (bf16[144,768]{1,0:T(8,128)(2,1)S(1)}, bf16[144,768]{1,0:T(8,128)(2,1)S(1)}, u32[]{:S(2)}, u32[]{:S(2)}) collective-permute-start(bf16[144,768]{1,0:T(8,128)(2,1)S(1)} %collective-permute-done.11.refs_1_), channel_id=1, source_target_pairs={{0,8},{4,12},{8,16},{12,20},{16,24},{20,28},{24,0},{28,4},{1,9},{5... | collective-permute-start | bytes 663560 | tf_op jit(solution)/shard_map/ppermute | solution.py:666
  31.8 11.3 %collective-permute-start.6 = (bf16[3,70,768]{2,1,0:T(8,128)(2,1)S(1)}, bf16[3,70,768]{2,1,0:T(8,128)(2,1)S(1)}, u32[]{:S(2)}, u32[]{:S(2)}) collective-permute-start(bf16[3,70,768]{2,1,0:T(8,128)(2,1)S(1)} %collective-permute-done.5.refs_2_), channel_id=1, source_target_pairs={{0,1},{1,0},{2,3},{3,2},{4,5},{5,4},{6,7},{7,6},{8,9},{9,8},{10,11... | collective-permute-start | bytes 967688 | tf_op jit(solution)/shard_map/ppermute | solution.py:660
  36.0 4.2 %collective-permute-start.8 = (bf16[96,640]{1,0:T(8,128)(2,1)S(1)}, bf16[96,640]{1,0:T(8,128)(2,1)S(1)}, u32[]{:S(2)}, u32[]{:S(2)}) collective-permute-start(bf16[96,640]{1,0:T(8,128)(2,1)S(1)} %collective-permute-done.1.refs_4_), channel_id=1, source_target_pairs={{0,4},{4,0},{8,12},{12,8},{16,20},{20,16},{24,28},{28,24},{1,5},{5... | collective-permute-start | bytes 368648 | tf_op jit(solution)/shard_map/ppermute | solution.py:663
  38.1 9.0 %collective-permute-start.14 = (bf16[144,768]{1,0:T(8,128)(2,1)S(1)}, bf16[144,768]{1,0:T(8,128)(2,1)S(1)}, u32[]{:S(2)}, u32[]{:S(2)}) collective-permute-start(bf16[144,768]{1,0:T(8,128)(2,1)S(1)} %pack_up.1.refs_0_), channel_id=1, source_target_pairs={{0,4},{4,0},{8,12},{12,8},{16,20},{20,16},{24,28},{28,24},{1,5},{5... | collective-permute-start | bytes 663560 | tf_op jit(solution)/shard_map/ppermute | solution.py:663
  40.2 16.5 %collective-permute-start.17 = (bf16[144,768]{1,0:T(8,128)(2,1)S(1)}, bf16[144,768]{1,0:T(8,128)(2,1)S(1)}, u32[]{:S(2)}, u32[]{:S(2)}) collective-permute-start(bf16[144,768]{1,0:T(8,128)(2,1)S(1)} %collective-permute-done.13.refs_3_), channel_id=1, source_target_pairs={{0,4},{4,0},{8,12},{12,8},{16,20},{20,16},{24,28},{28,24},{1,5},{5... | collective-permute-start | bytes 663560 | tf_op jit(solution)/shard_map/ppermute | solution.py:663
  41.7 15.1 %collective-permute-start.15 = (bf16[144,768]{1,0:T(8,128)(2,1)S(1)}, bf16[144,768]{1,0:T(8,128)(2,1)S(1)}, u32[]{:S(2)}, u32[]{:S(2)}) collective-permute-start(bf16[144,768]{1,0:T(8,128)(2,1)S(1)} %collective-permute-done.11.refs_1_), channel_id=1, source_target_pairs={{0,4},{4,0},{8,12},{12,8},{16,20},{20,16},{24,28},{28,24},{1,5},{5... | collective-permute-start | bytes 663560 | tf_op jit(solution)/shard_map/ppermute | solution.py:663
  41.7 15.3 %collective-permute-start.16 = (bf16[144,768]{1,0:T(8,128)(2,1)S(1)}, bf16[144,768]{1,0:T(8,128)(2,1)S(1)}, u32[]{:S(2)}, u32[]{:S(2)}) collective-permute-start(bf16[144,768]{1,0:T(8,128)(2,1)S(1)} %collective-permute-done.12.refs_2_), channel_id=1, source_target_pairs={{0,4},{4,0},{8,12},{12,8},{16,20},{20,16},{24,28},{28,24},{1,5},{5... | collective-permute-start | bytes 663560 | tf_op jit(solution)/shard_map/ppermute | solution.py:663
  43.1 19.5 %collective-permute-start.20 = (bf16[3,70,768]{2,1,0:T(8,128)(2,1)S(1)}, bf16[3,70,768]{2,1,0:T(8,128)(2,1)S(1)}, u32[]{:S(2)}, u32[]{:S(2)}) collective-permute-start(bf16[3,70,768]{2,1,0:T(8,128)(2,1)S(1)} %copy-done.1), channel_id=1, source_target_pairs={{0,2},{1,3},{2,0},{3,1},{4,6},{5,7},{6,4},{7,5},{8,10},{9,11},{10,... | collective-permute-start | bytes 967688 | tf_op jit(solution)/shard_map/ppermute | solution.py:660
  46.1 3.1 %copy-start.4 = (bf16[96,640]{1,0:T(8,128)(2,1)S(1)}, bf16[96,640]{1,0:T(8,128)(2,1)}, u32[]{:S(2)}) copy-start(bf16[96,640]{1,0:T(8,128)(2,1)} %pack.1.refs_3_) | copy-start | bytes 368644
  46.1 3.1 %copy-start.6 = (s32[3,40]{1,0:T(4,128)S(1)}, s32[3,40]{1,0:T(4,128)}, u32[]{:S(2)}) copy-start(s32[3,40]{1,0:T(4,128)} %refs_0_.5) | copy-start | bytes 1444
  47.1 14.5 %collective-permute-start.29 = (bf16[96,768]{1,0:T(8,128)(2,1)S(1)}, bf16[96,768]{1,0:T(8,128)(2,1)S(1)}, u32[]{:S(2)}, u32[]{:S(2)}) collective-permute-start(bf16[96,768]{1,0:T(8,128)(2,1)S(1)} %join_down.1.refs_3_), channel_id=1, source_target_pairs={{0,24},{4,28},{8,0},{12,4},{16,8},{20,12},{24,16},{28,20},{1,25},{... | collective-permute-start | bytes 442376 | tf_op jit(solution)/shard_map/ppermute | solution.py:666
  56.7 18.4 %collective-permute-start.23 = (bf16[480,384]{1,0:T(8,128)(2,1)S(1)}, bf16[480,384]{1,0:T(8,128)(2,1)S(1)}, u32[]{:S(2)}, u32[]{:S(2)}) collective-permute-start(bf16[480,384]{1,0:T(8,128)(2,1)S(1)} %get-tuple-element.131.refs_4_), channel_id=1, source_target_pairs={{0,2},{1,3},{2,0},{3,1},{4,6},{5,7},{6,4},{7,5},{8,10},{9,11},{10,... | collective-permute-start | bytes 1105928 | tf_op jit(solution)/shard_map/ppermute | solution.py:660
  56.8 5.8 %collective-permute-start.27 = (bf16[96,768]{1,0:T(8,128)(2,1)S(1)}, bf16[96,768]{1,0:T(8,128)(2,1)S(1)}, u32[]{:S(2)}, u32[]{:S(2)}) collective-permute-start(bf16[96,768]{1,0:T(8,128)(2,1)S(1)} %join_down.1.refs_3_), channel_id=1, source_target_pairs={{0,8},{4,12},{8,16},{12,20},{16,24},{20,28},{24,0},{28,4},{1,9},{5... | collective-permute-start | bytes 442376 | tf_op jit(solution)/shard_map/ppermute | solution.py:666
  57.0 12.9 %collective-permute-start.19 = (bf16[3,70,768]{2,1,0:T(8,128)(2,1)S(1)}, bf16[3,70,768]{2,1,0:T(8,128)(2,1)S(1)}, u32[]{:S(2)}, u32[]{:S(2)}) collective-permute-start(bf16[3,70,768]{2,1,0:T(8,128)(2,1)S(1)} %copy-done.1), channel_id=1, source_target_pairs={{0,1},{1,0},{2,3},{3,2},{4,5},{5,4},{6,7},{7,6},{8,9},{9,8},{10,11... | collective-permute-start | bytes 967688 | tf_op jit(solution)/shard_map/ppermute | solution.py:660
  61.6 15.2 %collective-permute-start.18 = (bf16[768,384]{1,0:T(8,128)(2,1)S(1)}, bf16[768,384]{1,0:T(8,128)(2,1)S(1)}, u32[]{:S(2)}, u32[]{:S(2)}) collective-permute-start(bf16[768,384]{1,0:T(8,128)(2,1)S(1)} %get-tuple-element.128.refs_0_), channel_id=1, source_target_pairs={{0,1},{1,0},{2,3},{3,2},{4,5},{5,4},{6,7},{7,6},{8,9},{9,8},{10,11... | collective-permute-start | bytes 1769480 | tf_op jit(solution)/shard_map/ppermute | solution.py:660
  62.6 6.0 %collective-permute-start.28 = (bf16[96,768]{1,0:T(8,128)(2,1)S(1)}, bf16[96,768]{1,0:T(8,128)(2,1)S(1)}, u32[]{:S(2)}, u32[]{:S(2)}) collective-permute-start(bf16[96,768]{1,0:T(8,128)(2,1)S(1)} %collective-permute-done.27.refs_0_.refs_4_), channel_id=1, source_target_pairs={{0,8},{4,12},{8,16},{12,20},{16,24},{20,28},{24,0},{28,4},{1,9},{5... | collective-permute-start | bytes 442376 | tf_op jit(solution)/shard_map/ppermute | solution.py:666
  62.6 12.5 %collective-permute-start.21 = (bf16[3,70,768]{2,1,0:T(8,128)(2,1)S(1)}, bf16[3,70,768]{2,1,0:T(8,128)(2,1)S(1)}, u32[]{:S(2)}, u32[]{:S(2)}) collective-permute-start(bf16[3,70,768]{2,1,0:T(8,128)(2,1)S(1)} %collective-permute-done.20.refs_4_), channel_id=1, source_target_pairs={{0,1},{1,0},{2,3},{3,2},{4,5},{5,4},{6,7},{7,6},{8,9},{9,8},{10,11... | collective-permute-start | bytes 967688 | tf_op jit(solution)/shard_map/ppermute | solution.py:660
  68.7 15.8 %collective-permute-start.31 = (bf16[3,96,768]{2,1,0:T(8,128)(2,1)S(1)}, bf16[3,96,768]{2,1,0:T(8,128)(2,1)S(1)}, u32[]{:S(2)}, u32[]{:S(2)}) collective-permute-start(bf16[3,96,768]{2,1,0:T(8,128)(2,1)S(1)} %stack_down.1), channel_id=1, source_target_pairs={{0,4},{4,0},{8,12},{12,8},{16,20},{20,16},{24,28},{28,24},{1,5},{5... | collective-permute-start | bytes 1327112 | tf_op jit(solution)/shard_map/ppermute | solution.py:663
  69.9 7.5 %collective-permute-start.22 = (bf16[480,384]{1,0:T(8,128)(2,1)S(1)}, bf16[480,384]{1,0:T(8,128)(2,1)S(1)}, u32[]{:S(2)}, u32[]{:S(2)}) collective-permute-start(bf16[480,384]{1,0:T(8,128)(2,1)S(1)} %get-tuple-element.131.refs_4_), channel_id=1, source_target_pairs={{0,1},{1,0},{2,3},{3,2},{4,5},{5,4},{6,7},{7,6},{8,9},{9,8},{10,11... | collective-permute-start | bytes 1105928 | tf_op jit(solution)/shard_map/ppermute | solution.py:660
  75.1 2.3 %collective-permute-start.24 = (bf16[480,384]{1,0:T(8,128)(2,1)S(1)}, bf16[480,384]{1,0:T(8,128)(2,1)S(1)}, u32[]{:S(2)}, u32[]{:S(2)}) collective-permute-start(bf16[480,384]{1,0:T(8,128)(2,1)S(1)} %collective-permute-done.23.refs_6_), channel_id=1, source_target_pairs={{0,1},{1,0},{2,3},{3,2},{4,5},{5,4},{6,7},{7,6},{8,9},{9,8},{10,11... | collective-permute-start | bytes 1105928 | tf_op jit(solution)/shard_map/ppermute | solution.py:660
  75.2 9.3 %collective-permute-start.30 = (bf16[96,768]{1,0:T(8,128)(2,1)S(1)}, bf16[96,768]{1,0:T(8,128)(2,1)S(1)}, u32[]{:S(2)}, u32[]{:S(2)}) collective-permute-start(bf16[96,768]{1,0:T(8,128)(2,1)S(1)} %join_down.1.refs_3_), channel_id=1, source_target_pairs={{0,4},{4,0},{8,12},{12,8},{16,20},{20,16},{24,28},{28,24},{1,5},{5... | collective-permute-start | bytes 442376 | tf_op jit(solution)/shard_map/ppermute | solution.py:663
  87.8 3.8 %collective-permute-start.32 = (bf16[2,240,768]{2,1,0:T(8,128)(2,1)S(1)}, bf16[2,240,768]{2,1,0:T(8,128)(2,1)S(1)}, u32[]{:S(2)}, u32[]{:S(2)}) collective-permute-start(bf16[2,240,768]{2,1,0:T(8,128)(2,1)S(1)} %get-tuple-element.146), channel_id=1, source_target_pairs={{0,1},{1,0},{2,3},{3,2},{4,5},{5,4},{6,7},{7,6},{8,9},{9,8},{10,11... | collective-permute-start | bytes 2211848 | tf_op jit(solution)/shard_map/ppermute | solution.py:660
  89.8 17.7 %collective-permute-start.34 = (bf16[4,96,768]{2,1,0:T(8,128)(2,1)S(1)}, bf16[4,96,768]{2,1,0:T(8,128)(2,1)S(1)}, u32[]{:S(2)}, u32[]{:S(2)}) collective-permute-start(bf16[4,96,768]{2,1,0:T(8,128)(2,1)S(1)} %get-tuple-element.159), channel_id=1, source_target_pairs={{0,4},{4,0},{8,12},{12,8},{16,20},{20,16},{24,28},{28,24},{1,5},{5... | collective-permute-start | bytes 1769480 | tf_op jit(solution)/shard_map/ppermute | solution.py:663
  91.7 9.9 %collective-permute-start.33 = (bf16[240,768]{1,0:T(8,128)(2,1)S(1)}, bf16[240,768]{1,0:T(8,128)(2,1)S(1)}, u32[]{:S(2)}, u32[]{:S(2)}) collective-permute-start(bf16[240,768]{1,0:T(8,128)(2,1)S(1)} %pair2.1), channel_id=1, source_target_pairs={{0,2},{1,3},{2,0},{3,1},{4,6},{5,7},{6,4},{7,5},{8,10},{9,11},{10,... | collective-permute-start | bytes 1105928 | tf_op jit(solution)/shard_map/ppermute | solution.py:660
  93.3 28.5 %collective-permute-start.38 = (bf16[4,96,768]{2,1,0:T(8,128)(2,1)S(1)}, bf16[4,96,768]{2,1,0:T(8,128)(2,1)S(1)}, u32[]{:S(2)}, u32[]{:S(2)}) collective-permute-start(bf16[4,96,768]{2,1,0:T(8,128)(2,1)S(1)} %get-tuple-element.169), channel_id=1, source_target_pairs={{0,4},{4,0},{8,12},{12,8},{16,20},{20,16},{24,28},{28,24},{1,5},{5... | collective-permute-start | bytes 1769480 | tf_op jit(solution)/shard_map/ppermute | solution.py:663
  102.6 5.1 %collective-permute-start.35 = (bf16[240,384]{1,0:T(8,128)(2,1)S(1)}, bf16[240,384]{1,0:T(8,128)(2,1)S(1)}, u32[]{:S(2)}, u32[]{:S(2)}) collective-permute-start(bf16[240,384]{1,0:T(8,128)(2,1)S(1)} %get-tuple-element.162), channel_id=1, source_target_pairs={{0,1},{1,0},{2,3},{3,2},{4,5},{5,4},{6,7},{7,6},{8,9},{9,8},{10,11... | collective-permute-start | bytes 552968 | tf_op jit(solution)/shard_map/ppermute | solution.py:660
  103.9 6.2 %collective-permute-start.36 = (bf16[240,384]{1,0:T(8,128)(2,1)S(1)}, bf16[240,384]{1,0:T(8,128)(2,1)S(1)}, u32[]{:S(2)}, u32[]{:S(2)}) collective-permute-start(bf16[240,384]{1,0:T(8,128)(2,1)S(1)} %get-tuple-element.163), channel_id=1, source_target_pairs={{0,2},{1,3},{2,0},{3,1},{4,6},{5,7},{6,4},{7,5},{8,10},{9,11},{10,... | collective-permute-start | bytes 552968 | tf_op jit(solution)/shard_map/ppermute | solution.py:660
  103.9 10.6 %collective-permute-start.37 = (bf16[240,384]{1,0:T(8,128)(2,1)S(1)}, bf16[240,384]{1,0:T(8,128)(2,1)S(1)}, u32[]{:S(2)}, u32[]{:S(2)}) collective-permute-start(bf16[240,384]{1,0:T(8,128)(2,1)S(1)} %get-tuple-element.164), channel_id=1, source_target_pairs={{0,3},{1,2},{2,1},{3,0},{4,7},{5,6},{6,5},{7,4},{8,11},{9,10},{10,... | collective-permute-start | bytes 552968 | tf_op jit(solution)/shard_map/ppermute | solution.py:660
  107.6 18.6 %collective-permute-start.40 = (bf16[96,768]{1,0:T(8,128)(2,1)S(1)}, bf16[96,768]{1,0:T(8,128)(2,1)S(1)}, u32[]{:S(2)}, u32[]{:S(2)}) collective-permute-start(bf16[96,768]{1,0:T(8,128)(2,1)S(1)} %get-tuple-element.174), channel_id=1, source_target_pairs={{0,8},{4,12},{8,16},{12,20},{16,24},{20,28},{24,0},{28,4},{1,9},{5... | collective-permute-start | bytes 442376 | tf_op jit(solution)/shard_map/ppermute | solution.py:666
  107.7 18.5 %collective-permute-start.41 = (bf16[96,768]{1,0:T(8,128)(2,1)S(1)}, bf16[96,768]{1,0:T(8,128)(2,1)S(1)}, u32[]{:S(2)}, u32[]{:S(2)}) collective-permute-start(bf16[96,768]{1,0:T(8,128)(2,1)S(1)} %get-tuple-element.175), channel_id=1, source_target_pairs={{0,16},{4,20},{8,24},{12,28},{16,0},{20,4},{24,8},{28,12},{1,17},{... | collective-permute-start | bytes 442376 | tf_op jit(solution)/shard_map/ppermute | solution.py:666
  110.1 16.1 %collective-permute-start.42 = (bf16[96,768]{1,0:T(8,128)(2,1)S(1)}, bf16[96,768]{1,0:T(8,128)(2,1)S(1)}, u32[]{:S(2)}, u32[]{:S(2)}) collective-permute-start(bf16[96,768]{1,0:T(8,128)(2,1)S(1)} %get-tuple-element.176), channel_id=1, source_target_pairs={{0,24},{4,28},{8,0},{12,4},{16,8},{20,12},{24,16},{28,20},{1,25},{... | collective-permute-start | bytes 442376 | tf_op jit(solution)/shard_map/ppermute | solution.py:666
  117.2 8.8 %collective-permute-start.39 = (bf16[4,96,384]{2,1,0:T(8,128)(2,1)S(1)}, bf16[4,96,384]{2,1,0:T(8,128)(2,1)S(1)}, u32[]{:S(2)}, u32[]{:S(2)}) collective-permute-start(bf16[4,96,384]{2,1,0:T(8,128)(2,1)S(1)} %get-tuple-element.171), channel_id=1, source_target_pairs={{0,4},{4,0},{8,12},{12,8},{16,20},{20,16},{24,28},{28,24},{1,5},{5... | collective-permute-start | bytes 884744 | tf_op jit(solution)/shard_map/ppermute | solution.py:663
  128.7 10.9 %collective-permute-start.46 = (bf16[2,480,768]{2,1,0:T(8,128)(2,1)S(1)}, bf16[2,480,768]{2,1,0:T(8,128)(2,1)S(1)}, u32[]{:S(2)}, u32[]{:S(2)}) collective-permute-start(bf16[2,480,768]{2,1,0:T(8,128)(2,1)S(1)} %get-tuple-element.192), channel_id=1, source_target_pairs={{0,1},{1,0},{2,3},{3,2},{4,5},{5,4},{6,7},{7,6},{8,9},{9,8},{10,11... | collective-permute-start | bytes 4423688 | tf_op jit(solution)/shard_map/ppermute | solution.py:660
  130.6 15.6 %collective-permute-start.43 = (bf16[4,96,384]{2,1,0:T(8,128)(2,1)S(1)}, bf16[4,96,384]{2,1,0:T(8,128)(2,1)S(1)}, u32[]{:S(2)}, u32[]{:S(2)}) collective-permute-start(bf16[4,96,384]{2,1,0:T(8,128)(2,1)S(1)} %get-tuple-element.189), channel_id=1, source_target_pairs={{0,4},{4,0},{8,12},{12,8},{16,20},{20,16},{24,28},{28,24},{1,5},{5... | collective-permute-start | bytes 884744 | tf_op jit(solution)/shard_map/ppermute | solution.py:663
  130.7 1.8 %collective-permute-start.44 = (f32[16,768]{1,0:T(8,128)S(1)}, f32[16,768]{1,0:T(8,128)S(1)}, u32[]{:S(2)}, u32[]{:S(2)}) collective-permute-start(f32[16,768]{1,0:T(8,128)S(1)} %get-tuple-element.186.refs_0_), channel_id=1, source_target_pairs={{0,1},{1,0},{2,3},{3,2},{4,5},{5,4},{6,7},{7,6},{8,9},{9,8},{10,11... | collective-permute-start | bytes 147464 | tf_op jit(solution)/shard_map/ppermute | solution.py:660
  132.5 7.1 %collective-permute-start.45 = (f32[16,768]{1,0:T(8,128)S(1)}, f32[16,768]{1,0:T(8,128)S(1)}, u32[]{:S(2)}, u32[]{:S(2)}) collective-permute-start(f32[16,768]{1,0:T(8,128)S(1)} %add_core.1.refs_0_), channel_id=1, source_target_pairs={{0,2},{1,3},{2,0},{3,1},{4,6},{5,7},{6,4},{7,5},{8,10},{9,11},{10,... | collective-permute-start | bytes 147464 | tf_op jit(solution)/shard_map/ppermute | solution.py:660
  132.6 8.6 %collective-permute-start.52 = (bf16[96,384]{1,0:T(8,128)(2,1)S(1)}, bf16[96,384]{1,0:T(8,128)(2,1)S(1)}, u32[]{:S(2)}, u32[]{:S(2)}) collective-permute-start(bf16[96,384]{1,0:T(8,128)(2,1)S(1)} %get-tuple-element.177), channel_id=1, source_target_pairs={{0,0},{1,8},{2,16},{3,24},{4,4},{5,12},{6,20},{7,28},{8,1},{9,9},{... | collective-permute-start | bytes 221192 | tf_op jit(solution)/shard_map/ppermute | solution.py:700
  137.1 8.3 %collective-permute-start.53 = (bf16[96,384]{1,0:T(8,128)(2,1)S(1)}, bf16[96,384]{1,0:T(8,128)(2,1)S(1)}, u32[]{:S(2)}, u32[]{:S(2)}) collective-permute-start(bf16[96,384]{1,0:T(8,128)(2,1)S(1)} %get-tuple-element.207), channel_id=1, source_target_pairs={{0,4},{1,12},{2,20},{3,28},{4,0},{5,8},{6,16},{7,24},{8,5},{9,13},... | collective-permute-start | bytes 221192 | tf_op jit(solution)/shard_map/ppermute | solution.py:700
  139.8 8.5 %collective-permute-start.47 = (f32[16,768]{1,0:T(8,128)S(1)}, f32[16,768]{1,0:T(8,128)S(1)}, u32[]{:S(2)}, u32[]{:S(2)}) collective-permute-start(f32[16,768]{1,0:T(8,128)S(1)} %add_far.1.refs_2_), channel_id=1, source_target_pairs={{0,4},{4,0},{8,12},{12,8},{16,20},{20,16},{24,28},{28,24},{1,5},{5... | collective-permute-start | bytes 147464 | tf_op jit(solution)/shard_map/ppermute | solution.py:663
  140.5 8.6 %collective-permute-start.48 = (bf16[144,768]{1,0:T(8,128)(2,1)S(1)}, bf16[144,768]{1,0:T(8,128)(2,1)S(1)}, u32[]{:S(2)}, u32[]{:S(2)}) collective-permute-start(bf16[144,768]{1,0:T(8,128)(2,1)S(1)} %get-tuple-element.197), channel_id=1, source_target_pairs={{0,8},{4,12},{8,16},{12,20},{16,24},{20,28},{24,0},{28,4},{1,9},{5... | collective-permute-start | bytes 663560 | tf_op jit(solution)/shard_map/ppermute | solution.py:666
  141.2 17.7 %collective-permute-start.49 = (bf16[144,768]{1,0:T(8,128)(2,1)S(1)}, bf16[144,768]{1,0:T(8,128)(2,1)S(1)}, u32[]{:S(2)}, u32[]{:S(2)}) collective-permute-start(bf16[144,768]{1,0:T(8,128)(2,1)S(1)} %get-tuple-element.198), channel_id=1, source_target_pairs={{0,16},{4,20},{8,24},{12,28},{16,0},{20,4},{24,8},{28,12},{1,17},{... | collective-permute-start | bytes 663560 | tf_op jit(solution)/shard_map/ppermute | solution.py:666
  145.5 21.0 %collective-permute-start.50 = (bf16[144,768]{1,0:T(8,128)(2,1)S(1)}, bf16[144,768]{1,0:T(8,128)(2,1)S(1)}, u32[]{:S(2)}, u32[]{:S(2)}) collective-permute-start(bf16[144,768]{1,0:T(8,128)(2,1)S(1)} %get-tuple-element.199), channel_id=1, source_target_pairs={{0,24},{4,28},{8,0},{12,4},{16,8},{20,12},{24,16},{28,20},{1,25},{... | collective-permute-start | bytes 663560 | tf_op jit(solution)/shard_map/ppermute | solution.py:666
  146.2 26.1 %collective-permute-start.51 = (bf16[480,768]{1,0:T(8,128)(2,1)S(1)}, bf16[480,768]{1,0:T(8,128)(2,1)S(1)}, u32[]{:S(2)}, u32[]{:S(2)}) collective-permute-start(bf16[480,768]{1,0:T(8,128)(2,1)S(1)} %pair1.1), channel_id=1, source_target_pairs={{0,2},{1,3},{2,0},{3,1},{4,6},{5,7},{6,4},{7,5},{8,10},{9,11},{10,... | collective-permute-start | bytes 2211848 | tf_op jit(solution)/shard_map/ppermute | solution.py:660
  148.4 19.4 %collective-permute-start.55 = (bf16[128,384]{1,0:T(8,128)(2,1)S(1)}, bf16[128,384]{1,0:T(8,128)(2,1)S(1)}, u32[]{:S(2)}, u32[]{:S(2)}) collective-permute-start(bf16[128,384]{1,0:T(8,128)(2,1)S(1)} %get-tuple-element.212), channel_id=1, source_target_pairs={{0,16},{4,20},{8,24},{12,28},{16,0},{20,4},{24,8},{28,12},{1,17},{... | collective-permute-start | bytes 294920 | tf_op jit(solution)/shard_map/ppermute | solution.py:666
  149.1 18.6 %collective-permute-start.56 = (bf16[128,384]{1,0:T(8,128)(2,1)S(1)}, bf16[128,384]{1,0:T(8,128)(2,1)S(1)}, u32[]{:S(2)}, u32[]{:S(2)}) collective-permute-start(bf16[128,384]{1,0:T(8,128)(2,1)S(1)} %get-tuple-element.213), channel_id=1, source_target_pairs={{0,24},{4,28},{8,0},{12,4},{16,8},{20,12},{24,16},{28,20},{1,25},{... | collective-permute-start | bytes 294920 | tf_op jit(solution)/shard_map/ppermute | solution.py:666
  158.9 12.5 %collective-permute-start.54 = (bf16[128,384]{1,0:T(8,128)(2,1)S(1)}, bf16[128,384]{1,0:T(8,128)(2,1)S(1)}, u32[]{:S(2)}, u32[]{:S(2)}) collective-permute-start(bf16[128,384]{1,0:T(8,128)(2,1)S(1)} %get-tuple-element.211), channel_id=1, source_target_pairs={{0,8},{4,12},{8,16},{12,20},{16,24},{20,28},{24,0},{28,4},{1,9},{5... | collective-permute-start | bytes 294920 | tf_op jit(solution)/shard_map/ppermute | solution.py:666
  (1 other events, 3.1 us)

commit v4 on v3

--- a/solution.py
+++ b/solution.py
@@ -9,8 +9,8 @@
 from jax.sharding import PartitionSpec as P
 
 HEADS = 12
-COST = {'up_grad': 10000000000, 'branch': 10000000000, 'value_back': 10000000000, 'attend_back': 10000000000, 'finish': 10000000000, 'pack': 3000000000, 'sum_down': 1000, 'sum_up': 1000, 'last_x': 30000000000, 'hidden_back': 3000000000, 'qk_grad': 1000000000}
-CFG = {'pair': 1, 'add': 1, 'za': 'direct', 'zu': 'bidir', 'zd': 'bidir', 'xu': 0, 'xd': 0, 'norm': 3, 'held': 0, 'split': 3, 'cot': 1, 'tok': 1, 'ord': 1, 'up': 0, 'vo': 0, 'br': 1, 'both': 0, 'og': 3, 'sa': 'each', 'su': 'each', 'sd': 'rest', 'gd': 2}
+COST = {'up_grad': 10000000000, 'branch': 10000000000, 'value_back': 10000000000, 'attend_back': 10000000000, 'finish': 10000000000, 'pack': 3000000000, 'sum_down': 1000, 'sum_up': 1000, 'last_x': 30000000000, 'hidden_back': 3000000000, 'qk_grad': 2000000000, 'stack_down': 5000000000, 'both_x': 500000000, 'split_down': 2000000000}
+CFG = {'pair': 1, 'add': 1, 'za': 'direct', 'zu': 'bidir', 'zd': 'bidir', 'xu': 0, 'xd': 0, 'norm': 2, 'held': 0, 'split': 3, 'cot': 1, 'tok': 1, 'ord': 1, 'up': 0, 'vo': 0, 'br': 1, 'both': 0, 'og': 3, 'sa': 'each', 'su': 'each', 'sd': 'rest', 'gd': 2, 'gx': 0}
 EPS = 1e-05
 LOW = jnp.bfloat16
 F32 = jnp.float32
@@ -938,10 +938,10 @@
         )
         both_z = to_z(both)
         halves = sum_down(up_own)
-        down_halves = [exchange(halves[k], k) for k in range(2)]
         g_last = gate(g_qk, halves[0])
 
-        def give_down(*after):
+        def give_down(*after, start=()):
+            down_halves = [exchange(gate(halves[k], *start), k) for k in range(2)]
             (out,) = pallas(
                 fn(give_down_kernel, m),
                 [shape(WH, S * m.hrows, dtype=F32)],
@@ -975,6 +975,9 @@
     vec_core, core1 = seq_to(vec, 1), seq_to(send, 1)
     vec = add(vec, vec_core, "add_core")
     vec_far = seq_to(vec, 2)
+    if m.fast and CFG["gd"] == 3:
+        g_down = give_down(vec)
+        keep1 = gate(keep1, g_down)
     pair1 = add_pair(gate(keep1, *([vec_far] if CFG["pair"] else [vec])), core1, "pair1")
     far1 = seq_to(pair1, 2)
     if m.fast:
@@ -988,7 +991,7 @@
                 name="both_out",
             )
 
-        if CFG["gd"]:
+        if CFG["gd"] in (1, 2):
             g_down = give_down(pair1)
         vec = add(gate(vec, *([pair1] if CFG["add"] else []), *([g_down] if CFG["gd"] == 1 else [])), vec_far, "add_far")
         vec_got = x_swap(vec)
@@ -1030,7 +1033,7 @@
         if CFG["both"] == 1:
             g_up, g_value, g_out = both_out(result)
         if not CFG["gd"]:
-            g_down = give_down(g_value, result)
+            g_down = give_down(g_value, result, start=[qk_own] if CFG["gx"] == 1 else qk_z if CFG["gx"] == 2 else [])
         g_down = g_down.T
         g_query, g_key, *vec_outs = pallas(
             fn(last_z_kernel, m),

time: 174 us -> 173 us (level)
  starting transfers between devices: 81.8 us -> 67.9 us
  waiting for transfers between devices: 49.5 us -> 61.9 us
    ppermute x20, starting transfers between devices: 36.6 us -> 16.2 us  [seq_to(): return lax.ppermute(x, 'seq', [(i, i ^ e) for i in range(S)])]
    ppermute x18, waiting for transfers between devices: 19.6 us -> 29.2 us  [z_shift(): return lax.ppermute(x, 'dp', [(i, (i + 2 * k) % N) for i in range(N)])]
    ppermute x18, starting transfers between devices: 19.5 us -> 27.3 us  [z_shift(): return lax.ppermute(x, 'dp', [(i, (i + 2 * k) % N) for i in range(N)])]
    ppermute x15, waiting for transfers between devices: 6.42 us -> 2.65 us  [x_swap(): return lax.ppermute(x, 'dp', [(i, i ^ 1) for i in range(N)])]
    ppermute x20, waiting for transfers between devices: 15.5 us -> 19.2 us  [seq_to(): return lax.ppermute(x, 'seq', [(i, i ^ e) for i in range(S)])]
    ppermute x15, starting transfers between devices: 12.7 us -> 9.44 us  [x_swap(): return lax.ppermute(x, 'dp', [(i, i ^ 1) for i in range(N)])]
    ppermute x4, waiting for transfers between devices: 8.02 us -> 10.8 us  [exchange(): return lax.ppermute(x, ('dp', 'seq'), pairs)]
    ppermute x4, starting transfers between devices: 13 us -> 15 us  [exchange(): return lax.ppermute(x, ('dp', 'seq'), pairs)]
  transfers between devices with their start and end apart: 57 -> 57, of which waited for: 21 -> 16; matrix products, arithmetic and copies ran while one was open for 0% -> 0% of each run, Pallas kernels for 19% -> 19%
where the time goes in v4:
time: 173 us; the launch traced here: 172 us
  starting transfers between devices  67.9 us (39%)
  waiting for transfers between devices  61.9 us (36%)
  Pallas kernels  41.5 us (24%)
    pallas_call x31, Pallas kernels, pallas(): pl.pallas_call(run, out_shape=outs, in_specs=[pl.BlockSpec(memory_space=p...  41.5 us
    ppermute x18, waiting for transfers between devices, z_shift(): return lax.ppermute(x, 'dp', [(i, (i + 2 * k) % N) for i in range(N)])  29.2 us
    ppermute x18, starting transfers between devices, z_shift(): return lax.ppermute(x, 'dp', [(i, (i + 2 * k) % N) for i in range(N)])  27.3 us
    ppermute x20, waiting for transfers between devices, seq_to(): return lax.ppermute(x, 'seq', [(i, i ^ e) for i in range(S)])  19.2 us
    ppermute x20, starting transfers between devices, seq_to(): return lax.ppermute(x, 'seq', [(i, i ^ e) for i in range(S)])  16.2 us
    ppermute x4, starting transfers between devices, exchange(): return lax.ppermute(x, ('dp', 'seq'), pairs)  15 us
    ppermute x4, waiting for transfers between devices, exchange(): return lax.ppermute(x, ('dp', 'seq'), pairs)  10.8 us
    ppermute x15, starting transfers between devices, x_swap(): return lax.ppermute(x, 'dp', [(i, i ^ 1) for i in range(N)])  9.44 us
  transfers between devices with their start and end apart: 57, of which 16 were waited for; matrix products, arithmetic and copies ran while one was open for 0% of the time, Pallas kernels for 19%

profile of v4, /device:TPU:5, one launch (start us, length us, event | category | flops | bytes accessed | tf_op | source)
XLA Modules:
  0.0 172.3 jit_solution(5683283232556287191)
XLA Ops:
  0.7 1.9 %pack.1.refs_3_ = bf16[96,640]{1,0:T(8,128)(2,1)} custom-call(bf16[96,192]{1,0:T(8,128)(2,1)} %refs_0_.2, bf16[96,192]{1,0:T(8,128)(2,1)} %refs_1_.3, bf16[96,192]{1,0:T(8,128)(2,1)} %refs_2_.1, bf16[96]{0:T(256)(128)(2,1)} %refs_3_.2, bf16[96]{0:T(256)(128)(2,1)} %refs_4_.1, bf16[96]{0:T(256)(128)(2,1)} %refs_5_.1, bf16[96]{0:T(256)(128)(2,1)} %refs_6_.1, ...), custom_call_target="tpu_custom_call" | custom-call | flops 3000000000 | bytes 235776 | tf_op jit(solution)/shard_map/pack/pallas_call | solution.py:58
  2.6 1.3 collective-permute-start.1
  3.9 1.2 collective-permute-start.9
  5.1 2.0 %collective-permute-start.8 = (bf16[96,640]{1,0:T(8,128)(2,1)}, bf16[96,640]{1,0:T(8,128)(2,1)S(1)}, u32[]{:S(2)}, u32[]{:S(2)}) collective-permute-start(bf16[96,640]{1,0:T(8,128)(2,1)} %pack.1.refs_3_), channel_id=1, source_target_pairs={{0,24},{4,28},{8,0},{12,4},{16,8},{20,12},{24,16},{28,20},{1,25},{... | collective-permute-start | bytes 368648 | tf_op jit(solution)/shard_map/ppermute | solution.py:666
  7.8 1.1 collective-permute-done.1.refs_4_
  9.4 3.1 %collective-permute-done.8.refs_6_ = bf16[96,640]{1,0:T(8,128)(2,1)S(1)} collective-permute-done((bf16[96,640]{1,0:T(8,128)(2,1)}, bf16[96,640]{1,0:T(8,128)(2,1)S(1)}, u32[]{:S(2)}, u32[]{:S(2)}) %collective-permute-start.8) | collective-permute-done | bytes 122912 | tf_op jit(solution)/shard_map/ppermute | solution.py:666
  12.5 5.5 %collective-permute-start.2 = (bf16[96,384]{1,0:T(8,128)(2,1)S(1)}, bf16[96,384]{1,0:T(8,128)(2,1)S(1)}, u32[]{:S(2)}, u32[]{:S(2)}) collective-permute-start(bf16[96,384]{1,0:T(8,128)(2,1)S(1)} %get-tuple-element.126), channel_id=1, source_target_pairs={{0,0},{1,8},{2,16},{3,24},{4,4},{5,12},{6,20},{7,28},{8,1},{9,9},{... | collective-permute-start | bytes 221192 | tf_op jit(solution)/shard_map/ppermute | solution.py:700
  18.0 0.5 collective-permute-start.12
  18.5 1.9 %collective-permute-start.3 = (bf16[96,384]{1,0:T(8,128)(2,1)S(1)}, bf16[96,384]{1,0:T(8,128)(2,1)S(1)}, u32[]{:S(2)}, u32[]{:S(2)}) collective-permute-start(bf16[96,384]{1,0:T(8,128)(2,1)S(1)} %get-tuple-element.127), channel_id=1, source_target_pairs={{0,4},{1,12},{2,20},{3,28},{4,0},{5,8},{6,16},{7,24},{8,5},{9,13},... | collective-permute-start | bytes 221192 | tf_op jit(solution)/shard_map/ppermute | solution.py:700
  20.4 0.7 collective-permute-start.11
  21.1 0.7 collective-permute-start.10
  21.9 4.0 %collective-permute-done.3.refs_1_ = bf16[96,384]{1,0:T(8,128)(2,1)S(1)} collective-permute-done((bf16[96,384]{1,0:T(8,128)(2,1)S(1)}, bf16[96,384]{1,0:T(8,128)(2,1)S(1)}, u32[]{:S(2)}, u32[]{:S(2)}) %collective-permute-start.3) | collective-permute-done | bytes 73760 | tf_op jit(solution)/shard_map/ppermute | solution.py:700
  26.0 2.8 %collective-permute-start.4 = (bf16[3,70,768]{2,1,0:T(8,128)(2,1)S(1)}, bf16[3,70,768]{2,1,0:T(8,128)(2,1)S(1)}, u32[]{:S(2)}, u32[]{:S(2)}) collective-permute-start(bf16[3,70,768]{2,1,0:T(8,128)(2,1)S(1)} %copy-done), channel_id=1, source_target_pairs={{0,1},{1,0},{2,3},{3,2},{4,5},{5,4},{6,7},{7,6},{8,9},{9,8},{10,11... | collective-permute-start | bytes 967688 | tf_op jit(solution)/shard_map/ppermute | solution.py:660
  28.8 3.5 %collective-permute-start.15 = (bf16[144,768]{1,0:T(8,128)(2,1)S(1)}, bf16[144,768]{1,0:T(8,128)(2,1)S(1)}, u32[]{:S(2)}, u32[]{:S(2)}) collective-permute-start(bf16[144,768]{1,0:T(8,128)(2,1)S(1)} %pack_up.1.refs_0_), channel_id=1, source_target_pairs={{0,24},{4,28},{8,0},{12,4},{16,8},{20,12},{24,16},{28,20},{1,25},{... | collective-permute-start | bytes 663560 | tf_op jit(solution)/shard_map/ppermute | solution.py:666
  32.8 9.1 %collective-permute-done.15.refs_3_ = bf16[144,768]{1,0:T(8,128)(2,1)S(1)} collective-permute-done((bf16[144,768]{1,0:T(8,128)(2,1)S(1)}, bf16[144,768]{1,0:T(8,128)(2,1)S(1)}, u32[]{:S(2)}, u32[]{:S(2)}) %collective-permute-start.15) | collective-permute-done | bytes 221216 | tf_op jit(solution)/shard_map/ppermute | solution.py:666
  41.9 1.2 collective-permute-start.19
  43.4 5.2 %collective-permute-done.27.refs_0_.refs_4_ = bf16[96,768]{1,0:T(8,128)(2,1)S(1)} collective-permute-done((bf16[96,768]{1,0:T(8,128)(2,1)S(1)}, bf16[96,768]{1,0:T(8,128)(2,1)S(1)}, u32[]{:S(2)}, u32[]{:S(2)}) %collective-permute-start.27) | collective-permute-done | bytes 147488 | tf_op jit(solution)/shard_map/ppermute | solution.py:666
  48.6 2.7 %collective-permute-start.29 = (bf16[96,768]{1,0:T(8,128)(2,1)S(1)}, bf16[96,768]{1,0:T(8,128)(2,1)S(1)}, u32[]{:S(2)}, u32[]{:S(2)}) collective-permute-start(bf16[96,768]{1,0:T(8,128)(2,1)S(1)} %join_down.1.refs_3_), channel_id=1, source_target_pairs={{0,24},{4,28},{8,0},{12,4},{16,8},{20,12},{24,16},{28,20},{1,25},{... | collective-permute-start | bytes 442376 | tf_op jit(solution)/shard_map/ppermute | solution.py:666
  51.3 0.9 norm.1.refs_2_
  52.3 7.5 %attend.1 = (bf16[960,576]{1,0:T(8,128)(2,1)S(1)}, bf16[960,768]{1,0:T(8,128)(2,1)S(1)}, bf16[9,320,320]{2,1,0:T(8,128)(2,1)S(1)}, bf16[480,384]{1,0:T(8,128)(2,...) custom-call(s32[3,40]{1,0:T(4,128)S(1)} %copy-done.5, s32[3]{0:T(128)S(1)} %copy-done.6, ...), custom_call_target="tpu_custom_call" | custom-call | flops 1000 | bytes 9757164 | tf_op jit(solution)/shard_map/attend/pallas_call | solution.py:58
  59.8 3.3 %collective-permute-start.21 = (bf16[3,70,768]{2,1,0:T(8,128)(2,1)S(1)}, bf16[3,70,768]{2,1,0:T(8,128)(2,1)S(1)}, u32[]{:S(2)}, u32[]{:S(2)}) collective-permute-start(bf16[3,70,768]{2,1,0:T(8,128)(2,1)S(1)} %copy-done.1), channel_id=1, source_target_pairs={{0,1},{1,0},{2,3},{3,2},{4,5},{5,4},{6,7},{7,6},{8,9},{9,8},{10,11... | collective-permute-start | bytes 967688 | tf_op jit(solution)/shard_map/ppermute | solution.py:660
  63.5 0.5 collective-permute-start.20
  64.0 0.5 collective-permute-start.31
  64.8 8.5 %collective-permute-done.25.refs_6_ = bf16[480,384]{1,0:T(8,128)(2,1)S(1)} collective-permute-done((bf16[480,384]{1,0:T(8,128)(2,1)S(1)}, bf16[480,384]{1,0:T(8,128)(2,1)S(1)}, u32[]{:S(2)}, u32[]{:S(2)}) %collective-permute-start.25) | collective-permute-done | bytes 368672 | tf_op jit(solution)/shard_map/ppermute | solution.py:660
  73.3 0.9 collective-permute-start.26
  74.5 0.6 join.1
  75.4 5.5 %forward.1 = (bf16[960,768]{1,0:T(8,128)(2,1)S(1)}, bf16[960,768]{1,0:T(8,128)(2,1)S(1)}, f32[960,768]{1,0:T(8,128)S(1)}, bf16[960,768]{1,0:T(8,128)(2,1)S(1)}, ...) custom-call(bf16[3,70,768]{2,1,0:T(8,128)(2,1)S(1)} %copy-done, ...), custom_call_target="tpu_custom_call" | custom-call | flops 1000 | bytes 14143488 | tf_op jit(solution)/shard_map/forward/pallas_call | solution.py:58
  81.0 1.6 down_grad.1
  82.6 3.3 %hidden_back.1 = (bf16[960,768]{1,0:T(8,128)(2,1)S(1)}, bf16[768,768]{1,0:T(8,128)(2,1)S(1)}, bf16[240,768]{1,0:T(8,128)(2,1)S(1)}, bf16[240,768]{1,0:T(8,128)(2,1)S(1)}, bf16[2,240,768]{2,1,0:T(8,128)(2,1)S(1)}) custom-call(bf16[960,768]{1,0:T(8,128)(2,1)S(1)} %get-tuple-element.133.refs_0_.refs_5_.refs_3_, f32[960,768]{1,0:T(8,128)S(1)} %get-tuple-element.141.refs_1_, ...), custom_call_target="tpu_custom_call" | custom-call | flops 3000000000 | bytes 10911744 | tf_op jit(solution)/shard_map/hidden_back/pallas_call | solution.py:58
  86.3 0.7 collective-permute-start.34
  87.0 1.2 collective-permute-done.32.refs_1_
  88.4 1.6 up_grad.1
  89.9 0.8 collective-permute-start.38
  90.7 7.4 %collective-permute-done.33.refs_2_ = bf16[240,768]{1,0:T(8,128)(2,1)S(1)} collective-permute-done((bf16[240,768]{1,0:T(8,128)(2,1)S(1)}, bf16[240,768]{1,0:T(8,128)(2,1)S(1)}, u32[]{:S(2)}, u32[]{:S(2)}) %collective-permute-start.33) | collective-permute-done | bytes 368672 | tf_op jit(solution)/shard_map/ppermute | solution.py:660
  98.2 1.1 middle.1
  99.3 1.3 collective-permute-start.35
  100.6 1.7 collective-permute-start.37
  102.3 1.8 %branch.1 = (bf16[240,768]{1,0:T(8,128)(2,1)S(1)}, bf16[240,768]{1,0:T(8,128)(2,1)S(1)}, bf16[2,240,768]{2,1,0:T(8,128)(2,1)S(1)}, f32[8,768]{1,0:T(8,128)S(1)}) custom-call(bf16[960,768]{1,0:T(8,128)(2,1)S(1)} %get-tuple-element.154.refs_1_.refs_0_, bf16[768,768]{1,0:T(8,128)(2,1)S(1)} %get-tuple-element.155.refs_1_, ...), custom_call_target="tpu_custom_call" | custom-call | flops 10000000000 | bytes 7102464 | tf_op jit(solution)/shard_map/branch/pallas_call | solution.py:58
  104.4 3.7 %collective-permute-start.41 = (bf16[96,768]{1,0:T(8,128)(2,1)S(1)}, bf16[96,768]{1,0:T(8,128)(2,1)S(1)}, u32[]{:S(2)}, u32[]{:S(2)}) collective-permute-start(bf16[96,768]{1,0:T(8,128)(2,1)S(1)} %get-tuple-element.175), channel_id=1, source_target_pairs={{0,16},{4,20},{8,24},{12,28},{16,0},{20,4},{24,8},{28,12},{1,17},{... | collective-permute-start | bytes 442376 | tf_op jit(solution)/shard_map/ppermute | solution.py:666
  108.2 2.2 %collective-permute-start.42 = (bf16[96,768]{1,0:T(8,128)(2,1)S(1)}, bf16[96,768]{1,0:T(8,128)(2,1)S(1)}, u32[]{:S(2)}, u32[]{:S(2)}) collective-permute-start(bf16[96,768]{1,0:T(8,128)(2,1)S(1)} %get-tuple-element.176), channel_id=1, source_target_pairs={{0,24},{4,28},{8,0},{12,4},{16,8},{20,12},{24,16},{28,20},{1,25},{... | collective-permute-start | bytes 442376 | tf_op jit(solution)/shard_map/ppermute | solution.py:666
  110.3 0.9 collective-permute-done.37.refs_4_
  111.2 2.7 %value_back.1 = (bf16[960,192]{1,0:T(8,128)(2,1)S(1)}, bf16[960,192]{1,0:T(8,128)(2,1)S(1)}, bf16[4,96,384]{2,1,0:T(8,128)(2,1)S(1)}, bf16[4,96,384]{2,1,0:T(8,128)(2,1)S(1)}) custom-call(bf16[9,320,320]{2,1,0:T(8,128)(2,1)S(1)} %get-tuple-element.130.refs_0_.refs_1_, bf16[240,384]{1,0:T(8,128)(2,1)S(1)} %get-tuple-element.161.refs_1_, ...), custom_call_target="tpu_custom_call" | custom-call | flops 10000000000 | bytes 6856704 | tf_op jit(solution)/shard_map/value_back/pallas_call | solution.py:58
  113.9 0.8 collective-permute-start.39
  114.7 4.5 %attend_back.1.refs_0_.refs_1_ = bf16[960,384]{1,0:T(8,128)(2,1)S(1)} custom-call(bf16[960,576]{1,0:T(8,128)(2,1)S(1)} %get-tuple-element.129.refs_0_, bf16[9,320,320]{2,1,0:T(8,128)(2,1)S(1)} %get-tuple-element.130.refs_0_.refs_1_, bf16[960,192]{1,0:T(8,128)(2,1)S(1)} %get-tuple-element.167.refs_2_), custom_call_target="tpu_custom_call" | custom-call | flops 10000000000 | bytes 4055040 | tf_op jit(solution)/shard_map/attend_back/pallas_call | solution.py:58
  119.2 2.6 %collective-permute-done.39.refs_3_ = bf16[4,96,384]{2,1,0:T(8,128)(2,1)S(1)} collective-permute-done((bf16[4,96,384]{2,1,0:T(8,128)(2,1)S(1)}, bf16[4,96,384]{2,1,0:T(8,128)(2,1)S(1)}, u32[]{:S(2)}, u32[]{:S(2)}) %collective-permute-start.39) | collective-permute-done | bytes 294944 | tf_op jit(solution)/shard_map/ppermute | solution.py:663
  122.3 2.1 %input_back.1 = (bf16[240,768]{1,0:T(8,128)(2,1)S(1)}, bf16[480,768]{1,0:T(8,128)(2,1)S(1)}, bf16[2,480,768]{2,1,0:T(8,128)(2,1)S(1)}, f32[16,768]{1,0:T(8,128)S(1)}) custom-call(bf16[960,384]{1,0:T(8,128)(2,1)S(1)} %attend_back.1.refs_0_.refs_1_, bf16[960,192]{1,0:T(8,128)(2,1)S(1)} %get-tuple-element.179.refs_1_, f32[960,768]{1,0:T(8,128)S(1)} %norm.1.refs_2_, ...), custom_call_target="tpu_custom_call" | custom-call | flops 1000 | bytes 8822784 | tf_op jit(solution)/shard_map/input_back/pallas_call | solution.py:58
  124.5 1.7 collective-permute-start.46
  126.1 1.1 qk_grad.1
  127.2 0.8 collective-permute-start.43
  128.3 0.9 collective-permute-done.44.refs_1_
  129.4 7.1 %collective-permute-start.52 = (bf16[96,384]{1,0:T(8,128)(2,1)S(1)}, bf16[96,384]{1,0:T(8,128)(2,1)S(1)}, u32[]{:S(2)}, u32[]{:S(2)}) collective-permute-start(bf16[96,384]{1,0:T(8,128)(2,1)S(1)} %get-tuple-element.177), channel_id=1, source_target_pairs={{0,0},{1,8},{2,16},{3,24},{4,4},{5,12},{6,20},{7,28},{8,1},{9,9},{... | collective-permute-start | bytes 221192 | tf_op jit(solution)/shard_map/ppermute | solution.py:700
  136.4 0.5 collective-permute-start.53
  137.1 0.8 collective-permute-start.47
  138.0 0.6 collective-permute-done.52.refs_0_
  138.6 6.2 %collective-permute-done.53.refs_1_ = bf16[96,384]{1,0:T(8,128)(2,1)S(1)} collective-permute-done((bf16[96,384]{1,0:T(8,128)(2,1)S(1)}, bf16[96,384]{1,0:T(8,128)(2,1)S(1)}, u32[]{:S(2)}, u32[]{:S(2)}) %collective-permute-start.53) | collective-permute-done | bytes 73760 | tf_op jit(solution)/shard_map/ppermute | solution.py:700
  144.7 0.7 give_down.1
  145.5 1.7 collective-permute-start.51
  147.3 1.9 %collective-permute-start.56 = (bf16[128,384]{1,0:T(8,128)(2,1)S(1)}, bf16[128,384]{1,0:T(8,128)(2,1)S(1)}, u32[]{:S(2)}, u32[]{:S(2)}) collective-permute-start(bf16[128,384]{1,0:T(8,128)(2,1)S(1)} %get-tuple-element.213), channel_id=1, source_target_pairs={{0,24},{4,28},{8,0},{12,4},{16,8},{20,12},{24,16},{28,20},{1,25},{... | collective-permute-start | bytes 294920 | tf_op jit(solution)/shard_map/ppermute | solution.py:666
  149.2 7.0 %collective-permute-done.49.refs_3_ = bf16[144,768]{1,0:T(8,128)(2,1)S(1)} collective-permute-done((bf16[144,768]{1,0:T(8,128)(2,1)S(1)}, bf16[144,768]{1,0:T(8,128)(2,1)S(1)}, u32[]{:S(2)}, u32[]{:S(2)}) %collective-permute-start.49) | collective-permute-done | bytes 221216 | tf_op jit(solution)/shard_map/ppermute | solution.py:666
  156.2 9.2 %collective-permute-start.54 = (bf16[128,384]{1,0:T(8,128)(2,1)S(1)}, bf16[128,384]{1,0:T(8,128)(2,1)S(1)}, u32[]{:S(2)}, u32[]{:S(2)}) collective-permute-start(bf16[128,384]{1,0:T(8,128)(2,1)S(1)} %get-tuple-element.211), channel_id=1, source_target_pairs={{0,8},{4,12},{8,16},{12,20},{16,24},{20,28},{24,0},{28,4},{1,9},{5... | collective-permute-start | bytes 294920 | tf_op jit(solution)/shard_map/ppermute | solution.py:666
  165.4 0.9 both_out.1
  166.3 3.7 %collective-permute-done.54.refs_2_ = bf16[128,384]{1,0:T(8,128)(2,1)S(1)} collective-permute-done((bf16[128,384]{1,0:T(8,128)(2,1)S(1)}, bf16[128,384]{1,0:T(8,128)(2,1)S(1)}, u32[]{:S(2)}, u32[]{:S(2)}) %collective-permute-start.54) | collective-permute-done | bytes 98336 | tf_op jit(solution)/shard_map/ppermute | solution.py:666
  170.0 0.8 query_key.1
  170.8 1.5 finish.1
  (97 shorter events, 5.9 us)
Async XLA Ops:
  0.7 8.2 %copy-start = (bf16[3,70,768]{2,1,0:T(8,128)(2,1)S(1)}, bf16[3,70,768]{2,1,0:T(8,128)(2,1)}, u32[]{:S(2)}) copy-start(bf16[3,70,768]{2,1,0:T(8,128)(2,1)} %refs_3_.3) | copy-start | bytes 967684
  0.7 8.7 %copy-start.7 = (bf16[384,192]{0,1:T(8,128)(2,1)S(1)}, bf16[384,192]{0,1:T(8,128)(2,1)}, u32[]{:S(2)}) copy-start(bf16[384,192]{0,1:T(8,128)(2,1)} %param.28) | copy-start | bytes 442372
  2.6 6.3 %collective-permute-start.1 = (bf16[96,640]{1,0:T(8,128)(2,1)}, bf16[96,640]{1,0:T(8,128)(2,1)S(1)}, u32[]{:S(2)}, u32[]{:S(2)}) collective-permute-start(bf16[96,640]{1,0:T(8,128)(2,1)} %pack.1.refs_3_), channel_id=1, source_target_pairs={{0,8},{4,12},{8,16},{12,20},{16,24},{20,28},{24,0},{28,4},{1,9},{5... | collective-permute-start | bytes 368648 | tf_op jit(solution)/shard_map/ppermute | solution.py:666
  3.9 16.5 %collective-permute-start.9 = (bf16[96,640]{1,0:T(8,128)(2,1)}, bf16[96,640]{1,0:T(8,128)(2,1)S(1)}, u32[]{:S(2)}, u32[]{:S(2)}) collective-permute-start(bf16[96,640]{1,0:T(8,128)(2,1)} %pack.1.refs_3_), channel_id=1, source_target_pairs={{0,4},{4,0},{8,12},{12,8},{16,20},{20,16},{24,28},{28,24},{1,5},{5... | collective-permute-start | bytes 368648 | tf_op jit(solution)/shard_map/ppermute | solution.py:663
  5.1 7.4 %collective-permute-start.8 = (bf16[96,640]{1,0:T(8,128)(2,1)}, bf16[96,640]{1,0:T(8,128)(2,1)S(1)}, u32[]{:S(2)}, u32[]{:S(2)}) collective-permute-start(bf16[96,640]{1,0:T(8,128)(2,1)} %pack.1.refs_3_), channel_id=1, source_target_pairs={{0,24},{4,28},{8,0},{12,4},{16,8},{20,12},{24,16},{28,20},{1,25},{... | collective-permute-start | bytes 368648 | tf_op jit(solution)/shard_map/ppermute | solution.py:666
  7.1 11.4 %collective-permute-start.7 = (bf16[96,640]{1,0:T(8,128)(2,1)}, bf16[96,640]{1,0:T(8,128)(2,1)S(1)}, u32[]{:S(2)}, u32[]{:S(2)}) collective-permute-start(bf16[96,640]{1,0:T(8,128)(2,1)} %pack.1.refs_3_), channel_id=1, source_target_pairs={{0,16},{4,20},{8,24},{12,28},{16,0},{20,4},{24,8},{28,12},{1,17},{... | collective-permute-start | bytes 368648 | tf_op jit(solution)/shard_map/ppermute | solution.py:666
  7.5 10.4 %collective-permute-start = (bf16[96,192]{1,0:T(8,128)(2,1)S(1)}, bf16[96,192]{1,0:T(8,128)(2,1)S(1)}, u32[]{:S(2)}, u32[]{:S(2)}) collective-permute-start(bf16[96,192]{1,0:T(8,128)(2,1)S(1)} %copy-done.4), channel_id=1, source_target_pairs={{0,2},{1,3},{2,0},{3,1},{4,6},{5,7},{6,4},{7,5},{8,10},{9,11},{10,... | collective-permute-start | bytes 110600 | tf_op jit(solution)/shard_map/ppermute | solution.py:660
  8.9 23.4 %collective-permute-start.5 = (bf16[3,70,768]{2,1,0:T(8,128)(2,1)S(1)}, bf16[3,70,768]{2,1,0:T(8,128)(2,1)S(1)}, u32[]{:S(2)}, u32[]{:S(2)}) collective-permute-start(bf16[3,70,768]{2,1,0:T(8,128)(2,1)S(1)} %copy-done), channel_id=1, source_target_pairs={{0,2},{1,3},{2,0},{3,1},{4,6},{5,7},{6,4},{7,5},{8,10},{9,11},{10,... | collective-permute-start | bytes 967688 | tf_op jit(solution)/shard_map/ppermute | solution.py:660
  9.4 12.5 %copy-start.2 = (bf16[96,768]{1,0:T(8,128)(2,1)S(1)}, bf16[96,768]{1,0:T(8,128)(2,1)}, u32[]{:S(2)}) copy-start(bf16[96,768]{1,0:T(8,128)(2,1)} %refs_0_.3) | copy-start | bytes 442372
  9.4 33.7 %copy-start.1 = (bf16[3,70,768]{2,1,0:T(8,128)(2,1)S(1)}, bf16[3,70,768]{2,1,0:T(8,128)(2,1)}, u32[]{:S(2)}) copy-start(bf16[3,70,768]{2,1,0:T(8,128)(2,1)} %refs_2_.2) | copy-start | bytes 967684
  12.5 8.6 %collective-permute-start.2 = (bf16[96,384]{1,0:T(8,128)(2,1)S(1)}, bf16[96,384]{1,0:T(8,128)(2,1)S(1)}, u32[]{:S(2)}, u32[]{:S(2)}) collective-permute-start(bf16[96,384]{1,0:T(8,128)(2,1)S(1)} %get-tuple-element.126), channel_id=1, source_target_pairs={{0,0},{1,8},{2,16},{3,24},{4,4},{5,12},{6,20},{7,28},{8,1},{9,9},{... | collective-permute-start | bytes 221192 | tf_op jit(solution)/shard_map/ppermute | solution.py:700
  18.0 8.0 %collective-permute-start.12 = (bf16[96,640]{1,0:T(8,128)(2,1)S(1)}, bf16[96,640]{1,0:T(8,128)(2,1)S(1)}, u32[]{:S(2)}, u32[]{:S(2)}) collective-permute-start(bf16[96,640]{1,0:T(8,128)(2,1)S(1)} %collective-permute-done.8.refs_6_), channel_id=1, source_target_pairs={{0,4},{4,0},{8,12},{12,8},{16,20},{20,16},{24,28},{28,24},{1,5},{5... | collective-permute-start | bytes 368648 | tf_op jit(solution)/shard_map/ppermute | solution.py:663
  18.5 7.5 %collective-permute-start.3 = (bf16[96,384]{1,0:T(8,128)(2,1)S(1)}, bf16[96,384]{1,0:T(8,128)(2,1)S(1)}, u32[]{:S(2)}, u32[]{:S(2)}) collective-permute-start(bf16[96,384]{1,0:T(8,128)(2,1)S(1)} %get-tuple-element.127), channel_id=1, source_target_pairs={{0,4},{1,12},{2,20},{3,28},{4,0},{5,8},{6,16},{7,24},{8,5},{9,13},... | collective-permute-start | bytes 221192 | tf_op jit(solution)/shard_map/ppermute | solution.py:700
  20.4 8.4 %collective-permute-start.11 = (bf16[96,640]{1,0:T(8,128)(2,1)S(1)}, bf16[96,640]{1,0:T(8,128)(2,1)S(1)}, u32[]{:S(2)}, u32[]{:S(2)}) collective-permute-start(bf16[96,640]{1,0:T(8,128)(2,1)S(1)} %collective-permute-done.7.refs_5_), channel_id=1, source_target_pairs={{0,4},{4,0},{8,12},{12,8},{16,20},{20,16},{24,28},{28,24},{1,5},{5... | collective-permute-start | bytes 368648 | tf_op jit(solution)/shard_map/ppermute | solution.py:663
  21.1 11.2 %collective-permute-start.10 = (bf16[96,640]{1,0:T(8,128)(2,1)S(1)}, bf16[96,640]{1,0:T(8,128)(2,1)S(1)}, u32[]{:S(2)}, u32[]{:S(2)}) collective-permute-start(bf16[96,640]{1,0:T(8,128)(2,1)S(1)} %collective-permute-done.1.refs_4_), channel_id=1, source_target_pairs={{0,4},{4,0},{8,12},{12,8},{16,20},{20,16},{24,28},{28,24},{1,5},{5... | collective-permute-start | bytes 368648 | tf_op jit(solution)/shard_map/ppermute | solution.py:663
  26.0 6.8 %collective-permute-start.13 = (bf16[144,768]{1,0:T(8,128)(2,1)S(1)}, bf16[144,768]{1,0:T(8,128)(2,1)S(1)}, u32[]{:S(2)}, u32[]{:S(2)}) collective-permute-start(bf16[144,768]{1,0:T(8,128)(2,1)S(1)} %pack_up.1.refs_0_), channel_id=1, source_target_pairs={{0,8},{4,12},{8,16},{12,20},{16,24},{20,28},{24,0},{28,4},{1,9},{5... | collective-permute-start | bytes 663560 | tf_op jit(solution)/shard_map/ppermute | solution.py:666
  26.0 17.1 %collective-permute-start.4 = (bf16[3,70,768]{2,1,0:T(8,128)(2,1)S(1)}, bf16[3,70,768]{2,1,0:T(8,128)(2,1)S(1)}, u32[]{:S(2)}, u32[]{:S(2)}) collective-permute-start(bf16[3,70,768]{2,1,0:T(8,128)(2,1)S(1)} %copy-done), channel_id=1, source_target_pairs={{0,1},{1,0},{2,3},{3,2},{4,5},{5,4},{6,7},{7,6},{8,9},{9,8},{10,11... | collective-permute-start | bytes 967688 | tf_op jit(solution)/shard_map/ppermute | solution.py:660
  28.8 13.1 %collective-permute-start.15 = (bf16[144,768]{1,0:T(8,128)(2,1)S(1)}, bf16[144,768]{1,0:T(8,128)(2,1)S(1)}, u32[]{:S(2)}, u32[]{:S(2)}) collective-permute-start(bf16[144,768]{1,0:T(8,128)(2,1)S(1)} %pack_up.1.refs_0_), channel_id=1, source_target_pairs={{0,24},{4,28},{8,0},{12,4},{16,8},{20,12},{24,16},{28,20},{1,25},{... | collective-permute-start | bytes 663560 | tf_op jit(solution)/shard_map/ppermute | solution.py:666
  32.3 9.6 %collective-permute-start.16 = (bf16[144,768]{1,0:T(8,128)(2,1)S(1)}, bf16[144,768]{1,0:T(8,128)(2,1)S(1)}, u32[]{:S(2)}, u32[]{:S(2)}) collective-permute-start(bf16[144,768]{1,0:T(8,128)(2,1)S(1)} %pack_up.1.refs_0_), channel_id=1, source_target_pairs={{0,4},{4,0},{8,12},{12,8},{16,20},{20,16},{24,28},{28,24},{1,5},{5... | collective-permute-start | bytes 663560 | tf_op jit(solution)/shard_map/ppermute | solution.py:663
  32.3 19.0 %collective-permute-start.6 = (bf16[3,70,768]{2,1,0:T(8,128)(2,1)S(1)}, bf16[3,70,768]{2,1,0:T(8,128)(2,1)S(1)}, u32[]{:S(2)}, u32[]{:S(2)}) collective-permute-start(bf16[3,70,768]{2,1,0:T(8,128)(2,1)S(1)} %collective-permute-done.5.refs_2_), channel_id=1, source_target_pairs={{0,1},{1,0},{2,3},{3,2},{4,5},{5,4},{6,7},{7,6},{8,9},{9,8},{10,11... | collective-permute-start | bytes 967688 | tf_op jit(solution)/shard_map/ppermute | solution.py:660
  32.8 10.3 %collective-permute-start.14 = (bf16[144,768]{1,0:T(8,128)(2,1)S(1)}, bf16[144,768]{1,0:T(8,128)(2,1)S(1)}, u32[]{:S(2)}, u32[]{:S(2)}) collective-permute-start(bf16[144,768]{1,0:T(8,128)(2,1)S(1)} %collective-permute-done.13.refs_1_), channel_id=1, source_target_pairs={{0,8},{4,12},{8,16},{12,20},{16,24},{20,28},{24,0},{28,4},{1,9},{5... | collective-permute-start | bytes 663560 | tf_op jit(solution)/shard_map/ppermute | solution.py:666
  32.8 19.5 %copy-start.3 = (bf16[96,640]{1,0:T(8,128)(2,1)S(1)}, bf16[96,640]{1,0:T(8,128)(2,1)}, u32[]{:S(2)}) copy-start(bf16[96,640]{1,0:T(8,128)(2,1)} %pack.1.refs_3_) | copy-start | bytes 368644
  32.8 19.5 %copy-start.5 = (s32[3,40]{1,0:T(4,128)S(1)}, s32[3,40]{1,0:T(4,128)}, u32[]{:S(2)}) copy-start(s32[3,40]{1,0:T(4,128)} %refs_0_.5) | copy-start | bytes 1444
  32.8 19.5 %copy-start.6 = (s32[3]{0:T(128)S(1)}, s32[3]{0:T(128)}, u32[]{:S(2)}) copy-start(s32[3]{0:T(128)} %refs_1_.5) | copy-start | bytes 40
  41.9 6.7 %collective-permute-start.27 = (bf16[96,768]{1,0:T(8,128)(2,1)S(1)}, bf16[96,768]{1,0:T(8,128)(2,1)S(1)}, u32[]{:S(2)}, u32[]{:S(2)}) collective-permute-start(bf16[96,768]{1,0:T(8,128)(2,1)S(1)} %join_down.1.refs_3_), channel_id=1, source_target_pairs={{0,8},{4,12},{8,16},{12,20},{16,24},{20,28},{24,0},{28,4},{1,9},{5... | collective-permute-start | bytes 442376 | tf_op jit(solution)/shard_map/ppermute | solution.py:666
  41.9 6.7 %collective-permute-start.19 = (bf16[144,768]{1,0:T(8,128)(2,1)S(1)}, bf16[144,768]{1,0:T(8,128)(2,1)S(1)}, u32[]{:S(2)}, u32[]{:S(2)}) collective-permute-start(bf16[144,768]{1,0:T(8,128)(2,1)S(1)} %collective-permute-done.15.refs_3_), channel_id=1, source_target_pairs={{0,4},{4,0},{8,12},{12,8},{16,20},{20,16},{24,28},{28,24},{1,5},{5... | collective-permute-start | bytes 663560 | tf_op jit(solution)/shard_map/ppermute | solution.py:663
  43.0 20.1 %collective-permute-start.22 = (bf16[3,70,768]{2,1,0:T(8,128)(2,1)S(1)}, bf16[3,70,768]{2,1,0:T(8,128)(2,1)S(1)}, u32[]{:S(2)}, u32[]{:S(2)}) collective-permute-start(bf16[3,70,768]{2,1,0:T(8,128)(2,1)S(1)} %copy-done.1), channel_id=1, source_target_pairs={{0,2},{1,3},{2,0},{3,1},{4,6},{5,7},{6,4},{7,5},{8,10},{9,11},{10,... | collective-permute-start | bytes 967688 | tf_op jit(solution)/shard_map/ppermute | solution.py:660
  43.1 16.8 %collective-permute-start.17 = (bf16[144,768]{1,0:T(8,128)(2,1)S(1)}, bf16[144,768]{1,0:T(8,128)(2,1)S(1)}, u32[]{:S(2)}, u32[]{:S(2)}) collective-permute-start(bf16[144,768]{1,0:T(8,128)(2,1)S(1)} %collective-permute-done.13.refs_1_), channel_id=1, source_target_pairs={{0,4},{4,0},{8,12},{12,8},{16,20},{20,16},{24,28},{28,24},{1,5},{5... | collective-permute-start | bytes 663560 | tf_op jit(solution)/shard_map/ppermute | solution.py:663
  48.6 14.5 %collective-permute-start.18 = (bf16[144,768]{1,0:T(8,128)(2,1)S(1)}, bf16[144,768]{1,0:T(8,128)(2,1)S(1)}, u32[]{:S(2)}, u32[]{:S(2)}) collective-permute-start(bf16[144,768]{1,0:T(8,128)(2,1)S(1)} %collective-permute-done.14.refs_2_), channel_id=1, source_target_pairs={{0,4},{4,0},{8,12},{12,8},{16,20},{20,16},{24,28},{28,24},{1,5},{5... | collective-permute-start | bytes 663560 | tf_op jit(solution)/shard_map/ppermute | solution.py:663
  48.6 14.8 %collective-permute-start.29 = (bf16[96,768]{1,0:T(8,128)(2,1)S(1)}, bf16[96,768]{1,0:T(8,128)(2,1)S(1)}, u32[]{:S(2)}, u32[]{:S(2)}) collective-permute-start(bf16[96,768]{1,0:T(8,128)(2,1)S(1)} %join_down.1.refs_3_), channel_id=1, source_target_pairs={{0,24},{4,28},{8,0},{12,4},{16,8},{20,12},{24,16},{28,20},{1,25},{... | collective-permute-start | bytes 442376 | tf_op jit(solution)/shard_map/ppermute | solution.py:666
  51.3 12.6 %collective-permute-start.28 = (bf16[96,768]{1,0:T(8,128)(2,1)S(1)}, bf16[96,768]{1,0:T(8,128)(2,1)S(1)}, u32[]{:S(2)}, u32[]{:S(2)}) collective-permute-start(bf16[96,768]{1,0:T(8,128)(2,1)S(1)} %collective-permute-done.27.refs_0_.refs_4_), channel_id=1, source_target_pairs={{0,8},{4,12},{8,16},{12,20},{16,24},{20,28},{24,0},{28,4},{1,9},{5... | collective-permute-start | bytes 442376 | tf_op jit(solution)/shard_map/ppermute | solution.py:666
  59.8 4.6 %collective-permute-start.21 = (bf16[3,70,768]{2,1,0:T(8,128)(2,1)S(1)}, bf16[3,70,768]{2,1,0:T(8,128)(2,1)S(1)}, u32[]{:S(2)}, u32[]{:S(2)}) collective-permute-start(bf16[3,70,768]{2,1,0:T(8,128)(2,1)S(1)} %copy-done.1), channel_id=1, source_target_pairs={{0,1},{1,0},{2,3},{3,2},{4,5},{5,4},{6,7},{7,6},{8,9},{9,8},{10,11... | collective-permute-start | bytes 967688 | tf_op jit(solution)/shard_map/ppermute | solution.py:660
  63.1 10.2 %collective-permute-start.25 = (bf16[480,384]{1,0:T(8,128)(2,1)S(1)}, bf16[480,384]{1,0:T(8,128)(2,1)S(1)}, u32[]{:S(2)}, u32[]{:S(2)}) collective-permute-start(bf16[480,384]{1,0:T(8,128)(2,1)S(1)} %get-tuple-element.134.refs_4_), channel_id=1, source_target_pairs={{0,2},{1,3},{2,0},{3,1},{4,6},{5,7},{6,4},{7,5},{8,10},{9,11},{10,... | collective-permute-start | bytes 1105928 | tf_op jit(solution)/shard_map/ppermute | solution.py:660
  63.1 11.0 %collective-permute-start.23 = (bf16[3,70,768]{2,1,0:T(8,128)(2,1)S(1)}, bf16[3,70,768]{2,1,0:T(8,128)(2,1)S(1)}, u32[]{:S(2)}, u32[]{:S(2)}) collective-permute-start(bf16[3,70,768]{2,1,0:T(8,128)(2,1)S(1)} %collective-permute-done.22.refs_4_), channel_id=1, source_target_pairs={{0,1},{1,0},{2,3},{3,2},{4,5},{5,4},{6,7},{7,6},{8,9},{9,8},{10,11... | collective-permute-start | bytes 967688 | tf_op jit(solution)/shard_map/ppermute | solution.py:660
  63.5 11.1 %collective-permute-start.20 = (bf16[768,384]{1,0:T(8,128)(2,1)S(1)}, bf16[768,384]{1,0:T(8,128)(2,1)S(1)}, u32[]{:S(2)}, u32[]{:S(2)}) collective-permute-start(bf16[768,384]{1,0:T(8,128)(2,1)S(1)} %get-tuple-element.131.refs_0_), channel_id=1, source_target_pairs={{0,1},{1,0},{2,3},{3,2},{4,5},{5,4},{6,7},{7,6},{8,9},{9,8},{10,11... | collective-permute-start | bytes 1769480 | tf_op jit(solution)/shard_map/ppermute | solution.py:660
  64.0 18.6 %collective-permute-start.31 = (bf16[3,96,768]{2,1,0:T(8,128)(2,1)S(1)}, bf16[3,96,768]{2,1,0:T(8,128)(2,1)S(1)}, u32[]{:S(2)}, u32[]{:S(2)}) collective-permute-start(bf16[3,96,768]{2,1,0:T(8,128)(2,1)S(1)} %stack_down.1), channel_id=1, source_target_pairs={{0,4},{4,0},{8,12},{12,8},{16,20},{20,16},{24,28},{28,24},{1,5},{5... | collective-permute-start | bytes 1327112 | tf_op jit(solution)/shard_map/ppermute | solution.py:663
  64.5 10.7 %collective-permute-start.24 = (bf16[480,384]{1,0:T(8,128)(2,1)S(1)}, bf16[480,384]{1,0:T(8,128)(2,1)S(1)}, u32[]{:S(2)}, u32[]{:S(2)}) collective-permute-start(bf16[480,384]{1,0:T(8,128)(2,1)S(1)} %get-tuple-element.134.refs_4_), channel_id=1, source_target_pairs={{0,1},{1,0},{2,3},{3,2},{4,5},{5,4},{6,7},{7,6},{8,9},{9,8},{10,11... | collective-permute-start | bytes 1105928 | tf_op jit(solution)/shard_map/ppermute | solution.py:660
  73.3 2.2 %collective-permute-start.26 = (bf16[480,384]{1,0:T(8,128)(2,1)S(1)}, bf16[480,384]{1,0:T(8,128)(2,1)S(1)}, u32[]{:S(2)}, u32[]{:S(2)}) collective-permute-start(bf16[480,384]{1,0:T(8,128)(2,1)S(1)} %collective-permute-done.25.refs_6_), channel_id=1, source_target_pairs={{0,1},{1,0},{2,3},{3,2},{4,5},{5,4},{6,7},{7,6},{8,9},{9,8},{10,11... | collective-permute-start | bytes 1105928 | tf_op jit(solution)/shard_map/ppermute | solution.py:660
  74.1 8.4 %collective-permute-start.30 = (bf16[96,768]{1,0:T(8,128)(2,1)S(1)}, bf16[96,768]{1,0:T(8,128)(2,1)S(1)}, u32[]{:S(2)}, u32[]{:S(2)}) collective-permute-start(bf16[96,768]{1,0:T(8,128)(2,1)S(1)} %join_down.1.refs_3_), channel_id=1, source_target_pairs={{0,4},{4,0},{8,12},{12,8},{16,20},{20,16},{24,28},{28,24},{1,5},{5... | collective-permute-start | bytes 442376 | tf_op jit(solution)/shard_map/ppermute | solution.py:663
  85.9 2.3 %collective-permute-start.32 = (bf16[2,240,768]{2,1,0:T(8,128)(2,1)S(1)}, bf16[2,240,768]{2,1,0:T(8,128)(2,1)S(1)}, u32[]{:S(2)}, u32[]{:S(2)}) collective-permute-start(bf16[2,240,768]{2,1,0:T(8,128)(2,1)S(1)} %get-tuple-element.146), channel_id=1, source_target_pairs={{0,1},{1,0},{2,3},{3,2},{4,5},{5,4},{6,7},{7,6},{8,9},{9,8},{10,11... | collective-permute-start | bytes 2211848 | tf_op jit(solution)/shard_map/ppermute | solution.py:660
  86.3 17.8 %collective-permute-start.34 = (bf16[4,96,768]{2,1,0:T(8,128)(2,1)S(1)}, bf16[4,96,768]{2,1,0:T(8,128)(2,1)S(1)}, u32[]{:S(2)}, u32[]{:S(2)}) collective-permute-start(bf16[4,96,768]{2,1,0:T(8,128)(2,1)S(1)} %get-tuple-element.159), channel_id=1, source_target_pairs={{0,4},{4,0},{8,12},{12,8},{16,20},{20,16},{24,28},{28,24},{1,5},{5... | collective-permute-start | bytes 1769480 | tf_op jit(solution)/shard_map/ppermute | solution.py:663
  88.3 9.9 %collective-permute-start.33 = (bf16[240,768]{1,0:T(8,128)(2,1)S(1)}, bf16[240,768]{1,0:T(8,128)(2,1)S(1)}, u32[]{:S(2)}, u32[]{:S(2)}) collective-permute-start(bf16[240,768]{1,0:T(8,128)(2,1)S(1)} %pair2.1), channel_id=1, source_target_pairs={{0,2},{1,3},{2,0},{3,1},{4,6},{5,7},{6,4},{7,5},{8,10},{9,11},{10,... | collective-permute-start | bytes 1105928 | tf_op jit(solution)/shard_map/ppermute | solution.py:660
  89.9 29.2 %collective-permute-start.38 = (bf16[4,96,768]{2,1,0:T(8,128)(2,1)S(1)}, bf16[4,96,768]{2,1,0:T(8,128)(2,1)S(1)}, u32[]{:S(2)}, u32[]{:S(2)}) collective-permute-start(bf16[4,96,768]{2,1,0:T(8,128)(2,1)S(1)} %get-tuple-element.169), channel_id=1, source_target_pairs={{0,4},{4,0},{8,12},{12,8},{16,20},{20,16},{24,28},{28,24},{1,5},{5... | collective-permute-start | bytes 1769480 | tf_op jit(solution)/shard_map/ppermute | solution.py:663
  99.3 5.2 %collective-permute-start.35 = (bf16[240,384]{1,0:T(8,128)(2,1)S(1)}, bf16[240,384]{1,0:T(8,128)(2,1)S(1)}, u32[]{:S(2)}, u32[]{:S(2)}) collective-permute-start(bf16[240,384]{1,0:T(8,128)(2,1)S(1)} %get-tuple-element.162), channel_id=1, source_target_pairs={{0,1},{1,0},{2,3},{3,2},{4,5},{5,4},{6,7},{7,6},{8,9},{9,8},{10,11... | collective-permute-start | bytes 552968 | tf_op jit(solution)/shard_map/ppermute | solution.py:660
  100.6 7.6 %collective-permute-start.36 = (bf16[240,384]{1,0:T(8,128)(2,1)S(1)}, bf16[240,384]{1,0:T(8,128)(2,1)S(1)}, u32[]{:S(2)}, u32[]{:S(2)}) collective-permute-start(bf16[240,384]{1,0:T(8,128)(2,1)S(1)} %get-tuple-element.163), channel_id=1, source_target_pairs={{0,2},{1,3},{2,0},{3,1},{4,6},{5,7},{6,4},{7,5},{8,10},{9,11},{10,... | collective-permute-start | bytes 552968 | tf_op jit(solution)/shard_map/ppermute | solution.py:660
  100.6 10.6 %collective-permute-start.37 = (bf16[240,384]{1,0:T(8,128)(2,1)S(1)}, bf16[240,384]{1,0:T(8,128)(2,1)S(1)}, u32[]{:S(2)}, u32[]{:S(2)}) collective-permute-start(bf16[240,384]{1,0:T(8,128)(2,1)S(1)} %get-tuple-element.164), channel_id=1, source_target_pairs={{0,3},{1,2},{2,1},{3,0},{4,7},{5,6},{6,5},{7,4},{8,11},{9,10},{10,... | collective-permute-start | bytes 552968 | tf_op jit(solution)/shard_map/ppermute | solution.py:660
  104.3 17.7 %collective-permute-start.40 = (bf16[96,768]{1,0:T(8,128)(2,1)S(1)}, bf16[96,768]{1,0:T(8,128)(2,1)S(1)}, u32[]{:S(2)}, u32[]{:S(2)}) collective-permute-start(bf16[96,768]{1,0:T(8,128)(2,1)S(1)} %get-tuple-element.174), channel_id=1, source_target_pairs={{0,8},{4,12},{8,16},{12,20},{16,24},{20,28},{24,0},{28,4},{1,9},{5... | collective-permute-start | bytes 442376 | tf_op jit(solution)/shard_map/ppermute | solution.py:666
  104.4 17.5 %collective-permute-start.41 = (bf16[96,768]{1,0:T(8,128)(2,1)S(1)}, bf16[96,768]{1,0:T(8,128)(2,1)S(1)}, u32[]{:S(2)}, u32[]{:S(2)}) collective-permute-start(bf16[96,768]{1,0:T(8,128)(2,1)S(1)} %get-tuple-element.175), channel_id=1, source_target_pairs={{0,16},{4,20},{8,24},{12,28},{16,0},{20,4},{24,8},{28,12},{1,17},{... | collective-permute-start | bytes 442376 | tf_op jit(solution)/shard_map/ppermute | solution.py:666
  108.2 13.9 %collective-permute-start.42 = (bf16[96,768]{1,0:T(8,128)(2,1)S(1)}, bf16[96,768]{1,0:T(8,128)(2,1)S(1)}, u32[]{:S(2)}, u32[]{:S(2)}) collective-permute-start(bf16[96,768]{1,0:T(8,128)(2,1)S(1)} %get-tuple-element.176), channel_id=1, source_target_pairs={{0,24},{4,28},{8,0},{12,4},{16,8},{20,12},{24,16},{28,20},{1,25},{... | collective-permute-start | bytes 442376 | tf_op jit(solution)/shard_map/ppermute | solution.py:666
  113.9 7.9 %collective-permute-start.39 = (bf16[4,96,384]{2,1,0:T(8,128)(2,1)S(1)}, bf16[4,96,384]{2,1,0:T(8,128)(2,1)S(1)}, u32[]{:S(2)}, u32[]{:S(2)}) collective-permute-start(bf16[4,96,384]{2,1,0:T(8,128)(2,1)S(1)} %get-tuple-element.171), channel_id=1, source_target_pairs={{0,4},{4,0},{8,12},{12,8},{16,20},{20,16},{24,28},{28,24},{1,5},{5... | collective-permute-start | bytes 884744 | tf_op jit(solution)/shard_map/ppermute | solution.py:663
  124.5 12.5 %collective-permute-start.46 = (bf16[2,480,768]{2,1,0:T(8,128)(2,1)S(1)}, bf16[2,480,768]{2,1,0:T(8,128)(2,1)S(1)}, u32[]{:S(2)}, u32[]{:S(2)}) collective-permute-start(bf16[2,480,768]{2,1,0:T(8,128)(2,1)S(1)} %get-tuple-element.192), channel_id=1, source_target_pairs={{0,1},{1,0},{2,3},{3,2},{4,5},{5,4},{6,7},{7,6},{8,9},{9,8},{10,11... | collective-permute-start | bytes 4423688 | tf_op jit(solution)/shard_map/ppermute | solution.py:660
  127.2 18.2 %collective-permute-start.43 = (bf16[4,96,384]{2,1,0:T(8,128)(2,1)S(1)}, bf16[4,96,384]{2,1,0:T(8,128)(2,1)S(1)}, u32[]{:S(2)}, u32[]{:S(2)}) collective-permute-start(bf16[4,96,384]{2,1,0:T(8,128)(2,1)S(1)} %get-tuple-element.189), channel_id=1, source_target_pairs={{0,4},{4,0},{8,12},{12,8},{16,20},{20,16},{24,28},{28,24},{1,5},{5... | collective-permute-start | bytes 884744 | tf_op jit(solution)/shard_map/ppermute | solution.py:663
  128.0 1.2 collective-permute-start.44
  129.3 7.7 %collective-permute-start.45 = (f32[16,768]{1,0:T(8,128)S(1)}, f32[16,768]{1,0:T(8,128)S(1)}, u32[]{:S(2)}, u32[]{:S(2)}) collective-permute-start(f32[16,768]{1,0:T(8,128)S(1)} %add_core.1.refs_0_), channel_id=1, source_target_pairs={{0,2},{1,3},{2,0},{3,1},{4,6},{5,7},{6,4},{7,5},{8,10},{9,11},{10,... | collective-permute-start | bytes 147464 | tf_op jit(solution)/shard_map/ppermute | solution.py:660
  129.4 9.2 %collective-permute-start.52 = (bf16[96,384]{1,0:T(8,128)(2,1)S(1)}, bf16[96,384]{1,0:T(8,128)(2,1)S(1)}, u32[]{:S(2)}, u32[]{:S(2)}) collective-permute-start(bf16[96,384]{1,0:T(8,128)(2,1)S(1)} %get-tuple-element.177), channel_id=1, source_target_pairs={{0,0},{1,8},{2,16},{3,24},{4,4},{5,12},{6,20},{7,28},{8,1},{9,9},{... | collective-permute-start | bytes 221192 | tf_op jit(solution)/shard_map/ppermute | solution.py:700
  136.4 8.3 %collective-permute-start.53 = (bf16[96,384]{1,0:T(8,128)(2,1)S(1)}, bf16[96,384]{1,0:T(8,128)(2,1)S(1)}, u32[]{:S(2)}, u32[]{:S(2)}) collective-permute-start(bf16[96,384]{1,0:T(8,128)(2,1)S(1)} %get-tuple-element.207), channel_id=1, source_target_pairs={{0,4},{1,12},{2,20},{3,28},{4,0},{5,8},{6,16},{7,24},{8,5},{9,13},... | collective-permute-start | bytes 221192 | tf_op jit(solution)/shard_map/ppermute | solution.py:700
  137.1 10.0 %collective-permute-start.47 = (f32[16,768]{1,0:T(8,128)S(1)}, f32[16,768]{1,0:T(8,128)S(1)}, u32[]{:S(2)}, u32[]{:S(2)}) collective-permute-start(f32[16,768]{1,0:T(8,128)S(1)} %add_far.1.refs_2_), channel_id=1, source_target_pairs={{0,4},{4,0},{8,12},{12,8},{16,20},{20,16},{24,28},{28,24},{1,5},{5... | collective-permute-start | bytes 147464 | tf_op jit(solution)/shard_map/ppermute | solution.py:663
  137.9 9.4 %collective-permute-start.48 = (bf16[144,768]{1,0:T(8,128)(2,1)S(1)}, bf16[144,768]{1,0:T(8,128)(2,1)S(1)}, u32[]{:S(2)}, u32[]{:S(2)}) collective-permute-start(bf16[144,768]{1,0:T(8,128)(2,1)S(1)} %get-tuple-element.197), channel_id=1, source_target_pairs={{0,8},{4,12},{8,16},{12,20},{16,24},{20,28},{24,0},{28,4},{1,9},{5... | collective-permute-start | bytes 663560 | tf_op jit(solution)/shard_map/ppermute | solution.py:666
  138.6 17.6 %collective-permute-start.49 = (bf16[144,768]{1,0:T(8,128)(2,1)S(1)}, bf16[144,768]{1,0:T(8,128)(2,1)S(1)}, u32[]{:S(2)}, u32[]{:S(2)}) collective-permute-start(bf16[144,768]{1,0:T(8,128)(2,1)S(1)} %get-tuple-element.198), channel_id=1, source_target_pairs={{0,16},{4,20},{8,24},{12,28},{16,0},{20,4},{24,8},{28,12},{1,17},{... | collective-permute-start | bytes 663560 | tf_op jit(solution)/shard_map/ppermute | solution.py:666
  144.7 20.7 %collective-permute-start.50 = (bf16[144,768]{1,0:T(8,128)(2,1)S(1)}, bf16[144,768]{1,0:T(8,128)(2,1)S(1)}, u32[]{:S(2)}, u32[]{:S(2)}) collective-permute-start(bf16[144,768]{1,0:T(8,128)(2,1)S(1)} %get-tuple-element.199), channel_id=1, source_target_pairs={{0,24},{4,28},{8,0},{12,4},{16,8},{20,12},{24,16},{28,20},{1,25},{... | collective-permute-start | bytes 663560 | tf_op jit(solution)/shard_map/ppermute | solution.py:666
  145.5 25.3 %collective-permute-start.51 = (bf16[480,768]{1,0:T(8,128)(2,1)S(1)}, bf16[480,768]{1,0:T(8,128)(2,1)S(1)}, u32[]{:S(2)}, u32[]{:S(2)}) collective-permute-start(bf16[480,768]{1,0:T(8,128)(2,1)S(1)} %pair1.1), channel_id=1, source_target_pairs={{0,2},{1,3},{2,0},{3,1},{4,6},{5,7},{6,4},{7,5},{8,10},{9,11},{10,... | collective-permute-start | bytes 2211848 | tf_op jit(solution)/shard_map/ppermute | solution.py:660
  147.2 19.1 %collective-permute-start.55 = (bf16[128,384]{1,0:T(8,128)(2,1)S(1)}, bf16[128,384]{1,0:T(8,128)(2,1)S(1)}, u32[]{:S(2)}, u32[]{:S(2)}) collective-permute-start(bf16[128,384]{1,0:T(8,128)(2,1)S(1)} %get-tuple-element.212), channel_id=1, source_target_pairs={{0,16},{4,20},{8,24},{12,28},{16,0},{20,4},{24,8},{28,12},{1,17},{... | collective-permute-start | bytes 294920 | tf_op jit(solution)/shard_map/ppermute | solution.py:666
  147.3 19.0 %collective-permute-start.56 = (bf16[128,384]{1,0:T(8,128)(2,1)S(1)}, bf16[128,384]{1,0:T(8,128)(2,1)S(1)}, u32[]{:S(2)}, u32[]{:S(2)}) collective-permute-start(bf16[128,384]{1,0:T(8,128)(2,1)S(1)} %get-tuple-element.213), channel_id=1, source_target_pairs={{0,24},{4,28},{8,0},{12,4},{16,8},{20,12},{24,16},{28,20},{1,25},{... | collective-permute-start | bytes 294920 | tf_op jit(solution)/shard_map/ppermute | solution.py:666
  156.2 13.8 %collective-permute-start.54 = (bf16[128,384]{1,0:T(8,128)(2,1)S(1)}, bf16[128,384]{1,0:T(8,128)(2,1)S(1)}, u32[]{:S(2)}, u32[]{:S(2)}) collective-permute-start(bf16[128,384]{1,0:T(8,128)(2,1)S(1)} %get-tuple-element.211), channel_id=1, source_target_pairs={{0,8},{4,12},{8,16},{12,20},{16,24},{20,28},{24,0},{28,4},{1,9},{5... | collective-permute-start | bytes 294920 | tf_op jit(solution)/shard_map/ppermute | solution.py:666
  (1 other events, 6.9 us)

commit v5 on v4

--- a/solution.py
+++ b/solution.py
@@ -226,7 +226,7 @@
             packed[ds(b * half, half), m.WH + h * m.hd : m.WH + (h + 1) * m.hd] = o[half:]
         return carry
 
-    lax.fori_loop(0, m.B, item, 0)
+    lax.fori_loop(0, m.B, item, 0, unroll=True)
 
 
 def assemble_kernel(m, nparts, *refs):
@@ -426,7 +426,7 @@
             g_value[at, lanes] = t_dot(probs[b * m.H + h], g_mixed[at, lanes]).astype(LOW)
         return carry
 
-    lax.fori_loop(0, m.B, item, 0)
+    lax.fori_loop(0, m.B, item, 0, unroll=True)
     total[:, : m.WH] = t_dot(normed[...], g_value[...])
     g_out = t_dot(mixed[...], ga_scr[...])
     for e in range(m.S):
@@ -451,7 +451,7 @@
             g_qk[at, m.WH + h * m.hd : m.WH + (h + 1) * m.hd] = (t_dot(gs, q) * scale).astype(LOW)
         return carry
 
-    lax.fori_loop(0, m.B, item, 0)
+    lax.fori_loop(0, m.B, item, 0, unroll=True)
 
 
 def input_back_kernel(m, sc, g_qk, g_value, xhat, w, vec_mid, vec_ff, b_keep1, b_send, keep0, keep1, send, v_scr):

time: 173 us -> 172 us (level)
  transfers between devices with their start and end apart: 57 -> 57, of which waited for: 16 -> 16; matrix products, arithmetic and copies ran while one was open for 0% -> 0% of each run, Pallas kernels for 19% -> 18%
where the time goes in v5:
time: 172 us
  starting transfers between devices  67.9 us (39%)
  waiting for transfers between devices  62.3 us (36%)
  Pallas kernels  40.3 us (23%)
    pallas_call x31, Pallas kernels, pallas(): pl.pallas_call(run, out_shape=outs, in_specs=[pl.BlockSpec(memory_space=p...  40.3 us
    ppermute x18, waiting for transfers between devices, z_shift(): return lax.ppermute(x, 'dp', [(i, (i + 2 * k) % N) for i in range(N)])  29.2 us
    ppermute x18, starting transfers between devices, z_shift(): return lax.ppermute(x, 'dp', [(i, (i + 2 * k) % N) for i in range(N)])  27.3 us
    ppermute x20, waiting for transfers between devices, seq_to(): return lax.ppermute(x, 'seq', [(i, i ^ e) for i in range(S)])  19.2 us
    ppermute x20, starting transfers between devices, seq_to(): return lax.ppermute(x, 'seq', [(i, i ^ e) for i in range(S)])  16.2 us
    ppermute x4, starting transfers between devices, exchange(): return lax.ppermute(x, ('dp', 'seq'), pairs)  15 us
    ppermute x4, waiting for transfers between devices, exchange(): return lax.ppermute(x, ('dp', 'seq'), pairs)  10.8 us
    ppermute x15, starting transfers between devices, x_swap(): return lax.ppermute(x, 'dp', [(i, i ^ 1) for i in range(N)])  9.45 us
  transfers between devices with their start and end apart: 57, of which 16 were waited for; matrix products, arithmetic and copies ran while one was open for 0% of the time, Pallas kernels for 18%

profile of v5, /device:TPU:5, one launch (start us, length us, event | category | flops | bytes accessed | tf_op | source)
XLA Modules:
  0.0 171.7 jit_solution(13992595507405726690)
XLA Ops:
  0.7 1.9 %pack.1.refs_3_ = bf16[96,640]{1,0:T(8,128)(2,1)} custom-call(bf16[96,192]{1,0:T(8,128)(2,1)} %refs_0_.2, bf16[96,192]{1,0:T(8,128)(2,1)} %refs_1_.3, bf16[96,192]{1,0:T(8,128)(2,1)} %refs_2_.1, bf16[96]{0:T(256)(128)(2,1)} %refs_3_.2, bf16[96]{0:T(256)(128)(2,1)} %refs_4_.1, bf16[96]{0:T(256)(128)(2,1)} %refs_5_.1, bf16[96]{0:T(256)(128)(2,1)} %refs_6_.1, ...), custom_call_target="tpu_custom_call" | custom-call | flops 3000000000 | bytes 235776 | tf_op jit(solution)/shard_map/pack/pallas_call | solution.py:58
  2.6 1.3 collective-permute-start.1
  3.9 1.2 collective-permute-start.9
  5.1 2.0 %collective-permute-start.8 = (bf16[96,640]{1,0:T(8,128)(2,1)}, bf16[96,640]{1,0:T(8,128)(2,1)S(1)}, u32[]{:S(2)}, u32[]{:S(2)}) collective-permute-start(bf16[96,640]{1,0:T(8,128)(2,1)} %pack.1.refs_3_), channel_id=1, source_target_pairs={{0,24},{4,28},{8,0},{12,4},{16,8},{20,12},{24,16},{28,20},{1,25},{... | collective-permute-start | bytes 368648 | tf_op jit(solution)/shard_map/ppermute | solution.py:666
  7.8 1.1 collective-permute-done.1.refs_4_
  9.4 3.1 %collective-permute-done.8.refs_6_ = bf16[96,640]{1,0:T(8,128)(2,1)S(1)} collective-permute-done((bf16[96,640]{1,0:T(8,128)(2,1)}, bf16[96,640]{1,0:T(8,128)(2,1)S(1)}, u32[]{:S(2)}, u32[]{:S(2)}) %collective-permute-start.8) | collective-permute-done | bytes 122912 | tf_op jit(solution)/shard_map/ppermute | solution.py:666
  12.5 5.5 %collective-permute-start.2 = (bf16[96,384]{1,0:T(8,128)(2,1)S(1)}, bf16[96,384]{1,0:T(8,128)(2,1)S(1)}, u32[]{:S(2)}, u32[]{:S(2)}) collective-permute-start(bf16[96,384]{1,0:T(8,128)(2,1)S(1)} %get-tuple-element.126), channel_id=1, source_target_pairs={{0,0},{1,8},{2,16},{3,24},{4,4},{5,12},{6,20},{7,28},{8,1},{9,9},{... | collective-permute-start | bytes 221192 | tf_op jit(solution)/shard_map/ppermute | solution.py:700
  18.0 0.5 collective-permute-start.12
  18.5 1.9 %collective-permute-start.3 = (bf16[96,384]{1,0:T(8,128)(2,1)S(1)}, bf16[96,384]{1,0:T(8,128)(2,1)S(1)}, u32[]{:S(2)}, u32[]{:S(2)}) collective-permute-start(bf16[96,384]{1,0:T(8,128)(2,1)S(1)} %get-tuple-element.127), channel_id=1, source_target_pairs={{0,4},{1,12},{2,20},{3,28},{4,0},{5,8},{6,16},{7,24},{8,5},{9,13},... | collective-permute-start | bytes 221192 | tf_op jit(solution)/shard_map/ppermute | solution.py:700
  20.4 0.7 collective-permute-start.11
  21.1 0.7 collective-permute-start.10
  21.9 4.0 %collective-permute-done.3.refs_1_ = bf16[96,384]{1,0:T(8,128)(2,1)S(1)} collective-permute-done((bf16[96,384]{1,0:T(8,128)(2,1)S(1)}, bf16[96,384]{1,0:T(8,128)(2,1)S(1)}, u32[]{:S(2)}, u32[]{:S(2)}) %collective-permute-start.3) | collective-permute-done | bytes 73760 | tf_op jit(solution)/shard_map/ppermute | solution.py:700
  26.0 2.8 %collective-permute-start.4 = (bf16[3,70,768]{2,1,0:T(8,128)(2,1)S(1)}, bf16[3,70,768]{2,1,0:T(8,128)(2,1)S(1)}, u32[]{:S(2)}, u32[]{:S(2)}) collective-permute-start(bf16[3,70,768]{2,1,0:T(8,128)(2,1)S(1)} %copy-done), channel_id=1, source_target_pairs={{0,1},{1,0},{2,3},{3,2},{4,5},{5,4},{6,7},{7,6},{8,9},{9,8},{10,11... | collective-permute-start | bytes 967688 | tf_op jit(solution)/shard_map/ppermute | solution.py:660
  28.8 3.5 %collective-permute-start.15 = (bf16[144,768]{1,0:T(8,128)(2,1)S(1)}, bf16[144,768]{1,0:T(8,128)(2,1)S(1)}, u32[]{:S(2)}, u32[]{:S(2)}) collective-permute-start(bf16[144,768]{1,0:T(8,128)(2,1)S(1)} %pack_up.1.refs_0_), channel_id=1, source_target_pairs={{0,24},{4,28},{8,0},{12,4},{16,8},{20,12},{24,16},{28,20},{1,25},{... | collective-permute-start | bytes 663560 | tf_op jit(solution)/shard_map/ppermute | solution.py:666
  32.8 9.1 %collective-permute-done.15.refs_3_ = bf16[144,768]{1,0:T(8,128)(2,1)S(1)} collective-permute-done((bf16[144,768]{1,0:T(8,128)(2,1)S(1)}, bf16[144,768]{1,0:T(8,128)(2,1)S(1)}, u32[]{:S(2)}, u32[]{:S(2)}) %collective-permute-start.15) | collective-permute-done | bytes 221216 | tf_op jit(solution)/shard_map/ppermute | solution.py:666
  41.9 1.2 collective-permute-start.19
  43.4 5.2 %collective-permute-done.27.refs_0_.refs_4_ = bf16[96,768]{1,0:T(8,128)(2,1)S(1)} collective-permute-done((bf16[96,768]{1,0:T(8,128)(2,1)S(1)}, bf16[96,768]{1,0:T(8,128)(2,1)S(1)}, u32[]{:S(2)}, u32[]{:S(2)}) %collective-permute-start.27) | collective-permute-done | bytes 147488 | tf_op jit(solution)/shard_map/ppermute | solution.py:666
  48.6 2.7 %collective-permute-start.29 = (bf16[96,768]{1,0:T(8,128)(2,1)S(1)}, bf16[96,768]{1,0:T(8,128)(2,1)S(1)}, u32[]{:S(2)}, u32[]{:S(2)}) collective-permute-start(bf16[96,768]{1,0:T(8,128)(2,1)S(1)} %join_down.1.refs_3_), channel_id=1, source_target_pairs={{0,24},{4,28},{8,0},{12,4},{16,8},{20,12},{24,16},{28,20},{1,25},{... | collective-permute-start | bytes 442376 | tf_op jit(solution)/shard_map/ppermute | solution.py:666
  51.3 0.9 norm.1.refs_2_
  52.3 6.6 %attend.1 = (bf16[960,576]{1,0:T(8,128)(2,1)S(1)}, bf16[960,768]{1,0:T(8,128)(2,1)S(1)}, bf16[9,320,320]{2,1,0:T(8,128)(2,1)S(1)}, bf16[480,384]{1,0:T(8,128)(2,...) custom-call(s32[3,40]{1,0:T(4,128)S(1)} %copy-done.5, s32[3]{0:T(128)S(1)} %copy-done.6, ...), custom_call_target="tpu_custom_call" | custom-call | flops 1000 | bytes 9757164 | tf_op jit(solution)/shard_map/attend/pallas_call | solution.py:58
  58.9 3.3 %collective-permute-start.21 = (bf16[3,70,768]{2,1,0:T(8,128)(2,1)S(1)}, bf16[3,70,768]{2,1,0:T(8,128)(2,1)S(1)}, u32[]{:S(2)}, u32[]{:S(2)}) collective-permute-start(bf16[3,70,768]{2,1,0:T(8,128)(2,1)S(1)} %copy-done.1), channel_id=1, source_target_pairs={{0,1},{1,0},{2,3},{3,2},{4,5},{5,4},{6,7},{7,6},{8,9},{9,8},{10,11... | collective-permute-start | bytes 967688 | tf_op jit(solution)/shard_map/ppermute | solution.py:660
  62.5 0.5 collective-permute-start.20
  63.1 0.5 collective-permute-start.31
  63.9 8.5 %collective-permute-done.25.refs_6_ = bf16[480,384]{1,0:T(8,128)(2,1)S(1)} collective-permute-done((bf16[480,384]{1,0:T(8,128)(2,1)S(1)}, bf16[480,384]{1,0:T(8,128)(2,1)S(1)}, u32[]{:S(2)}, u32[]{:S(2)}) %collective-permute-start.25) | collective-permute-done | bytes 368672 | tf_op jit(solution)/shard_map/ppermute | solution.py:660
  72.4 0.9 collective-permute-start.26
  73.6 0.6 join.1
  74.5 5.5 %forward.1 = (bf16[960,768]{1,0:T(8,128)(2,1)S(1)}, bf16[960,768]{1,0:T(8,128)(2,1)S(1)}, f32[960,768]{1,0:T(8,128)S(1)}, bf16[960,768]{1,0:T(8,128)(2,1)S(1)}, ...) custom-call(bf16[3,70,768]{2,1,0:T(8,128)(2,1)S(1)} %copy-done, ...), custom_call_target="tpu_custom_call" | custom-call | flops 1000 | bytes 14143488 | tf_op jit(solution)/shard_map/forward/pallas_call | solution.py:58
  80.1 1.6 down_grad.1
  81.7 3.3 %hidden_back.1 = (bf16[960,768]{1,0:T(8,128)(2,1)S(1)}, bf16[768,768]{1,0:T(8,128)(2,1)S(1)}, bf16[240,768]{1,0:T(8,128)(2,1)S(1)}, bf16[240,768]{1,0:T(8,128)(2,1)S(1)}, bf16[2,240,768]{2,1,0:T(8,128)(2,1)S(1)}) custom-call(bf16[960,768]{1,0:T(8,128)(2,1)S(1)} %get-tuple-element.133.refs_0_.refs_5_.refs_3_, f32[960,768]{1,0:T(8,128)S(1)} %get-tuple-element.141.refs_1_, ...), custom_call_target="tpu_custom_call" | custom-call | flops 3000000000 | bytes 10911744 | tf_op jit(solution)/shard_map/hidden_back/pallas_call | solution.py:58
  85.4 0.7 collective-permute-start.34
  86.1 1.2 collective-permute-done.32.refs_1_
  87.5 1.6 up_grad.1
  89.0 0.8 collective-permute-start.38
  89.8 7.4 %collective-permute-done.33.refs_2_ = bf16[240,768]{1,0:T(8,128)(2,1)S(1)} collective-permute-done((bf16[240,768]{1,0:T(8,128)(2,1)S(1)}, bf16[240,768]{1,0:T(8,128)(2,1)S(1)}, u32[]{:S(2)}, u32[]{:S(2)}) %collective-permute-start.33) | collective-permute-done | bytes 368672 | tf_op jit(solution)/shard_map/ppermute | solution.py:660
  97.2 1.1 middle.1
  98.4 1.3 collective-permute-start.35
  99.7 1.7 collective-permute-start.37
  101.4 1.8 %branch.1 = (bf16[240,768]{1,0:T(8,128)(2,1)S(1)}, bf16[240,768]{1,0:T(8,128)(2,1)S(1)}, bf16[2,240,768]{2,1,0:T(8,128)(2,1)S(1)}, f32[8,768]{1,0:T(8,128)S(1)}) custom-call(bf16[960,768]{1,0:T(8,128)(2,1)S(1)} %get-tuple-element.154.refs_1_.refs_0_, bf16[768,768]{1,0:T(8,128)(2,1)S(1)} %get-tuple-element.155.refs_1_, ...), custom_call_target="tpu_custom_call" | custom-call | flops 10000000000 | bytes 7102464 | tf_op jit(solution)/shard_map/branch/pallas_call | solution.py:58
  103.5 3.7 %collective-permute-start.41 = (bf16[96,768]{1,0:T(8,128)(2,1)S(1)}, bf16[96,768]{1,0:T(8,128)(2,1)S(1)}, u32[]{:S(2)}, u32[]{:S(2)}) collective-permute-start(bf16[96,768]{1,0:T(8,128)(2,1)S(1)} %get-tuple-element.175), channel_id=1, source_target_pairs={{0,16},{4,20},{8,24},{12,28},{16,0},{20,4},{24,8},{28,12},{1,17},{... | collective-permute-start | bytes 442376 | tf_op jit(solution)/shard_map/ppermute | solution.py:666
  107.3 2.2 %collective-permute-start.42 = (bf16[96,768]{1,0:T(8,128)(2,1)S(1)}, bf16[96,768]{1,0:T(8,128)(2,1)S(1)}, u32[]{:S(2)}, u32[]{:S(2)}) collective-permute-start(bf16[96,768]{1,0:T(8,128)(2,1)S(1)} %get-tuple-element.176), channel_id=1, source_target_pairs={{0,24},{4,28},{8,0},{12,4},{16,8},{20,12},{24,16},{28,20},{1,25},{... | collective-permute-start | bytes 442376 | tf_op jit(solution)/shard_map/ppermute | solution.py:666
  109.4 0.9 collective-permute-done.37.refs_4_
  110.3 3.1 %value_back.1 = (bf16[960,192]{1,0:T(8,128)(2,1)S(1)}, bf16[960,192]{1,0:T(8,128)(2,1)S(1)}, bf16[4,96,384]{2,1,0:T(8,128)(2,1)S(1)}, bf16[4,96,384]{2,1,0:T(8,128)(2,1)S(1)}) custom-call(bf16[9,320,320]{2,1,0:T(8,128)(2,1)S(1)} %get-tuple-element.130.refs_0_.refs_1_, bf16[240,384]{1,0:T(8,128)(2,1)S(1)} %get-tuple-element.161.refs_1_, ...), custom_call_target="tpu_custom_call" | custom-call | flops 10000000000 | bytes 6856704 | tf_op jit(solution)/shard_map/value_back/pallas_call | solution.py:58
  113.4 0.8 collective-permute-start.39
  114.2 4.0 %attend_back.1.refs_0_.refs_1_ = bf16[960,384]{1,0:T(8,128)(2,1)S(1)} custom-call(bf16[960,576]{1,0:T(8,128)(2,1)S(1)} %get-tuple-element.129.refs_0_, bf16[9,320,320]{2,1,0:T(8,128)(2,1)S(1)} %get-tuple-element.130.refs_0_.refs_1_, bf16[960,192]{1,0:T(8,128)(2,1)S(1)} %get-tuple-element.167.refs_2_), custom_call_target="tpu_custom_call" | custom-call | flops 10000000000 | bytes 4055040 | tf_op jit(solution)/shard_map/attend_back/pallas_call | solution.py:58
  118.2 3.1 %collective-permute-done.39.refs_3_ = bf16[4,96,384]{2,1,0:T(8,128)(2,1)S(1)} collective-permute-done((bf16[4,96,384]{2,1,0:T(8,128)(2,1)S(1)}, bf16[4,96,384]{2,1,0:T(8,128)(2,1)S(1)}, u32[]{:S(2)}, u32[]{:S(2)}) %collective-permute-start.39) | collective-permute-done | bytes 294944 | tf_op jit(solution)/shard_map/ppermute | solution.py:663
  121.7 2.1 %input_back.1 = (bf16[240,768]{1,0:T(8,128)(2,1)S(1)}, bf16[480,768]{1,0:T(8,128)(2,1)S(1)}, bf16[2,480,768]{2,1,0:T(8,128)(2,1)S(1)}, f32[16,768]{1,0:T(8,128)S(1)}) custom-call(bf16[960,384]{1,0:T(8,128)(2,1)S(1)} %attend_back.1.refs_0_.refs_1_, bf16[960,192]{1,0:T(8,128)(2,1)S(1)} %get-tuple-element.179.refs_1_, f32[960,768]{1,0:T(8,128)S(1)} %norm.1.refs_2_, ...), custom_call_target="tpu_custom_call" | custom-call | flops 1000 | bytes 8822784 | tf_op jit(solution)/shard_map/input_back/pallas_call | solution.py:58
  123.8 1.7 collective-permute-start.46
  125.4 1.1 qk_grad.1
  126.6 0.8 collective-permute-start.43
  127.7 0.9 collective-permute-done.44.refs_1_
  128.7 7.1 %collective-permute-start.52 = (bf16[96,384]{1,0:T(8,128)(2,1)S(1)}, bf16[96,384]{1,0:T(8,128)(2,1)S(1)}, u32[]{:S(2)}, u32[]{:S(2)}) collective-permute-start(bf16[96,384]{1,0:T(8,128)(2,1)S(1)} %get-tuple-element.177), channel_id=1, source_target_pairs={{0,0},{1,8},{2,16},{3,24},{4,4},{5,12},{6,20},{7,28},{8,1},{9,9},{... | collective-permute-start | bytes 221192 | tf_op jit(solution)/shard_map/ppermute | solution.py:700
  135.8 0.5 collective-permute-start.53
  136.5 0.8 collective-permute-start.47
  137.3 0.6 collective-permute-done.52.refs_0_
  137.9 6.1 %collective-permute-done.53.refs_1_ = bf16[96,384]{1,0:T(8,128)(2,1)S(1)} collective-permute-done((bf16[96,384]{1,0:T(8,128)(2,1)S(1)}, bf16[96,384]{1,0:T(8,128)(2,1)S(1)}, u32[]{:S(2)}, u32[]{:S(2)}) %collective-permute-start.53) | collective-permute-done | bytes 73760 | tf_op jit(solution)/shard_map/ppermute | solution.py:700
  144.1 0.7 give_down.1
  144.8 1.7 collective-permute-start.51
  146.7 1.9 %collective-permute-start.56 = (bf16[128,384]{1,0:T(8,128)(2,1)S(1)}, bf16[128,384]{1,0:T(8,128)(2,1)S(1)}, u32[]{:S(2)}, u32[]{:S(2)}) collective-permute-start(bf16[128,384]{1,0:T(8,128)(2,1)S(1)} %get-tuple-element.213), channel_id=1, source_target_pairs={{0,24},{4,28},{8,0},{12,4},{16,8},{20,12},{24,16},{28,20},{1,25},{... | collective-permute-start | bytes 294920 | tf_op jit(solution)/shard_map/ppermute | solution.py:666
  148.5 7.0 %collective-permute-done.49.refs_3_ = bf16[144,768]{1,0:T(8,128)(2,1)S(1)} collective-permute-done((bf16[144,768]{1,0:T(8,128)(2,1)S(1)}, bf16[144,768]{1,0:T(8,128)(2,1)S(1)}, u32[]{:S(2)}, u32[]{:S(2)}) %collective-permute-start.49) | collective-permute-done | bytes 221216 | tf_op jit(solution)/shard_map/ppermute | solution.py:666
  155.5 9.2 %collective-permute-start.54 = (bf16[128,384]{1,0:T(8,128)(2,1)S(1)}, bf16[128,384]{1,0:T(8,128)(2,1)S(1)}, u32[]{:S(2)}, u32[]{:S(2)}) collective-permute-start(bf16[128,384]{1,0:T(8,128)(2,1)S(1)} %get-tuple-element.211), channel_id=1, source_target_pairs={{0,8},{4,12},{8,16},{12,20},{16,24},{20,28},{24,0},{28,4},{1,9},{5... | collective-permute-start | bytes 294920 | tf_op jit(solution)/shard_map/ppermute | solution.py:666
  164.8 0.9 both_out.1
  165.6 3.7 %collective-permute-done.54.refs_2_ = bf16[128,384]{1,0:T(8,128)(2,1)S(1)} collective-permute-done((bf16[128,384]{1,0:T(8,128)(2,1)S(1)}, bf16[128,384]{1,0:T(8,128)(2,1)S(1)}, u32[]{:S(2)}, u32[]{:S(2)}) %collective-permute-start.54) | collective-permute-done | bytes 98336 | tf_op jit(solution)/shard_map/ppermute | solution.py:666
  169.3 0.8 query_key.1
  170.1 1.5 finish.1
  (97 shorter events, 5.6 us)
Async XLA Ops:
  0.7 8.2 %copy-start = (bf16[3,70,768]{2,1,0:T(8,128)(2,1)S(1)}, bf16[3,70,768]{2,1,0:T(8,128)(2,1)}, u32[]{:S(2)}) copy-start(bf16[3,70,768]{2,1,0:T(8,128)(2,1)} %refs_3_.3) | copy-start | bytes 967684
  0.7 8.7 %copy-start.7 = (bf16[384,192]{0,1:T(8,128)(2,1)S(1)}, bf16[384,192]{0,1:T(8,128)(2,1)}, u32[]{:S(2)}) copy-start(bf16[384,192]{0,1:T(8,128)(2,1)} %param.28) | copy-start | bytes 442372
  2.6 6.3 %collective-permute-start.1 = (bf16[96,640]{1,0:T(8,128)(2,1)}, bf16[96,640]{1,0:T(8,128)(2,1)S(1)}, u32[]{:S(2)}, u32[]{:S(2)}) collective-permute-start(bf16[96,640]{1,0:T(8,128)(2,1)} %pack.1.refs_3_), channel_id=1, source_target_pairs={{0,8},{4,12},{8,16},{12,20},{16,24},{20,28},{24,0},{28,4},{1,9},{5... | collective-permute-start | bytes 368648 | tf_op jit(solution)/shard_map/ppermute | solution.py:666
  3.9 16.5 %collective-permute-start.9 = (bf16[96,640]{1,0:T(8,128)(2,1)}, bf16[96,640]{1,0:T(8,128)(2,1)S(1)}, u32[]{:S(2)}, u32[]{:S(2)}) collective-permute-start(bf16[96,640]{1,0:T(8,128)(2,1)} %pack.1.refs_3_), channel_id=1, source_target_pairs={{0,4},{4,0},{8,12},{12,8},{16,20},{20,16},{24,28},{28,24},{1,5},{5... | collective-permute-start | bytes 368648 | tf_op jit(solution)/shard_map/ppermute | solution.py:663
  5.1 7.4 %collective-permute-start.8 = (bf16[96,640]{1,0:T(8,128)(2,1)}, bf16[96,640]{1,0:T(8,128)(2,1)S(1)}, u32[]{:S(2)}, u32[]{:S(2)}) collective-permute-start(bf16[96,640]{1,0:T(8,128)(2,1)} %pack.1.refs_3_), channel_id=1, source_target_pairs={{0,24},{4,28},{8,0},{12,4},{16,8},{20,12},{24,16},{28,20},{1,25},{... | collective-permute-start | bytes 368648 | tf_op jit(solution)/shard_map/ppermute | solution.py:666
  7.1 11.4 %collective-permute-start.7 = (bf16[96,640]{1,0:T(8,128)(2,1)}, bf16[96,640]{1,0:T(8,128)(2,1)S(1)}, u32[]{:S(2)}, u32[]{:S(2)}) collective-permute-start(bf16[96,640]{1,0:T(8,128)(2,1)} %pack.1.refs_3_), channel_id=1, source_target_pairs={{0,16},{4,20},{8,24},{12,28},{16,0},{20,4},{24,8},{28,12},{1,17},{... | collective-permute-start | bytes 368648 | tf_op jit(solution)/shard_map/ppermute | solution.py:666
  7.5 10.4 %collective-permute-start = (bf16[96,192]{1,0:T(8,128)(2,1)S(1)}, bf16[96,192]{1,0:T(8,128)(2,1)S(1)}, u32[]{:S(2)}, u32[]{:S(2)}) collective-permute-start(bf16[96,192]{1,0:T(8,128)(2,1)S(1)} %copy-done.4), channel_id=1, source_target_pairs={{0,2},{1,3},{2,0},{3,1},{4,6},{5,7},{6,4},{7,5},{8,10},{9,11},{10,... | collective-permute-start | bytes 110600 | tf_op jit(solution)/shard_map/ppermute | solution.py:660
  8.9 23.4 %collective-permute-start.5 = (bf16[3,70,768]{2,1,0:T(8,128)(2,1)S(1)}, bf16[3,70,768]{2,1,0:T(8,128)(2,1)S(1)}, u32[]{:S(2)}, u32[]{:S(2)}) collective-permute-start(bf16[3,70,768]{2,1,0:T(8,128)(2,1)S(1)} %copy-done), channel_id=1, source_target_pairs={{0,2},{1,3},{2,0},{3,1},{4,6},{5,7},{6,4},{7,5},{8,10},{9,11},{10,... | collective-permute-start | bytes 967688 | tf_op jit(solution)/shard_map/ppermute | solution.py:660
  9.4 12.5 %copy-start.2 = (bf16[96,768]{1,0:T(8,128)(2,1)S(1)}, bf16[96,768]{1,0:T(8,128)(2,1)}, u32[]{:S(2)}) copy-start(bf16[96,768]{1,0:T(8,128)(2,1)} %refs_0_.3) | copy-start | bytes 442372
  9.4 33.7 %copy-start.1 = (bf16[3,70,768]{2,1,0:T(8,128)(2,1)S(1)}, bf16[3,70,768]{2,1,0:T(8,128)(2,1)}, u32[]{:S(2)}) copy-start(bf16[3,70,768]{2,1,0:T(8,128)(2,1)} %refs_2_.2) | copy-start | bytes 967684
  12.5 8.6 %collective-permute-start.2 = (bf16[96,384]{1,0:T(8,128)(2,1)S(1)}, bf16[96,384]{1,0:T(8,128)(2,1)S(1)}, u32[]{:S(2)}, u32[]{:S(2)}) collective-permute-start(bf16[96,384]{1,0:T(8,128)(2,1)S(1)} %get-tuple-element.126), channel_id=1, source_target_pairs={{0,0},{1,8},{2,16},{3,24},{4,4},{5,12},{6,20},{7,28},{8,1},{9,9},{... | collective-permute-start | bytes 221192 | tf_op jit(solution)/shard_map/ppermute | solution.py:700
  18.0 8.0 %collective-permute-start.12 = (bf16[96,640]{1,0:T(8,128)(2,1)S(1)}, bf16[96,640]{1,0:T(8,128)(2,1)S(1)}, u32[]{:S(2)}, u32[]{:S(2)}) collective-permute-start(bf16[96,640]{1,0:T(8,128)(2,1)S(1)} %collective-permute-done.8.refs_6_), channel_id=1, source_target_pairs={{0,4},{4,0},{8,12},{12,8},{16,20},{20,16},{24,28},{28,24},{1,5},{5... | collective-permute-start | bytes 368648 | tf_op jit(solution)/shard_map/ppermute | solution.py:663
  18.5 7.5 %collective-permute-start.3 = (bf16[96,384]{1,0:T(8,128)(2,1)S(1)}, bf16[96,384]{1,0:T(8,128)(2,1)S(1)}, u32[]{:S(2)}, u32[]{:S(2)}) collective-permute-start(bf16[96,384]{1,0:T(8,128)(2,1)S(1)} %get-tuple-element.127), channel_id=1, source_target_pairs={{0,4},{1,12},{2,20},{3,28},{4,0},{5,8},{6,16},{7,24},{8,5},{9,13},... | collective-permute-start | bytes 221192 | tf_op jit(solution)/shard_map/ppermute | solution.py:700
  20.4 8.4 %collective-permute-start.11 = (bf16[96,640]{1,0:T(8,128)(2,1)S(1)}, bf16[96,640]{1,0:T(8,128)(2,1)S(1)}, u32[]{:S(2)}, u32[]{:S(2)}) collective-permute-start(bf16[96,640]{1,0:T(8,128)(2,1)S(1)} %collective-permute-done.7.refs_5_), channel_id=1, source_target_pairs={{0,4},{4,0},{8,12},{12,8},{16,20},{20,16},{24,28},{28,24},{1,5},{5... | collective-permute-start | bytes 368648 | tf_op jit(solution)/shard_map/ppermute | solution.py:663
  21.1 11.2 %collective-permute-start.10 = (bf16[96,640]{1,0:T(8,128)(2,1)S(1)}, bf16[96,640]{1,0:T(8,128)(2,1)S(1)}, u32[]{:S(2)}, u32[]{:S(2)}) collective-permute-start(bf16[96,640]{1,0:T(8,128)(2,1)S(1)} %collective-permute-done.1.refs_4_), channel_id=1, source_target_pairs={{0,4},{4,0},{8,12},{12,8},{16,20},{20,16},{24,28},{28,24},{1,5},{5... | collective-permute-start | bytes 368648 | tf_op jit(solution)/shard_map/ppermute | solution.py:663
  26.0 6.8 %collective-permute-start.13 = (bf16[144,768]{1,0:T(8,128)(2,1)S(1)}, bf16[144,768]{1,0:T(8,128)(2,1)S(1)}, u32[]{:S(2)}, u32[]{:S(2)}) collective-permute-start(bf16[144,768]{1,0:T(8,128)(2,1)S(1)} %pack_up.1.refs_0_), channel_id=1, source_target_pairs={{0,8},{4,12},{8,16},{12,20},{16,24},{20,28},{24,0},{28,4},{1,9},{5... | collective-permute-start | bytes 663560 | tf_op jit(solution)/shard_map/ppermute | solution.py:666
  26.0 17.1 %collective-permute-start.4 = (bf16[3,70,768]{2,1,0:T(8,128)(2,1)S(1)}, bf16[3,70,768]{2,1,0:T(8,128)(2,1)S(1)}, u32[]{:S(2)}, u32[]{:S(2)}) collective-permute-start(bf16[3,70,768]{2,1,0:T(8,128)(2,1)S(1)} %copy-done), channel_id=1, source_target_pairs={{0,1},{1,0},{2,3},{3,2},{4,5},{5,4},{6,7},{7,6},{8,9},{9,8},{10,11... | collective-permute-start | bytes 967688 | tf_op jit(solution)/shard_map/ppermute | solution.py:660
  28.8 13.1 %collective-permute-start.15 = (bf16[144,768]{1,0:T(8,128)(2,1)S(1)}, bf16[144,768]{1,0:T(8,128)(2,1)S(1)}, u32[]{:S(2)}, u32[]{:S(2)}) collective-permute-start(bf16[144,768]{1,0:T(8,128)(2,1)S(1)} %pack_up.1.refs_0_), channel_id=1, source_target_pairs={{0,24},{4,28},{8,0},{12,4},{16,8},{20,12},{24,16},{28,20},{1,25},{... | collective-permute-start | bytes 663560 | tf_op jit(solution)/shard_map/ppermute | solution.py:666
  32.3 9.6 %collective-permute-start.16 = (bf16[144,768]{1,0:T(8,128)(2,1)S(1)}, bf16[144,768]{1,0:T(8,128)(2,1)S(1)}, u32[]{:S(2)}, u32[]{:S(2)}) collective-permute-start(bf16[144,768]{1,0:T(8,128)(2,1)S(1)} %pack_up.1.refs_0_), channel_id=1, source_target_pairs={{0,4},{4,0},{8,12},{12,8},{16,20},{20,16},{24,28},{28,24},{1,5},{5... | collective-permute-start | bytes 663560 | tf_op jit(solution)/shard_map/ppermute | solution.py:663
  32.3 19.0 %collective-permute-start.6 = (bf16[3,70,768]{2,1,0:T(8,128)(2,1)S(1)}, bf16[3,70,768]{2,1,0:T(8,128)(2,1)S(1)}, u32[]{:S(2)}, u32[]{:S(2)}) collective-permute-start(bf16[3,70,768]{2,1,0:T(8,128)(2,1)S(1)} %collective-permute-done.5.refs_2_), channel_id=1, source_target_pairs={{0,1},{1,0},{2,3},{3,2},{4,5},{5,4},{6,7},{7,6},{8,9},{9,8},{10,11... | collective-permute-start | bytes 967688 | tf_op jit(solution)/shard_map/ppermute | solution.py:660
  32.8 10.3 %collective-permute-start.14 = (bf16[144,768]{1,0:T(8,128)(2,1)S(1)}, bf16[144,768]{1,0:T(8,128)(2,1)S(1)}, u32[]{:S(2)}, u32[]{:S(2)}) collective-permute-start(bf16[144,768]{1,0:T(8,128)(2,1)S(1)} %collective-permute-done.13.refs_1_), channel_id=1, source_target_pairs={{0,8},{4,12},{8,16},{12,20},{16,24},{20,28},{24,0},{28,4},{1,9},{5... | collective-permute-start | bytes 663560 | tf_op jit(solution)/shard_map/ppermute | solution.py:666
  32.8 19.5 %copy-start.3 = (bf16[96,640]{1,0:T(8,128)(2,1)S(1)}, bf16[96,640]{1,0:T(8,128)(2,1)}, u32[]{:S(2)}) copy-start(bf16[96,640]{1,0:T(8,128)(2,1)} %pack.1.refs_3_) | copy-start | bytes 368644
  32.8 19.5 %copy-start.5 = (s32[3,40]{1,0:T(4,128)S(1)}, s32[3,40]{1,0:T(4,128)}, u32[]{:S(2)}) copy-start(s32[3,40]{1,0:T(4,128)} %refs_0_.5) | copy-start | bytes 1444
  32.8 19.5 %copy-start.6 = (s32[3]{0:T(128)S(1)}, s32[3]{0:T(128)}, u32[]{:S(2)}) copy-start(s32[3]{0:T(128)} %refs_1_.5) | copy-start | bytes 40
  41.9 6.7 %collective-permute-start.27 = (bf16[96,768]{1,0:T(8,128)(2,1)S(1)}, bf16[96,768]{1,0:T(8,128)(2,1)S(1)}, u32[]{:S(2)}, u32[]{:S(2)}) collective-permute-start(bf16[96,768]{1,0:T(8,128)(2,1)S(1)} %join_down.1.refs_3_), channel_id=1, source_target_pairs={{0,8},{4,12},{8,16},{12,20},{16,24},{20,28},{24,0},{28,4},{1,9},{5... | collective-permute-start | bytes 442376 | tf_op jit(solution)/shard_map/ppermute | solution.py:666
  41.9 6.7 %collective-permute-start.19 = (bf16[144,768]{1,0:T(8,128)(2,1)S(1)}, bf16[144,768]{1,0:T(8,128)(2,1)S(1)}, u32[]{:S(2)}, u32[]{:S(2)}) collective-permute-start(bf16[144,768]{1,0:T(8,128)(2,1)S(1)} %collective-permute-done.15.refs_3_), channel_id=1, source_target_pairs={{0,4},{4,0},{8,12},{12,8},{16,20},{20,16},{24,28},{28,24},{1,5},{5... | collective-permute-start | bytes 663560 | tf_op jit(solution)/shard_map/ppermute | solution.py:663
  43.0 19.2 %collective-permute-start.22 = (bf16[3,70,768]{2,1,0:T(8,128)(2,1)S(1)}, bf16[3,70,768]{2,1,0:T(8,128)(2,1)S(1)}, u32[]{:S(2)}, u32[]{:S(2)}) collective-permute-start(bf16[3,70,768]{2,1,0:T(8,128)(2,1)S(1)} %copy-done.1), channel_id=1, source_target_pairs={{0,2},{1,3},{2,0},{3,1},{4,6},{5,7},{6,4},{7,5},{8,10},{9,11},{10,... | collective-permute-start | bytes 967688 | tf_op jit(solution)/shard_map/ppermute | solution.py:660
  43.1 15.9 %collective-permute-start.17 = (bf16[144,768]{1,0:T(8,128)(2,1)S(1)}, bf16[144,768]{1,0:T(8,128)(2,1)S(1)}, u32[]{:S(2)}, u32[]{:S(2)}) collective-permute-start(bf16[144,768]{1,0:T(8,128)(2,1)S(1)} %collective-permute-done.13.refs_1_), channel_id=1, source_target_pairs={{0,4},{4,0},{8,12},{12,8},{16,20},{20,16},{24,28},{28,24},{1,5},{5... | collective-permute-start | bytes 663560 | tf_op jit(solution)/shard_map/ppermute | solution.py:663
  48.6 13.6 %collective-permute-start.18 = (bf16[144,768]{1,0:T(8,128)(2,1)S(1)}, bf16[144,768]{1,0:T(8,128)(2,1)S(1)}, u32[]{:S(2)}, u32[]{:S(2)}) collective-permute-start(bf16[144,768]{1,0:T(8,128)(2,1)S(1)} %collective-permute-done.14.refs_2_), channel_id=1, source_target_pairs={{0,4},{4,0},{8,12},{12,8},{16,20},{20,16},{24,28},{28,24},{1,5},{5... | collective-permute-start | bytes 663560 | tf_op jit(solution)/shard_map/ppermute | solution.py:663
  48.6 13.9 %collective-permute-start.29 = (bf16[96,768]{1,0:T(8,128)(2,1)S(1)}, bf16[96,768]{1,0:T(8,128)(2,1)S(1)}, u32[]{:S(2)}, u32[]{:S(2)}) collective-permute-start(bf16[96,768]{1,0:T(8,128)(2,1)S(1)} %join_down.1.refs_3_), channel_id=1, source_target_pairs={{0,24},{4,28},{8,0},{12,4},{16,8},{20,12},{24,16},{28,20},{1,25},{... | collective-permute-start | bytes 442376 | tf_op jit(solution)/shard_map/ppermute | solution.py:666
  51.3 11.7 %collective-permute-start.28 = (bf16[96,768]{1,0:T(8,128)(2,1)S(1)}, bf16[96,768]{1,0:T(8,128)(2,1)S(1)}, u32[]{:S(2)}, u32[]{:S(2)}) collective-permute-start(bf16[96,768]{1,0:T(8,128)(2,1)S(1)} %collective-permute-done.27.refs_0_.refs_4_), channel_id=1, source_target_pairs={{0,8},{4,12},{8,16},{12,20},{16,24},{20,28},{24,0},{28,4},{1,9},{5... | collective-permute-start | bytes 442376 | tf_op jit(solution)/shard_map/ppermute | solution.py:666
  58.9 4.6 %collective-permute-start.21 = (bf16[3,70,768]{2,1,0:T(8,128)(2,1)S(1)}, bf16[3,70,768]{2,1,0:T(8,128)(2,1)S(1)}, u32[]{:S(2)}, u32[]{:S(2)}) collective-permute-start(bf16[3,70,768]{2,1,0:T(8,128)(2,1)S(1)} %copy-done.1), channel_id=1, source_target_pairs={{0,1},{1,0},{2,3},{3,2},{4,5},{5,4},{6,7},{7,6},{8,9},{9,8},{10,11... | collective-permute-start | bytes 967688 | tf_op jit(solution)/shard_map/ppermute | solution.py:660
  62.2 10.2 %collective-permute-start.25 = (bf16[480,384]{1,0:T(8,128)(2,1)S(1)}, bf16[480,384]{1,0:T(8,128)(2,1)S(1)}, u32[]{:S(2)}, u32[]{:S(2)}) collective-permute-start(bf16[480,384]{1,0:T(8,128)(2,1)S(1)} %get-tuple-element.134.refs_4_), channel_id=1, source_target_pairs={{0,2},{1,3},{2,0},{3,1},{4,6},{5,7},{6,4},{7,5},{8,10},{9,11},{10,... | collective-permute-start | bytes 1105928 | tf_op jit(solution)/shard_map/ppermute | solution.py:660
  62.2 11.0 %collective-permute-start.23 = (bf16[3,70,768]{2,1,0:T(8,128)(2,1)S(1)}, bf16[3,70,768]{2,1,0:T(8,128)(2,1)S(1)}, u32[]{:S(2)}, u32[]{:S(2)}) collective-permute-start(bf16[3,70,768]{2,1,0:T(8,128)(2,1)S(1)} %collective-permute-done.22.refs_4_), channel_id=1, source_target_pairs={{0,1},{1,0},{2,3},{3,2},{4,5},{5,4},{6,7},{7,6},{8,9},{9,8},{10,11... | collective-permute-start | bytes 967688 | tf_op jit(solution)/shard_map/ppermute | solution.py:660
  62.5 11.1 %collective-permute-start.20 = (bf16[768,384]{1,0:T(8,128)(2,1)S(1)}, bf16[768,384]{1,0:T(8,128)(2,1)S(1)}, u32[]{:S(2)}, u32[]{:S(2)}) collective-permute-start(bf16[768,384]{1,0:T(8,128)(2,1)S(1)} %get-tuple-element.131.refs_0_), channel_id=1, source_target_pairs={{0,1},{1,0},{2,3},{3,2},{4,5},{5,4},{6,7},{7,6},{8,9},{9,8},{10,11... | collective-permute-start | bytes 1769480 | tf_op jit(solution)/shard_map/ppermute | solution.py:660
  63.1 18.6 %collective-permute-start.31 = (bf16[3,96,768]{2,1,0:T(8,128)(2,1)S(1)}, bf16[3,96,768]{2,1,0:T(8,128)(2,1)S(1)}, u32[]{:S(2)}, u32[]{:S(2)}) collective-permute-start(bf16[3,96,768]{2,1,0:T(8,128)(2,1)S(1)} %stack_down.1), channel_id=1, source_target_pairs={{0,4},{4,0},{8,12},{12,8},{16,20},{20,16},{24,28},{28,24},{1,5},{5... | collective-permute-start | bytes 1327112 | tf_op jit(solution)/shard_map/ppermute | solution.py:663
  63.5 10.7 %collective-permute-start.24 = (bf16[480,384]{1,0:T(8,128)(2,1)S(1)}, bf16[480,384]{1,0:T(8,128)(2,1)S(1)}, u32[]{:S(2)}, u32[]{:S(2)}) collective-permute-start(bf16[480,384]{1,0:T(8,128)(2,1)S(1)} %get-tuple-element.134.refs_4_), channel_id=1, source_target_pairs={{0,1},{1,0},{2,3},{3,2},{4,5},{5,4},{6,7},{7,6},{8,9},{9,8},{10,11... | collective-permute-start | bytes 1105928 | tf_op jit(solution)/shard_map/ppermute | solution.py:660
  72.4 2.2 %collective-permute-start.26 = (bf16[480,384]{1,0:T(8,128)(2,1)S(1)}, bf16[480,384]{1,0:T(8,128)(2,1)S(1)}, u32[]{:S(2)}, u32[]{:S(2)}) collective-permute-start(bf16[480,384]{1,0:T(8,128)(2,1)S(1)} %collective-permute-done.25.refs_6_), channel_id=1, source_target_pairs={{0,1},{1,0},{2,3},{3,2},{4,5},{5,4},{6,7},{7,6},{8,9},{9,8},{10,11... | collective-permute-start | bytes 1105928 | tf_op jit(solution)/shard_map/ppermute | solution.py:660
  73.2 8.4 %collective-permute-start.30 = (bf16[96,768]{1,0:T(8,128)(2,1)S(1)}, bf16[96,768]{1,0:T(8,128)(2,1)S(1)}, u32[]{:S(2)}, u32[]{:S(2)}) collective-permute-start(bf16[96,768]{1,0:T(8,128)(2,1)S(1)} %join_down.1.refs_3_), channel_id=1, source_target_pairs={{0,4},{4,0},{8,12},{12,8},{16,20},{20,16},{24,28},{28,24},{1,5},{5... | collective-permute-start | bytes 442376 | tf_op jit(solution)/shard_map/ppermute | solution.py:663
  85.0 2.3 %collective-permute-start.32 = (bf16[2,240,768]{2,1,0:T(8,128)(2,1)S(1)}, bf16[2,240,768]{2,1,0:T(8,128)(2,1)S(1)}, u32[]{:S(2)}, u32[]{:S(2)}) collective-permute-start(bf16[2,240,768]{2,1,0:T(8,128)(2,1)S(1)} %get-tuple-element.146), channel_id=1, source_target_pairs={{0,1},{1,0},{2,3},{3,2},{4,5},{5,4},{6,7},{7,6},{8,9},{9,8},{10,11... | collective-permute-start | bytes 2211848 | tf_op jit(solution)/shard_map/ppermute | solution.py:660
  85.4 17.8 %collective-permute-start.34 = (bf16[4,96,768]{2,1,0:T(8,128)(2,1)S(1)}, bf16[4,96,768]{2,1,0:T(8,128)(2,1)S(1)}, u32[]{:S(2)}, u32[]{:S(2)}) collective-permute-start(bf16[4,96,768]{2,1,0:T(8,128)(2,1)S(1)} %get-tuple-element.159), channel_id=1, source_target_pairs={{0,4},{4,0},{8,12},{12,8},{16,20},{20,16},{24,28},{28,24},{1,5},{5... | collective-permute-start | bytes 1769480 | tf_op jit(solution)/shard_map/ppermute | solution.py:663
  87.4 9.9 %collective-permute-start.33 = (bf16[240,768]{1,0:T(8,128)(2,1)S(1)}, bf16[240,768]{1,0:T(8,128)(2,1)S(1)}, u32[]{:S(2)}, u32[]{:S(2)}) collective-permute-start(bf16[240,768]{1,0:T(8,128)(2,1)S(1)} %pair2.1), channel_id=1, source_target_pairs={{0,2},{1,3},{2,0},{3,1},{4,6},{5,7},{6,4},{7,5},{8,10},{9,11},{10,... | collective-permute-start | bytes 1105928 | tf_op jit(solution)/shard_map/ppermute | solution.py:660
  89.0 29.2 %collective-permute-start.38 = (bf16[4,96,768]{2,1,0:T(8,128)(2,1)S(1)}, bf16[4,96,768]{2,1,0:T(8,128)(2,1)S(1)}, u32[]{:S(2)}, u32[]{:S(2)}) collective-permute-start(bf16[4,96,768]{2,1,0:T(8,128)(2,1)S(1)} %get-tuple-element.169), channel_id=1, source_target_pairs={{0,4},{4,0},{8,12},{12,8},{16,20},{20,16},{24,28},{28,24},{1,5},{5... | collective-permute-start | bytes 1769480 | tf_op jit(solution)/shard_map/ppermute | solution.py:663
  98.4 5.2 %collective-permute-start.35 = (bf16[240,384]{1,0:T(8,128)(2,1)S(1)}, bf16[240,384]{1,0:T(8,128)(2,1)S(1)}, u32[]{:S(2)}, u32[]{:S(2)}) collective-permute-start(bf16[240,384]{1,0:T(8,128)(2,1)S(1)} %get-tuple-element.162), channel_id=1, source_target_pairs={{0,1},{1,0},{2,3},{3,2},{4,5},{5,4},{6,7},{7,6},{8,9},{9,8},{10,11... | collective-permute-start | bytes 552968 | tf_op jit(solution)/shard_map/ppermute | solution.py:660
  99.7 7.6 %collective-permute-start.36 = (bf16[240,384]{1,0:T(8,128)(2,1)S(1)}, bf16[240,384]{1,0:T(8,128)(2,1)S(1)}, u32[]{:S(2)}, u32[]{:S(2)}) collective-permute-start(bf16[240,384]{1,0:T(8,128)(2,1)S(1)} %get-tuple-element.163), channel_id=1, source_target_pairs={{0,2},{1,3},{2,0},{3,1},{4,6},{5,7},{6,4},{7,5},{8,10},{9,11},{10,... | collective-permute-start | bytes 552968 | tf_op jit(solution)/shard_map/ppermute | solution.py:660
  99.7 10.6 %collective-permute-start.37 = (bf16[240,384]{1,0:T(8,128)(2,1)S(1)}, bf16[240,384]{1,0:T(8,128)(2,1)S(1)}, u32[]{:S(2)}, u32[]{:S(2)}) collective-permute-start(bf16[240,384]{1,0:T(8,128)(2,1)S(1)} %get-tuple-element.164), channel_id=1, source_target_pairs={{0,3},{1,2},{2,1},{3,0},{4,7},{5,6},{6,5},{7,4},{8,11},{9,10},{10,... | collective-permute-start | bytes 552968 | tf_op jit(solution)/shard_map/ppermute | solution.py:660
  103.4 18.2 %collective-permute-start.40 = (bf16[96,768]{1,0:T(8,128)(2,1)S(1)}, bf16[96,768]{1,0:T(8,128)(2,1)S(1)}, u32[]{:S(2)}, u32[]{:S(2)}) collective-permute-start(bf16[96,768]{1,0:T(8,128)(2,1)S(1)} %get-tuple-element.174), channel_id=1, source_target_pairs={{0,8},{4,12},{8,16},{12,20},{16,24},{20,28},{24,0},{28,4},{1,9},{5... | collective-permute-start | bytes 442376 | tf_op jit(solution)/shard_map/ppermute | solution.py:666
  103.5 18.0 %collective-permute-start.41 = (bf16[96,768]{1,0:T(8,128)(2,1)S(1)}, bf16[96,768]{1,0:T(8,128)(2,1)S(1)}, u32[]{:S(2)}, u32[]{:S(2)}) collective-permute-start(bf16[96,768]{1,0:T(8,128)(2,1)S(1)} %get-tuple-element.175), channel_id=1, source_target_pairs={{0,16},{4,20},{8,24},{12,28},{16,0},{20,4},{24,8},{28,12},{1,17},{... | collective-permute-start | bytes 442376 | tf_op jit(solution)/shard_map/ppermute | solution.py:666
  107.3 14.3 %collective-permute-start.42 = (bf16[96,768]{1,0:T(8,128)(2,1)S(1)}, bf16[96,768]{1,0:T(8,128)(2,1)S(1)}, u32[]{:S(2)}, u32[]{:S(2)}) collective-permute-start(bf16[96,768]{1,0:T(8,128)(2,1)S(1)} %get-tuple-element.176), channel_id=1, source_target_pairs={{0,24},{4,28},{8,0},{12,4},{16,8},{20,12},{24,16},{28,20},{1,25},{... | collective-permute-start | bytes 442376 | tf_op jit(solution)/shard_map/ppermute | solution.py:666
  113.4 7.9 %collective-permute-start.39 = (bf16[4,96,384]{2,1,0:T(8,128)(2,1)S(1)}, bf16[4,96,384]{2,1,0:T(8,128)(2,1)S(1)}, u32[]{:S(2)}, u32[]{:S(2)}) collective-permute-start(bf16[4,96,384]{2,1,0:T(8,128)(2,1)S(1)} %get-tuple-element.171), channel_id=1, source_target_pairs={{0,4},{4,0},{8,12},{12,8},{16,20},{20,16},{24,28},{28,24},{1,5},{5... | collective-permute-start | bytes 884744 | tf_op jit(solution)/shard_map/ppermute | solution.py:663
  123.8 12.5 %collective-permute-start.46 = (bf16[2,480,768]{2,1,0:T(8,128)(2,1)S(1)}, bf16[2,480,768]{2,1,0:T(8,128)(2,1)S(1)}, u32[]{:S(2)}, u32[]{:S(2)}) collective-permute-start(bf16[2,480,768]{2,1,0:T(8,128)(2,1)S(1)} %get-tuple-element.192), channel_id=1, source_target_pairs={{0,1},{1,0},{2,3},{3,2},{4,5},{5,4},{6,7},{7,6},{8,9},{9,8},{10,11... | collective-permute-start | bytes 4423688 | tf_op jit(solution)/shard_map/ppermute | solution.py:660
  126.6 18.3 %collective-permute-start.43 = (bf16[4,96,384]{2,1,0:T(8,128)(2,1)S(1)}, bf16[4,96,384]{2,1,0:T(8,128)(2,1)S(1)}, u32[]{:S(2)}, u32[]{:S(2)}) collective-permute-start(bf16[4,96,384]{2,1,0:T(8,128)(2,1)S(1)} %get-tuple-element.189), channel_id=1, source_target_pairs={{0,4},{4,0},{8,12},{12,8},{16,20},{20,16},{24,28},{28,24},{1,5},{5... | collective-permute-start | bytes 884744 | tf_op jit(solution)/shard_map/ppermute | solution.py:663
  127.4 1.2 collective-permute-start.44
  128.6 7.7 %collective-permute-start.45 = (f32[16,768]{1,0:T(8,128)S(1)}, f32[16,768]{1,0:T(8,128)S(1)}, u32[]{:S(2)}, u32[]{:S(2)}) collective-permute-start(f32[16,768]{1,0:T(8,128)S(1)} %add_core.1.refs_0_), channel_id=1, source_target_pairs={{0,2},{1,3},{2,0},{3,1},{4,6},{5,7},{6,4},{7,5},{8,10},{9,11},{10,... | collective-permute-start | bytes 147464 | tf_op jit(solution)/shard_map/ppermute | solution.py:660
  128.7 9.2 %collective-permute-start.52 = (bf16[96,384]{1,0:T(8,128)(2,1)S(1)}, bf16[96,384]{1,0:T(8,128)(2,1)S(1)}, u32[]{:S(2)}, u32[]{:S(2)}) collective-permute-start(bf16[96,384]{1,0:T(8,128)(2,1)S(1)} %get-tuple-element.177), channel_id=1, source_target_pairs={{0,0},{1,8},{2,16},{3,24},{4,4},{5,12},{6,20},{7,28},{8,1},{9,9},{... | collective-permute-start | bytes 221192 | tf_op jit(solution)/shard_map/ppermute | solution.py:700
  135.8 8.3 %collective-permute-start.53 = (bf16[96,384]{1,0:T(8,128)(2,1)S(1)}, bf16[96,384]{1,0:T(8,128)(2,1)S(1)}, u32[]{:S(2)}, u32[]{:S(2)}) collective-permute-start(bf16[96,384]{1,0:T(8,128)(2,1)S(1)} %get-tuple-element.207), channel_id=1, source_target_pairs={{0,4},{1,12},{2,20},{3,28},{4,0},{5,8},{6,16},{7,24},{8,5},{9,13},... | collective-permute-start | bytes 221192 | tf_op jit(solution)/shard_map/ppermute | solution.py:700
  136.5 10.0 %collective-permute-start.47 = (f32[16,768]{1,0:T(8,128)S(1)}, f32[16,768]{1,0:T(8,128)S(1)}, u32[]{:S(2)}, u32[]{:S(2)}) collective-permute-start(f32[16,768]{1,0:T(8,128)S(1)} %add_far.1.refs_2_), channel_id=1, source_target_pairs={{0,4},{4,0},{8,12},{12,8},{16,20},{20,16},{24,28},{28,24},{1,5},{5... | collective-permute-start | bytes 147464 | tf_op jit(solution)/shard_map/ppermute | solution.py:663
  137.3 9.4 %collective-permute-start.48 = (bf16[144,768]{1,0:T(8,128)(2,1)S(1)}, bf16[144,768]{1,0:T(8,128)(2,1)S(1)}, u32[]{:S(2)}, u32[]{:S(2)}) collective-permute-start(bf16[144,768]{1,0:T(8,128)(2,1)S(1)} %get-tuple-element.197), channel_id=1, source_target_pairs={{0,8},{4,12},{8,16},{12,20},{16,24},{20,28},{24,0},{28,4},{1,9},{5... | collective-permute-start | bytes 663560 | tf_op jit(solution)/shard_map/ppermute | solution.py:666
  137.9 17.6 %collective-permute-start.49 = (bf16[144,768]{1,0:T(8,128)(2,1)S(1)}, bf16[144,768]{1,0:T(8,128)(2,1)S(1)}, u32[]{:S(2)}, u32[]{:S(2)}) collective-permute-start(bf16[144,768]{1,0:T(8,128)(2,1)S(1)} %get-tuple-element.198), channel_id=1, source_target_pairs={{0,16},{4,20},{8,24},{12,28},{16,0},{20,4},{24,8},{28,12},{1,17},{... | collective-permute-start | bytes 663560 | tf_op jit(solution)/shard_map/ppermute | solution.py:666
  144.1 20.7 %collective-permute-start.50 = (bf16[144,768]{1,0:T(8,128)(2,1)S(1)}, bf16[144,768]{1,0:T(8,128)(2,1)S(1)}, u32[]{:S(2)}, u32[]{:S(2)}) collective-permute-start(bf16[144,768]{1,0:T(8,128)(2,1)S(1)} %get-tuple-element.199), channel_id=1, source_target_pairs={{0,24},{4,28},{8,0},{12,4},{16,8},{20,12},{24,16},{28,20},{1,25},{... | collective-permute-start | bytes 663560 | tf_op jit(solution)/shard_map/ppermute | solution.py:666
  144.8 25.3 %collective-permute-start.51 = (bf16[480,768]{1,0:T(8,128)(2,1)S(1)}, bf16[480,768]{1,0:T(8,128)(2,1)S(1)}, u32[]{:S(2)}, u32[]{:S(2)}) collective-permute-start(bf16[480,768]{1,0:T(8,128)(2,1)S(1)} %pair1.1), channel_id=1, source_target_pairs={{0,2},{1,3},{2,0},{3,1},{4,6},{5,7},{6,4},{7,5},{8,10},{9,11},{10,... | collective-permute-start | bytes 2211848 | tf_op jit(solution)/shard_map/ppermute | solution.py:660
  146.6 19.1 %collective-permute-start.55 = (bf16[128,384]{1,0:T(8,128)(2,1)S(1)}, bf16[128,384]{1,0:T(8,128)(2,1)S(1)}, u32[]{:S(2)}, u32[]{:S(2)}) collective-permute-start(bf16[128,384]{1,0:T(8,128)(2,1)S(1)} %get-tuple-element.212), channel_id=1, source_target_pairs={{0,16},{4,20},{8,24},{12,28},{16,0},{20,4},{24,8},{28,12},{1,17},{... | collective-permute-start | bytes 294920 | tf_op jit(solution)/shard_map/ppermute | solution.py:666
  146.7 19.0 %collective-permute-start.56 = (bf16[128,384]{1,0:T(8,128)(2,1)S(1)}, bf16[128,384]{1,0:T(8,128)(2,1)S(1)}, u32[]{:S(2)}, u32[]{:S(2)}) collective-permute-start(bf16[128,384]{1,0:T(8,128)(2,1)S(1)} %get-tuple-element.213), channel_id=1, source_target_pairs={{0,24},{4,28},{8,0},{12,4},{16,8},{20,12},{24,16},{28,20},{1,25},{... | collective-permute-start | bytes 294920 | tf_op jit(solution)/shard_map/ppermute | solution.py:666
  155.5 13.8 %collective-permute-start.54 = (bf16[128,384]{1,0:T(8,128)(2,1)S(1)}, bf16[128,384]{1,0:T(8,128)(2,1)S(1)}, u32[]{:S(2)}, u32[]{:S(2)}) collective-permute-start(bf16[128,384]{1,0:T(8,128)(2,1)S(1)} %get-tuple-element.211), channel_id=1, source_target_pairs={{0,8},{4,12},{8,16},{12,20},{16,24},{20,28},{24,0},{28,4},{1,9},{5... | collective-permute-start | bytes 294920 | tf_op jit(solution)/shard_map/ppermute | solution.py:666
  (1 other events, 6.9 us)
